TPU v7x, 32 devices: a whole 2x2x4 slice. The times are simulated.
32 devices in a mesh: groups: 2 (over y), dom: 4 (over z), sub: 2 (over x), chip: 2 (over core).
Axes of the slice: x: 2, y: 2, z: 4, core: 2. Of those that a mesh axis runs over, the one named last changes fastest.
Arguments:
- fine_nodes: bfloat16 [65536, 128], P(('groups', 'dom', 'sub', 'chip')), parts along dimension 0, may hold values from -6 to 6
- fine_src: int32 [512, 768], P(('groups', 'dom', 'sub', 'chip')), parts along dimension 0, may hold values from 0 to 3071, as said below
- fine_dst: int32 [512, 768], P(('groups', 'dom', 'sub', 'chip')), parts along dimension 0, may hold values from -1 to 127
- halo_send: int32 [32, 4, 256], P(('groups', 'dom', 'sub', 'chip')), parts along dimension 0, may hold values from 0 to 2048, as said below
- pool_send: int32 [32, 4, 64], P(('groups', 'dom', 'sub', 'chip')), parts along dimension 0, may hold values from 0 to 2048, as said below
- coarse_src: int32 [64, 768], P(('groups', 'dom', 'sub', 'chip')), parts along dimension 0, may hold values from 0 to 767, as said below
- coarse_dst: int32 [64, 768], P(('groups', 'dom', 'sub', 'chip')), parts along dimension 0, may hold values from -1 to 127, as said below
- coarse_send: int32 [32, 4, 128], P(('groups', 'dom', 'sub', 'chip')), parts along dimension 0, may hold values from 0 to 256, as said below
- prolong_idx: int32 [65536], P(('groups', 'dom', 'sub', 'chip')), parts along dimension 0, may hold values from 0 to 63, as said below
- fine_weights: bfloat16 [2, 4, 128, 128], replicated, may hold values from -0.5 to 0.5
- coarse_weights: bfloat16 [4, 128, 128], replicated, may hold values from -0.5 to 0.5
- prolong_weight: bfloat16 [128, 128], replicated, may hold values from -0.5 to 0.5
Outputs:
- fine_out: bfloat16 [65536, 128], P(('groups', 'dom', 'sub', 'chip')), parts along dimension 0
There are 2 independent parts, one for each index of `groups`. A program takes and returns all parts, laid end to end along the dimension named above; an argument that names none is the same for every part. Nothing has to cross between parts.
Inputs may be any that keep to these rules, and one draw needn't show every extreme that they name: `halo_send`: rows of a device (d, q) go only to partitions d + 1, d - 1 and d + 2 (cyclic over 4); each list names at most 256 live rows in front, the rest is 2048; some receiver gets 256 live rows from each of its three senders. `fine_src`: in block b the first 576 slots name own rows from s to s + w - 1, with w = min(384, 2048) and s = min(max(128 * b - 128, 0), 2048 - w); the other slots name live halo rows. `pool_send`: only devices whose q is a multiple of 4 are coarse owners; live rows stand in front, at most 64 to one owner, distinct rows of a device; in partition 0 the first owner is full from every source. `coarse_src`: only owners have coarse edges and send lists; senders name live coarse slots or live coarse halo rows. `coarse_dst`: empty slots hold -1; all slots of non-owners are empty. `coarse_send`: same partner pattern as the fine lists among owners, live coarse slots in front, at most 128; the rest is 256. `prolong_idx`: each entry names a row that the device sent to an owner.
All inputs are finite; a program needn't handle non-finite values.
Results may differ from a plain program's by a relative error of at most 0.0075.
Values may be sent and summed in bfloat16 or wider, within the bound.
No kernel may reach another device: no remote copies, remote signals or barrier semaphores. Data moves between devices by JAX's collectives and lax.ppermute only.
A program may use at most 64 MiB of HBM per device.

v0:
```python
import jax
import jax.numpy as jnp
from jax import lax
from jax.sharding import PartitionSpec as P


def layer_rest(latent, sender_terms, source_ids, target_ids, weights, windowed):
    feature_count = latent.shape[1]
    node_count = latent.shape[0]
    block_count = source_ids.shape[0]
    slot_count = source_ids.shape[1]
    local_count = slot_count * 3 // 4
    window = min(384, node_count)
    target_terms = jnp.dot(latent, weights[1], preferred_element_type=jnp.float32).astype(
        jnp.bfloat16
    )
    target_blocks = target_terms.reshape(block_count, 128, feature_count)
    columns = jnp.arange(128, dtype=jnp.int32)
    window_columns = jnp.arange(window, dtype=jnp.int32)
    block_ids = jnp.arange(block_count, dtype=jnp.int32)

    def one_block(block_sources, block_targets, block_terms, block_id):
        if windowed:
            start = jnp.clip(block_id * 128 - 128, 0, node_count - window)
            window_rows = lax.dynamic_slice_in_dim(sender_terms, start, window, 0)
            near_hot = (
                (block_sources[:local_count] - start)[:, None] == window_columns[None, :]
            ).astype(jnp.bfloat16)
            near_rows = jnp.dot(near_hot, window_rows, preferred_element_type=jnp.float32)
            far_rows = jnp.take(sender_terms, block_sources[local_count:], axis=0).astype(
                jnp.float32
            )
            picked = jnp.concatenate([near_rows, far_rows], axis=0)
        else:
            picked = jnp.take(sender_terms, block_sources, axis=0).astype(jnp.float32)
        one_hot = (block_targets[:, None] == columns[None, :]).astype(jnp.bfloat16)
        target_rows = jnp.dot(one_hot, block_terms, preferred_element_type=jnp.float32)
        message = jax.nn.silu(picked + target_rows).astype(jnp.bfloat16)
        block_sum = lax.dot_general(
            one_hot, message, (((0,), (0,)), ((), ())), preferred_element_type=jnp.float32
        )
        return block_sum.astype(jnp.bfloat16)

    summed = jax.vmap(one_block)(source_ids, target_ids, target_blocks, block_ids).reshape(
        node_count, feature_count
    )
    update = jnp.dot(summed, weights[2], preferred_element_type=jnp.float32) + jnp.dot(
        latent, weights[3], preferred_element_type=jnp.float32
    )
    return (latent.astype(jnp.float32) + jax.nn.silu(update)).astype(jnp.bfloat16)


def move_halo(node_rows, send_list, level_name):
    feature_count = node_rows.shape[1]
    padded = jnp.concatenate([node_rows, jnp.zeros((1, feature_count), node_rows.dtype)], axis=0)
    buffer = jnp.take(padded, send_list, axis=0)
    if level_name == "fine":
        arrived_rows = lax.all_to_all(buffer, "dom", split_axis=0, concat_axis=0, tiled=True)
    else:
        arrived_rows = lax.all_to_all(buffer, "dom", split_axis=0, concat_axis=0, tiled=True)
    return arrived_rows.reshape(-1, feature_count)


def run_layer(latent, send_list, source_ids, target_ids, weights, level_name):
    halo_latent = move_halo(latent, send_list, level_name)
    extended = jnp.concatenate([latent, halo_latent], axis=0)
    sender_terms = jnp.dot(extended, weights[0], preferred_element_type=jnp.float32).astype(
        jnp.bfloat16
    )
    return layer_rest(latent, sender_terms, source_ids, target_ids, weights, level_name == "fine")


def owner_trade(buffer, direction_name):
    if direction_name == "gather_up":
        moved = lax.all_to_all(buffer, ("sub", "chip"), split_axis=0, concat_axis=0, tiled=True)
    else:
        moved = lax.all_to_all(buffer, ("sub", "chip"), split_axis=0, concat_axis=0, tiled=True)
    return moved


def prolong_rows(returned, prolong_idx):
    slot_columns = jnp.arange(returned.shape[0], dtype=jnp.int32)
    one_hot = (prolong_idx[:, None] == slot_columns[None, :]).astype(jnp.bfloat16)
    return jnp.dot(one_hot, returned, preferred_element_type=jnp.float32).astype(jnp.bfloat16)


def body(
    fine_nodes,
    fine_src,
    fine_dst,
    halo_send,
    pool_send,
    coarse_src,
    coarse_dst,
    coarse_send,
    prolong_idx,
    fine_weights,
    coarse_weights,
    prolong_weight,
):
    feature_count = fine_nodes.shape[1]
    first = run_layer(fine_nodes, halo_send[0], fine_src, fine_dst, fine_weights[0], "fine")
    padded = jnp.concatenate([first, jnp.zeros((1, feature_count), jnp.bfloat16)], axis=0)
    pooled = owner_trade(jnp.take(padded, pool_send[0], axis=0), "gather_up")
    coarse_rows = pooled.reshape(-1, feature_count)
    coarse = run_layer(
        coarse_rows, coarse_send[0], coarse_src, coarse_dst, coarse_weights, "coarse"
    )
    returned = owner_trade(coarse.reshape(pooled.shape), "send_back").reshape(-1, feature_count)
    picked = prolong_rows(returned, prolong_idx)
    lifted_terms = jnp.dot(picked, prolong_weight, preferred_element_type=jnp.float32)
    lifted = (first.astype(jnp.float32) + jax.nn.silu(lifted_terms)).astype(jnp.bfloat16)
    return run_layer(lifted, halo_send[0], fine_src, fine_dst, fine_weights[1], "fine")


def solution(mesh):
    return jax.shard_map(
        body,
        mesh=mesh,
        in_specs=(
            P(("groups", "dom", "sub", "chip"), None),
            P(("groups", "dom", "sub", "chip"), None),
            P(("groups", "dom", "sub", "chip"), None),
            P(("groups", "dom", "sub", "chip"), None, None),
            P(("groups", "dom", "sub", "chip"), None, None),
            P(("groups", "dom", "sub", "chip"), None),
            P(("groups", "dom", "sub", "chip"), None),
            P(("groups", "dom", "sub", "chip"), None, None),
            P(("groups", "dom", "sub", "chip")),
            P(),
            P(),
            P(),
        ),
        out_specs=P(("groups", "dom", "sub", "chip"), None),
        check_vma=False,
    )
```

profile of v0, /device:TPU:0, one launch (start us, length us, event | category | flops | bytes accessed | tf_op | source)
XLA Modules:
  0.0 185.0 jit_solution(10650057856030782777)
XLA Ops:
  2.6 3.2 %gather_fusion.3 = bf16[1024,128]{1,0:T(8,128)(2,1)S(1)} fusion(bf16[2049,128]{1,0:T(8,128)(2,1)S(1)} %concatenate.31, s32[1024]{0:T(1024)S(1)} %broadcast_clamp_fusion.1), kind=kCustom, calls=%fused_computation.clone | custom fusion | bytes 528384 | tf_op jit(solution)/shard_map/jit(_take)/gather | solution.py:56
  6.7 6.3 %all-to-all-start = ((bf16[4,256,128]{2,1,0:T(8,128)(2,1)}), bf16[4,256,128]{2,1,0:T(8,128)(2,1)S(1)}, u32[]{:S(2)}, u32[]{:S(2)}) async-start(bf16[4,256,128]{2,1,0:T(8,128)(2,1)} %broadcast_select_fusion.1), calls=%async_computation | async-start | bytes 524288 | tf_op jit(solution)/shard_map/all_to_all | solution.py:58
  13.9 8.0 %all-to-all-done = bf16[4,256,128]{2,1,0:T(8,128)(2,1)S(1)} async-done(((bf16[4,256,128]{2,1,0:T(8,128)(2,1)}), bf16[4,256,128]{2,1,0:T(8,128)(2,1)S(1)}, u32[]{:S(2)}, u32[]{:S(2)}) %all-to-all-start) | async-done | bytes 262176 | tf_op jit(solution)/shard_map/all_to_all | solution.py:58
  22.3 1.5 broadcast.157.clone
  23.8 30.6 %while.2 = (s32[]{:T(128)}, bf16[3072,128]{1,0:T(8,128)(2,1)S(1)}, s32[16,2]{0,1:T(2,128)S(1)}, bf16[16,384,128]{2,1,0:T(8,128)(2,1)}, s32[]{:T(128)}) while((s32[]{:T(128)}, bf16[3072,128]{1,0:T(8,128)(2,1)S(1)}, s32[16,2]{0,1:T(2,128)S(1)}, bf16[16,384,128]{2,1,0:T(8,128)(2,1)}, s32[]{:T(128)}) %tuple.29), condition=%wide.while_cond, body=%wide.while_body.sunk | while | flops 2 | bytes 197721 | solution.py:25
  33.9 1.3 bitcast_dynamic-update-slice_fusion.4
  35.8 1.3 bitcast_dynamic-update-slice_fusion.4
  39.7 1.3 bitcast_dynamic-update-slice_fusion.4
  47.3 1.3 bitcast_dynamic-update-slice_fusion.4
  54.4 9.2 %gather_fusion.4 = bf16[3072,128]{1,0:T(8,128)(2,1)S(1)} fusion(bf16[3072,128]{1,0:T(8,128)(2,1)S(1)} %get-tuple-element.119, s32[3072]{0:T(1024)S(1)} %broadcast_clamp_fusion), kind=kCustom, calls=%fused_computation.1.clone | custom fusion | bytes 1585152 | tf_op jit(solution)/shard_map/vmap(jit(_take))/gather | solution.py:30
  63.6 5.8 %fusion.1 = f32[16,576,128]{2,1,0:T(8,128)} fusion(bf16[16,384,128]{2,1,0:T(8,128)(2,1)} %get-tuple-element.14, s32[16,576]{1,0:T(8,128)S(1)} %slice_subtract_fusion), kind=kOutput, calls=%fused_computation.13 | convolution fusion | flops 909508608 | bytes 6328320 | tf_op jit(solution)/shard_map/vmap()/dot_general | solution.py:29
  69.3 1.5 select_convert_fusion.1
  70.8 6.6 %fusion.12 = bf16[16,128,128]{2,1,0:T(8,128)(2,1)S(1)} fusion(f32[16,192,128]{2,1,0:T(8,128)} %select_convert_fusion.1, f32[16,576,128]{2,1,0:T(8,128)} %fusion.1, bf16[16,128,128]{2,1,0:T(8,128)(2,1)S(1)} %bitcast.124, s32[16,768]{1,0:T(8,128)S(1)} %copy-done.8), kind=kOutput, calls=%fused_computation.37 | convolution fusion | flops 819724288 | bytes 7389184 | tf_op jit(solution)/shard_map/vmap()/dot_general | solution.py:39
  79.8 3.3 %all-to-all-start.1 = ((bf16[4,64,128]{2,1,0:T(8,128)(2,1)}), bf16[4,64,128]{2,1,0:T(8,128)(2,1)S(1)}, u32[]{:S(2)}, u32[]{:S(2)}) async-start(bf16[4,64,128]{2,1,0:T(8,128)(2,1)} %broadcast_select_fusion.3), calls=%async_computation.1 | async-start | bytes 131072 | tf_op jit(solution)/shard_map/all_to_all | solution.py:75
  83.1 4.1 %all-to-all-done.1 = bf16[4,64,128]{2,1,0:T(8,128)(2,1)S(1)} async-done(((bf16[4,64,128]{2,1,0:T(8,128)(2,1)}), bf16[4,64,128]{2,1,0:T(8,128)(2,1)S(1)}, u32[]{:S(2)}, u32[]{:S(2)}) %all-to-all-start.1) | async-done | bytes 65568 | tf_op jit(solution)/shard_map/all_to_all | solution.py:75
  87.2 1.3 gather_fusion.1
  89.3 3.3 %all-to-all-start.2 = ((bf16[4,128,128]{2,1,0:T(8,128)(2,1)}), bf16[4,128,128]{2,1,0:T(8,128)(2,1)S(1)}, u32[]{:S(2)}, u32[]{:S(2)}) async-start(bf16[4,128,128]{2,1,0:T(8,128)(2,1)} %broadcast_select_fusion.2), calls=%async_computation.2 | async-start | bytes 262144 | tf_op jit(solution)/shard_map/all_to_all | solution.py:60
  92.8 5.9 %all-to-all-done.2 = bf16[4,128,128]{2,1,0:T(8,128)(2,1)S(1)} async-done(((bf16[4,128,128]{2,1,0:T(8,128)(2,1)}), bf16[4,128,128]{2,1,0:T(8,128)(2,1)S(1)}, u32[]{:S(2)}, u32[]{:S(2)}) %all-to-all-start.2) | async-done | bytes 131104 | tf_op jit(solution)/shard_map/all_to_all | solution.py:60
  98.9 3.2 %gather_fusion.2 = bf16[1536,128]{1,0:T(8,128)(2,1)S(1)} fusion(bf16[768,128]{1,0:T(8,128)(2,1)S(1)} %convolution_convert_fusion.5, s32[2048]{0:T(1024)S(1)} %pad_clamp_fusion), kind=kCustom, calls=%fused_computation.6 | custom fusion | bytes 792576 | tf_op jit(solution)/shard_map/vmap(jit(_take))/gather | solution.py:35
  103.3 6.5 %all_to_all.25 = bf16[4,64,128]{2,1,0:T(8,128)(2,1)S(1)} all-to-all(bf16[4,64,128]{2,1,0:T(8,128)(2,1)S(1)} %bitcast.130), channel_id=1, replica_groups=mesh['groups'=2,'dom'=4,'sub'=2,'chip'=2] {'sub','chip'}, dimensions={0} | all-to-all | bytes 131072 | tf_op jit(solution)/shard_map/all_to_all | solution.py:77
  110.6 3.2 %gather_fusion.5 = bf16[1024,128]{1,0:T(8,128)(2,1)S(1)} fusion(bf16[2049,128]{1,0:T(8,128)(2,1)S(1)} %concatenate.38, s32[1024]{0:T(1024)S(1)} %broadcast_clamp_fusion.1), kind=kCustom, calls=%fused_computation.2.clone | custom fusion | bytes 528384 | tf_op jit(solution)/shard_map/jit(_take)/gather | solution.py:56
  114.7 3.6 %all-to-all-start.4 = ((bf16[4,256,128]{2,1,0:T(8,128)(2,1)}), bf16[4,256,128]{2,1,0:T(8,128)(2,1)S(1)}, u32[]{:S(2)}, u32[]{:S(2)}) async-start(bf16[4,256,128]{2,1,0:T(8,128)(2,1)} %broadcast_select_fusion), calls=%async_computation.4 | async-start | bytes 524288 | tf_op jit(solution)/shard_map/all_to_all | solution.py:58
  119.4 7.8 %all-to-all-done.4 = bf16[4,256,128]{2,1,0:T(8,128)(2,1)S(1)} async-done(((bf16[4,256,128]{2,1,0:T(8,128)(2,1)}), bf16[4,256,128]{2,1,0:T(8,128)(2,1)S(1)}, u32[]{:S(2)}, u32[]{:S(2)}) %all-to-all-start.4) | async-done | bytes 262176 | tf_op jit(solution)/shard_map/all_to_all | solution.py:58
  128.2 9.2 %gather_fusion.6 = bf16[3072,128]{1,0:T(8,128)(2,1)S(1)} fusion(bf16[3072,128]{1,0:T(8,128)(2,1)S(1)} %convolution_convert_fusion, s32[3072]{0:T(1024)S(1)} %broadcast_clamp_fusion), kind=kCustom, calls=%fused_computation.3.clone | custom fusion | bytes 1585152 | tf_op jit(solution)/shard_map/vmap(jit(_take))/gather | solution.py:30
  137.4 1.5 broadcast.157
  138.9 30.6 %while.3 = (s32[]{:T(128)}, bf16[3072,128]{1,0:T(8,128)(2,1)S(1)}, s32[16,2]{0,1:T(2,128)S(1)}, bf16[16,384,128]{2,1,0:T(8,128)(2,1)}, s32[]{:T(128)}) while((s32[]{:T(128)}, bf16[3072,128]{1,0:T(8,128)(2,1)S(1)}, s32[16,2]{0,1:T(2,128)S(1)}, bf16[16,384,128]{2,1,0:T(8,128)(2,1)}, s32[]{:T(128)}) %tuple.35), condition=%wide.while_cond.1, body=%wide.while_body.1.sunk | while | flops 2 | bytes 197721 | solution.py:25
  149.0 1.3 bitcast_dynamic-update-slice_fusion.5
  150.9 1.3 bitcast_dynamic-update-slice_fusion.5
  162.4 1.3 bitcast_dynamic-update-slice_fusion.5
  169.5 5.8 %fusion = f32[16,576,128]{2,1,0:T(8,128)} fusion(bf16[16,384,128]{2,1,0:T(8,128)(2,1)} %get-tuple-element.22, s32[16,576]{1,0:T(8,128)S(1)} %slice_subtract_fusion), kind=kOutput, calls=%fused_computation.12 | convolution fusion | flops 909508608 | bytes 6328320 | tf_op jit(solution)/shard_map/vmap()/dot_general | solution.py:29
  175.8 6.1 %fusion.13 = bf16[16,128,128]{2,1,0:T(8,128)(2,1)S(1)} fusion(f32[16,192,128]{2,1,0:T(8,128)S(1)} %select_convert_fusion, f32[16,576,128]{2,1,0:T(8,128)} %fusion, bf16[16,128,128]{2,1,0:T(8,128)(2,1)S(1)} %bitcast.123, s32[16,768]{1,0:T(8,128)S(1)} %copy-done.8), kind=kOutput, calls=%fused_computation.38 | convolution fusion | flops 819724288 | bytes 7389184 | tf_op jit(solution)/shard_map/vmap()/dot_general | solution.py:39
  183.0 2.0 %add_convert_fusion = bf16[2048,128]{1,0:T(8,128)(2,1)} fusion(f32[2048,128]{1,0:T(8,128)S(1)} %fusion.34, bf16[2048,128]{1,0:T(8,128)(2,1)S(1)} %add_convert_fusion.1, bf16[2,4,128,128]{3,2,1,0:T(8,128)(2,1)} %param.25), kind=kOutput, calls=%fused_computation.45 | convolution fusion | flops 69206016 | bytes 2654208 | tf_op jit(solution)/shard_map/dot_general | solution.py:47
  (157 shorter events, 66.5 us)
Async XLA Ops:
  0.0 109.8 %copy-start = (bf16[128,128]{1,0:T(8,128)(2,1)S(1)}, bf16[128,128]{1,0:T(8,128)(2,1)}, u32[]{:S(2)}) copy-start(bf16[128,128]{1,0:T(8,128)(2,1)} %param.27) | copy-start | bytes 98308
  0.0 13.6 %copy-start.1 = (bf16[2048,128]{1,0:T(8,128)(2,1)S(1)}, bf16[2048,128]{1,0:T(8,128)(2,1)}, u32[]{:S(2)}) copy-start(bf16[2048,128]{1,0:T(8,128)(2,1)} %param.16) | copy-start | bytes 1572868
  0.0 13.1 %copy-start.3 = (s32[16,768]{1,0:T(8,128)S(1)}, s32[16,768]{1,0:T(8,128)}, u32[]{:S(2)}) copy-start(s32[16,768]{1,0:T(8,128)} %param.17) | copy-start | bytes 147460
  0.0 13.2 %copy-start.6 = (s32[1,4,64]{2,1,0:T(4,128)S(1)}, s32[1,4,64]{2,1,0:T(4,128)}, u32[]{:S(2)}) copy-start(s32[1,4,64]{2,1,0:T(4,128)} %param.20) | copy-start | bytes 3076
  0.0 13.2 %copy-start.7 = (s32[1,4,128]{2,1,0:T(4,128)S(1)}, s32[1,4,128]{2,1,0:T(4,128)}, u32[]{:S(2)}) copy-start(s32[1,4,128]{2,1,0:T(4,128)} %param.23) | copy-start | bytes 6148
  0.0 13.3 %copy-start.5 = (s32[2,768]{1,0:T(2,128)S(1)}, s32[2,768]{1,0:T(2,128)}, u32[]{:S(2)}) copy-start(s32[2,768]{1,0:T(2,128)} %param.21) | copy-start | bytes 18436
  0.0 13.6 %copy-start.2 = (bf16[2,4,128,128]{3,2,1,0:T(8,128)(2,1)S(1)}, bf16[2,4,128,128]{3,2,1,0:T(8,128)(2,1)}, u32[]{:S(2)}) copy-start(bf16[2,4,128,128]{3,2,1,0:T(8,128)(2,1)} %param.25) | copy-start | bytes 786436
  6.7 15.3 %all-to-all-start = ((bf16[4,256,128]{2,1,0:T(8,128)(2,1)}), bf16[4,256,128]{2,1,0:T(8,128)(2,1)S(1)}, u32[]{:S(2)}, u32[]{:S(2)}) async-start(bf16[4,256,128]{2,1,0:T(8,128)(2,1)} %broadcast_select_fusion.1), calls=%async_computation | async-start | bytes 524288 | tf_op jit(solution)/shard_map/all_to_all | solution.py:58
  63.6 7.3 %copy-start.8 = (s32[16,768]{1,0:T(8,128)S(1)}, s32[16,768]{1,0:T(8,128)}, u32[]{:S(2)}) copy-start(s32[16,768]{1,0:T(8,128)} %param.18) | copy-start | bytes 147460
  78.2 14.5 %copy-start.4 = (bf16[4,128,128]{2,1,0:T(8,128)(2,1)S(1)}, bf16[4,128,128]{2,1,0:T(8,128)(2,1)}, u32[]{:S(2)}) copy-start(bf16[4,128,128]{2,1,0:T(8,128)(2,1)} %param.26) | copy-start | bytes 393220
  79.1 23.1 %copy-start.10 = (s32[2,768]{1,0:T(2,128)S(1)}, s32[2,768]{1,0:T(2,128)}, u32[]{:S(2)}) copy-start(s32[2,768]{1,0:T(2,128)} %param.22) | copy-start | bytes 18436
  79.8 7.4 %all-to-all-start.1 = ((bf16[4,64,128]{2,1,0:T(8,128)(2,1)}), bf16[4,64,128]{2,1,0:T(8,128)(2,1)S(1)}, u32[]{:S(2)}, u32[]{:S(2)}) async-start(bf16[4,64,128]{2,1,0:T(8,128)(2,1)} %broadcast_select_fusion.3), calls=%async_computation.1 | async-start | bytes 131072 | tf_op jit(solution)/shard_map/all_to_all | solution.py:75
  89.3 9.4 %all-to-all-start.2 = ((bf16[4,128,128]{2,1,0:T(8,128)(2,1)}), bf16[4,128,128]{2,1,0:T(8,128)(2,1)S(1)}, u32[]{:S(2)}, u32[]{:S(2)}) async-start(bf16[4,128,128]{2,1,0:T(8,128)(2,1)} %broadcast_select_fusion.2), calls=%async_computation.2 | async-start | bytes 262144 | tf_op jit(solution)/shard_map/all_to_all | solution.py:60
  102.1 7.6 %copy-start.9 = (s32[2048]{0:T(1024)S(1)}, s32[2048]{0:T(1024)}, u32[]{:S(2)}) copy-start(s32[2048]{0:T(1024)} %param.24) | copy-start | bytes 24580
  114.7 12.4 %all-to-all-start.4 = ((bf16[4,256,128]{2,1,0:T(8,128)(2,1)}), bf16[4,256,128]{2,1,0:T(8,128)(2,1)S(1)}, u32[]{:S(2)}, u32[]{:S(2)}) async-start(bf16[4,256,128]{2,1,0:T(8,128)(2,1)} %broadcast_select_fusion), calls=%async_computation.4 | async-start | bytes 524288 | tf_op jit(solution)/shard_map/all_to_all | solution.py:58
where the time goes:
time: 186 us; the launch traced here: 185 us
  local copies, waits for them, and re-layouts  95.6 us (51%)
  matrix products  33 us (18%)
  waiting for transfers between devices  25.7 us (14%)
  starting transfers between devices  16.5 us (9%)
  other arithmetic  7.16 us (4%)
  blocking collectives  6.49 us (3%)
    gather x96, local copies, waits for them, and re-layouts  61.1 us
    all_to_all x3, waiting for transfers between devices, move_halo(): lax.all_to_all(buffer, 'dom', split_axis=0, concat_axis=0, tiled=True)  21.7 us
    gather x2, local copies, waits for them, and re-layouts, one_block(): jnp.take(sender_terms, block_sources[local_count:], axis=0)  18.3 us
    dot_general x3, matrix products, one_block(): lax.dot_general(one_hot, message, (((0,), (0,)), ((), ())), preferred_ele...  13.4 us
    all_to_all x3, starting transfers between devices, move_halo(): lax.all_to_all(buffer, 'dom', split_axis=0, concat_axis=0, tiled=True)  13.3 us
    dot_general x2, matrix products, one_block(): jnp.dot(near_hot, window_rows, preferred_element_type=jnp.float32)  11.5 us
    gather x3, local copies, waits for them, and re-layouts, move_halo(): buffer = jnp.take(padded, send_list, axis=0)  7.74 us
    all_to_all x1, blocking collectives, owner_trade(): lax.all_to_all(buffer, ('sub', 'chip'), split_axis=0, concat_axis=0, tile...  6.49 us
  transfers between devices with their start and end apart: 4, of which 4 were waited for; matrix products, arithmetic and copies ran while one was open for 1% of the time, Pallas kernels for 0%

commit v1 on v0

v1 whole, which is shorter than its diff:
```python
import functools

import jax
import jax.numpy as jnp
from jax import lax
from jax.experimental import pallas as pl
from jax.experimental.pallas import tpu as pltpu
from jax.sharding import PartitionSpec as P

BF16 = jnp.bfloat16
F32 = jnp.float32
I32 = jnp.int32
BLOCK = 128
VMEM_BYTES = 32 << 20


def dot(left, right):
    return jnp.dot(left, right, preferred_element_type=F32)


def dot_last(left, right):
    return lax.dot_general(left, right, (((1,), (1,)), ((), ())), preferred_element_type=F32)


def rows_hot(index_row, height):
    shape = (height, index_row.shape[1])
    index = jnp.broadcast_to(index_row, shape).astype(jnp.int16)
    return jnp.where(
        index == lax.broadcasted_iota(jnp.int16, shape, 0), jnp.ones((), BF16), jnp.zeros((), BF16)
    )


def columns_hot(index_column, width, wrap=None):
    shape = (index_column.shape[0], width)
    columns = lax.broadcasted_iota(I32, shape, 1)
    if wrap is not None:
        columns = lax.rem(columns, wrap)
    return jnp.where(index_column == columns, 1.0, 0.0).astype(BF16)


def silu_of_half(half):
    return half + half * jnp.tanh(half)


def halved(weight):
    return weight * jnp.asarray(0.5, BF16)


def partner_offsets(dom_count):
    offsets = []
    for offset in (1, dom_count - 1, 2 % dom_count):
        if offset not in offsets:
            offsets.append(offset)
    return tuple(offsets)


def partner_place(source_dom, own_dom, dom_count, offsets):
    step = own_dom - source_dom
    step = jnp.where(step < 0, step + dom_count, step)
    place = jnp.zeros_like(step)
    for index, offset in enumerate(offsets):
        place = jnp.where(step == offset, index, place)
    return place


def terms_of(latent, weights):
    features = latent.shape[1]
    both = jnp.concatenate([halved(weights[0]), halved(weights[1])], axis=1)
    terms = dot(latent, both).astype(BF16)
    return terms[:, :features].T, terms[:, features:].T


def emit_halo(sender_terms, lists_ref, out_refs, dom_count, offsets):
    own_dom = lax.axis_index("dom")
    for offset, out_ref in zip(offsets, out_refs):
        partner = lax.rem(own_dom + offset, dom_count)
        index_row = lists_ref[pl.ds(partner, 1), :]
        hot = rows_hot(index_row, sender_terms.shape[1])
        out_ref[...] = dot(sender_terms, hot).astype(BF16)


def terms_kernel(dom_count, offsets, latent_ref, lists_ref, weights_ref, sender_ref, target_ref, *sent_refs):
    sender, target = terms_of(latent_ref[...], weights_ref)
    sender_ref[...] = sender
    target_ref[...] = target
    emit_halo(sender, lists_ref, sent_refs, dom_count, offsets)


def near_kernel(sender_ref, target_ref, source_ref, place_ref, sums_ref):
    node_count = sender_ref.shape[1]
    block_count, slot_count = source_ref.shape
    local_count = slot_count * 3 // 4
    window = min(3 * BLOCK, node_count)

    def messages(block):
        start = min(max(block * BLOCK - BLOCK, 0), node_count - window)
        table = jnp.concatenate(
            [sender_ref[:, start : start + window], target_ref[:, block * BLOCK : (block + 1) * BLOCK]], axis=1
        )
        places = rows_hot(place_ref[block : block + 1, :local_count], BLOCK)
        sources = rows_hot(source_ref[block : block + 1, :local_count] - start, window)
        picked = dot(table, jnp.concatenate([sources, places], axis=0))
        return silu_of_half(picked).astype(BF16)

    def add_up(block, message):
        places = rows_hot(place_ref[block : block + 1, :local_count], BLOCK)
        sums_ref[block * BLOCK : (block + 1) * BLOCK, :] = dot_last(places, message)

    waiting = None
    for block in range(block_count):
        message = messages(block)
        if waiting is not None:
            add_up(*waiting)
        waiting = (block, message)
    add_up(*waiting)


def far_layer(dom_count, offsets, latent_ref, target_ref, source_ref, place_ref, sums_ref, weights_ref, halo_refs, out_ref):
    node_count, features = latent_ref.shape
    block_count, slot_count = source_ref.shape
    local_count = slot_count * 3 // 4
    capacity = halo_refs[0].shape[1]
    halo = jnp.concatenate([ref[...] for ref in halo_refs], axis=1)
    halo_rows = halo.shape[1]
    own_dom = lax.axis_index("dom")
    update_weights = jnp.concatenate([halved(weights_ref[2]), halved(weights_ref[3])], axis=0)
    shift = capacity.bit_length() - 1

    slots = source_ref[:, local_count:] - node_count
    source_dom = lax.shift_right_logical(slots, shift)
    far_sources = partner_place(source_dom, own_dom, dom_count, offsets) * capacity + (slots & (capacity - 1))

    def messages(block):
        table = jnp.concatenate([halo, target_ref[:, block * BLOCK : (block + 1) * BLOCK]], axis=1)
        places = rows_hot(place_ref[block : block + 1, local_count:], BLOCK)
        sources = rows_hot(far_sources[block : block + 1, :], halo_rows)
        picked = dot(table, jnp.concatenate([sources, places], axis=0))
        return silu_of_half(picked).astype(BF16)

    def add_up(block, message):
        rows = slice(block * BLOCK, (block + 1) * BLOCK)
        places = rows_hot(place_ref[block : block + 1, local_count:], BLOCK)
        summed = (sums_ref[rows, :] + dot_last(places, message)).astype(BF16)
        latent = latent_ref[rows, :]
        update = dot(jnp.concatenate([summed, latent], axis=1), update_weights)
        out_ref[rows, :] = (latent.astype(F32) + silu_of_half(update)).astype(BF16)

    waiting = None
    for block in range(block_count):
        message = messages(block)
        if waiting is not None:
            add_up(*waiting)
        waiting = (block, message)
    add_up(*waiting)


def lane_rows(ref):
    pieces = []
    for block in range(ref.shape[0]):
        for start in range(0, ref.shape[1], BLOCK):
            pieces.append(ref[block : block + 1, start : start + BLOCK])
    return pieces


def far_pool_kernel(
    dom_count,
    offsets,
    latent_ref,
    target_ref,
    source_ref,
    place_ref,
    sums_ref,
    weights_ref,
    pool_ref,
    coarse_source_ref,
    coarse_place_ref,
    coarse_send_ref,
    *rest,
):
    halo_refs, (out_ref, packet_ref) = rest[:-2], rest[-2:]
    far_layer(dom_count, offsets, latent_ref, target_ref, source_ref, place_ref, sums_ref, weights_ref, halo_refs, out_ref)
    owners = range(0, pool_ref.shape[0], 4)
    capacity = pool_ref.shape[1]
    first = out_ref[...]
    lists = jnp.concatenate([pool_ref[owner : owner + 1, :] for owner in owners], axis=1).T
    packet_ref[: len(owners) * capacity, :] = dot(columns_hot(lists, first.shape[0]), first).astype(BF16)
    pieces = lane_rows(coarse_source_ref) + [coarse_send_ref[...]] + lane_rows(coarse_place_ref)
    spare = -sum(piece.shape[0] for piece in pieces) % 16
    if spare:
        pieces.append(jnp.zeros((spare, BLOCK), I32))
    whole = jnp.concatenate(pieces, axis=0) + 1
    high = lax.shift_right_logical(whole, 8)
    packet_ref[len(owners) * capacity :, :] = jnp.concatenate(
        [high.astype(F32), (whole & 255).astype(F32)], axis=0
    ).astype(BF16)


def packet_rows(count):
    return -(-count // 16) * 16


def far_kernel(dom_count, offsets, latent_ref, target_ref, source_ref, place_ref, sums_ref, weights_ref, *rest):
    far_layer(
        dom_count, offsets, latent_ref, target_ref, source_ref, place_ref, sums_ref, weights_ref, rest[:-1], rest[-1]
    )


def own_place(grid):
    return lax.axis_index("sub") * grid.chip_count + lax.axis_index("chip")


class Grid:
    def __init__(self, mesh, pool_capacity, coarse_capacity, coarse_blocks, slot_count):
        self.dom_count = mesh.shape["dom"]
        self.sub_count = mesh.shape["sub"]
        self.chip_count = mesh.shape["chip"]
        self.places = self.sub_count * self.chip_count
        self.offsets = partner_offsets(self.dom_count)
        self.owners = len(range(0, self.places, 4))
        self.swapped = self.sub_count == 2 and self.chip_count == 2
        self.pool_capacity = pool_capacity
        self.coarse_capacity = coarse_capacity
        self.blocks = coarse_blocks
        self.pieces = slot_count // BLOCK
        self.slots = self.places * pool_capacity
        self.pooled_rows = self.owners * pool_capacity
        self.list_rows = 2 * coarse_blocks * self.pieces + self.dom_count
        self.packed_rows = packet_rows(self.list_rows)
        self.packet = self.pooled_rows + 2 * self.packed_rows


def owner_lists(grid, packets, owner, place):
    if grid.swapped:
        rows = packets[0][grid.pooled_rows :, :].astype(F32)
        for other in range(1, grid.places):
            rows = jnp.where(place == other, packets[other][grid.pooled_rows :, :].astype(F32), rows)
    else:
        rows = packets[4 * owner][grid.pooled_rows :, :].astype(F32)
    whole = rows[: grid.packed_rows] * 256.0 + rows[grid.packed_rows :]
    return whole.astype(I32) - 1


def owner_table(grid, packets, owner):
    start = owner * grid.pool_capacity
    return jnp.concatenate([packet[start : start + grid.pool_capacity, :] for packet in packets], axis=0)


def slot_order(grid, slots, place):
    return slots ^ (place * grid.pool_capacity) if grid.swapped else slots


def coarse_send_kernel(grid, weights_ref, *refs):
    packets = refs[: grid.places]
    outs = refs[grid.places : grid.places + len(grid.offsets)]
    lists_ref = refs[-1]
    place = own_place(grid)
    own_dom = lax.axis_index("dom")
    first_list = grid.blocks * grid.pieces
    for owner in range(grid.owners):
        lists_ref[...] = owner_lists(grid, packets, owner, place)
        table = owner_table(grid, packets, owner)
        terms = dot(table, halved(weights_ref[0])).astype(BF16).T
        for offset, out_ref in zip(grid.offsets, outs):
            partner = lax.rem(own_dom + offset, grid.dom_count)
            index_row = slot_order(grid, lists_ref[pl.ds(first_list + partner, 1), :], place)
            picked = dot(terms, rows_hot(index_row, grid.slots))
            out_ref[owner * BLOCK : (owner + 1) * BLOCK, :] = picked.astype(BF16)


def coarse_own_kernel(grid, weights_ref, *refs):
    packets = refs[: grid.places]
    picked_ref, source_out, place_out, rows_out, lists_ref = refs[grid.places :]
    place = own_place(grid)
    own_dom = lax.axis_index("dom")
    first_slot = place * grid.pool_capacity
    block = lax.shift_right_logical(first_slot, BLOCK.bit_length() - 1)
    within = first_slot & (BLOCK - 1)
    shift = grid.coarse_capacity.bit_length() - 1
    for owner in range(grid.owners):
        lists_ref[...] = owner_lists(grid, packets, owner, place)
        sources = jnp.concatenate(
            [lists_ref[pl.ds(block * grid.pieces + piece, 1), :] for piece in range(grid.pieces)], axis=1
        )
        offset = grid.blocks * grid.pieces + grid.dom_count
        places = jnp.concatenate(
            [lists_ref[pl.ds(offset + block * grid.pieces + piece, 1), :] for piece in range(grid.pieces)], axis=1
        )
        places = places - within
        places = jnp.where((places >= 0) & (places < grid.pool_capacity), places, -1)
        halo_slots = sources - grid.slots
        source_dom = lax.shift_right_arithmetic(halo_slots, shift)
        halo_sources = partner_place(source_dom, own_dom, grid.dom_count, grid.offsets) * grid.coarse_capacity + (
            halo_slots & (grid.coarse_capacity - 1)
        )
        is_halo = halo_slots >= 0
        source_out[owner : owner + 1, :] = jnp.where(is_halo, halo_sources, -1)
        place_out[owner : owner + 1, :] = places
        own_sources = jnp.where(is_halo, -1, slot_order(grid, sources, place))

        table = owner_table(grid, packets, owner)
        if grid.swapped:
            rows = table[: grid.pool_capacity]
        else:
            rows = table[: grid.pool_capacity]
            for other in range(1, grid.places):
                other_rows = table[other * grid.pool_capacity : (other + 1) * grid.pool_capacity]
                rows = jnp.where(place == other, other_rows, rows)
        rows_out[owner * grid.pool_capacity : (owner + 1) * grid.pool_capacity, :] = rows
        sender = dot(table, halved(weights_ref[0])).astype(BF16).T
        target = dot(rows, halved(weights_ref[1])).astype(BF16).T
        hot = jnp.concatenate([rows_hot(own_sources, grid.slots), rows_hot(places, grid.pool_capacity)], axis=0)
        picked_ref[owner] = dot(jnp.concatenate([sender, target], axis=1), hot)


def lift_kernel(
    grid,
    picked_ref,
    source_ref,
    place_ref,
    rows_ref,
    coarse_weights_ref,
    prolong_weight_ref,
    prolong_ref,
    first_ref,
    weights_ref,
    lists_ref,
    *rest,
):
    count = len(grid.offsets)
    halo_refs = rest[:count]
    lifted_ref, sender_ref, target_ref = rest[count : count + 3]
    sent_refs = rest[count + 3 :]
    update_weights = jnp.concatenate([halved(coarse_weights_ref[2]), halved(coarse_weights_ref[3])], axis=0)
    prolonged = []
    for owner in range(grid.owners):
        halo = jnp.concatenate([ref[owner * BLOCK : (owner + 1) * BLOCK, :] for ref in halo_refs], axis=1)
        picked = picked_ref[owner] + dot(halo, rows_hot(source_ref[owner : owner + 1, :], halo.shape[1]))
        message = silu_of_half(picked).astype(BF16)
        places = rows_hot(place_ref[owner : owner + 1, :], grid.pool_capacity)
        summed = dot_last(places, message).astype(BF16)
        rows = rows_ref[owner * grid.pool_capacity : (owner + 1) * grid.pool_capacity, :]
        update = dot(jnp.concatenate([summed, rows], axis=1), update_weights)
        coarse = (rows.astype(F32) + silu_of_half(update)).astype(BF16)
        prolonged.append(dot(coarse, halved(prolong_weight_ref[...])))
    prolonged = jnp.concatenate(prolonged, axis=0)
    high = prolonged.astype(BF16)
    low = (prolonged - high.astype(F32)).astype(BF16)
    table = jnp.concatenate([high, low], axis=0)
    indices = prolong_ref[...]
    shift = (4 * grid.pool_capacity).bit_length() - 1
    indices = lax.shift_right_logical(indices, shift) * grid.pool_capacity + (indices & (grid.pool_capacity - 1))
    columns = indices.T
    node_count = first_ref.shape[0]
    for block in range(node_count // BLOCK):
        rows = slice(block * BLOCK, (block + 1) * BLOCK)
        hot = columns_hot(columns[:, block : block + 1], table.shape[0], grid.pooled_rows)
        lifted_ref[rows, :] = (first_ref[rows, :].astype(F32) + silu_of_half(dot(hot, table))).astype(BF16)
    sender, target = terms_of(lifted_ref[...], weights_ref)
    sender_ref[...] = sender
    target_ref[...] = target
    emit_halo(sender, lists_ref, sent_refs, grid.dom_count, grid.offsets)


def call(kernel, outs, scratch=(), flops=0, name=None):
    return pl.pallas_call(
        kernel,
        out_shape=tuple(jax.ShapeDtypeStruct(shape, dtype) for shape, dtype in outs),
        scratch_shapes=list(scratch),
        compiler_params=pltpu.CompilerParams(vmem_limit_bytes=VMEM_BYTES),
        cost_estimate=pl.CostEstimate(flops=flops, bytes_accessed=4 << 20, transcendentals=0),
        name=name,
    )


def swap_dom(arrays, dom_count, offsets):
    return [
        lax.ppermute(array, "dom", [(place, (place + offset) % dom_count) for place in range(dom_count)])
        for array, offset in zip(arrays, offsets)
    ]


def trade_packets(grid, packet):
    if grid.swapped:
        pairs = [(0, 1), (1, 0)]
        across = lax.ppermute(packet, "chip", pairs)
        return [packet, across, lax.ppermute(packet, "sub", pairs), lax.ppermute(across, "sub", pairs)]
    gathered = lax.all_gather(packet, ("sub", "chip"), axis=0, tiled=False)
    return [gathered[place] for place in range(grid.places)]


def body(
    mesh,
    fine_nodes,
    fine_src,
    fine_dst,
    halo_send,
    pool_send,
    coarse_src,
    coarse_dst,
    coarse_send,
    prolong_idx,
    fine_weights,
    coarse_weights,
    prolong_weight,
):
    node_count, features = fine_nodes.shape
    slot_count = fine_src.shape[1]
    grid = Grid(mesh, pool_send.shape[2], coarse_send.shape[2], coarse_src.shape[0], coarse_src.shape[1])
    halo_capacity = halo_send.shape[2]
    dom_count, offsets = grid.dom_count, grid.offsets
    lists = halo_send[0]
    table = ((features, node_count), BF16)
    halo_outs = [((features, halo_capacity), BF16)] * len(offsets)
    nodes = ((node_count, features), BF16)
    big = 1 << 30

    sender, target, *sent = call(
        functools.partial(terms_kernel, dom_count, offsets), [table, table, *halo_outs], flops=big, name="terms"
    )(fine_nodes, lists, fine_weights[0])
    halo = swap_dom(sent, dom_count, offsets)
    (sums,) = call(near_kernel, [((node_count, features), F32)], flops=4 * big, name="near")(
        sender, target, fine_src, fine_dst
    )
    first, packet = call(
        functools.partial(far_pool_kernel, dom_count, offsets),
        [nodes, ((grid.packet, features), BF16)],
        flops=2 * big,
        name="far_pool",
    )(
        fine_nodes,
        target,
        fine_src,
        fine_dst,
        sums,
        fine_weights[0],
        pool_send[0],
        coarse_src,
        coarse_dst,
        coarse_send[0],
        *halo,
    )
    packets = trade_packets(grid, packet)
    lists_scratch = pltpu.VMEM((grid.packed_rows, BLOCK), I32)
    sent = call(
        functools.partial(coarse_send_kernel, grid),
        [((grid.owners * features, grid.coarse_capacity), BF16)] * len(offsets),
        [lists_scratch],
        flops=big // 2,
        name="coarse_send",
    )(coarse_weights, *packets)
    coarse_halo = swap_dom(sent, dom_count, offsets)
    coarse_slots = coarse_src.shape[1]
    picked, sources, places, rows = call(
        functools.partial(coarse_own_kernel, grid),
        [
            ((grid.owners, features, coarse_slots), F32),
            ((grid.owners, coarse_slots), I32),
            ((grid.owners, coarse_slots), I32),
            ((grid.pooled_rows, features), BF16),
        ],
        [lists_scratch],
        flops=4 * big,
        name="coarse_own",
    )(coarse_weights, *packets)
    lifted, sender, target, *sent = call(
        functools.partial(lift_kernel, grid), [nodes, table, table, *halo_outs], flops=2 * big, name="lift"
    )(
        picked,
        sources,
        places,
        rows,
        coarse_weights,
        prolong_weight,
        prolong_idx.reshape(node_count // BLOCK, BLOCK),
        first,
        fine_weights[1],
        lists,
        *coarse_halo,
    )
    halo = swap_dom(sent, dom_count, offsets)
    (sums,) = call(near_kernel, [((node_count, features), F32)], flops=4 * big, name="near")(
        sender, target, fine_src, fine_dst
    )
    (fine_out,) = call(functools.partial(far_kernel, dom_count, offsets), [nodes], flops=2 * big, name="far")(
        lifted, target, fine_src, fine_dst, sums, fine_weights[1], *halo
    )
    return fine_out


def solution(mesh):
    split = ("groups", "dom", "sub", "chip")
    return jax.shard_map(
        functools.partial(body, mesh),
        mesh=mesh,
        in_specs=(
            P(split, None),
            P(split, None),
            P(split, None),
            P(split, None, None),
            P(split, None, None),
            P(split, None),
            P(split, None),
            P(split, None, None),
            P(split),
            P(),
            P(),
            P(),
        ),
        out_specs=P(split, None),
        check_vma=False,
    )
```

time: 186 us -> 49.6 us (0.27)
  local copies, waits for them, and re-layouts: 95.6 us -> 2.57 us
  matrix products: 33 us -> 0 us
  Pallas kernels: 0 us -> 18.1 us
  waiting for transfers between devices: 25.7 us -> 11.9 us
  other arithmetic: 7.16 us -> 0 us
  blocking collectives: 6.49 us -> 0 us
    gather x103 -> x0, local copies, waits for them, and re-layouts: 91.2 us -> none
    dot_general x18 -> x0, matrix products: 33 us -> none  [the longest x3 13.4 us: one_block(): lax.dot_general(one_hot, message, (((0,), (0,)), ((), ())), preferred_ele...]
    all_to_all x4 -> x0, waiting for transfers between devices: 25.7 us -> none  [the longest x3 21.7 us: move_halo(): lax.all_to_all(buffer, 'dom', split_axis=0, concat_axis=0, tiled=True)]
    pallas_call x0 -> x8, Pallas kernels: none -> 18.1 us  [the longest x2 5.56 us: body(): call(near_kernel, [((node_count, features), F32)], flops=4 * big, name='n...]
    ppermute x0 -> x12, starting transfers between devices: none -> 16.6 us  [the longest x9 13.9 us: swap_dom(): lax.ppermute(array, 'dom', [(place, (place + offset) % dom_count) for pla...]
    all_to_all x4 -> x0, starting transfers between devices: 16.5 us -> none  [the longest x3 13.3 us: move_halo(): lax.all_to_all(buffer, 'dom', split_axis=0, concat_axis=0, tiled=True)]
    ppermute x0 -> x12, waiting for transfers between devices: none -> 11.9 us  [the longest x9 9.14 us: swap_dom(): lax.ppermute(array, 'dom', [(place, (place + offset) % dom_count) for pla...]
    all_to_all x1 -> x0, blocking collectives: 6.49 us -> none  [owner_trade(): lax.all_to_all(buffer, ('sub', 'chip'), split_axis=0, concat_axis=0, tile...]
  transfers between devices with their start and end apart: 4 -> 12, of which waited for: 4 -> 6; matrix products, arithmetic and copies ran while one was open for 1% -> 0% of each run, Pallas kernels for 0% -> 12%
where the time goes in v1:
time: 49.6 us; the launch traced here: 49.4 us
  Pallas kernels  18.1 us (36%)
  starting transfers between devices  16.6 us (33%)
  waiting for transfers between devices  11.9 us (24%)
  local copies, waits for them, and re-layouts  2.57 us (5%)
    ppermute x9, starting transfers between devices, swap_dom(): lax.ppermute(array, 'dom', [(place, (place + offset) % dom_count) for pla...  13.9 us
    ppermute x9, waiting for transfers between devices, swap_dom(): lax.ppermute(array, 'dom', [(place, (place + offset) % dom_count) for pla...  9.14 us
    pallas_call x2, Pallas kernels, body(): call(near_kernel, [((node_count, features), F32)], flops=4 * big, name='n...  5.56 us
    pallas_call x1, Pallas kernels, body(): call(functools.partial(far_kernel, dom_count, offsets), [nodes], flops=2...  4.62 us
    pallas_call x1, Pallas kernels, body(): call(functools.partial(far_pool_kernel, dom_count, offsets), [nodes, ((gr...  4.01 us
    pallas_call x1, Pallas kernels, body(): call(functools.partial(lift_kernel, grid), [nodes, table, table, *halo_ou...  1.99 us
    ppermute x1, starting transfers between devices, trade_packets(): lax.ppermute(packet, 'sub', pairs)  1.55 us
    unnamed x24, local copies, waits for them, and re-layouts  1.53 us
  transfers between devices with their start and end apart: 12, of which 6 were waited for; matrix products, arithmetic and copies ran while one was open for 0% of the time, Pallas kernels for 12%

profile of v1, /device:TPU:0, one launch (start us, length us, event | category | flops | bytes accessed | tf_op | source)
XLA Modules:
  0.0 49.4 jit_solution(1310500511568105695)
XLA Ops:
  0.0 1.0 %slice_bitcast_fusion = (bf16[4,128,128]{2,1,0:T(8,128)(2,1)S(1)}, bf16[4,128,128]{2,1,0:T(8,128)(2,1)S(1)}) fusion(bf16[2,4,128,128]{3,2,1,0:T(8,128)(2,1)} %param.21), kind=kLoop, calls=%fused_computation | loop fusion | bytes 524288 | tf_op jit(solution)/shard_map/squeeze | solution.py:476
  1.1 0.1 copy-done
  1.2 0.7 %copy-done.8 = s32[1,4,256]{2,1,0:T(4,128)S(1)} copy-done((s32[1,4,256]{2,1,0:T(4,128)S(1)}, s32[1,4,256]{2,1,0:T(4,128)}, u32[]{:S(2)}) %copy-start.8) | copy-done | bytes 4120
  1.9 1.1 %terms.1 = (bf16[128,2048]{1,0:T(8,128)(2,1)S(1)}, bf16[128,2048]{1,0:T(8,128)(2,1)S(1)}, bf16[128,256]{1,0:T(8,128)(2,1)S(1)}, bf16[128,256]{1,0:T(8,128)(2,1)S(1)}, bf16[128,256]{1,0:T(8,128)(2,1)S(1)}) custom-call(bf16[2048,128]{1,0:T(8,128)(2,1)S(1)} %copy-done, s32[4,256]{1,0:T(4,128)S(1)} %bitcast.9, bf16[4,128,128]{2,1,0:T(8,128)(2,1)S(1)} %get-tuple-element.46.weights_ref), custom_call_target="tpu_custom_call" | custom-call | flops 1073741824 | bytes 4194304 | tf_op jit(solution)/shard_map/terms/pallas_call | solution.py:417
  2.9 3.1 %collective-permute-start = (bf16[128,256]{1,0:T(8,128)(2,1)S(1)}, bf16[128,256]{1,0:T(8,128)(2,1)S(1)}, u32[]{:S(2)}, u32[]{:S(2)}) collective-permute-start(bf16[128,256]{1,0:T(8,128)(2,1)S(1)} %get-tuple-element.27), channel_id=1, source_target_pairs={{0,4},{4,8},{8,12},{12,0},{1,5},{5,9},{9,13},{13,1},{2,6},{6,10},{... | collective-permute-start | bytes 196616 | tf_op jit(solution)/shard_map/ppermute | solution.py:377
  6.0 2.1 %collective-permute-start.1 = (bf16[128,256]{1,0:T(8,128)(2,1)S(1)}, bf16[128,256]{1,0:T(8,128)(2,1)S(1)}, u32[]{:S(2)}, u32[]{:S(2)}) collective-permute-start(bf16[128,256]{1,0:T(8,128)(2,1)S(1)} %get-tuple-element.28), channel_id=1, source_target_pairs={{0,12},{4,0},{8,4},{12,8},{1,13},{5,1},{9,5},{13,9},{2,14},{6,2},{... | collective-permute-start | bytes 196616 | tf_op jit(solution)/shard_map/ppermute | solution.py:377
  8.1 0.9 %collective-permute-start.2 = (bf16[128,256]{1,0:T(8,128)(2,1)S(1)}, bf16[128,256]{1,0:T(8,128)(2,1)S(1)}, u32[]{:S(2)}, u32[]{:S(2)}) collective-permute-start(bf16[128,256]{1,0:T(8,128)(2,1)S(1)} %get-tuple-element.29), channel_id=1, source_target_pairs={{0,8},{4,12},{8,0},{12,4},{1,9},{5,13},{9,1},{13,5},{2,10},{6,14},... | collective-permute-start | bytes 196616 | tf_op jit(solution)/shard_map/ppermute | solution.py:377
  9.1 0.0 copy-start.11
  9.1 2.8 %near.2.sums_ref = f32[2048,128]{1,0:T(8,128)S(1)} custom-call(bf16[128,2048]{1,0:T(8,128)(2,1)S(1)} %get-tuple-element.26.sender_ref, bf16[128,2048]{1,0:T(8,128)(2,1)S(1)} %get-tuple-element.25.target_ref, s32[16,768]{1,0:T(8,128)S(1)} %copy-done.2, s32[16,768]{1,0:T(8,128)S(1)} %copy-done.3), custom_call_target="tpu_custom_call" | custom-call | flops 4294967296 | bytes 4194304 | tf_op jit(solution)/shard_map/near/pallas_call | solution.py:421
  11.9 0.0 copy-start.10
  11.9 2.4 %collective-permute-done.2.rest_2_ = bf16[128,256]{1,0:T(8,128)(2,1)S(1)} collective-permute-done((bf16[128,256]{1,0:T(8,128)(2,1)S(1)}, bf16[128,256]{1,0:T(8,128)(2,1)S(1)}, u32[]{:S(2)}, u32[]{:S(2)}) %collective-permute-start.2) | collective-permute-done | bytes 65568 | tf_op jit(solution)/shard_map/ppermute | solution.py:377
  14.4 0.0 copy-start.1
  14.4 4.0 %far_pool.1 = (bf16[2048,128]{1,0:T(8,128)(2,1)S(1)}, bf16[128,128]{1,0:T(8,128)(2,1)S(1)}) custom-call(bf16[2048,128]{1,0:T(8,128)(2,1)S(1)} %copy-done, bf16[128,2048]{1,0:T(8,128)(2,1)S(1)} %get-tuple-element.25.target_ref, s32[16,768]{1,0:T(8,128)S(1)} %copy-done.2, s32[16,768]{1,0:T(8,128)S(1)} %copy-done.3, f32[2048,128]{1,0:T(8,128)S(1)} %near.2.sums_ref, ...), custom_call_target="tpu_custom_call" | custom-call | flops 2147483648 | bytes 4194304 | tf_op jit(solution)/shard_map/far_pool/pallas_call | solution.py:424
  18.4 0.1 collective-permute-start.3
  18.5 1.6 %collective-permute-start.4 = (bf16[128,128]{1,0:T(8,128)(2,1)S(1)}, bf16[128,128]{1,0:T(8,128)(2,1)S(1)}, u32[]{:S(2)}, u32[]{:S(2)}) collective-permute-start(bf16[128,128]{1,0:T(8,128)(2,1)S(1)} %get-tuple-element.30.refs_0_), channel_id=1, source_target_pairs={{0,2},{2,0},{1,3},{3,1},{4,6},{6,4},{5,7},{7,5},{8,10},{10,8},{9,1... | collective-permute-start | bytes 98312 | tf_op jit(solution)/shard_map/ppermute | solution.py:386
  20.0 1.1 %collective-permute-start.5 = (bf16[128,128]{1,0:T(8,128)(2,1)S(1)}, bf16[128,128]{1,0:T(8,128)(2,1)S(1)}, u32[]{:S(2)}, u32[]{:S(2)}) collective-permute-start(bf16[128,128]{1,0:T(8,128)(2,1)S(1)} %collective-permute-done.3.refs_1_), channel_id=1, source_target_pairs={{0,2},{2,0},{1,3},{3,1},{4,6},{6,4},{5,7},{7,5},{8,10},{10,8},{9,1... | collective-permute-start | bytes 98312 | tf_op jit(solution)/shard_map/ppermute | solution.py:386
  21.2 1.3 %collective-permute-done.4.refs_2_ = bf16[128,128]{1,0:T(8,128)(2,1)S(1)} collective-permute-done((bf16[128,128]{1,0:T(8,128)(2,1)S(1)}, bf16[128,128]{1,0:T(8,128)(2,1)S(1)}, u32[]{:S(2)}, u32[]{:S(2)}) %collective-permute-start.4) | collective-permute-done | bytes 32800 | tf_op jit(solution)/shard_map/ppermute | solution.py:386
  22.5 1.5 %collective-permute-done.5.refs_3_ = bf16[128,128]{1,0:T(8,128)(2,1)S(1)} collective-permute-done((bf16[128,128]{1,0:T(8,128)(2,1)S(1)}, bf16[128,128]{1,0:T(8,128)(2,1)S(1)}, u32[]{:S(2)}, u32[]{:S(2)}) %collective-permute-start.5) | collective-permute-done | bytes 32800 | tf_op jit(solution)/shard_map/ppermute | solution.py:386
  24.0 0.4 coarse_send.1
  24.4 0.1 collective-permute-start.6
  24.4 3.8 %collective-permute-start.7 = (bf16[128,128]{1,0:T(8,128)(2,1)S(1)}, bf16[128,128]{1,0:T(8,128)(2,1)S(1)}, u32[]{:S(2)}, u32[]{:S(2)}) collective-permute-start(bf16[128,128]{1,0:T(8,128)(2,1)S(1)} %get-tuple-element.37), channel_id=1, source_target_pairs={{0,12},{4,0},{8,4},{12,8},{1,13},{5,1},{9,5},{13,9},{2,14},{6,2},{... | collective-permute-start | bytes 98312 | tf_op jit(solution)/shard_map/ppermute | solution.py:377
  28.2 0.5 coarse_own.1
  28.7 0.0 copy-start.5
  28.7 1.4 %collective-permute-done.6.rest_0_ = bf16[128,128]{1,0:T(8,128)(2,1)S(1)} collective-permute-done((bf16[128,128]{1,0:T(8,128)(2,1)S(1)}, bf16[128,128]{1,0:T(8,128)(2,1)S(1)}, u32[]{:S(2)}, u32[]{:S(2)}) %collective-permute-start.6) | collective-permute-done | bytes 32800 | tf_op jit(solution)/shard_map/ppermute | solution.py:377
  30.1 2.9 %collective-permute-done.8.rest_2_ = bf16[128,128]{1,0:T(8,128)(2,1)S(1)} collective-permute-done((bf16[128,128]{1,0:T(8,128)(2,1)S(1)}, bf16[128,128]{1,0:T(8,128)(2,1)S(1)}, u32[]{:S(2)}, u32[]{:S(2)}) %collective-permute-start.8) | collective-permute-done | bytes 32800 | tf_op jit(solution)/shard_map/ppermute | solution.py:377
  33.1 0.7 %copy-done.9 = s32[1,4,256]{2,1,0:T(4,128)S(1)} copy-done((s32[1,4,256]{2,1,0:T(4,128)S(1)}, s32[1,4,256]{2,1,0:T(4,128)}, u32[]{:S(2)}) %copy-start.9) | copy-done | bytes 4120
  33.7 2.0 %lift.1 = (bf16[2048,128]{1,0:T(8,128)(2,1)S(1)}, bf16[128,2048]{1,0:T(8,128)(2,1)S(1)}, bf16[128,2048]{1,0:T(8,128)(2,1)S(1)}, bf16[128,256]{1,0:T(8,128)(2,1)S...) custom-call(f32[1,128,768]{2,1,0:T(8,128)S(1)} %get-tuple-element.31.picked_ref, ...), custom_call_target="tpu_custom_call" | custom-call | flops 2147483648 | bytes 4194304 | tf_op jit(solution)/shard_map/lift/pallas_call | solution.py:465
  35.7 0.1 collective-permute-start.9
  35.8 3.8 %collective-permute-start.10 = (bf16[128,256]{1,0:T(8,128)(2,1)S(1)}, bf16[128,256]{1,0:T(8,128)(2,1)S(1)}, u32[]{:S(2)}, u32[]{:S(2)}) collective-permute-start(bf16[128,256]{1,0:T(8,128)(2,1)S(1)} %get-tuple-element.43), channel_id=1, source_target_pairs={{0,12},{4,0},{8,4},{12,8},{1,13},{5,1},{9,5},{13,9},{2,14},{6,2},{... | collective-permute-start | bytes 196616 | tf_op jit(solution)/shard_map/ppermute | solution.py:377
  39.6 2.8 %near.3.sums_ref = f32[2048,128]{1,0:T(8,128)S(1)} custom-call(bf16[128,2048]{1,0:T(8,128)(2,1)S(1)} %get-tuple-element.41.sender_ref, bf16[128,2048]{1,0:T(8,128)(2,1)S(1)} %get-tuple-element.40.target_ref, s32[16,768]{1,0:T(8,128)S(1)} %copy-done.2, s32[16,768]{1,0:T(8,128)S(1)} %copy-done.3), custom_call_target="tpu_custom_call" | custom-call | flops 4294967296 | bytes 4194304 | tf_op jit(solution)/shard_map/near/pallas_call | solution.py:481
  42.4 2.4 %collective-permute-done.11.rest_2_ = bf16[128,256]{1,0:T(8,128)(2,1)S(1)} collective-permute-done((bf16[128,256]{1,0:T(8,128)(2,1)S(1)}, bf16[128,256]{1,0:T(8,128)(2,1)S(1)}, u32[]{:S(2)}, u32[]{:S(2)}) %collective-permute-start.11) | collective-permute-done | bytes 65568 | tf_op jit(solution)/shard_map/ppermute | solution.py:377
  44.8 4.6 %far.1 = bf16[2048,128]{1,0:T(8,128)(2,1)} custom-call(bf16[2048,128]{1,0:T(8,128)(2,1)S(1)} %get-tuple-element.39.latent_ref, bf16[128,2048]{1,0:T(8,128)(2,1)S(1)} %get-tuple-element.40.target_ref, s32[16,768]{1,0:T(8,128)S(1)} %copy-done.2, s32[16,768]{1,0:T(8,128)S(1)} %copy-done.3, f32[2048,128]{1,0:T(8,128)S(1)} %near.3.sums_ref, ...), custom_call_target="tpu_custom_call" | custom-call | flops 2147483648 | bytes 4194304 | tf_op jit(solution)/shard_map/far/pallas_call | solution.py:484
  (25 shorter events, 0.1 us)
Async XLA Ops:
  0.0 1.2 %copy-start = (bf16[2048,128]{1,0:T(8,128)(2,1)S(1)}, bf16[2048,128]{1,0:T(8,128)(2,1)}, u32[]{:S(2)}) copy-start(bf16[2048,128]{1,0:T(8,128)(2,1)} %latent_ref.3) | copy-start | bytes 1572868
  1.2 0.7 %copy-start.8 = (s32[1,4,256]{2,1,0:T(4,128)S(1)}, s32[1,4,256]{2,1,0:T(4,128)}, u32[]{:S(2)}) copy-start(s32[1,4,256]{2,1,0:T(4,128)} %param.15) | copy-start | bytes 12292
  1.9 7.2 %copy-start.2 = (s32[16,768]{1,0:T(8,128)S(1)}, s32[16,768]{1,0:T(8,128)}, u32[]{:S(2)}) copy-start(s32[16,768]{1,0:T(8,128)} %source_ref.7) | copy-start | bytes 147460
  1.9 7.2 %copy-start.3 = (s32[16,768]{1,0:T(8,128)S(1)}, s32[16,768]{1,0:T(8,128)}, u32[]{:S(2)}) copy-start(s32[16,768]{1,0:T(8,128)} %place_ref.7) | copy-start | bytes 147460
  2.9 8.9 %collective-permute-start = (bf16[128,256]{1,0:T(8,128)(2,1)S(1)}, bf16[128,256]{1,0:T(8,128)(2,1)S(1)}, u32[]{:S(2)}, u32[]{:S(2)}) collective-permute-start(bf16[128,256]{1,0:T(8,128)(2,1)S(1)} %get-tuple-element.27), channel_id=1, source_target_pairs={{0,4},{4,8},{8,12},{12,0},{1,5},{5,9},{9,13},{13,1},{2,6},{6,10},{... | collective-permute-start | bytes 196616 | tf_op jit(solution)/shard_map/ppermute | solution.py:377
  6.0 5.9 %collective-permute-start.1 = (bf16[128,256]{1,0:T(8,128)(2,1)S(1)}, bf16[128,256]{1,0:T(8,128)(2,1)S(1)}, u32[]{:S(2)}, u32[]{:S(2)}) collective-permute-start(bf16[128,256]{1,0:T(8,128)(2,1)S(1)} %get-tuple-element.28), channel_id=1, source_target_pairs={{0,12},{4,0},{8,4},{12,8},{1,13},{5,1},{9,5},{13,9},{2,14},{6,2},{... | collective-permute-start | bytes 196616 | tf_op jit(solution)/shard_map/ppermute | solution.py:377
  8.1 6.2 %collective-permute-start.2 = (bf16[128,256]{1,0:T(8,128)(2,1)S(1)}, bf16[128,256]{1,0:T(8,128)(2,1)S(1)}, u32[]{:S(2)}, u32[]{:S(2)}) collective-permute-start(bf16[128,256]{1,0:T(8,128)(2,1)S(1)} %get-tuple-element.29), channel_id=1, source_target_pairs={{0,8},{4,12},{8,0},{12,4},{1,9},{5,13},{9,1},{13,5},{2,10},{6,14},... | collective-permute-start | bytes 196616 | tf_op jit(solution)/shard_map/ppermute | solution.py:377
  9.1 5.3 %copy-start.6 = (s32[2,768]{1,0:T(2,128)S(1)}, s32[2,768]{1,0:T(2,128)}, u32[]{:S(2)}) copy-start(s32[2,768]{1,0:T(2,128)} %coarse_source_ref.1) | copy-start | bytes 18436
  9.1 5.3 %copy-start.7 = (s32[2,768]{1,0:T(2,128)S(1)}, s32[2,768]{1,0:T(2,128)}, u32[]{:S(2)}) copy-start(s32[2,768]{1,0:T(2,128)} %coarse_place_ref.1) | copy-start | bytes 18436
  9.1 5.3 %copy-start.11 = (s32[1,4,128]{2,1,0:T(4,128)S(1)}, s32[1,4,128]{2,1,0:T(4,128)}, u32[]{:S(2)}) copy-start(s32[1,4,128]{2,1,0:T(4,128)} %param.19) | copy-start | bytes 6148
  11.9 2.5 %copy-start.10 = (s32[1,4,64]{2,1,0:T(4,128)S(1)}, s32[1,4,64]{2,1,0:T(4,128)}, u32[]{:S(2)}) copy-start(s32[1,4,64]{2,1,0:T(4,128)} %param.16) | copy-start | bytes 3076
  14.4 9.6 %copy-start.1 = (bf16[4,128,128]{2,1,0:T(8,128)(2,1)S(1)}, bf16[4,128,128]{2,1,0:T(8,128)(2,1)}, u32[]{:S(2)}) copy-start(bf16[4,128,128]{2,1,0:T(8,128)(2,1)} %coarse_weights_ref.1) | copy-start | bytes 393220
  18.4 1.6 %collective-permute-start.3 = (bf16[128,128]{1,0:T(8,128)(2,1)S(1)}, bf16[128,128]{1,0:T(8,128)(2,1)S(1)}, u32[]{:S(2)}, u32[]{:S(2)}) collective-permute-start(bf16[128,128]{1,0:T(8,128)(2,1)S(1)} %get-tuple-element.30.refs_0_), channel_id=1, source_target_pairs={{0,1},{1,0},{2,3},{3,2},{4,5},{5,4},{6,7},{7,6},{8,9},{9,8},{10,11... | collective-permute-start | bytes 98312 | tf_op jit(solution)/shard_map/ppermute | solution.py:385
  18.5 4.0 %collective-permute-start.4 = (bf16[128,128]{1,0:T(8,128)(2,1)S(1)}, bf16[128,128]{1,0:T(8,128)(2,1)S(1)}, u32[]{:S(2)}, u32[]{:S(2)}) collective-permute-start(bf16[128,128]{1,0:T(8,128)(2,1)S(1)} %get-tuple-element.30.refs_0_), channel_id=1, source_target_pairs={{0,2},{2,0},{1,3},{3,1},{4,6},{6,4},{5,7},{7,5},{8,10},{10,8},{9,1... | collective-permute-start | bytes 98312 | tf_op jit(solution)/shard_map/ppermute | solution.py:386
  20.0 3.9 %collective-permute-start.5 = (bf16[128,128]{1,0:T(8,128)(2,1)S(1)}, bf16[128,128]{1,0:T(8,128)(2,1)S(1)}, u32[]{:S(2)}, u32[]{:S(2)}) collective-permute-start(bf16[128,128]{1,0:T(8,128)(2,1)S(1)} %collective-permute-done.3.refs_1_), channel_id=1, source_target_pairs={{0,2},{2,0},{1,3},{3,1},{4,6},{6,4},{5,7},{7,5},{8,10},{10,8},{9,1... | collective-permute-start | bytes 98312 | tf_op jit(solution)/shard_map/ppermute | solution.py:386
  24.4 5.8 %collective-permute-start.6 = (bf16[128,128]{1,0:T(8,128)(2,1)S(1)}, bf16[128,128]{1,0:T(8,128)(2,1)S(1)}, u32[]{:S(2)}, u32[]{:S(2)}) collective-permute-start(bf16[128,128]{1,0:T(8,128)(2,1)S(1)} %get-tuple-element.36), channel_id=1, source_target_pairs={{0,4},{4,8},{8,12},{12,0},{1,5},{5,9},{9,13},{13,1},{2,6},{6,10},{... | collective-permute-start | bytes 98312 | tf_op jit(solution)/shard_map/ppermute | solution.py:377
  24.4 5.7 %collective-permute-start.7 = (bf16[128,128]{1,0:T(8,128)(2,1)S(1)}, bf16[128,128]{1,0:T(8,128)(2,1)S(1)}, u32[]{:S(2)}, u32[]{:S(2)}) collective-permute-start(bf16[128,128]{1,0:T(8,128)(2,1)S(1)} %get-tuple-element.37), channel_id=1, source_target_pairs={{0,12},{4,0},{8,4},{12,8},{1,13},{5,1},{9,5},{13,9},{2,14},{6,2},{... | collective-permute-start | bytes 98312 | tf_op jit(solution)/shard_map/ppermute | solution.py:377
  28.2 4.8 %copy-start.4 = (bf16[128,128]{1,0:T(8,128)(2,1)S(1)}, bf16[128,128]{1,0:T(8,128)(2,1)}, u32[]{:S(2)}) copy-start(bf16[128,128]{1,0:T(8,128)(2,1)} %prolong_weight_ref.1) | copy-start | bytes 98308
  28.2 4.8 %collective-permute-start.8 = (bf16[128,128]{1,0:T(8,128)(2,1)S(1)}, bf16[128,128]{1,0:T(8,128)(2,1)S(1)}, u32[]{:S(2)}, u32[]{:S(2)}) collective-permute-start(bf16[128,128]{1,0:T(8,128)(2,1)S(1)} %get-tuple-element.38), channel_id=1, source_target_pairs={{0,8},{4,12},{8,0},{12,4},{1,9},{5,13},{9,1},{13,5},{2,10},{6,14},... | collective-permute-start | bytes 98312 | tf_op jit(solution)/shard_map/ppermute | solution.py:377
  28.7 4.4 %copy-start.5 = (s32[2048]{0:T(1024)S(1)}, s32[2048]{0:T(1024)}, u32[]{:S(2)}) copy-start(s32[2048]{0:T(1024)} %param.20) | copy-start | bytes 24580
  33.1 0.7 %copy-start.9 = (s32[1,4,256]{2,1,0:T(4,128)S(1)}, s32[1,4,256]{2,1,0:T(4,128)}, u32[]{:S(2)}) copy-start(s32[1,4,256]{2,1,0:T(4,128)} %param.15) | copy-start | bytes 12292
  35.7 6.7 %collective-permute-start.9 = (bf16[128,256]{1,0:T(8,128)(2,1)S(1)}, bf16[128,256]{1,0:T(8,128)(2,1)S(1)}, u32[]{:S(2)}, u32[]{:S(2)}) collective-permute-start(bf16[128,256]{1,0:T(8,128)(2,1)S(1)} %get-tuple-element.42), channel_id=1, source_target_pairs={{0,4},{4,8},{8,12},{12,0},{1,5},{5,9},{9,13},{13,1},{2,6},{6,10},{... | collective-permute-start | bytes 196616 | tf_op jit(solution)/shard_map/ppermute | solution.py:377
  35.8 6.6 %collective-permute-start.10 = (bf16[128,256]{1,0:T(8,128)(2,1)S(1)}, bf16[128,256]{1,0:T(8,128)(2,1)S(1)}, u32[]{:S(2)}, u32[]{:S(2)}) collective-permute-start(bf16[128,256]{1,0:T(8,128)(2,1)S(1)} %get-tuple-element.43), channel_id=1, source_target_pairs={{0,12},{4,0},{8,4},{12,8},{1,13},{5,1},{9,5},{13,9},{2,14},{6,2},{... | collective-permute-start | bytes 196616 | tf_op jit(solution)/shard_map/ppermute | solution.py:377
  39.6 5.2 %collective-permute-start.11 = (bf16[128,256]{1,0:T(8,128)(2,1)S(1)}, bf16[128,256]{1,0:T(8,128)(2,1)S(1)}, u32[]{:S(2)}, u32[]{:S(2)}) collective-permute-start(bf16[128,256]{1,0:T(8,128)(2,1)S(1)} %get-tuple-element.44), channel_id=1, source_target_pairs={{0,8},{4,12},{8,0},{12,4},{1,9},{5,13},{9,1},{13,5},{2,10},{6,14},... | collective-permute-start | bytes 196616 | tf_op jit(solution)/shard_map/ppermute | solution.py:377

commit v2 on v1

v2 whole, which is shorter than its diff:
```python
import functools

import jax
import jax.numpy as jnp
from jax import lax
from jax.experimental import pallas as pl
from jax.experimental.pallas import tpu as pltpu
from jax.sharding import PartitionSpec as P

BF16 = jnp.bfloat16
F32 = jnp.float32
I32 = jnp.int32
BLOCK = 128
VMEM_BYTES = 32 << 20
GROUP = 4
LAG = 2


def dot(left, right):
    return jnp.dot(left, right, preferred_element_type=F32)


def dot_last(left, right):
    return lax.dot_general(left, right, (((1,), (1,)), ((), ())), preferred_element_type=F32)


def rows_hot(index_row, height):
    shape = (height, index_row.shape[1])
    index = jnp.broadcast_to(index_row, shape).astype(jnp.int16)
    return jnp.where(
        index == lax.broadcasted_iota(jnp.int16, shape, 0), jnp.ones((), BF16), jnp.zeros((), BF16)
    )


def silu_of_half(half):
    return half + half * jnp.tanh(half)


def halved(weight):
    return weight * jnp.asarray(0.5, BF16)


class Grid:
    def __init__(self, mesh, pool_capacity, coarse_capacity, coarse_blocks, slot_count):
        self.dom_count = mesh.shape["dom"]
        self.sub_count = mesh.shape["sub"]
        self.chip_count = mesh.shape["chip"]
        self.places = self.sub_count * self.chip_count
        self.mirrored = self.dom_count == 4
        self.steps = (1, 2, 3) if self.mirrored else tuple(sorted({1, self.dom_count - 1, 2 % self.dom_count}))
        self.owners = len(range(0, self.places, 4))
        self.swapped = self.sub_count == 2 and self.chip_count == 2
        self.pool_capacity = pool_capacity
        self.coarse_capacity = coarse_capacity
        self.blocks = coarse_blocks
        self.pieces = slot_count // BLOCK
        self.slots = self.places * pool_capacity
        self.pooled_rows = self.owners * pool_capacity
        self.list_rows = 2 * coarse_blocks * self.pieces + self.dom_count
        self.packed_rows = -(-self.list_rows // 16) * 16
        self.packet = self.pooled_rows + 2 * self.packed_rows

    def partner(self, dom, step):
        return dom ^ step if self.mirrored else (dom + step) % self.dom_count

    def partner_here(self, step):
        own = lax.axis_index("dom")
        return own ^ step if self.mirrored else lax.rem(own + step, self.dom_count)

    def halo_place(self, source_dom):
        own = lax.axis_index("dom")
        if self.mirrored:
            step = source_dom ^ own
        else:
            step = own - source_dom
            step = jnp.where(step < 0, step + self.dom_count, step)
        place = jnp.zeros_like(step)
        for index, value in enumerate(self.steps):
            place = jnp.where(step == value, index, place)
        return place

    def own_place(self):
        return lax.axis_index("sub") * self.chip_count + lax.axis_index("chip")

    def slot_order(self, slots, place):
        return slots ^ (place * self.pool_capacity) if self.swapped else slots


def turned(weight):
    return halved(weight).T


def send_kernel(grid, latent_hbm, lists_hbm, weights_hbm, table_ref, *rest):
    sent_refs = rest[: len(grid.steps)]
    latent_ref, lists_ref, weight_ref, arrived = rest[len(grid.steps) :]
    copies = [
        pltpu.make_async_copy(lists_hbm.at[0], lists_ref, arrived.at[0]),
        pltpu.make_async_copy(weights_hbm.at[0, 0], weight_ref, arrived.at[1]),
        pltpu.make_async_copy(latent_hbm, latent_ref, arrived.at[2]),
    ]
    for copy in copies:
        copy.start()
    for copy in copies:
        copy.wait()
    table = latent_ref[...].T
    table_ref[...] = table
    weight = turned(weight_ref[...])
    for step, out_ref in zip(grid.steps, sent_refs):
        index_row = lists_ref[pl.ds(grid.partner_here(step), 1), :]
        picked = dot(table, rows_hot(index_row, table.shape[1])).astype(BF16)
        out_ref[...] = dot(weight, picked).astype(BF16)


def near_edges(table, source_ref, place_ref, weights_ref, layer, target_ref, sums_ref, terms_ref):
    features, node_count = table.shape
    block_count, slot_count = source_ref.shape
    local_count = slot_count * 3 // 4
    window = min(3 * BLOCK, node_count)
    both = jnp.concatenate([turned(weights_ref[layer, 0]), turned(weights_ref[layer, 1])], axis=0)
    terms_ref[...] = dot(both, table).astype(BF16)
    target_ref[...] = terms_ref[features:, :]

    def messages(block):
        start = min(max(block * BLOCK - BLOCK, 0), node_count - window)
        terms = jnp.concatenate(
            [
                terms_ref[:features, start : start + window],
                terms_ref[features:, block * BLOCK : (block + 1) * BLOCK],
            ],
            axis=1,
        )
        places = rows_hot(place_ref[block : block + 1, :local_count], BLOCK)
        sources = rows_hot(source_ref[block : block + 1, :local_count] - start, window)
        picked = dot(terms, jnp.concatenate([sources, places], axis=0))
        return silu_of_half(picked).astype(BF16)

    def add_up(block, message):
        places = rows_hot(place_ref[block : block + 1, :local_count], BLOCK)
        sums_ref[:, block * BLOCK : (block + 1) * BLOCK] = dot_last(message, places)

    waiting = None
    for block in range(block_count):
        message = messages(block)
        if waiting is not None:
            add_up(*waiting)
        waiting = (block, message)
    add_up(*waiting)


def near_kernel(layer, table_ref, source_ref, place_ref, weights_ref, target_ref, sums_ref, terms_ref):
    near_edges(table_ref[...], source_ref, place_ref, weights_ref, layer, target_ref, sums_ref, terms_ref)


def far_edges(grid, layer, table_ref, target_ref, source_ref, place_ref, sums_ref, weights_ref, halo_refs, both_ref, write):
    features, node_count = table_ref.shape
    block_count, slot_count = source_ref.shape
    local_count = slot_count * 3 // 4
    capacity = halo_refs[0].shape[1]
    halo = jnp.concatenate([ref[...] for ref in halo_refs], axis=1)
    halo_rows = halo.shape[1]
    update_weights = jnp.concatenate([turned(weights_ref[layer, 2]), turned(weights_ref[layer, 3])], axis=1)
    shift = capacity.bit_length() - 1
    slots = source_ref[:, local_count:] - node_count
    source_dom = lax.shift_right_logical(slots, shift)
    far_sources = grid.halo_place(source_dom) * capacity + (slots & (capacity - 1))
    both_ref[features:, :] = table_ref[...]

    def messages(block):
        terms = jnp.concatenate([halo, target_ref[:, block * BLOCK : (block + 1) * BLOCK]], axis=1)
        places = rows_hot(place_ref[block : block + 1, local_count:], BLOCK)
        sources = rows_hot(far_sources[block : block + 1, :], halo_rows)
        picked = dot(terms, jnp.concatenate([sources, places], axis=0))
        return silu_of_half(picked).astype(BF16)

    def add_up(block, message):
        columns = slice(block * BLOCK, (block + 1) * BLOCK)
        places = rows_hot(place_ref[block : block + 1, local_count:], BLOCK)
        both_ref[:features, columns] = (sums_ref[:, columns] + dot_last(message, places)).astype(BF16)

    def update(block):
        columns = slice((block - GROUP + 1) * BLOCK, (block + 1) * BLOCK)
        change = silu_of_half(dot(update_weights, both_ref[:, columns]))
        write(columns, (both_ref[features:, columns].astype(F32) + change).astype(BF16))

    waiting = []
    for block in range(block_count):
        waiting.append((block, messages(block)))
        if len(waiting) > LAG:
            done = waiting.pop(0)
            add_up(*done)
            if (done[0] + 1) % GROUP == 0 and done[0] >= 0:
                update(done[0])
    for done in waiting:
        add_up(*done)
        if (done[0] + 1) % GROUP == 0:
            update(done[0])


def lane_rows(ref):
    pieces = []
    for block in range(ref.shape[0]):
        for start in range(0, ref.shape[1], BLOCK):
            pieces.append(ref[block : block + 1, start : start + BLOCK])
    return pieces


def far_pool_kernel(
    grid,
    table_ref,
    target_ref,
    source_ref,
    place_ref,
    sums_ref,
    weights_ref,
    pool_ref,
    coarse_source_ref,
    coarse_place_ref,
    coarse_send_ref,
    *rest,
):
    halo_refs, (first_ref, packet_ref, both_ref) = rest[:-3], rest[-3:]

    def write(columns, value):
        first_ref[:, columns] = value

    pieces = lane_rows(coarse_source_ref) + [coarse_send_ref[0]] + lane_rows(coarse_place_ref)
    spare = grid.packed_rows - grid.list_rows
    if spare:
        pieces.append(jnp.zeros((spare, BLOCK), I32))
    whole = jnp.concatenate(pieces, axis=0) + 1
    high = lax.shift_right_logical(whole, 8)
    packet_ref[grid.pooled_rows :, :] = jnp.concatenate(
        [high.astype(F32), (whole & 255).astype(F32)], axis=0
    ).astype(BF16)
    far_edges(
        grid, 0, table_ref, target_ref, source_ref, place_ref, sums_ref, weights_ref, halo_refs, both_ref, write
    )
    for owner in range(grid.owners):
        hot = rows_hot(pool_ref[0, 4 * owner : 4 * owner + 1, :], first_ref.shape[1])
        pooled = dot(first_ref[...], hot).astype(BF16).T
        packet_ref[owner * grid.pool_capacity : (owner + 1) * grid.pool_capacity, :] = pooled


def far_kernel(grid, table_ref, target_ref, source_ref, place_ref, sums_ref, weights_ref, *rest):
    halo_refs, (out_ref, both_ref) = rest[:-2], rest[-2:]

    def write(columns, value):
        out_ref[columns, :] = value.T

    far_edges(
        grid, 1, table_ref, target_ref, source_ref, place_ref, sums_ref, weights_ref, halo_refs, both_ref, write
    )


def ahead_kernel(grid, first_ref, prolong_ref, lists_ref, out_ref):
    indices = prolong_ref[...]
    shift = (4 * grid.pool_capacity).bit_length() - 1
    indices = lax.shift_right_logical(indices, shift) * grid.pool_capacity + (indices & (grid.pool_capacity - 1))
    indices = indices.astype(F32)
    row = jnp.concatenate([indices[block : block + 1, :] for block in range(indices.shape[0])], axis=1)
    extra = jnp.concatenate([row, jnp.zeros((15, row.shape[1]), F32)], axis=0).astype(BF16)
    table = jnp.concatenate([first_ref[...], extra], axis=0)
    capacity = lists_ref.shape[2]
    for index, step in enumerate(grid.steps):
        index_row = lists_ref[0, pl.ds(grid.partner_here(step), 1), :]
        picked = dot(table, rows_hot(index_row, table.shape[1]))
        out_ref[:, index * capacity : (index + 1) * capacity] = picked.astype(BF16)


def owner_lists(grid, packets, owner, place):
    if grid.swapped:
        rows = packets[0][grid.pooled_rows :, :].astype(F32)
        for other in range(1, grid.places):
            rows = jnp.where(place == other, packets[other][grid.pooled_rows :, :].astype(F32), rows)
    else:
        rows = packets[4 * owner][grid.pooled_rows :, :].astype(F32)
    whole = rows[: grid.packed_rows] * 256.0 + rows[grid.packed_rows :]
    return whole.astype(I32) - 1


def owner_table(grid, packets, owner):
    start = owner * grid.pool_capacity
    return jnp.concatenate([packet[start : start + grid.pool_capacity, :] for packet in packets], axis=0)


def coarse_send_kernel(grid, weights_ref, *refs):
    packets = refs[: grid.places]
    outs = refs[grid.places : grid.places + len(grid.steps)]
    lists_ref = refs[-1]
    place = grid.own_place()
    first_list = grid.blocks * grid.pieces
    for owner in range(grid.owners):
        lists_ref[...] = owner_lists(grid, packets, owner, place)
        table = owner_table(grid, packets, owner)
        terms = dot(table, halved(weights_ref[0])).astype(BF16).T
        for step, out_ref in zip(grid.steps, outs):
            index_row = grid.slot_order(lists_ref[pl.ds(first_list + grid.partner_here(step), 1), :], place)
            picked = dot(terms, rows_hot(index_row, grid.slots))
            out_ref[owner * BLOCK : (owner + 1) * BLOCK, :] = picked.astype(BF16)


def coarse_own_kernel(grid, weights_ref, *refs):
    packets = refs[: grid.places]
    picked_ref, source_out, place_out, rows_out, lists_ref = refs[grid.places :]
    place = grid.own_place()
    first_slot = place * grid.pool_capacity
    block = lax.shift_right_logical(first_slot, BLOCK.bit_length() - 1)
    within = first_slot & (BLOCK - 1)
    shift = grid.coarse_capacity.bit_length() - 1
    for owner in range(grid.owners):
        lists_ref[...] = owner_lists(grid, packets, owner, place)
        sources = jnp.concatenate(
            [lists_ref[pl.ds(block * grid.pieces + piece, 1), :] for piece in range(grid.pieces)], axis=1
        )
        offset = grid.blocks * grid.pieces + grid.dom_count
        places = jnp.concatenate(
            [lists_ref[pl.ds(offset + block * grid.pieces + piece, 1), :] for piece in range(grid.pieces)], axis=1
        )
        places = places - within
        places = jnp.where((places >= 0) & (places < grid.pool_capacity), places, -1)
        halo_slots = sources - grid.slots
        source_dom = lax.shift_right_arithmetic(halo_slots, shift)
        halo_sources = grid.halo_place(source_dom) * grid.coarse_capacity + (halo_slots & (grid.coarse_capacity - 1))
        is_halo = halo_slots >= 0
        source_out[owner : owner + 1, :] = jnp.where(is_halo, halo_sources, -1)
        place_out[owner : owner + 1, :] = places
        own_sources = jnp.where(is_halo, -1, grid.slot_order(sources, place))

        table = owner_table(grid, packets, owner)
        rows = table[: grid.pool_capacity]
        if not grid.swapped:
            for other in range(1, grid.places):
                other_rows = table[other * grid.pool_capacity : (other + 1) * grid.pool_capacity]
                rows = jnp.where(place == other, other_rows, rows)
        rows_out[owner * grid.pool_capacity : (owner + 1) * grid.pool_capacity, :] = rows
        sender = dot(table, halved(weights_ref[0])).astype(BF16).T
        target = dot(rows, halved(weights_ref[1])).astype(BF16).T
        hot = jnp.concatenate([rows_hot(own_sources, grid.slots), rows_hot(places, grid.pool_capacity)], axis=0)
        picked_ref[owner] = dot(jnp.concatenate([sender, target], axis=1), hot)


def lift(table, prolonged, index_row):
    pooled_rows = prolonged.shape[1] // 2
    hot = rows_hot(index_row, pooled_rows)
    hot = jnp.concatenate([hot, hot], axis=0)
    return (table.astype(F32) + silu_of_half(dot(prolonged, hot))).astype(BF16)


def lift_halo_kernel(
    grid,
    picked_ref,
    source_ref,
    place_ref,
    rows_ref,
    ahead_ref,
    coarse_weights_ref,
    prolong_weight_ref,
    weights_ref,
    *rest,
):
    count = len(grid.steps)
    halo_refs, prolonged_ref, sent_refs = rest[:count], rest[count], rest[count + 1 :]
    features = rows_ref.shape[1]
    update_weights = jnp.concatenate([halved(coarse_weights_ref[2]), halved(coarse_weights_ref[3])], axis=0)
    prolonged = []
    for owner in range(grid.owners):
        halo = jnp.concatenate([ref[owner * BLOCK : (owner + 1) * BLOCK, :] for ref in halo_refs], axis=1)
        picked = picked_ref[owner] + dot(halo, rows_hot(source_ref[owner : owner + 1, :], halo.shape[1]))
        message = silu_of_half(picked).astype(BF16)
        places = rows_hot(place_ref[owner : owner + 1, :], grid.pool_capacity)
        summed = dot_last(places, message).astype(BF16)
        rows = rows_ref[owner * grid.pool_capacity : (owner + 1) * grid.pool_capacity, :]
        update = dot(jnp.concatenate([summed, rows], axis=1), update_weights)
        coarse = (rows.astype(F32) + silu_of_half(update)).astype(BF16)
        prolonged.append(dot(coarse, halved(prolong_weight_ref[...])))
    prolonged = jnp.concatenate(prolonged, axis=0)
    high = prolonged.astype(BF16)
    low = (prolonged - high.astype(F32)).astype(BF16)
    parts = jnp.concatenate([high, low], axis=0).T
    prolonged_ref[...] = parts
    weight = turned(weights_ref[1, 0])
    index_row = ahead_ref[features : features + 1, :].astype(F32).astype(I32)
    lifted = lift(ahead_ref[:features, :], parts, index_row)
    terms = dot(weight, lifted).astype(BF16)
    capacity = sent_refs[0].shape[1]
    for index, out_ref in enumerate(sent_refs):
        out_ref[...] = terms[:, index * capacity : (index + 1) * capacity]


def lift_near_kernel(
    grid,
    first_ref,
    prolonged_ref,
    prolong_ref,
    source_ref,
    place_ref,
    weights_ref,
    lifted_ref,
    target_ref,
    sums_ref,
    terms_ref,
):
    indices = prolong_ref[...]
    shift = (4 * grid.pool_capacity).bit_length() - 1
    indices = lax.shift_right_logical(indices, shift) * grid.pool_capacity + (indices & (grid.pool_capacity - 1))
    row = jnp.concatenate([indices[block : block + 1, :] for block in range(indices.shape[0])], axis=1)
    lifted = lift(first_ref[...], prolonged_ref[...], row)
    lifted_ref[...] = lifted
    near_edges(lifted, source_ref, place_ref, weights_ref, 1, target_ref, sums_ref, terms_ref)


def call(kernel, outs, scratch=(), flops=0, name=None, **specs):
    return pl.pallas_call(
        kernel,
        out_shape=tuple(jax.ShapeDtypeStruct(shape, dtype) for shape, dtype in outs),
        scratch_shapes=list(scratch),
        compiler_params=pltpu.CompilerParams(vmem_limit_bytes=VMEM_BYTES),
        cost_estimate=pl.CostEstimate(flops=flops, bytes_accessed=4 << 20, transcendentals=0),
        name=name,
        **specs,
    )


def swap_dom(grid, arrays):
    return [
        lax.ppermute(array, "dom", [(dom, grid.partner(dom, step)) for dom in range(grid.dom_count)])
        for array, step in zip(arrays, grid.steps)
    ]


def trade_packets(grid, packet):
    if grid.swapped:
        pairs = [(0, 1), (1, 0)]
        over = lax.ppermute(packet, "sub", pairs)
        across = lax.ppermute(packet, "chip", pairs)
        return [packet, across, over, lax.ppermute(over, "chip", pairs)]
    gathered = lax.all_gather(packet, ("sub", "chip"), axis=0, tiled=False)
    return [gathered[place] for place in range(grid.places)]


def body(
    mesh,
    fine_nodes,
    fine_src,
    fine_dst,
    halo_send,
    pool_send,
    coarse_src,
    coarse_dst,
    coarse_send,
    prolong_idx,
    fine_weights,
    coarse_weights,
    prolong_weight,
):
    node_count, features = fine_nodes.shape
    grid = Grid(mesh, pool_send.shape[2], coarse_send.shape[2], coarse_src.shape[0], coarse_src.shape[1])
    halo_capacity = halo_send.shape[2]
    steps = len(grid.steps)
    table = ((features, node_count), BF16)
    sums_table = ((features, node_count), F32)
    halo_outs = [((features, halo_capacity), BF16)] * steps
    two_tables = pltpu.VMEM((2 * features, node_count), BF16)
    prolong_rows = prolong_idx.reshape(node_count // BLOCK, BLOCK)
    big = 1 << 30
    in_hbm = pl.BlockSpec(memory_space=pltpu.HBM)

    nodes, *sent = call(
        functools.partial(send_kernel, grid),
        [table, *halo_outs],
        [
            pltpu.VMEM((node_count, features), BF16),
            pltpu.VMEM(halo_send.shape[1:], I32),
            pltpu.VMEM((features, features), BF16),
            pltpu.SemaphoreType.DMA((3,)),
        ],
        flops=big,
        name="send",
        in_specs=[in_hbm] * 3,
    )(fine_nodes, halo_send, fine_weights)
    halo = swap_dom(grid, sent)
    target, sums = call(
        functools.partial(near_kernel, 0), [table, sums_table], [two_tables], flops=4 * big, name="near"
    )(nodes, fine_src, fine_dst, fine_weights)
    first, packet = call(
        functools.partial(far_pool_kernel, grid),
        [table, ((grid.packet, features), BF16)],
        [two_tables],
        flops=2 * big,
        name="far_pool",
    )(
        nodes,
        target,
        fine_src,
        fine_dst,
        sums,
        fine_weights,
        pool_send,
        coarse_src,
        coarse_dst,
        coarse_send,
        *halo,
    )
    packets = trade_packets(grid, packet)
    (ahead,) = call(
        functools.partial(ahead_kernel, grid), [((features + 16, steps * halo_capacity), BF16)], flops=big, name="ahead"
    )(first, prolong_rows, halo_send)
    lists_scratch = pltpu.VMEM((grid.packed_rows, BLOCK), I32)
    sent = call(
        functools.partial(coarse_send_kernel, grid),
        [((grid.owners * features, grid.coarse_capacity), BF16)] * steps,
        [lists_scratch],
        flops=big // 2,
        name="coarse_send",
    )(coarse_weights, *packets)
    coarse_halo = swap_dom(grid, sent)
    coarse_slots = coarse_src.shape[1]
    picked, sources, places, rows = call(
        functools.partial(coarse_own_kernel, grid),
        [
            ((grid.owners, features, coarse_slots), F32),
            ((grid.owners, coarse_slots), I32),
            ((grid.owners, coarse_slots), I32),
            ((grid.pooled_rows, features), BF16),
        ],
        [lists_scratch],
        flops=4 * big,
        name="coarse_own",
    )(coarse_weights, *packets)
    prolonged, *sent = call(
        functools.partial(lift_halo_kernel, grid),
        [((features, 2 * grid.pooled_rows), BF16), *halo_outs],
        flops=big,
        name="lift_halo",
    )(picked, sources, places, rows, ahead, coarse_weights, prolong_weight, fine_weights, *coarse_halo)
    halo = swap_dom(grid, sent)
    lifted, target, sums = call(
        functools.partial(lift_near_kernel, grid),
        [table, table, sums_table],
        [two_tables],
        flops=4 * big,
        name="lift_near",
    )(first, prolonged, prolong_rows, fine_src, fine_dst, fine_weights)
    (fine_out,) = call(
        functools.partial(far_kernel, grid), [((node_count, features), BF16)], [two_tables], flops=2 * big, name="far"
    )(lifted, target, fine_src, fine_dst, sums, fine_weights, *halo)
    return fine_out


def solution(mesh):
    split = ("groups", "dom", "sub", "chip")
    return jax.shard_map(
        functools.partial(body, mesh),
        mesh=mesh,
        in_specs=(
            P(split, None),
            P(split, None),
            P(split, None),
            P(split, None, None),
            P(split, None, None),
            P(split, None),
            P(split, None),
            P(split, None, None),
            P(split),
            P(),
            P(),
            P(),
        ),
        out_specs=P(split, None),
        check_vma=False,
    )
```

time: 49.6 us -> 46.5 us (0.938)
  waiting for transfers between devices: 11.9 us -> 10.2 us
  Pallas kernels: 18.1 us -> 17 us
  starting transfers between devices: 16.6 us -> 16.1 us
    ppermute x11, waiting for transfers between devices: 11.9 us -> 10.2 us  [the longest x9 7.25 us: swap_dom(): lax.ppermute(array, 'dom', [(dom, grid.partner(dom, step)) for dom in ran...]
    unnamed x24 -> x28, local copies, waits for them, and re-layouts: 1.53 us -> 2.73 us
    pallas_call x6 -> x7, Pallas kernels: 17.3 us -> 16.1 us  [the longest x1 3.87 us: body(): call(functools.partial(far_kernel, grid), [((node_count, features), BF16)...]
    squeeze x1 -> x0, local copies, waits for them, and re-layouts: 1.04 us -> none  [body(): fine_weights[1]]
  transfers between devices with their start and end apart: 12 -> 12, of which waited for: 6 -> 6; matrix products, arithmetic and copies ran while one was open for 0% -> 0% of each run, Pallas kernels for 12% -> 16%
where the time goes in v2:
time: 46.5 us; the launch traced here: 46.2 us
  Pallas kernels  17 us (37%)
  starting transfers between devices  16.1 us (35%)
  waiting for transfers between devices  10.2 us (22%)
  local copies, waits for them, and re-layouts  2.73 us (6%)
    ppermute x9, starting transfers between devices, swap_dom(): lax.ppermute(array, 'dom', [(dom, grid.partner(dom, step)) for dom in ran...  14.6 us
    ppermute x9, waiting for transfers between devices, swap_dom(): lax.ppermute(array, 'dom', [(dom, grid.partner(dom, step)) for dom in ran...  7.25 us
    pallas_call x1, Pallas kernels, body(): call(functools.partial(far_kernel, grid), [((node_count, features), BF16)...  3.87 us
    pallas_call x1, Pallas kernels, body(): call(functools.partial(lift_near_kernel, grid), [table, table, sums_table...  3.2 us
    pallas_call x1, Pallas kernels, body(): call(functools.partial(far_pool_kernel, grid), [table, ((grid.packet, fea...  3.01 us
    pallas_call x1, Pallas kernels, body(): call(functools.partial(near_kernel, 0), [table, sums_table], [two_tables]...  3 us
    unnamed x28, local copies, waits for them, and re-layouts  2.73 us
    ppermute x1, waiting for transfers between devices, trade_packets(): over = lax.ppermute(packet, 'sub', pairs)  2.42 us
  transfers between devices with their start and end apart: 12, of which 6 were waited for; matrix products, arithmetic and copies ran while one was open for 0% of the time, Pallas kernels for 16%

profile of v2, /device:TPU:0, one launch (start us, length us, event | category | flops | bytes accessed | tf_op | source)
XLA Modules:
  0.0 46.2 jit_solution(10902276944837470732)
XLA Ops:
  0.0 1.0 %copy-done = bf16[2048,128]{1,0:T(8,128)(2,1)S(1)} copy-done((bf16[2048,128]{1,0:T(8,128)(2,1)S(1)}, bf16[2048,128]{1,0:T(8,128)(2,1)}, u32[]{:S(2)}) %copy-start) | copy-done | bytes 524312
  1.0 0.9 %copy-done.1 = bf16[2,4,128,128]{3,2,1,0:T(8,128)(2,1)S(1)} copy-done((bf16[2,4,128,128]{3,2,1,0:T(8,128)(2,1)S(1)}, bf16[2,4,128,128]{3,2,1,0:T(8,128)(2,1)}, u32[]{:S(2)}) %copy-start.1) | copy-done | bytes 262168
  2.0 0.7 %copy-done.10 = s32[1,4,256]{2,1,0:T(4,128)S(1)} copy-done((s32[1,4,256]{2,1,0:T(4,128)S(1)}, s32[1,4,256]{2,1,0:T(4,128)}, u32[]{:S(2)}) %copy-start.10) | copy-done | bytes 4120
  2.7 1.3 %send.1 = (bf16[128,2048]{1,0:T(8,128)(2,1)S(1)}, bf16[128,256]{1,0:T(8,128)(2,1)S(1)}, bf16[128,256]{1,0:T(8,128)(2,1)S(1)}, bf16[128,256]{1,0:T(8,128)(2,1)S(1)}) custom-call(bf16[2048,128]{1,0:T(8,128)(2,1)S(1)} %copy-done, s32[1,4,256]{2,1,0:T(4,128)S(1)} %copy-done.10, bf16[2,4,128,128]{3,2,1,0:T(8,128)(2,1)S(1)} %copy-done.1), custom_call_target="tpu_custom_call" | custom-call | flops 1073741824 | bytes 4194304 | tf_op jit(solution)/shard_map/send/pallas_call | solution.py:468
  4.0 3.1 %collective-permute-start = (bf16[128,256]{1,0:T(8,128)(2,1)S(1)}, bf16[128,256]{1,0:T(8,128)(2,1)S(1)}, u32[]{:S(2)}, u32[]{:S(2)}) collective-permute-start(bf16[128,256]{1,0:T(8,128)(2,1)S(1)} %get-tuple-element.30), channel_id=1, source_target_pairs={{0,4},{4,0},{8,12},{12,8},{1,5},{5,1},{9,13},{13,9},{2,6},{6,2},{1... | collective-permute-start | bytes 196616 | tf_op jit(solution)/shard_map/ppermute | solution.py:426
  7.1 2.6 %collective-permute-start.1 = (bf16[128,256]{1,0:T(8,128)(2,1)S(1)}, bf16[128,256]{1,0:T(8,128)(2,1)S(1)}, u32[]{:S(2)}, u32[]{:S(2)}) collective-permute-start(bf16[128,256]{1,0:T(8,128)(2,1)S(1)} %get-tuple-element.31), channel_id=1, source_target_pairs={{0,8},{4,12},{8,0},{12,4},{1,9},{5,13},{9,1},{13,5},{2,10},{6,14},... | collective-permute-start | bytes 196616 | tf_op jit(solution)/shard_map/ppermute | solution.py:426
  9.7 0.0 copy-start.8
  9.7 0.0 copy-start.9
  9.7 0.0 copy-start.13
  9.7 3.0 %near.1 = (bf16[128,2048]{1,0:T(8,128)(2,1)S(1)}, f32[128,2048]{1,0:T(8,128)S(1)}) custom-call(bf16[128,2048]{1,0:T(8,128)(2,1)S(1)} %get-tuple-element.27.table_ref, s32[16,768]{1,0:T(8,128)S(1)} %copy-done.4, s32[16,768]{1,0:T(8,128)S(1)} %copy-done.5, bf16[2,4,128,128]{3,2,1,0:T(8,128)(2,1)S(1)} %copy-done.2), custom_call_target="tpu_custom_call" | custom-call | flops 4294967296 | bytes 4194304 | tf_op jit(solution)/shard_map/near/pallas_call | solution.py:482
  12.7 1.6 %collective-permute-done.1.rest_1_ = bf16[128,256]{1,0:T(8,128)(2,1)S(1)} collective-permute-done((bf16[128,256]{1,0:T(8,128)(2,1)S(1)}, bf16[128,256]{1,0:T(8,128)(2,1)S(1)}, u32[]{:S(2)}, u32[]{:S(2)}) %collective-permute-start.1) | collective-permute-done | bytes 65568 | tf_op jit(solution)/shard_map/ppermute | solution.py:426
  14.3 1.4 %collective-permute-done.2.rest_2_ = bf16[128,256]{1,0:T(8,128)(2,1)S(1)} collective-permute-done((bf16[128,256]{1,0:T(8,128)(2,1)S(1)}, bf16[128,256]{1,0:T(8,128)(2,1)S(1)}, u32[]{:S(2)}, u32[]{:S(2)}) %collective-permute-start.2) | collective-permute-done | bytes 65568 | tf_op jit(solution)/shard_map/ppermute | solution.py:426
  15.8 0.0 copy-start.7
  15.8 3.0 %far_pool.1 = (bf16[128,2048]{1,0:T(8,128)(2,1)S(1)}, bf16[128,128]{1,0:T(8,128)(2,1)S(1)}) custom-call(bf16[128,2048]{1,0:T(8,128)(2,1)S(1)} %get-tuple-element.27.table_ref, bf16[128,2048]{1,0:T(8,128)(2,1)S(1)} %get-tuple-element.28.target_ref, s32[16,768]{1,0:T(8,128)S(1)} %copy-done.4, s32[16,768]{1,0:T(8,128)S(1)} %copy-done.5, ...), custom_call_target="tpu_custom_call" | custom-call | flops 2147483648 | bytes 4194304 | tf_op jit(solution)/shard_map/far_pool/pallas_call | solution.py:485
  18.8 1.5 %collective-permute-start.4 = (bf16[128,128]{1,0:T(8,128)(2,1)S(1)}, bf16[128,128]{1,0:T(8,128)(2,1)S(1)}, u32[]{:S(2)}, u32[]{:S(2)}) collective-permute-start(bf16[128,128]{1,0:T(8,128)(2,1)S(1)} %get-tuple-element.34.refs_0_), channel_id=1, source_target_pairs={{0,2},{2,0},{1,3},{3,1},{4,6},{6,4},{5,7},{7,5},{8,10},{10,8},{9,1... | collective-permute-start | bytes 98312 | tf_op jit(solution)/shard_map/ppermute | solution.py:434
  20.3 2.4 %collective-permute-done.4.refs_2_ = bf16[128,128]{1,0:T(8,128)(2,1)S(1)} collective-permute-done((bf16[128,128]{1,0:T(8,128)(2,1)S(1)}, bf16[128,128]{1,0:T(8,128)(2,1)S(1)}, u32[]{:S(2)}, u32[]{:S(2)}) %collective-permute-start.4) | collective-permute-done | bytes 32800 | tf_op jit(solution)/shard_map/ppermute | solution.py:434
  22.8 0.6 %ahead.1.ahead_ref = bf16[144,768]{1,0:T(8,128)(2,1)S(1)} custom-call(bf16[128,2048]{1,0:T(8,128)(2,1)S(1)} %get-tuple-element.33.first_ref, s32[16,128]{1,0:T(8,128)S(1)} %bitcast.1, s32[1,4,256]{2,1,0:T(4,128)S(1)} %copy-done.11), custom_call_target="tpu_custom_call" | custom-call | flops 1073741824 | bytes 4194304 | tf_op jit(solution)/shard_map/ahead/pallas_call | solution.py:505
  23.4 0.5 %collective-permute-done.5.refs_3_ = bf16[128,128]{1,0:T(8,128)(2,1)S(1)} collective-permute-done((bf16[128,128]{1,0:T(8,128)(2,1)S(1)}, bf16[128,128]{1,0:T(8,128)(2,1)S(1)}, u32[]{:S(2)}, u32[]{:S(2)}) %collective-permute-start.5) | collective-permute-done | bytes 32800 | tf_op jit(solution)/shard_map/ppermute | solution.py:436
  24.0 0.4 coarse_send.1
  24.4 0.1 collective-permute-start.6
  24.5 2.3 %collective-permute-start.7 = (bf16[128,128]{1,0:T(8,128)(2,1)S(1)}, bf16[128,128]{1,0:T(8,128)(2,1)S(1)}, u32[]{:S(2)}, u32[]{:S(2)}) collective-permute-start(bf16[128,128]{1,0:T(8,128)(2,1)S(1)} %get-tuple-element.40), channel_id=1, source_target_pairs={{0,8},{4,12},{8,0},{12,4},{1,9},{5,13},{9,1},{13,5},{2,10},{6,14},... | collective-permute-start | bytes 98312 | tf_op jit(solution)/shard_map/ppermute | solution.py:426
  26.8 2.0 %collective-permute-start.8 = (bf16[128,128]{1,0:T(8,128)(2,1)S(1)}, bf16[128,128]{1,0:T(8,128)(2,1)S(1)}, u32[]{:S(2)}, u32[]{:S(2)}) collective-permute-start(bf16[128,128]{1,0:T(8,128)(2,1)S(1)} %get-tuple-element.41), channel_id=1, source_target_pairs={{0,12},{4,8},{8,4},{12,0},{1,13},{5,9},{9,5},{13,1},{2,14},{6,10},... | collective-permute-start | bytes 98312 | tf_op jit(solution)/shard_map/ppermute | solution.py:426
  28.8 0.5 coarse_own.1
  29.3 0.0 collective-permute-done.7.rest_1_
  29.3 3.2 %collective-permute-done.8.rest_2_ = bf16[128,128]{1,0:T(8,128)(2,1)S(1)} collective-permute-done((bf16[128,128]{1,0:T(8,128)(2,1)S(1)}, bf16[128,128]{1,0:T(8,128)(2,1)S(1)}, u32[]{:S(2)}, u32[]{:S(2)}) %collective-permute-start.8) | collective-permute-done | bytes 32800 | tf_op jit(solution)/shard_map/ppermute | solution.py:426
  32.5 1.1 %lift_halo.1 = (bf16[128,128]{1,0:T(8,128)(2,1)S(1)}, bf16[128,256]{1,0:T(8,128)(2,1)S(1)}, bf16[128,256]{1,0:T(8,128)(2,1)S(1)}, bf16[128,256]{1,0:T(8,128)(2,1)S(1)}) custom-call(f32[1,128,768]{2,1,0:T(8,128)S(1)} %get-tuple-element.35.picked_ref, s32[1,768]{1,0:T(1,128)S(1)} %get-tuple-element.36.source_ref, s32[1,768]{1,0:T(1,128)S(1)} %get-tuple-element.37.place_ref, ...), custom_call_target="tpu_custom_call" | custom-call | flops 1073741824 | bytes 4194304 | tf_op jit(solution)/shard_map/lift_halo/pallas_call | solution.py:530
  33.6 0.1 collective-permute-start.9
  33.7 2.6 %collective-permute-start.10 = (bf16[128,256]{1,0:T(8,128)(2,1)S(1)}, bf16[128,256]{1,0:T(8,128)(2,1)S(1)}, u32[]{:S(2)}, u32[]{:S(2)}) collective-permute-start(bf16[128,256]{1,0:T(8,128)(2,1)S(1)} %get-tuple-element.47), channel_id=1, source_target_pairs={{0,8},{4,12},{8,0},{12,4},{1,9},{5,13},{9,1},{13,5},{2,10},{6,14},... | collective-permute-start | bytes 196616 | tf_op jit(solution)/shard_map/ppermute | solution.py:426
  36.3 1.8 %collective-permute-start.11 = (bf16[128,256]{1,0:T(8,128)(2,1)S(1)}, bf16[128,256]{1,0:T(8,128)(2,1)S(1)}, u32[]{:S(2)}, u32[]{:S(2)}) collective-permute-start(bf16[128,256]{1,0:T(8,128)(2,1)S(1)} %get-tuple-element.48), channel_id=1, source_target_pairs={{0,12},{4,8},{8,4},{12,0},{1,13},{5,9},{9,5},{13,1},{2,14},{6,10},... | collective-permute-start | bytes 196616 | tf_op jit(solution)/shard_map/ppermute | solution.py:426
  38.1 3.2 %lift_near.1 = (bf16[128,2048]{1,0:T(8,128)(2,1)S(1)}, bf16[128,2048]{1,0:T(8,128)(2,1)S(1)}, f32[128,2048]{1,0:T(8,128)S(1)}) custom-call(bf16[128,2048]{1,0:T(8,128)(2,1)S(1)} %get-tuple-element.33.first_ref, bf16[128,128]{1,0:T(8,128)(2,1)S(1)} %get-tuple-element.42.prolonged_ref, s32[16,128]{1,0:T(8,128)S(1)} %bitcast.2, s32[16,768]{1,0:T(8,128)S(1)} %copy-done.4, ...), custom_call_target="tpu_custom_call" | custom-call | flops 4294967296 | bytes 4194304 | tf_op jit(solution)/shard_map/lift_near/pallas_call | solution.py:537
  41.3 1.1 %collective-permute-done.11.rest_2_ = bf16[128,256]{1,0:T(8,128)(2,1)S(1)} collective-permute-done((bf16[128,256]{1,0:T(8,128)(2,1)S(1)}, bf16[128,256]{1,0:T(8,128)(2,1)S(1)}, u32[]{:S(2)}, u32[]{:S(2)}) %collective-permute-start.11) | collective-permute-done | bytes 65568 | tf_op jit(solution)/shard_map/ppermute | solution.py:426
  42.4 3.9 %far.1 = bf16[2048,128]{1,0:T(8,128)(2,1)} custom-call(bf16[128,2048]{1,0:T(8,128)(2,1)S(1)} %get-tuple-element.43.table_ref, bf16[128,2048]{1,0:T(8,128)(2,1)S(1)} %get-tuple-element.44.target_ref, s32[16,768]{1,0:T(8,128)S(1)} %copy-done.4, s32[16,768]{1,0:T(8,128)S(1)} %copy-done.5, f32[128,2048]{1,0:T(8,128)S(1)} %get-tuple-element.45.sums_ref, ...), custom_call_target="tpu_custom_call" | custom-call | flops 2147483648 | bytes 4194304 | tf_op jit(solution)/shard_map/far/pallas_call | solution.py:544
  (29 shorter events, 0.1 us)
Async XLA Ops:
  0.0 1.0 %copy-start = (bf16[2048,128]{1,0:T(8,128)(2,1)S(1)}, bf16[2048,128]{1,0:T(8,128)(2,1)}, u32[]{:S(2)}) copy-start(bf16[2048,128]{1,0:T(8,128)(2,1)} %latent_hbm.1) | copy-start | bytes 1572868
  1.0 0.9 %copy-start.1 = (bf16[2,4,128,128]{3,2,1,0:T(8,128)(2,1)S(1)}, bf16[2,4,128,128]{3,2,1,0:T(8,128)(2,1)}, u32[]{:S(2)}) copy-start(bf16[2,4,128,128]{3,2,1,0:T(8,128)(2,1)} %weights_ref.13) | copy-start | bytes 786436
  2.0 0.7 %copy-start.10 = (s32[1,4,256]{2,1,0:T(4,128)S(1)}, s32[1,4,256]{2,1,0:T(4,128)}, u32[]{:S(2)}) copy-start(s32[1,4,256]{2,1,0:T(4,128)} %lists_ref.1) | copy-start | bytes 12292
  2.7 7.0 %copy-start.2 = (bf16[2,4,128,128]{3,2,1,0:T(8,128)(2,1)S(1)}, bf16[2,4,128,128]{3,2,1,0:T(8,128)(2,1)}, u32[]{:S(2)}) copy-start(bf16[2,4,128,128]{3,2,1,0:T(8,128)(2,1)} %weights_ref.13) | copy-start | bytes 786436
  2.7 7.0 %copy-start.4 = (s32[16,768]{1,0:T(8,128)S(1)}, s32[16,768]{1,0:T(8,128)}, u32[]{:S(2)}) copy-start(s32[16,768]{1,0:T(8,128)} %source_ref.7) | copy-start | bytes 147460
  2.7 7.0 %copy-start.5 = (s32[16,768]{1,0:T(8,128)S(1)}, s32[16,768]{1,0:T(8,128)}, u32[]{:S(2)}) copy-start(s32[16,768]{1,0:T(8,128)} %place_ref.7) | copy-start | bytes 147460
  4.0 8.8 %collective-permute-start = (bf16[128,256]{1,0:T(8,128)(2,1)S(1)}, bf16[128,256]{1,0:T(8,128)(2,1)S(1)}, u32[]{:S(2)}, u32[]{:S(2)}) collective-permute-start(bf16[128,256]{1,0:T(8,128)(2,1)S(1)} %get-tuple-element.30), channel_id=1, source_target_pairs={{0,4},{4,0},{8,12},{12,8},{1,5},{5,1},{9,13},{13,9},{2,6},{6,2},{1... | collective-permute-start | bytes 196616 | tf_op jit(solution)/shard_map/ppermute | solution.py:426
  7.1 7.3 %collective-permute-start.1 = (bf16[128,256]{1,0:T(8,128)(2,1)S(1)}, bf16[128,256]{1,0:T(8,128)(2,1)S(1)}, u32[]{:S(2)}, u32[]{:S(2)}) collective-permute-start(bf16[128,256]{1,0:T(8,128)(2,1)S(1)} %get-tuple-element.31), channel_id=1, source_target_pairs={{0,8},{4,12},{8,0},{12,4},{1,9},{5,13},{9,1},{13,5},{2,10},{6,14},... | collective-permute-start | bytes 196616 | tf_op jit(solution)/shard_map/ppermute | solution.py:426
  9.7 6.1 %collective-permute-start.2 = (bf16[128,256]{1,0:T(8,128)(2,1)S(1)}, bf16[128,256]{1,0:T(8,128)(2,1)S(1)}, u32[]{:S(2)}, u32[]{:S(2)}) collective-permute-start(bf16[128,256]{1,0:T(8,128)(2,1)S(1)} %get-tuple-element.32), channel_id=1, source_target_pairs={{0,12},{4,8},{8,4},{12,0},{1,13},{5,9},{9,5},{13,1},{2,14},{6,10},... | collective-permute-start | bytes 196616 | tf_op jit(solution)/shard_map/ppermute | solution.py:426
  9.7 6.1 %copy-start.8 = (s32[2,768]{1,0:T(2,128)S(1)}, s32[2,768]{1,0:T(2,128)}, u32[]{:S(2)}) copy-start(s32[2,768]{1,0:T(2,128)} %coarse_source_ref.1) | copy-start | bytes 18436
  9.7 6.0 %copy-start.9 = (s32[2,768]{1,0:T(2,128)S(1)}, s32[2,768]{1,0:T(2,128)}, u32[]{:S(2)}) copy-start(s32[2,768]{1,0:T(2,128)} %coarse_place_ref.1) | copy-start | bytes 18436
  9.7 6.0 %copy-start.13 = (s32[1,4,128]{2,1,0:T(4,128)S(1)}, s32[1,4,128]{2,1,0:T(4,128)}, u32[]{:S(2)}) copy-start(s32[1,4,128]{2,1,0:T(4,128)} %coarse_send_ref.1) | copy-start | bytes 6148
  12.7 3.0 %copy-start.12 = (s32[1,4,64]{2,1,0:T(4,128)S(1)}, s32[1,4,64]{2,1,0:T(4,128)}, u32[]{:S(2)}) copy-start(s32[1,4,64]{2,1,0:T(4,128)} %pool_ref.1) | copy-start | bytes 3076
  15.8 7.0 %copy-start.7 = (s32[2048]{0:T(1024)S(1)}, s32[2048]{0:T(1024)}, u32[]{:S(2)}) copy-start(s32[2048]{0:T(1024)} %param.20) | copy-start | bytes 24580
  18.8 4.0 %copy-start.11 = (s32[1,4,256]{2,1,0:T(4,128)S(1)}, s32[1,4,256]{2,1,0:T(4,128)}, u32[]{:S(2)}) copy-start(s32[1,4,256]{2,1,0:T(4,128)} %lists_ref.1) | copy-start | bytes 12292
  18.8 4.0 %collective-permute-start.4 = (bf16[128,128]{1,0:T(8,128)(2,1)S(1)}, bf16[128,128]{1,0:T(8,128)(2,1)S(1)}, u32[]{:S(2)}, u32[]{:S(2)}) collective-permute-start(bf16[128,128]{1,0:T(8,128)(2,1)S(1)} %get-tuple-element.34.refs_0_), channel_id=1, source_target_pairs={{0,2},{2,0},{1,3},{3,1},{4,6},{6,4},{5,7},{7,5},{8,10},{10,8},{9,1... | collective-permute-start | bytes 98312 | tf_op jit(solution)/shard_map/ppermute | solution.py:434
  20.3 3.1 %collective-permute-start.3 = (bf16[128,128]{1,0:T(8,128)(2,1)S(1)}, bf16[128,128]{1,0:T(8,128)(2,1)S(1)}, u32[]{:S(2)}, u32[]{:S(2)}) collective-permute-start(bf16[128,128]{1,0:T(8,128)(2,1)S(1)} %get-tuple-element.34.refs_0_), channel_id=1, source_target_pairs={{0,1},{1,0},{2,3},{3,2},{4,5},{5,4},{6,7},{7,6},{8,9},{9,8},{10,11... | collective-permute-start | bytes 98312 | tf_op jit(solution)/shard_map/ppermute | solution.py:435
  22.8 1.2 %collective-permute-start.5 = (bf16[128,128]{1,0:T(8,128)(2,1)S(1)}, bf16[128,128]{1,0:T(8,128)(2,1)S(1)}, u32[]{:S(2)}, u32[]{:S(2)}) collective-permute-start(bf16[128,128]{1,0:T(8,128)(2,1)S(1)} %collective-permute-done.4.refs_2_), channel_id=1, source_target_pairs={{0,1},{1,0},{2,3},{3,2},{4,5},{5,4},{6,7},{7,6},{8,9},{9,8},{10,11... | collective-permute-start | bytes 98312 | tf_op jit(solution)/shard_map/ppermute | solution.py:436
  22.8 1.2 %copy-start.3 = (bf16[4,128,128]{2,1,0:T(8,128)(2,1)S(1)}, bf16[4,128,128]{2,1,0:T(8,128)(2,1)}, u32[]{:S(2)}) copy-start(bf16[4,128,128]{2,1,0:T(8,128)(2,1)} %coarse_weights_ref.1) | copy-start | bytes 393220
  24.4 4.9 %collective-permute-start.6 = (bf16[128,128]{1,0:T(8,128)(2,1)S(1)}, bf16[128,128]{1,0:T(8,128)(2,1)S(1)}, u32[]{:S(2)}, u32[]{:S(2)}) collective-permute-start(bf16[128,128]{1,0:T(8,128)(2,1)S(1)} %get-tuple-element.39), channel_id=1, source_target_pairs={{0,4},{4,0},{8,12},{12,8},{1,5},{5,1},{9,13},{13,9},{2,6},{6,2},{1... | collective-permute-start | bytes 98312 | tf_op jit(solution)/shard_map/ppermute | solution.py:426
  24.5 4.9 %collective-permute-start.7 = (bf16[128,128]{1,0:T(8,128)(2,1)S(1)}, bf16[128,128]{1,0:T(8,128)(2,1)S(1)}, u32[]{:S(2)}, u32[]{:S(2)}) collective-permute-start(bf16[128,128]{1,0:T(8,128)(2,1)S(1)} %get-tuple-element.40), channel_id=1, source_target_pairs={{0,8},{4,12},{8,0},{12,4},{1,9},{5,13},{9,1},{13,5},{2,10},{6,14},... | collective-permute-start | bytes 98312 | tf_op jit(solution)/shard_map/ppermute | solution.py:426
  26.8 5.7 %copy-start.6 = (bf16[128,128]{1,0:T(8,128)(2,1)S(1)}, bf16[128,128]{1,0:T(8,128)(2,1)}, u32[]{:S(2)}) copy-start(bf16[128,128]{1,0:T(8,128)(2,1)} %prolong_weight_ref.1) | copy-start | bytes 98308
  26.8 5.7 %collective-permute-start.8 = (bf16[128,128]{1,0:T(8,128)(2,1)S(1)}, bf16[128,128]{1,0:T(8,128)(2,1)S(1)}, u32[]{:S(2)}, u32[]{:S(2)}) collective-permute-start(bf16[128,128]{1,0:T(8,128)(2,1)S(1)} %get-tuple-element.41), channel_id=1, source_target_pairs={{0,12},{4,8},{8,4},{12,0},{1,13},{5,9},{9,5},{13,1},{2,14},{6,10},... | collective-permute-start | bytes 98312 | tf_op jit(solution)/shard_map/ppermute | solution.py:426
  33.6 7.7 %collective-permute-start.9 = (bf16[128,256]{1,0:T(8,128)(2,1)S(1)}, bf16[128,256]{1,0:T(8,128)(2,1)S(1)}, u32[]{:S(2)}, u32[]{:S(2)}) collective-permute-start(bf16[128,256]{1,0:T(8,128)(2,1)S(1)} %get-tuple-element.46), channel_id=1, source_target_pairs={{0,4},{4,0},{8,12},{12,8},{1,5},{5,1},{9,13},{13,9},{2,6},{6,2},{1... | collective-permute-start | bytes 196616 | tf_op jit(solution)/shard_map/ppermute | solution.py:426
  33.7 7.6 %collective-permute-start.10 = (bf16[128,256]{1,0:T(8,128)(2,1)S(1)}, bf16[128,256]{1,0:T(8,128)(2,1)S(1)}, u32[]{:S(2)}, u32[]{:S(2)}) collective-permute-start(bf16[128,256]{1,0:T(8,128)(2,1)S(1)} %get-tuple-element.47), channel_id=1, source_target_pairs={{0,8},{4,12},{8,0},{12,4},{1,9},{5,13},{9,1},{13,5},{2,10},{6,14},... | collective-permute-start | bytes 196616 | tf_op jit(solution)/shard_map/ppermute | solution.py:426
  36.3 6.1 %collective-permute-start.11 = (bf16[128,256]{1,0:T(8,128)(2,1)S(1)}, bf16[128,256]{1,0:T(8,128)(2,1)S(1)}, u32[]{:S(2)}, u32[]{:S(2)}) collective-permute-start(bf16[128,256]{1,0:T(8,128)(2,1)S(1)} %get-tuple-element.48), channel_id=1, source_target_pairs={{0,12},{4,8},{8,4},{12,0},{1,13},{5,9},{9,5},{13,1},{2,14},{6,10},... | collective-permute-start | bytes 196616 | tf_op jit(solution)/shard_map/ppermute | solution.py:426

commit v3 on v2

--- a/solution.py
+++ b/solution.py
@@ -12,8 +12,9 @@
 I32 = jnp.int32
 BLOCK = 128
 VMEM_BYTES = 32 << 20
-GROUP = 4
-LAG = 2
+BATCH = 4
+PARTS = 4
+PAIR = 2
 
 
 def dot(left, right):
@@ -41,15 +42,16 @@
 
 
 class Grid:
-    def __init__(self, mesh, pool_capacity, coarse_capacity, coarse_blocks, slot_count):
+    def __init__(self, mesh, halo_capacity, pool_capacity, coarse_capacity, coarse_blocks, slot_count):
         self.dom_count = mesh.shape["dom"]
         self.sub_count = mesh.shape["sub"]
         self.chip_count = mesh.shape["chip"]
         self.places = self.sub_count * self.chip_count
         self.mirrored = self.dom_count == 4
-        self.steps = (1, 2, 3) if self.mirrored else tuple(sorted({1, self.dom_count - 1, 2 % self.dom_count}))
+        self.steps = (2, 3, 1) if self.mirrored else (1, self.dom_count - 1, 2)
         self.owners = len(range(0, self.places, 4))
         self.swapped = self.sub_count == 2 and self.chip_count == 2
+        self.halo_capacity = halo_capacity
         self.pool_capacity = pool_capacity
         self.coarse_capacity = coarse_capacity
         self.blocks = coarse_blocks
@@ -90,35 +92,59 @@
     return halved(weight).T
 
 
-def send_kernel(grid, latent_hbm, lists_hbm, weights_hbm, table_ref, *rest):
+def send_kernel(grid, latent_hbm, lists_hbm, weights_hbm, *rest):
     sent_refs = rest[: len(grid.steps)]
     latent_ref, lists_ref, weight_ref, arrived = rest[len(grid.steps) :]
+    node_count = latent_ref.shape[0]
+    part = node_count // PARTS
     copies = [
         pltpu.make_async_copy(lists_hbm.at[0], lists_ref, arrived.at[0]),
         pltpu.make_async_copy(weights_hbm.at[0, 0], weight_ref, arrived.at[1]),
-        pltpu.make_async_copy(latent_hbm, latent_ref, arrived.at[2]),
     ]
+    for index in range(PARTS):
+        rows = pl.ds(index * part, part)
+        copies.append(pltpu.make_async_copy(latent_hbm.at[rows], latent_ref.at[rows], arrived.at[2 + index]))
     for copy in copies:
         copy.start()
-    for copy in copies:
-        copy.wait()
-    table = latent_ref[...].T
-    table_ref[...] = table
+    copies[0].wait()
+    copies[1].wait()
     weight = turned(weight_ref[...])
+    tables = []
+    for index in range(PARTS):
+        copies[2 + index].wait()
+        tables.append(latent_ref[index * part : (index + 1) * part, :].T)
+    table = jnp.concatenate(tables, axis=1)
     for step, out_ref in zip(grid.steps, sent_refs):
         index_row = lists_ref[pl.ds(grid.partner_here(step), 1), :]
         picked = dot(table, rows_hot(index_row, table.shape[1])).astype(BF16)
         out_ref[...] = dot(weight, picked).astype(BF16)
 
 
-def near_edges(table, source_ref, place_ref, weights_ref, layer, target_ref, sums_ref, terms_ref):
+def far_rows(source_ref, place_ref, batch):
+    local_count = source_ref.shape[1] * 3 // 4
+    sources, places = [], []
+    for index in range(BATCH):
+        row = slice(batch * BATCH + index, batch * BATCH + index + 1)
+        sources.append(source_ref[row, local_count:])
+        place = place_ref[row, local_count:]
+        places.append(jnp.where(place >= 0, place + index * BLOCK, -1))
+    return jnp.concatenate(sources, axis=1), jnp.concatenate(places, axis=1)
+
+
+def near_edges(table, source_ref, place_ref, places_ref, weights_ref, layer, aimed_ref, sums_ref, terms_ref):
     features, node_count = table.shape
     block_count, slot_count = source_ref.shape
     local_count = slot_count * 3 // 4
     window = min(3 * BLOCK, node_count)
     both = jnp.concatenate([turned(weights_ref[layer, 0]), turned(weights_ref[layer, 1])], axis=0)
     terms_ref[...] = dot(both, table).astype(BF16)
-    target_ref[...] = terms_ref[features:, :]
+
+    def far_targets(batch):
+        columns = slice(batch * BATCH * BLOCK, (batch + 1) * BATCH * BLOCK)
+        hot = rows_hot(places_ref[batch : batch + 1, :], BATCH * BLOCK)
+        aimed_ref[:, batch * hot.shape[1] : (batch + 1) * hot.shape[1]] = dot(
+            terms_ref[features:, columns], hot
+        ).astype(BF16)
 
     def messages(block):
         start = min(max(block * BLOCK - BLOCK, 0), node_count - window)
@@ -144,56 +170,86 @@
         if waiting is not None:
             add_up(*waiting)
         waiting = (block, message)
+        if block % BATCH == 0:
+            far_targets(block // BATCH)
     add_up(*waiting)
 
 
-def near_kernel(layer, table_ref, source_ref, place_ref, weights_ref, target_ref, sums_ref, terms_ref):
-    near_edges(table_ref[...], source_ref, place_ref, weights_ref, layer, target_ref, sums_ref, terms_ref)
-
-
-def far_edges(grid, layer, table_ref, target_ref, source_ref, place_ref, sums_ref, weights_ref, halo_refs, both_ref, write):
+def near_kernel(
+    grid,
+    latent_ref,
+    source_ref,
+    place_ref,
+    weights_ref,
+    coarse_source_ref,
+    coarse_place_ref,
+    coarse_send_ref,
+    table_ref,
+    sources_ref,
+    places_ref,
+    aimed_ref,
+    sums_ref,
+    packed_ref,
+    terms_ref,
+):
+    table = latent_ref[...].T
+    table_ref[...] = table
+    halo_capacity = grid.halo_capacity
+    for batch in range(source_ref.shape[0] // BATCH):
+        sources, places = far_rows(source_ref, place_ref, batch)
+        slots = sources - table.shape[1]
+        source_dom = lax.shift_right_logical(slots, halo_capacity.bit_length() - 1)
+        sources_ref[batch : batch + 1, :] = grid.halo_place(source_dom) * halo_capacity + (
+            slots & (halo_capacity - 1)
+        )
+        places_ref[batch : batch + 1, :] = places
+    near_edges(table, source_ref, place_ref, places_ref, weights_ref, 0, aimed_ref, sums_ref, terms_ref)
+
+    pieces = lane_rows(coarse_source_ref) + [coarse_send_ref[0]] + lane_rows(coarse_place_ref)
+    spare = grid.packed_rows - grid.list_rows
+    if spare:
+        pieces.append(jnp.zeros((spare, BLOCK), I32))
+    whole = jnp.concatenate(pieces, axis=0) + 1
+    high = lax.shift_right_logical(whole, 8)
+    packed_ref[...] = jnp.concatenate([high.astype(F32), (whole & 255).astype(F32)], axis=0).astype(BF16)
+
+
+def far_edges(layer, table_ref, aimed_ref, sources_ref, places_ref, sums_ref, weights_ref, halo_refs, both_ref, write):
     features, node_count = table_ref.shape
-    block_count, slot_count = source_ref.shape
-    local_count = slot_count * 3 // 4
-    capacity = halo_refs[0].shape[1]
+    batch_count, slot_count = sources_ref.shape
     halo = jnp.concatenate([ref[...] for ref in halo_refs], axis=1)
-    halo_rows = halo.shape[1]
     update_weights = jnp.concatenate([turned(weights_ref[layer, 2]), turned(weights_ref[layer, 3])], axis=1)
-    shift = capacity.bit_length() - 1
-    slots = source_ref[:, local_count:] - node_count
-    source_dom = lax.shift_right_logical(slots, shift)
-    far_sources = grid.halo_place(source_dom) * capacity + (slots & (capacity - 1))
+    pair_slots = slot_count * PAIR // BATCH
+    pair_rows = PAIR * BLOCK
+    batch_rows = BATCH * BLOCK
     both_ref[features:, :] = table_ref[...]
 
-    def messages(block):
-        terms = jnp.concatenate([halo, target_ref[:, block * BLOCK : (block + 1) * BLOCK]], axis=1)
-        places = rows_hot(place_ref[block : block + 1, local_count:], BLOCK)
-        sources = rows_hot(far_sources[block : block + 1, :], halo_rows)
-        picked = dot(terms, jnp.concatenate([sources, places], axis=0))
-        return silu_of_half(picked).astype(BF16)
-
-    def add_up(block, message):
-        columns = slice(block * BLOCK, (block + 1) * BLOCK)
-        places = rows_hot(place_ref[block : block + 1, local_count:], BLOCK)
-        both_ref[:features, columns] = (sums_ref[:, columns] + dot_last(message, places)).astype(BF16)
-
-    def update(block):
-        columns = slice((block - GROUP + 1) * BLOCK, (block + 1) * BLOCK)
+    def messages(batch):
+        aimed = aimed_ref[:, batch * slot_count : (batch + 1) * slot_count].astype(F32)
+        hot = rows_hot(sources_ref[batch : batch + 1, :], halo.shape[1])
+        return silu_of_half(dot(halo, hot) + aimed).astype(BF16)
+
+    def add_up(batch, message):
+        for pair in range(BATCH // PAIR):
+            slots = slice(pair * pair_slots, (pair + 1) * pair_slots)
+            first = batch * batch_rows + pair * pair_rows
+            columns = slice(first, first + pair_rows)
+            hot = rows_hot(places_ref[batch : batch + 1, slots] - pair * pair_rows, pair_rows)
+            both_ref[:features, columns] = (sums_ref[:, columns] + dot_last(message[:, slots], hot)).astype(BF16)
+
+    def update(batch):
+        columns = slice(batch * batch_rows, (batch + 1) * batch_rows)
         change = silu_of_half(dot(update_weights, both_ref[:, columns]))
         write(columns, (both_ref[features:, columns].astype(F32) + change).astype(BF16))
 
-    waiting = []
-    for block in range(block_count):
-        waiting.append((block, messages(block)))
-        if len(waiting) > LAG:
-            done = waiting.pop(0)
-            add_up(*done)
-            if (done[0] + 1) % GROUP == 0 and done[0] >= 0:
-                update(done[0])
-    for done in waiting:
-        add_up(*done)
-        if (done[0] + 1) % GROUP == 0:
-            update(done[0])
+    message = messages(0)
+    for batch in range(batch_count):
+        following = messages(batch + 1) if batch + 1 < batch_count else None
+        add_up(batch, message)
+        if batch:
+            update(batch - 1)
+        message = following
+    update(batch_count - 1)
 
 
 def lane_rows(ref):
@@ -205,51 +261,34 @@
 
 
 def far_pool_kernel(
-    grid,
-    table_ref,
-    target_ref,
-    source_ref,
-    place_ref,
-    sums_ref,
-    weights_ref,
-    pool_ref,
-    coarse_source_ref,
-    coarse_place_ref,
-    coarse_send_ref,
-    *rest,
+    grid, table_ref, aimed_ref, sources_ref, places_ref, sums_ref, weights_ref, pool_ref, packed_ref, *rest
 ):
     halo_refs, (first_ref, packet_ref, both_ref) = rest[:-3], rest[-3:]
 
     def write(columns, value):
         first_ref[:, columns] = value
 
-    pieces = lane_rows(coarse_source_ref) + [coarse_send_ref[0]] + lane_rows(coarse_place_ref)
-    spare = grid.packed_rows - grid.list_rows
-    if spare:
-        pieces.append(jnp.zeros((spare, BLOCK), I32))
-    whole = jnp.concatenate(pieces, axis=0) + 1
-    high = lax.shift_right_logical(whole, 8)
-    packet_ref[grid.pooled_rows :, :] = jnp.concatenate(
-        [high.astype(F32), (whole & 255).astype(F32)], axis=0
-    ).astype(BF16)
-    far_edges(
-        grid, 0, table_ref, target_ref, source_ref, place_ref, sums_ref, weights_ref, halo_refs, both_ref, write
-    )
+    packet_ref[grid.pooled_rows :, :] = packed_ref[...]
+    far_edges(0, table_ref, aimed_ref, sources_ref, places_ref, sums_ref, weights_ref, halo_refs, both_ref, write)
     for owner in range(grid.owners):
         hot = rows_hot(pool_ref[0, 4 * owner : 4 * owner + 1, :], first_ref.shape[1])
         pooled = dot(first_ref[...], hot).astype(BF16).T
         packet_ref[owner * grid.pool_capacity : (owner + 1) * grid.pool_capacity, :] = pooled
 
 
-def far_kernel(grid, table_ref, target_ref, source_ref, place_ref, sums_ref, weights_ref, *rest):
-    halo_refs, (out_ref, both_ref) = rest[:-2], rest[-2:]
+def far_kernel(table_ref, aimed_ref, sources_ref, places_ref, sums_ref, weights_ref, *rest):
+    halo_refs, (out_hbm, both_ref, rows_ref, written) = rest[:-4], rest[-4:]
+    copies = []
 
     def write(columns, value):
-        out_ref[columns, :] = value.T
-
-    far_edges(
-        grid, 1, table_ref, target_ref, source_ref, place_ref, sums_ref, weights_ref, halo_refs, both_ref, write
-    )
+        rows_ref[columns, :] = value.T
+        rows = pl.ds(columns.start, columns.stop - columns.start)
+        copies.append(pltpu.make_async_copy(rows_ref.at[rows], out_hbm.at[rows], written.at[len(copies)]))
+        copies[-1].start()
+
+    far_edges(1, table_ref, aimed_ref, sources_ref, places_ref, sums_ref, weights_ref, halo_refs, both_ref, write)
+    for copy in copies:
+        copy.wait()
 
 
 def ahead_kernel(grid, first_ref, prolong_ref, lists_ref, out_ref):
@@ -332,7 +371,7 @@
             for other in range(1, grid.places):
                 other_rows = table[other * grid.pool_capacity : (other + 1) * grid.pool_capacity]
                 rows = jnp.where(place == other, other_rows, rows)
-        rows_out[owner * grid.pool_capacity : (owner + 1) * grid.pool_capacity, :] = rows
+        rows_out[owner] = rows.T
         sender = dot(table, halved(weights_ref[0])).astype(BF16).T
         target = dot(rows, halved(weights_ref[1])).astype(BF16).T
         hot = jnp.concatenate([rows_hot(own_sources, grid.slots), rows_hot(places, grid.pool_capacity)], axis=0)
@@ -361,22 +400,23 @@
     count = len(grid.steps)
     halo_refs, prolonged_ref, sent_refs = rest[:count], rest[count], rest[count + 1 :]
     features = rows_ref.shape[1]
-    update_weights = jnp.concatenate([halved(coarse_weights_ref[2]), halved(coarse_weights_ref[3])], axis=0)
+    update_weights = jnp.concatenate([turned(coarse_weights_ref[2]), turned(coarse_weights_ref[3])], axis=1)
+    prolong_weight = turned(prolong_weight_ref[...])
     prolonged = []
     for owner in range(grid.owners):
         halo = jnp.concatenate([ref[owner * BLOCK : (owner + 1) * BLOCK, :] for ref in halo_refs], axis=1)
         picked = picked_ref[owner] + dot(halo, rows_hot(source_ref[owner : owner + 1, :], halo.shape[1]))
         message = silu_of_half(picked).astype(BF16)
         places = rows_hot(place_ref[owner : owner + 1, :], grid.pool_capacity)
-        summed = dot_last(places, message).astype(BF16)
-        rows = rows_ref[owner * grid.pool_capacity : (owner + 1) * grid.pool_capacity, :]
-        update = dot(jnp.concatenate([summed, rows], axis=1), update_weights)
+        summed = dot_last(message, places).astype(BF16)
+        rows = rows_ref[owner]
+        update = dot(update_weights, jnp.concatenate([summed, rows], axis=0))
         coarse = (rows.astype(F32) + silu_of_half(update)).astype(BF16)
-        prolonged.append(dot(coarse, halved(prolong_weight_ref[...])))
-    prolonged = jnp.concatenate(prolonged, axis=0)
+        prolonged.append(dot(prolong_weight, coarse))
+    prolonged = jnp.concatenate(prolonged, axis=1)
     high = prolonged.astype(BF16)
     low = (prolonged - high.astype(F32)).astype(BF16)
-    parts = jnp.concatenate([high, low], axis=0).T
+    parts = jnp.concatenate([high, low], axis=1)
     prolonged_ref[...] = parts
     weight = turned(weights_ref[1, 0])
     index_row = ahead_ref[features : features + 1, :].astype(F32).astype(I32)
@@ -394,9 +434,10 @@
     prolong_ref,
     source_ref,
     place_ref,
+    places_ref,
     weights_ref,
     lifted_ref,
-    target_ref,
+    aimed_ref,
     sums_ref,
     terms_ref,
 ):
@@ -406,26 +447,29 @@
     row = jnp.concatenate([indices[block : block + 1, :] for block in range(indices.shape[0])], axis=1)
     lifted = lift(first_ref[...], prolonged_ref[...], row)
     lifted_ref[...] = lifted
-    near_edges(lifted, source_ref, place_ref, weights_ref, 1, target_ref, sums_ref, terms_ref)
-
-
-def call(kernel, outs, scratch=(), flops=0, name=None, **specs):
+    near_edges(lifted, source_ref, place_ref, places_ref, weights_ref, 1, aimed_ref, sums_ref, terms_ref)
+
+
+def call(kernel, outs, scratch=(), flops=0, name=None, limit=VMEM_BYTES, **specs):
     return pl.pallas_call(
         kernel,
         out_shape=tuple(jax.ShapeDtypeStruct(shape, dtype) for shape, dtype in outs),
         scratch_shapes=list(scratch),
-        compiler_params=pltpu.CompilerParams(vmem_limit_bytes=VMEM_BYTES),
+        compiler_params=pltpu.CompilerParams(vmem_limit_bytes=limit),
         cost_estimate=pl.CostEstimate(flops=flops, bytes_accessed=4 << 20, transcendentals=0),
         name=name,
         **specs,
     )
 
 
-def swap_dom(grid, arrays):
-    return [
-        lax.ppermute(array, "dom", [(dom, grid.partner(dom, step)) for dom in range(grid.dom_count)])
-        for array, step in zip(arrays, grid.steps)
-    ]
+def swap_dom(grid, arrays, order=(0, 1, 2)):
+    arrived = {}
+    for index in order:
+        step = grid.steps[index]
+        arrived[index] = lax.ppermute(
+            arrays[index], "dom", [(dom, grid.partner(dom, step)) for dom in range(grid.dom_count)]
+        )
+    return [arrived[index] for index in range(len(arrays))]
 
 
 def trade_packets(grid, packet):
@@ -433,7 +477,8 @@
         pairs = [(0, 1), (1, 0)]
         over = lax.ppermute(packet, "sub", pairs)
         across = lax.ppermute(packet, "chip", pairs)
-        return [packet, across, over, lax.ppermute(over, "chip", pairs)]
+        both = lax.ppermute(packet, ("sub", "chip"), [(0, 3), (1, 2), (2, 1), (3, 0)])
+        return [packet, across, over, both]
     gathered = lax.all_gather(packet, ("sub", "chip"), axis=0, tiled=False)
     return [gathered[place] for place in range(grid.places)]
 
@@ -454,53 +499,51 @@
     prolong_weight,
 ):
     node_count, features = fine_nodes.shape
-    grid = Grid(mesh, pool_send.shape[2], coarse_send.shape[2], coarse_src.shape[0], coarse_src.shape[1])
     halo_capacity = halo_send.shape[2]
+    coarse_blocks, coarse_slots = coarse_src.shape
+    grid = Grid(mesh, halo_capacity, pool_send.shape[2], coarse_send.shape[2], coarse_blocks, coarse_slots)
     steps = len(grid.steps)
+    block_count, slot_count = fine_src.shape
+    far_count = slot_count - slot_count * 3 // 4
     table = ((features, node_count), BF16)
     sums_table = ((features, node_count), F32)
+    aimed_table = ((features, block_count * far_count), BF16)
+    far_lists = ((block_count // BATCH, BATCH * far_count), I32)
     halo_outs = [((features, halo_capacity), BF16)] * steps
     two_tables = pltpu.VMEM((2 * features, node_count), BF16)
     prolong_rows = prolong_idx.reshape(node_count // BLOCK, BLOCK)
     big = 1 << 30
     in_hbm = pl.BlockSpec(memory_space=pltpu.HBM)
 
-    nodes, *sent = call(
+    sent = call(
         functools.partial(send_kernel, grid),
-        [table, *halo_outs],
+        halo_outs,
         [
             pltpu.VMEM((node_count, features), BF16),
             pltpu.VMEM(halo_send.shape[1:], I32),
             pltpu.VMEM((features, features), BF16),
-            pltpu.SemaphoreType.DMA((3,)),
+            pltpu.SemaphoreType.DMA((2 + PARTS,)),
         ],
         flops=big,
         name="send",
+        limit=63 << 20,
         in_specs=[in_hbm] * 3,
     )(fine_nodes, halo_send, fine_weights)
     halo = swap_dom(grid, sent)
-    target, sums = call(
-        functools.partial(near_kernel, 0), [table, sums_table], [two_tables], flops=4 * big, name="near"
-    )(nodes, fine_src, fine_dst, fine_weights)
+    nodes, far_sources, far_places, aimed, sums, packed = call(
+        functools.partial(near_kernel, grid),
+        [table, far_lists, far_lists, aimed_table, sums_table, ((2 * grid.packed_rows, features), BF16)],
+        [two_tables],
+        flops=4 * big,
+        name="near",
+    )(fine_nodes, fine_src, fine_dst, fine_weights, coarse_src, coarse_dst, coarse_send)
     first, packet = call(
         functools.partial(far_pool_kernel, grid),
         [table, ((grid.packet, features), BF16)],
         [two_tables],
         flops=2 * big,
         name="far_pool",
-    )(
-        nodes,
-        target,
-        fine_src,
-        fine_dst,
-        sums,
-        fine_weights,
-        pool_send,
-        coarse_src,
-        coarse_dst,
-        coarse_send,
-        *halo,
-    )
+    )(nodes, aimed, far_sources, far_places, sums, fine_weights, pool_send, packed, *halo)
     packets = trade_packets(grid, packet)
     (ahead,) = call(
         functools.partial(ahead_kernel, grid), [((features + 16, steps * halo_capacity), BF16)], flops=big, name="ahead"
@@ -514,14 +557,13 @@
         name="coarse_send",
     )(coarse_weights, *packets)
     coarse_halo = swap_dom(grid, sent)
-    coarse_slots = coarse_src.shape[1]
     picked, sources, places, rows = call(
         functools.partial(coarse_own_kernel, grid),
         [
             ((grid.owners, features, coarse_slots), F32),
             ((grid.owners, coarse_slots), I32),
             ((grid.owners, coarse_slots), I32),
-            ((grid.pooled_rows, features), BF16),
+            ((grid.owners, features, grid.pool_capacity), BF16),
         ],
         [lists_scratch],
         flops=4 * big,
@@ -534,16 +576,25 @@
         name="lift_halo",
     )(picked, sources, places, rows, ahead, coarse_weights, prolong_weight, fine_weights, *coarse_halo)
     halo = swap_dom(grid, sent)
-    lifted, target, sums = call(
+    lifted, aimed, sums = call(
         functools.partial(lift_near_kernel, grid),
-        [table, table, sums_table],
+        [table, aimed_table, sums_table],
         [two_tables],
         flops=4 * big,
         name="lift_near",
-    )(first, prolonged, prolong_rows, fine_src, fine_dst, fine_weights)
+    )(first, prolonged, prolong_rows, fine_src, fine_dst, far_places, fine_weights)
     (fine_out,) = call(
-        functools.partial(far_kernel, grid), [((node_count, features), BF16)], [two_tables], flops=2 * big, name="far"
-    )(lifted, target, fine_src, fine_dst, sums, fine_weights, *halo)
+        far_kernel,
+        [((node_count, features), BF16)],
+        [
+            two_tables,
+            pltpu.VMEM((node_count, features), BF16),
+            pltpu.SemaphoreType.DMA((block_count // BATCH,)),
+        ],
+        flops=2 * big,
+        name="far",
+        out_specs=(pl.BlockSpec(memory_space=pltpu.HBM),),
+    )(lifted, aimed, far_sources, far_places, sums, fine_weights, *halo)
     return fine_out
 
 

time: 46.5 us -> 41.2 us (0.89)
  waiting for transfers between devices: 10.2 us -> 7.69 us
  local copies, waits for them, and re-layouts: 2.73 us -> 0.73 us
  starting transfers between devices: 16.1 us -> 15.4 us
    ppermute x1, waiting for transfers between devices: 2.42 us -> 0.4 us  [trade_packets(): over = lax.ppermute(packet, 'sub', pairs)]
    unnamed x28 -> x24, local copies, waits for them, and re-layouts: 2.73 us -> 0.73 us
    pallas_call x4, Pallas kernels: 11.4 us -> 12.6 us  [the longest x1 3.6 us: body(): call(functools.partial(lift_near_kernel, grid), [table, aimed_table, sums...]
    pallas_call x1, Pallas kernels: 3.01 us -> 1.8 us  [body(): call(functools.partial(far_pool_kernel, grid), [table, ((grid.packet, fea...]
    ppermute x10, starting transfers between devices: 14.6 us -> 13.6 us  [the longest x9 13.5 us: swap_dom(): lax.ppermute(arrays[index], 'dom', [(dom, grid.partner(dom, step)) for do...]
    ppermute x10, waiting for transfers between devices: 7.77 us -> 7.28 us  [the longest x9 6.17 us: swap_dom(): lax.ppermute(arrays[index], 'dom', [(dom, grid.partner(dom, step)) for do...]
  transfers between devices with their start and end apart: 12 -> 12, of which waited for: 6 -> 7; matrix products, arithmetic and copies ran while one was open for 0% -> 0% of each run, Pallas kernels for 16% -> 20%
where the time goes in v3:
time: 41.2 us; the launch traced here: 41 us
  Pallas kernels  17 us (41%)
  starting transfers between devices  15.4 us (37%)
  waiting for transfers between devices  7.69 us (19%)
  local copies, waits for them, and re-layouts  0.73 us (2%)
    ppermute x9, starting transfers between devices, swap_dom(): lax.ppermute(arrays[index], 'dom', [(dom, grid.partner(dom, step)) for do...  13.5 us
    ppermute x9, waiting for transfers between devices, swap_dom(): lax.ppermute(arrays[index], 'dom', [(dom, grid.partner(dom, step)) for do...  6.17 us
    pallas_call x1, Pallas kernels, body(): call(functools.partial(lift_near_kernel, grid), [table, aimed_table, sums...  3.6 us
    pallas_call x1, Pallas kernels, body(): call(functools.partial(near_kernel, grid), [table, far_lists, far_lists,...  3.47 us
    pallas_call x1, Pallas kernels, body(): call(functools.partial(send_kernel, grid), halo_outs, [pltpu.VMEM((node_c...  3.13 us
    pallas_call x1, Pallas kernels, body(): call(far_kernel, [((node_count, features), BF16)], [two_tables, pltpu.VME...  2.38 us
    pallas_call x1, Pallas kernels, body(): call(functools.partial(far_pool_kernel, grid), [table, ((grid.packet, fea...  1.8 us
    ppermute x1, starting transfers between devices, trade_packets(): over = lax.ppermute(packet, 'sub', pairs)  1.56 us
  transfers between devices with their start and end apart: 12, of which 7 were waited for; matrix products, arithmetic and copies ran while one was open for 0% of the time, Pallas kernels for 20%

profile of v3, /device:TPU:0, one launch (start us, length us, event | category | flops | bytes accessed | tf_op | source)
XLA Modules:
  0.0 41.0 jit_solution(14668665266579216801)
XLA Ops:
  0.0 3.1 %send.1 = (bf16[128,256]{1,0:T(8,128)(2,1)}, bf16[128,256]{1,0:T(8,128)(2,1)}, bf16[128,256]{1,0:T(8,128)(2,1)}) custom-call(bf16[2048,128]{1,0:T(8,128)(2,1)} %latent_hbm.1, s32[1,4,256]{2,1,0:T(4,128)} %lists_ref.1, bf16[2,4,128,128]{3,2,1,0:T(8,128)(2,1)} %weights_ref.13), custom_call_target="tpu_custom_call" | custom-call | flops 1073741824 | bytes 4194304 | tf_op jit(solution)/shard_map/send/pallas_call | solution.py:518
  3.2 0.0 copy-start.10
  3.2 4.1 %collective-permute-start = (bf16[128,256]{1,0:T(8,128)(2,1)}, bf16[128,256]{1,0:T(8,128)(2,1)S(1)}, u32[]{:S(2)}, u32[]{:S(2)}) collective-permute-start(bf16[128,256]{1,0:T(8,128)(2,1)} %get-tuple-element.36), channel_id=1, source_target_pairs={{0,8},{4,12},{8,0},{12,4},{1,9},{5,13},{9,1},{13,5},{2,10},{6,14},... | collective-permute-start | bytes 196616 | tf_op jit(solution)/shard_map/ppermute | solution.py:469
  7.3 1.3 %collective-permute-start.1 = (bf16[128,256]{1,0:T(8,128)(2,1)}, bf16[128,256]{1,0:T(8,128)(2,1)S(1)}, u32[]{:S(2)}, u32[]{:S(2)}) collective-permute-start(bf16[128,256]{1,0:T(8,128)(2,1)} %get-tuple-element.37), channel_id=1, source_target_pairs={{0,12},{4,8},{8,4},{12,0},{1,13},{5,9},{9,5},{13,1},{2,14},{6,10},... | collective-permute-start | bytes 196616 | tf_op jit(solution)/shard_map/ppermute | solution.py:469
  8.6 0.2 collective-permute-start.2
  8.9 3.5 %near.1 = (bf16[128,2048]{1,0:T(8,128)(2,1)S(1)}, s32[4,768]{1,0:T(4,128)S(1)}, s32[4,768]{1,0:T(4,128)S(1)}, bf16[128,3072]{1,0:T(8,128)(2,1)S(1)}, f32[128,204...) custom-call(bf16[2048,128]{1,0:T(8,128)(2,1)S(1)} %copy-done, s32[16,768]{1,0:T(8,128)S(1)} %copy-done.3, ...), custom_call_target="tpu_custom_call" | custom-call | flops 4294967296 | bytes 4194304 | tf_op jit(solution)/shard_map/near/pallas_call | solution.py:533
  12.4 0.0 collective-permute-done.rest_0_
  12.4 1.3 %collective-permute-done.1.rest_1_ = bf16[128,256]{1,0:T(8,128)(2,1)S(1)} collective-permute-done((bf16[128,256]{1,0:T(8,128)(2,1)}, bf16[128,256]{1,0:T(8,128)(2,1)S(1)}, u32[]{:S(2)}, u32[]{:S(2)}) %collective-permute-start.1) | collective-permute-done | bytes 65568 | tf_op jit(solution)/shard_map/ppermute | solution.py:469
  13.7 0.1 collective-permute-done.2.rest_2_
  13.8 0.7 %copy-done.11 = s32[1,4,64]{2,1,0:T(4,128)S(1)} copy-done((s32[1,4,64]{2,1,0:T(4,128)S(1)}, s32[1,4,64]{2,1,0:T(4,128)}, u32[]{:S(2)}) %copy-start.11) | copy-done | bytes 1048
  14.5 1.8 %far_pool.1 = (bf16[128,2048]{1,0:T(8,128)(2,1)S(1)}, bf16[128,128]{1,0:T(8,128)(2,1)S(1)}) custom-call(bf16[128,2048]{1,0:T(8,128)(2,1)S(1)} %get-tuple-element.30.table_ref, bf16[128,3072]{1,0:T(8,128)(2,1)S(1)} %get-tuple-element.31.aimed_ref, s32[4,768]{1,0:T(4,128)S(1)} %get-tuple-element.32.sources_ref, s32[4,768]{1,0:T(4,128)S(1)} %get-tuple-element.33.places_ref, ...), custom_call_target="tpu_custom_call" | custom-call | flops 2147483648 | bytes 4194304 | tf_op jit(solution)/shard_map/far_pool/pallas_call | solution.py:540
  16.3 0.1 collective-permute-start.5
  16.4 1.6 %collective-permute-start.4 = (bf16[128,128]{1,0:T(8,128)(2,1)S(1)}, bf16[128,128]{1,0:T(8,128)(2,1)S(1)}, u32[]{:S(2)}, u32[]{:S(2)}) collective-permute-start(bf16[128,128]{1,0:T(8,128)(2,1)S(1)} %get-tuple-element.40.refs_0_), channel_id=1, source_target_pairs={{0,2},{2,0},{1,3},{3,1},{4,6},{6,4},{5,7},{7,5},{8,10},{10,8},{9,1... | collective-permute-start | bytes 98312 | tf_op jit(solution)/shard_map/ppermute | solution.py:478
  17.9 0.3 collective-permute-start.3
  18.2 0.6 %ahead.1.ahead_ref = bf16[144,768]{1,0:T(8,128)(2,1)S(1)} custom-call(bf16[128,2048]{1,0:T(8,128)(2,1)S(1)} %get-tuple-element.39.first_ref, s32[16,128]{1,0:T(8,128)S(1)} %bitcast.1, s32[1,4,256]{2,1,0:T(4,128)S(1)} %copy-done.9), custom_call_target="tpu_custom_call" | custom-call | flops 1073741824 | bytes 4194304 | tf_op jit(solution)/shard_map/ahead/pallas_call | solution.py:548
  18.9 1.1 %collective-permute-done.5.refs_3_ = bf16[128,128]{1,0:T(8,128)(2,1)S(1)} collective-permute-done((bf16[128,128]{1,0:T(8,128)(2,1)S(1)}, bf16[128,128]{1,0:T(8,128)(2,1)S(1)}, u32[]{:S(2)}, u32[]{:S(2)}) %collective-permute-start.5) | collective-permute-done | bytes 32800 | tf_op jit(solution)/shard_map/ppermute | solution.py:480
  20.0 0.4 collective-permute-done.4.refs_2_
  20.4 0.4 coarse_send.1
  20.8 3.6 %collective-permute-start.6 = (bf16[128,128]{1,0:T(8,128)(2,1)S(1)}, bf16[128,128]{1,0:T(8,128)(2,1)S(1)}, u32[]{:S(2)}, u32[]{:S(2)}) collective-permute-start(bf16[128,128]{1,0:T(8,128)(2,1)S(1)} %get-tuple-element.45), channel_id=1, source_target_pairs={{0,8},{4,12},{8,0},{12,4},{1,9},{5,13},{9,1},{13,5},{2,10},{6,14},... | collective-permute-start | bytes 98312 | tf_op jit(solution)/shard_map/ppermute | solution.py:469
  24.4 0.6 %collective-permute-start.7 = (bf16[128,128]{1,0:T(8,128)(2,1)S(1)}, bf16[128,128]{1,0:T(8,128)(2,1)S(1)}, u32[]{:S(2)}, u32[]{:S(2)}) collective-permute-start(bf16[128,128]{1,0:T(8,128)(2,1)S(1)} %get-tuple-element.46), channel_id=1, source_target_pairs={{0,12},{4,8},{8,4},{12,0},{1,13},{5,9},{9,5},{13,1},{2,14},{6,10},... | collective-permute-start | bytes 98312 | tf_op jit(solution)/shard_map/ppermute | solution.py:469
  25.0 0.0 collective-permute-start.8
  25.1 0.5 %coarse_own.1 = (f32[1,128,768]{2,1,0:T(8,128)S(1)}, s32[1,768]{1,0:T(1,128)S(1)}, s32[1,768]{1,0:T(1,128)S(1)}, bf16[1,128,64]{2,1,0:T(8,128)(2,1)S(1)}) custom-call(bf16[4,128,128]{2,1,0:T(8,128)(2,1)S(1)} %copy-done.2, bf16[128,128]{1,0:T(8,128)(2,1)S(1)} %get-tuple-element.40.refs_0_, bf16[128,128]{1,0:T(8,128)(2,1)S(1)} %collective-permute-done.3.refs_1_, ...), custom_call_target="tpu_custom_call" | custom-call | flops 4294967296 | bytes 4194304 | tf_op jit(solution)/shard_map/coarse_own/pallas_call | solution.py:560
  25.5 0.8 %collective-permute-done.6.rest_0_ = bf16[128,128]{1,0:T(8,128)(2,1)S(1)} collective-permute-done((bf16[128,128]{1,0:T(8,128)(2,1)S(1)}, bf16[128,128]{1,0:T(8,128)(2,1)S(1)}, u32[]{:S(2)}, u32[]{:S(2)}) %collective-permute-start.6) | collective-permute-done | bytes 32800 | tf_op jit(solution)/shard_map/ppermute | solution.py:469
  26.3 3.8 %collective-permute-done.7.rest_1_ = bf16[128,128]{1,0:T(8,128)(2,1)S(1)} collective-permute-done((bf16[128,128]{1,0:T(8,128)(2,1)S(1)}, bf16[128,128]{1,0:T(8,128)(2,1)S(1)}, u32[]{:S(2)}, u32[]{:S(2)}) %collective-permute-start.7) | collective-permute-done | bytes 32800 | tf_op jit(solution)/shard_map/ppermute | solution.py:469
  30.1 1.1 %lift_halo.1 = (bf16[128,128]{1,0:T(8,128)(2,1)S(1)}, bf16[128,256]{1,0:T(8,128)(2,1)S(1)}, bf16[128,256]{1,0:T(8,128)(2,1)S(1)}, bf16[128,256]{1,0:T(8,128)(2,1)S(1)}) custom-call(f32[1,128,768]{2,1,0:T(8,128)S(1)} %get-tuple-element.41.picked_ref, s32[1,768]{1,0:T(1,128)S(1)} %get-tuple-element.42.source_ref, s32[1,768]{1,0:T(1,128)S(1)} %get-tuple-element.43.place_ref, ...), custom_call_target="tpu_custom_call" | custom-call | flops 1073741824 | bytes 4194304 | tf_op jit(solution)/shard_map/lift_halo/pallas_call | solution.py:572
  31.3 1.0 %collective-permute-start.9 = (bf16[128,256]{1,0:T(8,128)(2,1)S(1)}, bf16[128,256]{1,0:T(8,128)(2,1)S(1)}, u32[]{:S(2)}, u32[]{:S(2)}) collective-permute-start(bf16[128,256]{1,0:T(8,128)(2,1)S(1)} %get-tuple-element.52), channel_id=1, source_target_pairs={{0,8},{4,12},{8,0},{12,4},{1,9},{5,13},{9,1},{13,5},{2,10},{6,14},... | collective-permute-start | bytes 196616 | tf_op jit(solution)/shard_map/ppermute | solution.py:469
  32.3 1.2 %collective-permute-start.10 = (bf16[128,256]{1,0:T(8,128)(2,1)S(1)}, bf16[128,256]{1,0:T(8,128)(2,1)S(1)}, u32[]{:S(2)}, u32[]{:S(2)}) collective-permute-start(bf16[128,256]{1,0:T(8,128)(2,1)S(1)} %get-tuple-element.53), channel_id=1, source_target_pairs={{0,12},{4,8},{8,4},{12,0},{1,13},{5,9},{9,5},{13,1},{2,14},{6,10},... | collective-permute-start | bytes 196616 | tf_op jit(solution)/shard_map/ppermute | solution.py:469
  33.5 1.4 %collective-permute-start.11 = (bf16[128,256]{1,0:T(8,128)(2,1)S(1)}, bf16[128,256]{1,0:T(8,128)(2,1)S(1)}, u32[]{:S(2)}, u32[]{:S(2)}) collective-permute-start(bf16[128,256]{1,0:T(8,128)(2,1)S(1)} %get-tuple-element.54), channel_id=1, source_target_pairs={{0,4},{4,0},{8,12},{12,8},{1,5},{5,1},{9,13},{13,9},{2,6},{6,2},{1... | collective-permute-start | bytes 196616 | tf_op jit(solution)/shard_map/ppermute | solution.py:469
  34.9 3.6 %lift_near.1 = (bf16[128,2048]{1,0:T(8,128)(2,1)S(1)}, bf16[128,3072]{1,0:T(8,128)(2,1)S(1)}, f32[128,2048]{1,0:T(8,128)S(1)}) custom-call(bf16[128,2048]{1,0:T(8,128)(2,1)S(1)} %get-tuple-element.39.first_ref, bf16[128,128]{1,0:T(8,128)(2,1)S(1)} %get-tuple-element.48.prolonged_ref, s32[16,128]{1,0:T(8,128)S(1)} %bitcast.2, s32[16,768]{1,0:T(8,128)S(1)} %copy-done.3, ...), custom_call_target="tpu_custom_call" | custom-call | flops 4294967296 | bytes 4194304 | tf_op jit(solution)/shard_map/lift_near/pallas_call | solution.py:579
  38.5 0.0 collective-permute-done.10.rest_1_
  38.5 0.1 collective-permute-done.11.rest_2_
  38.6 2.4 %far.1 = bf16[2048,128]{1,0:T(8,128)(2,1)} custom-call(bf16[128,2048]{1,0:T(8,128)(2,1)S(1)} %get-tuple-element.49.table_ref, bf16[128,3072]{1,0:T(8,128)(2,1)S(1)} %get-tuple-element.50.aimed_ref, s32[4,768]{1,0:T(4,128)S(1)} %get-tuple-element.32.sources_ref, s32[4,768]{1,0:T(4,128)S(1)} %get-tuple-element.33.places_ref, ...), custom_call_target="tpu_custom_call" | custom-call | flops 2147483648 | bytes 4194304 | tf_op jit(solution)/shard_map/far/pallas_call | solution.py:586
  (25 shorter events, 0.0 us)
Async XLA Ops:
  0.0 8.9 %copy-start.1 = (bf16[2,4,128,128]{3,2,1,0:T(8,128)(2,1)S(1)}, bf16[2,4,128,128]{3,2,1,0:T(8,128)(2,1)}, u32[]{:S(2)}) copy-start(bf16[2,4,128,128]{3,2,1,0:T(8,128)(2,1)} %weights_ref.13) | copy-start | bytes 786436
  0.0 8.9 %copy-start = (bf16[2048,128]{1,0:T(8,128)(2,1)S(1)}, bf16[2048,128]{1,0:T(8,128)(2,1)}, u32[]{:S(2)}) copy-start(bf16[2048,128]{1,0:T(8,128)(2,1)} %latent_hbm.1) | copy-start | bytes 1572868
  0.0 8.9 %copy-start.4 = (s32[16,768]{1,0:T(8,128)S(1)}, s32[16,768]{1,0:T(8,128)}, u32[]{:S(2)}) copy-start(s32[16,768]{1,0:T(8,128)} %place_ref.3) | copy-start | bytes 147460
  0.0 8.9 %copy-start.3 = (s32[16,768]{1,0:T(8,128)S(1)}, s32[16,768]{1,0:T(8,128)}, u32[]{:S(2)}) copy-start(s32[16,768]{1,0:T(8,128)} %source_ref.3) | copy-start | bytes 147460
  0.0 8.9 %copy-start.8 = (s32[2,768]{1,0:T(2,128)S(1)}, s32[2,768]{1,0:T(2,128)}, u32[]{:S(2)}) copy-start(s32[2,768]{1,0:T(2,128)} %coarse_place_ref.1) | copy-start | bytes 18436
  0.0 8.9 %copy-start.7 = (s32[2,768]{1,0:T(2,128)S(1)}, s32[2,768]{1,0:T(2,128)}, u32[]{:S(2)}) copy-start(s32[2,768]{1,0:T(2,128)} %coarse_source_ref.1) | copy-start | bytes 18436
  3.2 5.7 %copy-start.10 = (s32[1,4,128]{2,1,0:T(4,128)S(1)}, s32[1,4,128]{2,1,0:T(4,128)}, u32[]{:S(2)}) copy-start(s32[1,4,128]{2,1,0:T(4,128)} %coarse_send_ref.1) | copy-start | bytes 6148
  3.2 9.2 %collective-permute-start = (bf16[128,256]{1,0:T(8,128)(2,1)}, bf16[128,256]{1,0:T(8,128)(2,1)S(1)}, u32[]{:S(2)}, u32[]{:S(2)}) collective-permute-start(bf16[128,256]{1,0:T(8,128)(2,1)} %get-tuple-element.36), channel_id=1, source_target_pairs={{0,8},{4,12},{8,0},{12,4},{1,9},{5,13},{9,1},{13,5},{2,10},{6,14},... | collective-permute-start | bytes 196616 | tf_op jit(solution)/shard_map/ppermute | solution.py:469
  7.3 6.4 %collective-permute-start.1 = (bf16[128,256]{1,0:T(8,128)(2,1)}, bf16[128,256]{1,0:T(8,128)(2,1)S(1)}, u32[]{:S(2)}, u32[]{:S(2)}) collective-permute-start(bf16[128,256]{1,0:T(8,128)(2,1)} %get-tuple-element.37), channel_id=1, source_target_pairs={{0,12},{4,8},{8,4},{12,0},{1,13},{5,9},{9,5},{13,1},{2,14},{6,10},... | collective-permute-start | bytes 196616 | tf_op jit(solution)/shard_map/ppermute | solution.py:469
  8.6 5.2 %collective-permute-start.2 = (bf16[128,256]{1,0:T(8,128)(2,1)}, bf16[128,256]{1,0:T(8,128)(2,1)S(1)}, u32[]{:S(2)}, u32[]{:S(2)}) collective-permute-start(bf16[128,256]{1,0:T(8,128)(2,1)} %get-tuple-element.38), channel_id=1, source_target_pairs={{0,4},{4,0},{8,12},{12,8},{1,5},{5,1},{9,13},{13,9},{2,6},{6,2},{1... | collective-permute-start | bytes 196616 | tf_op jit(solution)/shard_map/ppermute | solution.py:469
  13.8 0.7 %copy-start.11 = (s32[1,4,64]{2,1,0:T(4,128)S(1)}, s32[1,4,64]{2,1,0:T(4,128)}, u32[]{:S(2)}) copy-start(s32[1,4,64]{2,1,0:T(4,128)} %pool_ref.1) | copy-start | bytes 3076
  14.5 3.7 %copy-start.6 = (s32[2048]{0:T(1024)S(1)}, s32[2048]{0:T(1024)}, u32[]{:S(2)}) copy-start(s32[2048]{0:T(1024)} %param.20) | copy-start | bytes 24580
  16.3 1.9 %copy-start.9 = (s32[1,4,256]{2,1,0:T(4,128)S(1)}, s32[1,4,256]{2,1,0:T(4,128)}, u32[]{:S(2)}) copy-start(s32[1,4,256]{2,1,0:T(4,128)} %lists_ref.1) | copy-start | bytes 12292
  16.3 3.7 %collective-permute-start.5 = (bf16[128,128]{1,0:T(8,128)(2,1)S(1)}, bf16[128,128]{1,0:T(8,128)(2,1)S(1)}, u32[]{:S(2)}, u32[]{:S(2)}) collective-permute-start(bf16[128,128]{1,0:T(8,128)(2,1)S(1)} %get-tuple-element.40.refs_0_), channel_id=1, source_target_pairs={{0,3},{1,2},{2,1},{3,0},{4,7},{5,6},{6,5},{7,4},{8,11},{9,10},{10,... | collective-permute-start | bytes 98312 | tf_op jit(solution)/shard_map/ppermute | solution.py:480
  16.4 4.0 %collective-permute-start.4 = (bf16[128,128]{1,0:T(8,128)(2,1)S(1)}, bf16[128,128]{1,0:T(8,128)(2,1)S(1)}, u32[]{:S(2)}, u32[]{:S(2)}) collective-permute-start(bf16[128,128]{1,0:T(8,128)(2,1)S(1)} %get-tuple-element.40.refs_0_), channel_id=1, source_target_pairs={{0,2},{2,0},{1,3},{3,1},{4,6},{6,4},{5,7},{7,5},{8,10},{10,8},{9,1... | collective-permute-start | bytes 98312 | tf_op jit(solution)/shard_map/ppermute | solution.py:478
  17.9 2.5 %collective-permute-start.3 = (bf16[128,128]{1,0:T(8,128)(2,1)S(1)}, bf16[128,128]{1,0:T(8,128)(2,1)S(1)}, u32[]{:S(2)}, u32[]{:S(2)}) collective-permute-start(bf16[128,128]{1,0:T(8,128)(2,1)S(1)} %get-tuple-element.40.refs_0_), channel_id=1, source_target_pairs={{0,1},{1,0},{2,3},{3,2},{4,5},{5,4},{6,7},{7,6},{8,9},{9,8},{10,11... | collective-permute-start | bytes 98312 | tf_op jit(solution)/shard_map/ppermute | solution.py:479
  18.2 2.2 %copy-start.2 = (bf16[4,128,128]{2,1,0:T(8,128)(2,1)S(1)}, bf16[4,128,128]{2,1,0:T(8,128)(2,1)}, u32[]{:S(2)}) copy-start(bf16[4,128,128]{2,1,0:T(8,128)(2,1)} %coarse_weights_ref.1) | copy-start | bytes 393220
  20.8 5.5 %collective-permute-start.6 = (bf16[128,128]{1,0:T(8,128)(2,1)S(1)}, bf16[128,128]{1,0:T(8,128)(2,1)S(1)}, u32[]{:S(2)}, u32[]{:S(2)}) collective-permute-start(bf16[128,128]{1,0:T(8,128)(2,1)S(1)} %get-tuple-element.45), channel_id=1, source_target_pairs={{0,8},{4,12},{8,0},{12,4},{1,9},{5,13},{9,1},{13,5},{2,10},{6,14},... | collective-permute-start | bytes 98312 | tf_op jit(solution)/shard_map/ppermute | solution.py:469
  24.4 5.7 %collective-permute-start.7 = (bf16[128,128]{1,0:T(8,128)(2,1)S(1)}, bf16[128,128]{1,0:T(8,128)(2,1)S(1)}, u32[]{:S(2)}, u32[]{:S(2)}) collective-permute-start(bf16[128,128]{1,0:T(8,128)(2,1)S(1)} %get-tuple-element.46), channel_id=1, source_target_pairs={{0,12},{4,8},{8,4},{12,0},{1,13},{5,9},{9,5},{13,1},{2,14},{6,10},... | collective-permute-start | bytes 98312 | tf_op jit(solution)/shard_map/ppermute | solution.py:469
  25.0 5.1 %copy-start.5 = (bf16[128,128]{1,0:T(8,128)(2,1)S(1)}, bf16[128,128]{1,0:T(8,128)(2,1)}, u32[]{:S(2)}) copy-start(bf16[128,128]{1,0:T(8,128)(2,1)} %prolong_weight_ref.1) | copy-start | bytes 98308
  25.0 5.1 %collective-permute-start.8 = (bf16[128,128]{1,0:T(8,128)(2,1)S(1)}, bf16[128,128]{1,0:T(8,128)(2,1)S(1)}, u32[]{:S(2)}, u32[]{:S(2)}) collective-permute-start(bf16[128,128]{1,0:T(8,128)(2,1)S(1)} %get-tuple-element.47), channel_id=1, source_target_pairs={{0,4},{4,0},{8,12},{12,8},{1,5},{5,1},{9,13},{13,9},{2,6},{6,2},{1... | collective-permute-start | bytes 98312 | tf_op jit(solution)/shard_map/ppermute | solution.py:469
  31.3 7.2 %collective-permute-start.9 = (bf16[128,256]{1,0:T(8,128)(2,1)S(1)}, bf16[128,256]{1,0:T(8,128)(2,1)S(1)}, u32[]{:S(2)}, u32[]{:S(2)}) collective-permute-start(bf16[128,256]{1,0:T(8,128)(2,1)S(1)} %get-tuple-element.52), channel_id=1, source_target_pairs={{0,8},{4,12},{8,0},{12,4},{1,9},{5,13},{9,1},{13,5},{2,10},{6,14},... | collective-permute-start | bytes 196616 | tf_op jit(solution)/shard_map/ppermute | solution.py:469
  32.3 6.2 %collective-permute-start.10 = (bf16[128,256]{1,0:T(8,128)(2,1)S(1)}, bf16[128,256]{1,0:T(8,128)(2,1)S(1)}, u32[]{:S(2)}, u32[]{:S(2)}) collective-permute-start(bf16[128,256]{1,0:T(8,128)(2,1)S(1)} %get-tuple-element.53), channel_id=1, source_target_pairs={{0,12},{4,8},{8,4},{12,0},{1,13},{5,9},{9,5},{13,1},{2,14},{6,10},... | collective-permute-start | bytes 196616 | tf_op jit(solution)/shard_map/ppermute | solution.py:469
  33.5 5.1 %collective-permute-start.11 = (bf16[128,256]{1,0:T(8,128)(2,1)S(1)}, bf16[128,256]{1,0:T(8,128)(2,1)S(1)}, u32[]{:S(2)}, u32[]{:S(2)}) collective-permute-start(bf16[128,256]{1,0:T(8,128)(2,1)S(1)} %get-tuple-element.54), channel_id=1, source_target_pairs={{0,4},{4,0},{8,12},{12,8},{1,5},{5,1},{9,13},{13,9},{2,6},{6,2},{1... | collective-permute-start | bytes 196616 | tf_op jit(solution)/shard_map/ppermute | solution.py:469

commit v4 on v3

--- a/solution.py
+++ b/solution.py
@@ -114,10 +114,14 @@
         copies[2 + index].wait()
         tables.append(latent_ref[index * part : (index + 1) * part, :].T)
     table = jnp.concatenate(tables, axis=1)
-    for step, out_ref in zip(grid.steps, sent_refs):
-        index_row = lists_ref[pl.ds(grid.partner_here(step), 1), :]
-        picked = dot(table, rows_hot(index_row, table.shape[1])).astype(BF16)
-        out_ref[...] = dot(weight, picked).astype(BF16)
+    index_row = jnp.concatenate(
+        [lists_ref[pl.ds(grid.partner_here(step), 1), :] for step in grid.steps], axis=1
+    )
+    picked = dot(table, rows_hot(index_row, node_count)).astype(BF16)
+    terms = dot(weight, picked).astype(BF16)
+    capacity = lists_ref.shape[1]
+    for index, out_ref in enumerate(sent_refs):
+        out_ref[...] = terms[:, index * capacity : (index + 1) * capacity]
 
 
 def far_rows(source_ref, place_ref, batch):
@@ -184,12 +188,14 @@
     coarse_source_ref,
     coarse_place_ref,
     coarse_send_ref,
+    pool_ref,
     table_ref,
     sources_ref,
     places_ref,
     aimed_ref,
     sums_ref,
     packed_ref,
+    pooled_ref,
     terms_ref,
 ):
     table = latent_ref[...].T
@@ -212,6 +218,8 @@
     whole = jnp.concatenate(pieces, axis=0) + 1
     high = lax.shift_right_logical(whole, 8)
     packed_ref[...] = jnp.concatenate([high.astype(F32), (whole & 255).astype(F32)], axis=0).astype(BF16)
+    for owner in range(grid.owners):
+        pooled_ref[owner : owner + 1, :] = pool_ref[0, 4 * owner : 4 * owner + 1, :]
 
 
 def far_edges(layer, table_ref, aimed_ref, sources_ref, places_ref, sums_ref, weights_ref, halo_refs, both_ref, write):
@@ -271,7 +279,7 @@
     packet_ref[grid.pooled_rows :, :] = packed_ref[...]
     far_edges(0, table_ref, aimed_ref, sources_ref, places_ref, sums_ref, weights_ref, halo_refs, both_ref, write)
     for owner in range(grid.owners):
-        hot = rows_hot(pool_ref[0, 4 * owner : 4 * owner + 1, :], first_ref.shape[1])
+        hot = rows_hot(pool_ref[owner : owner + 1, :], first_ref.shape[1])
         pooled = dot(first_ref[...], hot).astype(BF16).T
         packet_ref[owner * grid.pool_capacity : (owner + 1) * grid.pool_capacity, :] = pooled
 
@@ -530,20 +538,28 @@
         in_specs=[in_hbm] * 3,
     )(fine_nodes, halo_send, fine_weights)
     halo = swap_dom(grid, sent)
-    nodes, far_sources, far_places, aimed, sums, packed = call(
+    nodes, far_sources, far_places, aimed, sums, packed, pool_lists = call(
         functools.partial(near_kernel, grid),
-        [table, far_lists, far_lists, aimed_table, sums_table, ((2 * grid.packed_rows, features), BF16)],
+        [
+            table,
+            far_lists,
+            far_lists,
+            aimed_table,
+            sums_table,
+            ((2 * grid.packed_rows, features), BF16),
+            ((grid.owners, grid.pool_capacity), I32),
+        ],
         [two_tables],
         flops=4 * big,
         name="near",
-    )(fine_nodes, fine_src, fine_dst, fine_weights, coarse_src, coarse_dst, coarse_send)
+    )(fine_nodes, fine_src, fine_dst, fine_weights, coarse_src, coarse_dst, coarse_send, pool_send)
     first, packet = call(
         functools.partial(far_pool_kernel, grid),
         [table, ((grid.packet, features), BF16)],
         [two_tables],
         flops=2 * big,
         name="far_pool",
-    )(nodes, aimed, far_sources, far_places, sums, fine_weights, pool_send, packed, *halo)
+    )(nodes, aimed, far_sources, far_places, sums, fine_weights, pool_lists, packed, *halo)
     packets = trade_packets(grid, packet)
     (ahead,) = call(
         functools.partial(ahead_kernel, grid), [((features + 16, steps * halo_capacity), BF16)], flops=big, name="ahead"

time: 41.2 us -> 40.1 us (0.973)
  local copies, waits for them, and re-layouts: 0.73 us -> 0.05 us
    unnamed x24, local copies, waits for them, and re-layouts: 0.73 us -> 0.05 us
  transfers between devices with their start and end apart: 12 -> 12, of which waited for: 7 -> 7; matrix products, arithmetic and copies ran while one was open for 0% -> 0% of each run, Pallas kernels for 20% -> 21%
where the time goes in v4:
time: 40.1 us; the launch traced here: 39.9 us
  Pallas kernels  16.7 us (42%)
  starting transfers between devices  15.4 us (38%)
  waiting for transfers between devices  7.66 us (19%)
    ppermute x9, starting transfers between devices, swap_dom(): lax.ppermute(arrays[index], 'dom', [(dom, grid.partner(dom, step)) for do...  13.5 us
    ppermute x9, waiting for transfers between devices, swap_dom(): lax.ppermute(arrays[index], 'dom', [(dom, grid.partner(dom, step)) for do...  6.14 us
    pallas_call x1, Pallas kernels, body(): call(functools.partial(lift_near_kernel, grid), [table, aimed_table, sums...  3.61 us
    pallas_call x1, Pallas kernels, body(): call(functools.partial(near_kernel, grid), [table, far_lists, far_lists,...  3.47 us
    pallas_call x1, Pallas kernels, body(): call(functools.partial(send_kernel, grid), halo_outs, [pltpu.VMEM((node_c...  2.76 us
    pallas_call x1, Pallas kernels, body(): call(far_kernel, [((node_count, features), BF16)], [two_tables, pltpu.VME...  2.38 us
    pallas_call x1, Pallas kernels, body(): call(functools.partial(far_pool_kernel, grid), [table, ((grid.packet, fea...  1.8 us
    ppermute x1, starting transfers between devices, trade_packets(): over = lax.ppermute(packet, 'sub', pairs)  1.56 us
  transfers between devices with their start and end apart: 12, of which 7 were waited for; matrix products, arithmetic and copies ran while one was open for 0% of the time, Pallas kernels for 21%

profile of v4, /device:TPU:0, one launch (start us, length us, event | category | flops | bytes accessed | tf_op | source)
XLA Modules:
  0.0 39.9 jit_solution(5460017227630468910)
XLA Ops:
  0.0 2.8 %send.1 = (bf16[128,256]{1,0:T(8,128)(2,1)}, bf16[128,256]{1,0:T(8,128)(2,1)}, bf16[128,256]{1,0:T(8,128)(2,1)}) custom-call(bf16[2048,128]{1,0:T(8,128)(2,1)} %latent_hbm.1, s32[1,4,256]{2,1,0:T(4,128)} %lists_ref.1, bf16[2,4,128,128]{3,2,1,0:T(8,128)(2,1)} %weights_ref.13), custom_call_target="tpu_custom_call" | custom-call | flops 1073741824 | bytes 4194304 | tf_op jit(solution)/shard_map/send/pallas_call | solution.py:526
  2.8 0.0 copy-start.11
  2.8 0.0 copy-start.10
  2.8 4.1 %collective-permute-start = (bf16[128,256]{1,0:T(8,128)(2,1)}, bf16[128,256]{1,0:T(8,128)(2,1)S(1)}, u32[]{:S(2)}, u32[]{:S(2)}) collective-permute-start(bf16[128,256]{1,0:T(8,128)(2,1)} %get-tuple-element.38), channel_id=1, source_target_pairs={{0,8},{4,12},{8,0},{12,4},{1,9},{5,13},{9,1},{13,5},{2,10},{6,14},... | collective-permute-start | bytes 196616 | tf_op jit(solution)/shard_map/ppermute | solution.py:477
  6.9 1.3 %collective-permute-start.1 = (bf16[128,256]{1,0:T(8,128)(2,1)}, bf16[128,256]{1,0:T(8,128)(2,1)S(1)}, u32[]{:S(2)}, u32[]{:S(2)}) collective-permute-start(bf16[128,256]{1,0:T(8,128)(2,1)} %get-tuple-element.39), channel_id=1, source_target_pairs={{0,12},{4,8},{8,4},{12,0},{1,13},{5,9},{9,5},{13,1},{2,14},{6,10},... | collective-permute-start | bytes 196616 | tf_op jit(solution)/shard_map/ppermute | solution.py:477
  8.3 0.2 collective-permute-start.2
  8.6 3.5 %near.1 = (bf16[128,2048]{1,0:T(8,128)(2,1)S(1)}, s32[4,768]{1,0:T(4,128)S(1)}, s32[4,768]{1,0:T(4,128)S(1)}, bf16[128,3072]{1,0:T(8,128)(2,1)S(1)}, f32[128,204...) custom-call(bf16[2048,128]{1,0:T(8,128)(2,1)S(1)} %copy-done, s32[16,768]{1,0:T(8,128)S(1)} %copy-done.3, ...), custom_call_target="tpu_custom_call" | custom-call | flops 4294967296 | bytes 4194304 | tf_op jit(solution)/shard_map/near/pallas_call | solution.py:541
  12.0 0.0 collective-permute-done.rest_0_
  12.1 1.3 %collective-permute-done.1.rest_1_ = bf16[128,256]{1,0:T(8,128)(2,1)S(1)} collective-permute-done((bf16[128,256]{1,0:T(8,128)(2,1)}, bf16[128,256]{1,0:T(8,128)(2,1)S(1)}, u32[]{:S(2)}, u32[]{:S(2)}) %collective-permute-start.1) | collective-permute-done | bytes 65568 | tf_op jit(solution)/shard_map/ppermute | solution.py:477
  13.4 0.1 collective-permute-done.2.rest_2_
  13.5 1.8 %far_pool.1 = (bf16[128,2048]{1,0:T(8,128)(2,1)S(1)}, bf16[128,128]{1,0:T(8,128)(2,1)S(1)}) custom-call(bf16[128,2048]{1,0:T(8,128)(2,1)S(1)} %get-tuple-element.31.table_ref, bf16[128,3072]{1,0:T(8,128)(2,1)S(1)} %get-tuple-element.32.aimed_ref, s32[4,768]{1,0:T(4,128)S(1)} %get-tuple-element.33.sources_ref, s32[4,768]{1,0:T(4,128)S(1)} %get-tuple-element.34.places_ref, ...), custom_call_target="tpu_custom_call" | custom-call | flops 2147483648 | bytes 4194304 | tf_op jit(solution)/shard_map/far_pool/pallas_call | solution.py:556
  15.3 0.1 collective-permute-start.5
  15.3 1.6 %collective-permute-start.4 = (bf16[128,128]{1,0:T(8,128)(2,1)S(1)}, bf16[128,128]{1,0:T(8,128)(2,1)S(1)}, u32[]{:S(2)}, u32[]{:S(2)}) collective-permute-start(bf16[128,128]{1,0:T(8,128)(2,1)S(1)} %get-tuple-element.42.refs_0_), channel_id=1, source_target_pairs={{0,2},{2,0},{1,3},{3,1},{4,6},{6,4},{5,7},{7,5},{8,10},{10,8},{9,1... | collective-permute-start | bytes 98312 | tf_op jit(solution)/shard_map/ppermute | solution.py:486
  16.9 0.3 collective-permute-start.3
  17.2 0.6 %ahead.1.ahead_ref = bf16[144,768]{1,0:T(8,128)(2,1)S(1)} custom-call(bf16[128,2048]{1,0:T(8,128)(2,1)S(1)} %get-tuple-element.41.first_ref, s32[16,128]{1,0:T(8,128)S(1)} %bitcast.1, s32[1,4,256]{2,1,0:T(4,128)S(1)} %copy-done.9), custom_call_target="tpu_custom_call" | custom-call | flops 1073741824 | bytes 4194304 | tf_op jit(solution)/shard_map/ahead/pallas_call | solution.py:564
  17.8 1.1 %collective-permute-done.5.refs_3_ = bf16[128,128]{1,0:T(8,128)(2,1)S(1)} collective-permute-done((bf16[128,128]{1,0:T(8,128)(2,1)S(1)}, bf16[128,128]{1,0:T(8,128)(2,1)S(1)}, u32[]{:S(2)}, u32[]{:S(2)}) %collective-permute-start.5) | collective-permute-done | bytes 32800 | tf_op jit(solution)/shard_map/ppermute | solution.py:488
  19.0 0.4 %collective-permute-done.4.refs_2_ = bf16[128,128]{1,0:T(8,128)(2,1)S(1)} collective-permute-done((bf16[128,128]{1,0:T(8,128)(2,1)S(1)}, bf16[128,128]{1,0:T(8,128)(2,1)S(1)}, u32[]{:S(2)}, u32[]{:S(2)}) %collective-permute-start.4) | collective-permute-done | bytes 32800 | tf_op jit(solution)/shard_map/ppermute | solution.py:486
  19.4 0.4 %coarse_send.1 = (bf16[128,128]{1,0:T(8,128)(2,1)S(1)}, bf16[128,128]{1,0:T(8,128)(2,1)S(1)}, bf16[128,128]{1,0:T(8,128)(2,1)S(1)}) custom-call(bf16[4,128,128]{2,1,0:T(8,128)(2,1)S(1)} %copy-done.2, bf16[128,128]{1,0:T(8,128)(2,1)S(1)} %get-tuple-element.42.refs_0_, bf16[128,128]{1,0:T(8,128)(2,1)S(1)} %collective-permute-done.3.refs_1_, ...), custom_call_target="tpu_custom_call" | custom-call | flops 536870912 | bytes 4194304 | tf_op jit(solution)/shard_map/coarse_send/pallas_call | solution.py:568
  19.8 3.6 %collective-permute-start.6 = (bf16[128,128]{1,0:T(8,128)(2,1)S(1)}, bf16[128,128]{1,0:T(8,128)(2,1)S(1)}, u32[]{:S(2)}, u32[]{:S(2)}) collective-permute-start(bf16[128,128]{1,0:T(8,128)(2,1)S(1)} %get-tuple-element.47), channel_id=1, source_target_pairs={{0,8},{4,12},{8,0},{12,4},{1,9},{5,13},{9,1},{13,5},{2,10},{6,14},... | collective-permute-start | bytes 98312 | tf_op jit(solution)/shard_map/ppermute | solution.py:477
  23.4 0.6 %collective-permute-start.7 = (bf16[128,128]{1,0:T(8,128)(2,1)S(1)}, bf16[128,128]{1,0:T(8,128)(2,1)S(1)}, u32[]{:S(2)}, u32[]{:S(2)}) collective-permute-start(bf16[128,128]{1,0:T(8,128)(2,1)S(1)} %get-tuple-element.48), channel_id=1, source_target_pairs={{0,12},{4,8},{8,4},{12,0},{1,13},{5,9},{9,5},{13,1},{2,14},{6,10},... | collective-permute-start | bytes 98312 | tf_op jit(solution)/shard_map/ppermute | solution.py:477
  24.0 0.0 collective-permute-start.8
  24.0 0.5 %coarse_own.1 = (f32[1,128,768]{2,1,0:T(8,128)S(1)}, s32[1,768]{1,0:T(1,128)S(1)}, s32[1,768]{1,0:T(1,128)S(1)}, bf16[1,128,64]{2,1,0:T(8,128)(2,1)S(1)}) custom-call(bf16[4,128,128]{2,1,0:T(8,128)(2,1)S(1)} %copy-done.2, bf16[128,128]{1,0:T(8,128)(2,1)S(1)} %get-tuple-element.42.refs_0_, bf16[128,128]{1,0:T(8,128)(2,1)S(1)} %collective-permute-done.3.refs_1_, ...), custom_call_target="tpu_custom_call" | custom-call | flops 4294967296 | bytes 4194304 | tf_op jit(solution)/shard_map/coarse_own/pallas_call | solution.py:576
  24.5 0.8 %collective-permute-done.6.rest_0_ = bf16[128,128]{1,0:T(8,128)(2,1)S(1)} collective-permute-done((bf16[128,128]{1,0:T(8,128)(2,1)S(1)}, bf16[128,128]{1,0:T(8,128)(2,1)S(1)}, u32[]{:S(2)}, u32[]{:S(2)}) %collective-permute-start.6) | collective-permute-done | bytes 32800 | tf_op jit(solution)/shard_map/ppermute | solution.py:477
  25.3 3.8 %collective-permute-done.7.rest_1_ = bf16[128,128]{1,0:T(8,128)(2,1)S(1)} collective-permute-done((bf16[128,128]{1,0:T(8,128)(2,1)S(1)}, bf16[128,128]{1,0:T(8,128)(2,1)S(1)}, u32[]{:S(2)}, u32[]{:S(2)}) %collective-permute-start.7) | collective-permute-done | bytes 32800 | tf_op jit(solution)/shard_map/ppermute | solution.py:477
  29.1 1.2 %lift_halo.1 = (bf16[128,128]{1,0:T(8,128)(2,1)S(1)}, bf16[128,256]{1,0:T(8,128)(2,1)S(1)}, bf16[128,256]{1,0:T(8,128)(2,1)S(1)}, bf16[128,256]{1,0:T(8,128)(2,1)S(1)}) custom-call(f32[1,128,768]{2,1,0:T(8,128)S(1)} %get-tuple-element.43.picked_ref, s32[1,768]{1,0:T(1,128)S(1)} %get-tuple-element.44.source_ref, s32[1,768]{1,0:T(1,128)S(1)} %get-tuple-element.45.place_ref, ...), custom_call_target="tpu_custom_call" | custom-call | flops 1073741824 | bytes 4194304 | tf_op jit(solution)/shard_map/lift_halo/pallas_call | solution.py:588
  30.3 1.0 %collective-permute-start.9 = (bf16[128,256]{1,0:T(8,128)(2,1)S(1)}, bf16[128,256]{1,0:T(8,128)(2,1)S(1)}, u32[]{:S(2)}, u32[]{:S(2)}) collective-permute-start(bf16[128,256]{1,0:T(8,128)(2,1)S(1)} %get-tuple-element.54), channel_id=1, source_target_pairs={{0,8},{4,12},{8,0},{12,4},{1,9},{5,13},{9,1},{13,5},{2,10},{6,14},... | collective-permute-start | bytes 196616 | tf_op jit(solution)/shard_map/ppermute | solution.py:477
  31.2 1.2 %collective-permute-start.10 = (bf16[128,256]{1,0:T(8,128)(2,1)S(1)}, bf16[128,256]{1,0:T(8,128)(2,1)S(1)}, u32[]{:S(2)}, u32[]{:S(2)}) collective-permute-start(bf16[128,256]{1,0:T(8,128)(2,1)S(1)} %get-tuple-element.55), channel_id=1, source_target_pairs={{0,12},{4,8},{8,4},{12,0},{1,13},{5,9},{9,5},{13,1},{2,14},{6,10},... | collective-permute-start | bytes 196616 | tf_op jit(solution)/shard_map/ppermute | solution.py:477
  32.4 1.4 %collective-permute-start.11 = (bf16[128,256]{1,0:T(8,128)(2,1)S(1)}, bf16[128,256]{1,0:T(8,128)(2,1)S(1)}, u32[]{:S(2)}, u32[]{:S(2)}) collective-permute-start(bf16[128,256]{1,0:T(8,128)(2,1)S(1)} %get-tuple-element.56), channel_id=1, source_target_pairs={{0,4},{4,0},{8,12},{12,8},{1,5},{5,1},{9,13},{13,9},{2,6},{6,2},{1... | collective-permute-start | bytes 196616 | tf_op jit(solution)/shard_map/ppermute | solution.py:477
  33.8 3.6 %lift_near.1 = (bf16[128,2048]{1,0:T(8,128)(2,1)S(1)}, bf16[128,3072]{1,0:T(8,128)(2,1)S(1)}, f32[128,2048]{1,0:T(8,128)S(1)}) custom-call(bf16[128,2048]{1,0:T(8,128)(2,1)S(1)} %get-tuple-element.41.first_ref, bf16[128,128]{1,0:T(8,128)(2,1)S(1)} %get-tuple-element.50.prolonged_ref, s32[16,128]{1,0:T(8,128)S(1)} %bitcast.2, s32[16,768]{1,0:T(8,128)S(1)} %copy-done.3, ...), custom_call_target="tpu_custom_call" | custom-call | flops 4294967296 | bytes 4194304 | tf_op jit(solution)/shard_map/lift_near/pallas_call | solution.py:595
  37.4 0.0 collective-permute-done.10.rest_1_
  37.4 0.1 collective-permute-done.11.rest_2_
  37.6 2.4 %far.1 = bf16[2048,128]{1,0:T(8,128)(2,1)} custom-call(bf16[128,2048]{1,0:T(8,128)(2,1)S(1)} %get-tuple-element.51.table_ref, bf16[128,3072]{1,0:T(8,128)(2,1)S(1)} %get-tuple-element.52.aimed_ref, s32[4,768]{1,0:T(4,128)S(1)} %get-tuple-element.33.sources_ref, s32[4,768]{1,0:T(4,128)S(1)} %get-tuple-element.34.places_ref, ...), custom_call_target="tpu_custom_call" | custom-call | flops 2147483648 | bytes 4194304 | tf_op jit(solution)/shard_map/far/pallas_call | solution.py:602
  (25 shorter events, 0.0 us)
Async XLA Ops:
  0.0 8.5 %copy-start.1 = (bf16[2,4,128,128]{3,2,1,0:T(8,128)(2,1)S(1)}, bf16[2,4,128,128]{3,2,1,0:T(8,128)(2,1)}, u32[]{:S(2)}) copy-start(bf16[2,4,128,128]{3,2,1,0:T(8,128)(2,1)} %weights_ref.13) | copy-start | bytes 786436
  0.0 8.5 %copy-start = (bf16[2048,128]{1,0:T(8,128)(2,1)S(1)}, bf16[2048,128]{1,0:T(8,128)(2,1)}, u32[]{:S(2)}) copy-start(bf16[2048,128]{1,0:T(8,128)(2,1)} %latent_hbm.1) | copy-start | bytes 1572868
  0.0 8.5 %copy-start.4 = (s32[16,768]{1,0:T(8,128)S(1)}, s32[16,768]{1,0:T(8,128)}, u32[]{:S(2)}) copy-start(s32[16,768]{1,0:T(8,128)} %place_ref.3) | copy-start | bytes 147460
  0.0 8.5 %copy-start.3 = (s32[16,768]{1,0:T(8,128)S(1)}, s32[16,768]{1,0:T(8,128)}, u32[]{:S(2)}) copy-start(s32[16,768]{1,0:T(8,128)} %source_ref.3) | copy-start | bytes 147460
  0.0 8.5 %copy-start.8 = (s32[2,768]{1,0:T(2,128)S(1)}, s32[2,768]{1,0:T(2,128)}, u32[]{:S(2)}) copy-start(s32[2,768]{1,0:T(2,128)} %coarse_place_ref.1) | copy-start | bytes 18436
  0.0 8.5 %copy-start.7 = (s32[2,768]{1,0:T(2,128)S(1)}, s32[2,768]{1,0:T(2,128)}, u32[]{:S(2)}) copy-start(s32[2,768]{1,0:T(2,128)} %coarse_source_ref.1) | copy-start | bytes 18436
  2.8 5.8 %copy-start.11 = (s32[1,4,64]{2,1,0:T(4,128)S(1)}, s32[1,4,64]{2,1,0:T(4,128)}, u32[]{:S(2)}) copy-start(s32[1,4,64]{2,1,0:T(4,128)} %pool_ref.1) | copy-start | bytes 3076
  2.8 5.8 %copy-start.10 = (s32[1,4,128]{2,1,0:T(4,128)S(1)}, s32[1,4,128]{2,1,0:T(4,128)}, u32[]{:S(2)}) copy-start(s32[1,4,128]{2,1,0:T(4,128)} %coarse_send_ref.1) | copy-start | bytes 6148
  2.8 9.2 %collective-permute-start = (bf16[128,256]{1,0:T(8,128)(2,1)}, bf16[128,256]{1,0:T(8,128)(2,1)S(1)}, u32[]{:S(2)}, u32[]{:S(2)}) collective-permute-start(bf16[128,256]{1,0:T(8,128)(2,1)} %get-tuple-element.38), channel_id=1, source_target_pairs={{0,8},{4,12},{8,0},{12,4},{1,9},{5,13},{9,1},{13,5},{2,10},{6,14},... | collective-permute-start | bytes 196616 | tf_op jit(solution)/shard_map/ppermute | solution.py:477
  6.9 6.4 %collective-permute-start.1 = (bf16[128,256]{1,0:T(8,128)(2,1)}, bf16[128,256]{1,0:T(8,128)(2,1)S(1)}, u32[]{:S(2)}, u32[]{:S(2)}) collective-permute-start(bf16[128,256]{1,0:T(8,128)(2,1)} %get-tuple-element.39), channel_id=1, source_target_pairs={{0,12},{4,8},{8,4},{12,0},{1,13},{5,9},{9,5},{13,1},{2,14},{6,10},... | collective-permute-start | bytes 196616 | tf_op jit(solution)/shard_map/ppermute | solution.py:477
  8.3 5.2 %collective-permute-start.2 = (bf16[128,256]{1,0:T(8,128)(2,1)}, bf16[128,256]{1,0:T(8,128)(2,1)S(1)}, u32[]{:S(2)}, u32[]{:S(2)}) collective-permute-start(bf16[128,256]{1,0:T(8,128)(2,1)} %get-tuple-element.40), channel_id=1, source_target_pairs={{0,4},{4,0},{8,12},{12,8},{1,5},{5,1},{9,13},{13,9},{2,6},{6,2},{1... | collective-permute-start | bytes 196616 | tf_op jit(solution)/shard_map/ppermute | solution.py:477
  13.5 3.7 %copy-start.6 = (s32[2048]{0:T(1024)S(1)}, s32[2048]{0:T(1024)}, u32[]{:S(2)}) copy-start(s32[2048]{0:T(1024)} %param.20) | copy-start | bytes 24580
  15.3 1.9 %copy-start.9 = (s32[1,4,256]{2,1,0:T(4,128)S(1)}, s32[1,4,256]{2,1,0:T(4,128)}, u32[]{:S(2)}) copy-start(s32[1,4,256]{2,1,0:T(4,128)} %lists_ref.1) | copy-start | bytes 12292
  15.3 3.7 %collective-permute-start.5 = (bf16[128,128]{1,0:T(8,128)(2,1)S(1)}, bf16[128,128]{1,0:T(8,128)(2,1)S(1)}, u32[]{:S(2)}, u32[]{:S(2)}) collective-permute-start(bf16[128,128]{1,0:T(8,128)(2,1)S(1)} %get-tuple-element.42.refs_0_), channel_id=1, source_target_pairs={{0,3},{1,2},{2,1},{3,0},{4,7},{5,6},{6,5},{7,4},{8,11},{9,10},{10,... | collective-permute-start | bytes 98312 | tf_op jit(solution)/shard_map/ppermute | solution.py:488
  15.3 4.0 %collective-permute-start.4 = (bf16[128,128]{1,0:T(8,128)(2,1)S(1)}, bf16[128,128]{1,0:T(8,128)(2,1)S(1)}, u32[]{:S(2)}, u32[]{:S(2)}) collective-permute-start(bf16[128,128]{1,0:T(8,128)(2,1)S(1)} %get-tuple-element.42.refs_0_), channel_id=1, source_target_pairs={{0,2},{2,0},{1,3},{3,1},{4,6},{6,4},{5,7},{7,5},{8,10},{10,8},{9,1... | collective-permute-start | bytes 98312 | tf_op jit(solution)/shard_map/ppermute | solution.py:486
  16.9 2.5 %collective-permute-start.3 = (bf16[128,128]{1,0:T(8,128)(2,1)S(1)}, bf16[128,128]{1,0:T(8,128)(2,1)S(1)}, u32[]{:S(2)}, u32[]{:S(2)}) collective-permute-start(bf16[128,128]{1,0:T(8,128)(2,1)S(1)} %get-tuple-element.42.refs_0_), channel_id=1, source_target_pairs={{0,1},{1,0},{2,3},{3,2},{4,5},{5,4},{6,7},{7,6},{8,9},{9,8},{10,11... | collective-permute-start | bytes 98312 | tf_op jit(solution)/shard_map/ppermute | solution.py:487
  17.2 2.2 %copy-start.2 = (bf16[4,128,128]{2,1,0:T(8,128)(2,1)S(1)}, bf16[4,128,128]{2,1,0:T(8,128)(2,1)}, u32[]{:S(2)}) copy-start(bf16[4,128,128]{2,1,0:T(8,128)(2,1)} %coarse_weights_ref.1) | copy-start | bytes 393220
  19.8 5.5 %collective-permute-start.6 = (bf16[128,128]{1,0:T(8,128)(2,1)S(1)}, bf16[128,128]{1,0:T(8,128)(2,1)S(1)}, u32[]{:S(2)}, u32[]{:S(2)}) collective-permute-start(bf16[128,128]{1,0:T(8,128)(2,1)S(1)} %get-tuple-element.47), channel_id=1, source_target_pairs={{0,8},{4,12},{8,0},{12,4},{1,9},{5,13},{9,1},{13,5},{2,10},{6,14},... | collective-permute-start | bytes 98312 | tf_op jit(solution)/shard_map/ppermute | solution.py:477
  23.4 5.7 %collective-permute-start.7 = (bf16[128,128]{1,0:T(8,128)(2,1)S(1)}, bf16[128,128]{1,0:T(8,128)(2,1)S(1)}, u32[]{:S(2)}, u32[]{:S(2)}) collective-permute-start(bf16[128,128]{1,0:T(8,128)(2,1)S(1)} %get-tuple-element.48), channel_id=1, source_target_pairs={{0,12},{4,8},{8,4},{12,0},{1,13},{5,9},{9,5},{13,1},{2,14},{6,10},... | collective-permute-start | bytes 98312 | tf_op jit(solution)/shard_map/ppermute | solution.py:477
  24.0 5.1 %copy-start.5 = (bf16[128,128]{1,0:T(8,128)(2,1)S(1)}, bf16[128,128]{1,0:T(8,128)(2,1)}, u32[]{:S(2)}) copy-start(bf16[128,128]{1,0:T(8,128)(2,1)} %prolong_weight_ref.1) | copy-start | bytes 98308
  24.0 5.1 %collective-permute-start.8 = (bf16[128,128]{1,0:T(8,128)(2,1)S(1)}, bf16[128,128]{1,0:T(8,128)(2,1)S(1)}, u32[]{:S(2)}, u32[]{:S(2)}) collective-permute-start(bf16[128,128]{1,0:T(8,128)(2,1)S(1)} %get-tuple-element.49), channel_id=1, source_target_pairs={{0,4},{4,0},{8,12},{12,8},{1,5},{5,1},{9,13},{13,9},{2,6},{6,2},{1... | collective-permute-start | bytes 98312 | tf_op jit(solution)/shard_map/ppermute | solution.py:477
  30.3 7.2 %collective-permute-start.9 = (bf16[128,256]{1,0:T(8,128)(2,1)S(1)}, bf16[128,256]{1,0:T(8,128)(2,1)S(1)}, u32[]{:S(2)}, u32[]{:S(2)}) collective-permute-start(bf16[128,256]{1,0:T(8,128)(2,1)S(1)} %get-tuple-element.54), channel_id=1, source_target_pairs={{0,8},{4,12},{8,0},{12,4},{1,9},{5,13},{9,1},{13,5},{2,10},{6,14},... | collective-permute-start | bytes 196616 | tf_op jit(solution)/shard_map/ppermute | solution.py:477
  31.2 6.2 %collective-permute-start.10 = (bf16[128,256]{1,0:T(8,128)(2,1)S(1)}, bf16[128,256]{1,0:T(8,128)(2,1)S(1)}, u32[]{:S(2)}, u32[]{:S(2)}) collective-permute-start(bf16[128,256]{1,0:T(8,128)(2,1)S(1)} %get-tuple-element.55), channel_id=1, source_target_pairs={{0,12},{4,8},{8,4},{12,0},{1,13},{5,9},{9,5},{13,1},{2,14},{6,10},... | collective-permute-start | bytes 196616 | tf_op jit(solution)/shard_map/ppermute | solution.py:477
  32.4 5.1 %collective-permute-start.11 = (bf16[128,256]{1,0:T(8,128)(2,1)S(1)}, bf16[128,256]{1,0:T(8,128)(2,1)S(1)}, u32[]{:S(2)}, u32[]{:S(2)}) collective-permute-start(bf16[128,256]{1,0:T(8,128)(2,1)S(1)} %get-tuple-element.56), channel_id=1, source_target_pairs={{0,4},{4,0},{8,12},{12,8},{1,5},{5,1},{9,13},{13,9},{2,6},{6,2},{1... | collective-permute-start | bytes 196616 | tf_op jit(solution)/shard_map/ppermute | solution.py:477

commit v5 on v4

--- a/solution.py
+++ b/solution.py
@@ -58,9 +58,12 @@
         self.pieces = slot_count // BLOCK
         self.slots = self.places * pool_capacity
         self.pooled_rows = self.owners * pool_capacity
-        self.list_rows = 2 * coarse_blocks * self.pieces + self.dom_count
+        self.sent_blocks = 1 if self.swapped else coarse_blocks
+        self.list_rows = 2 * self.sent_blocks * self.pieces + self.dom_count
         self.packed_rows = -(-self.list_rows // 16) * 16
-        self.packet = self.pooled_rows + 2 * self.packed_rows
+        self.packet = self.pooled_rows + self.packed_rows
+        self.packets = 2 if self.swapped else 1
+        self.octaves = -(-(self.slots + self.dom_count * coarse_capacity) // BLOCK)
 
     def partner(self, dom, step):
         return dom ^ step if self.mirrored else (dom + step) % self.dom_count
@@ -81,6 +84,9 @@
             place = jnp.where(step == value, index, place)
         return place
 
+    def block_of(self, place):
+        return lax.div(place * self.pool_capacity, BLOCK)
+
     def own_place(self):
         return lax.axis_index("sub") * self.chip_count + lax.axis_index("chip")
 
@@ -92,34 +98,24 @@
     return halved(weight).T
 
 
-def send_kernel(grid, latent_hbm, lists_hbm, weights_hbm, *rest):
-    sent_refs = rest[: len(grid.steps)]
-    latent_ref, lists_ref, weight_ref, arrived = rest[len(grid.steps) :]
-    node_count = latent_ref.shape[0]
-    part = node_count // PARTS
-    copies = [
-        pltpu.make_async_copy(lists_hbm.at[0], lists_ref, arrived.at[0]),
-        pltpu.make_async_copy(weights_hbm.at[0, 0], weight_ref, arrived.at[1]),
-    ]
+def turn_kernel(latent_hbm, table_ref, latent_ref, arrived):
+    part = latent_ref.shape[0] // PARTS
+    copies = []
     for index in range(PARTS):
         rows = pl.ds(index * part, part)
-        copies.append(pltpu.make_async_copy(latent_hbm.at[rows], latent_ref.at[rows], arrived.at[2 + index]))
-    for copy in copies:
-        copy.start()
-    copies[0].wait()
-    copies[1].wait()
-    weight = turned(weight_ref[...])
-    tables = []
-    for index in range(PARTS):
-        copies[2 + index].wait()
-        tables.append(latent_ref[index * part : (index + 1) * part, :].T)
-    table = jnp.concatenate(tables, axis=1)
-    index_row = jnp.concatenate(
-        [lists_ref[pl.ds(grid.partner_here(step), 1), :] for step in grid.steps], axis=1
-    )
-    picked = dot(table, rows_hot(index_row, node_count)).astype(BF16)
-    terms = dot(weight, picked).astype(BF16)
-    capacity = lists_ref.shape[1]
+        copies.append(pltpu.make_async_copy(latent_hbm.at[rows], latent_ref.at[rows], arrived.at[index]))
+        copies[-1].start()
+    for index, copy in enumerate(copies):
+        copy.wait()
+        rows = slice(index * part, (index + 1) * part)
+        table_ref[:, rows] = latent_ref[rows, :].T
+
+
+def send_kernel(grid, table_ref, lists_ref, weights_ref, *sent_refs):
+    index_row = jnp.concatenate([lists_ref[0, pl.ds(grid.partner_here(step), 1), :] for step in grid.steps], axis=1)
+    picked = dot(table_ref[...], rows_hot(index_row, table_ref.shape[1])).astype(BF16)
+    terms = dot(turned(weights_ref[0, 0]), picked).astype(BF16)
+    capacity = lists_ref.shape[2]
     for index, out_ref in enumerate(sent_refs):
         out_ref[...] = terms[:, index * capacity : (index + 1) * capacity]
 
@@ -181,7 +177,7 @@
 
 def near_kernel(
     grid,
-    latent_ref,
+    table_ref,
     source_ref,
     place_ref,
     weights_ref,
@@ -189,17 +185,15 @@
     coarse_place_ref,
     coarse_send_ref,
     pool_ref,
-    table_ref,
     sources_ref,
     places_ref,
     aimed_ref,
     sums_ref,
-    packed_ref,
     pooled_ref,
-    terms_ref,
+    *rest,
 ):
-    table = latent_ref[...].T
-    table_ref[...] = table
+    packed_refs, terms_ref = rest[:-1], rest[-1]
+    table = table_ref[...]
     halo_capacity = grid.halo_capacity
     for batch in range(source_ref.shape[0] // BATCH):
         sources, places = far_rows(source_ref, place_ref, batch)
@@ -211,13 +205,21 @@
         places_ref[batch : batch + 1, :] = places
     near_edges(table, source_ref, place_ref, places_ref, weights_ref, 0, aimed_ref, sums_ref, terms_ref)
 
-    pieces = lane_rows(coarse_source_ref) + [coarse_send_ref[0]] + lane_rows(coarse_place_ref)
-    spare = grid.packed_rows - grid.list_rows
-    if spare:
-        pieces.append(jnp.zeros((spare, BLOCK), I32))
-    whole = jnp.concatenate(pieces, axis=0) + 1
-    high = lax.shift_right_logical(whole, 8)
-    packed_ref[...] = jnp.concatenate([high.astype(F32), (whole & 255).astype(F32)], axis=0).astype(BF16)
+    place = grid.own_place()
+    for index, packed_ref in enumerate(packed_refs):
+        if grid.swapped:
+            block = grid.block_of(place ^ (2 * index))
+            sources, places = coarse_source_ref[pl.ds(block, 1), :], coarse_place_ref[pl.ds(block, 1), :]
+        else:
+            sources, places = coarse_source_ref[...], coarse_place_ref[...]
+        lists = jnp.minimum(coarse_send_ref[0], grid.slots - 1)
+        pieces = lane_rows(sources) + [lists] + lane_rows(places + 1)
+        spare = grid.packed_rows - grid.list_rows
+        if spare:
+            pieces.append(jnp.zeros((spare, BLOCK), I32))
+        whole = jnp.concatenate(pieces, axis=0)
+        coded = lax.shift_left((whole & (BLOCK - 1)) + BLOCK, lax.shift_right_logical(whole, BLOCK.bit_length() - 1))
+        packed_ref[...] = coded.astype(F32).astype(BF16)
     for owner in range(grid.owners):
         pooled_ref[owner : owner + 1, :] = pool_ref[0, 4 * owner : 4 * owner + 1, :]
 
@@ -260,28 +262,32 @@
     update(batch_count - 1)
 
 
-def lane_rows(ref):
+def lane_rows(values):
     pieces = []
-    for block in range(ref.shape[0]):
-        for start in range(0, ref.shape[1], BLOCK):
-            pieces.append(ref[block : block + 1, start : start + BLOCK])
+    for block in range(values.shape[0]):
+        for start in range(0, values.shape[1], BLOCK):
+            pieces.append(values[block : block + 1, start : start + BLOCK])
     return pieces
 
 
 def far_pool_kernel(
-    grid, table_ref, aimed_ref, sources_ref, places_ref, sums_ref, weights_ref, pool_ref, packed_ref, *rest
+    grid, table_ref, aimed_ref, sources_ref, places_ref, sums_ref, weights_ref, pool_ref, *rest
 ):
-    halo_refs, (first_ref, packet_ref, both_ref) = rest[:-3], rest[-3:]
+    count = grid.packets
+    packed_refs, halo_refs = rest[:count], rest[count : count + len(grid.steps)]
+    first_ref, packet_refs, both_ref = rest[-2 - count], rest[-1 - count : -1], rest[-1]
 
     def write(columns, value):
         first_ref[:, columns] = value
 
-    packet_ref[grid.pooled_rows :, :] = packed_ref[...]
+    for packet_ref, packed_ref in zip(packet_refs, packed_refs):
+        packet_ref[grid.pooled_rows :, :] = packed_ref[...]
     far_edges(0, table_ref, aimed_ref, sources_ref, places_ref, sums_ref, weights_ref, halo_refs, both_ref, write)
     for owner in range(grid.owners):
         hot = rows_hot(pool_ref[owner : owner + 1, :], first_ref.shape[1])
         pooled = dot(first_ref[...], hot).astype(BF16).T
-        packet_ref[owner * grid.pool_capacity : (owner + 1) * grid.pool_capacity, :] = pooled
+        for packet_ref in packet_refs:
+            packet_ref[owner * grid.pool_capacity : (owner + 1) * grid.pool_capacity, :] = pooled
 
 
 def far_kernel(table_ref, aimed_ref, sources_ref, places_ref, sums_ref, weights_ref, *rest):
@@ -321,8 +327,11 @@
             rows = jnp.where(place == other, packets[other][grid.pooled_rows :, :].astype(F32), rows)
     else:
         rows = packets[4 * owner][grid.pooled_rows :, :].astype(F32)
-    whole = rows[: grid.packed_rows] * 256.0 + rows[grid.packed_rows :]
-    return whole.astype(I32) - 1
+    coded = rows.astype(I32)
+    octave = jnp.zeros_like(coded)
+    for power in range(1, grid.octaves):
+        octave = octave + jnp.where(coded >= BLOCK << power, 1, 0)
+    return octave * BLOCK + lax.shift_right_logical(coded, octave) - BLOCK
 
 
 def owner_table(grid, packets, owner):
@@ -335,15 +344,18 @@
     outs = refs[grid.places : grid.places + len(grid.steps)]
     lists_ref = refs[-1]
     place = grid.own_place()
-    first_list = grid.blocks * grid.pieces
+    first_list = grid.sent_blocks * grid.pieces
+    capacity = grid.coarse_capacity
     for owner in range(grid.owners):
         lists_ref[...] = owner_lists(grid, packets, owner, place)
         table = owner_table(grid, packets, owner)
         terms = dot(table, halved(weights_ref[0])).astype(BF16).T
-        for step, out_ref in zip(grid.steps, outs):
-            index_row = grid.slot_order(lists_ref[pl.ds(first_list + grid.partner_here(step), 1), :], place)
-            picked = dot(terms, rows_hot(index_row, grid.slots))
-            out_ref[owner * BLOCK : (owner + 1) * BLOCK, :] = picked.astype(BF16)
+        index_row = jnp.concatenate(
+            [lists_ref[pl.ds(first_list + grid.partner_here(step), 1), :] for step in grid.steps], axis=1
+        )
+        picked = dot(terms, rows_hot(grid.slot_order(index_row, place), grid.slots)).astype(BF16)
+        for index, out_ref in enumerate(outs):
+            out_ref[owner * BLOCK : (owner + 1) * BLOCK, :] = picked[:, index * capacity : (index + 1) * capacity]
 
 
 def coarse_own_kernel(grid, weights_ref, *refs):
@@ -351,7 +363,7 @@
     picked_ref, source_out, place_out, rows_out, lists_ref = refs[grid.places :]
     place = grid.own_place()
     first_slot = place * grid.pool_capacity
-    block = lax.shift_right_logical(first_slot, BLOCK.bit_length() - 1)
+    block = 0 if grid.swapped else grid.block_of(place)
     within = first_slot & (BLOCK - 1)
     shift = grid.coarse_capacity.bit_length() - 1
     for owner in range(grid.owners):
@@ -359,11 +371,11 @@
         sources = jnp.concatenate(
             [lists_ref[pl.ds(block * grid.pieces + piece, 1), :] for piece in range(grid.pieces)], axis=1
         )
-        offset = grid.blocks * grid.pieces + grid.dom_count
+        offset = grid.sent_blocks * grid.pieces + grid.dom_count
         places = jnp.concatenate(
             [lists_ref[pl.ds(offset + block * grid.pieces + piece, 1), :] for piece in range(grid.pieces)], axis=1
         )
-        places = places - within
+        places = places - 1 - within
         places = jnp.where((places >= 0) & (places < grid.pool_capacity), places, -1)
         halo_slots = sources - grid.slots
         source_dom = lax.shift_right_arithmetic(halo_slots, shift)
@@ -480,14 +492,15 @@
     return [arrived[index] for index in range(len(arrays))]
 
 
-def trade_packets(grid, packet):
+def trade_packets(grid, packets):
     if grid.swapped:
         pairs = [(0, 1), (1, 0)]
-        over = lax.ppermute(packet, "sub", pairs)
-        across = lax.ppermute(packet, "chip", pairs)
-        both = lax.ppermute(packet, ("sub", "chip"), [(0, 3), (1, 2), (2, 1), (3, 0)])
-        return [packet, across, over, both]
-    gathered = lax.all_gather(packet, ("sub", "chip"), axis=0, tiled=False)
+        near, far = packets
+        over = lax.ppermute(far, "sub", pairs)
+        across = lax.ppermute(near, "chip", pairs)
+        both = lax.ppermute(far, ("sub", "chip"), [(0, 3), (1, 2), (2, 1), (3, 0)])
+        return [near, across, over, both]
+    gathered = lax.all_gather(packets[0], ("sub", "chip"), axis=0, tiled=False)
     return [gathered[place] for place in range(grid.places)]
 
 
@@ -523,44 +536,40 @@
     big = 1 << 30
     in_hbm = pl.BlockSpec(memory_space=pltpu.HBM)
 
-    sent = call(
-        functools.partial(send_kernel, grid),
-        halo_outs,
-        [
-            pltpu.VMEM((node_count, features), BF16),
-            pltpu.VMEM(halo_send.shape[1:], I32),
-            pltpu.VMEM((features, features), BF16),
-            pltpu.SemaphoreType.DMA((2 + PARTS,)),
-        ],
-        flops=big,
-        name="send",
-        limit=63 << 20,
-        in_specs=[in_hbm] * 3,
-    )(fine_nodes, halo_send, fine_weights)
+    (nodes,) = call(
+        turn_kernel,
+        [table],
+        [pltpu.VMEM((node_count, features), BF16), pltpu.SemaphoreType.DMA((PARTS,))],
+        name="turn",
+        limit=5300 * 10486,
+        in_specs=[in_hbm],
+    )(fine_nodes)
+    sent = call(functools.partial(send_kernel, grid), halo_outs, flops=big, name="send")(
+        nodes, halo_send, fine_weights
+    )
     halo = swap_dom(grid, sent)
-    nodes, far_sources, far_places, aimed, sums, packed, pool_lists = call(
+    far_sources, far_places, aimed, sums, pool_lists, *packed = call(
         functools.partial(near_kernel, grid),
         [
-            table,
             far_lists,
             far_lists,
             aimed_table,
             sums_table,
-            ((2 * grid.packed_rows, features), BF16),
             ((grid.owners, grid.pool_capacity), I32),
+            *[((grid.packed_rows, features), BF16)] * grid.packets,
         ],
         [two_tables],
         flops=4 * big,
         name="near",
-    )(fine_nodes, fine_src, fine_dst, fine_weights, coarse_src, coarse_dst, coarse_send, pool_send)
-    first, packet = call(
+    )(nodes, fine_src, fine_dst, fine_weights, coarse_src, coarse_dst, coarse_send, pool_send)
+    first, *packets = call(
         functools.partial(far_pool_kernel, grid),
-        [table, ((grid.packet, features), BF16)],
+        [table, *[((grid.packet, features), BF16)] * grid.packets],
         [two_tables],
         flops=2 * big,
         name="far_pool",
-    )(nodes, aimed, far_sources, far_places, sums, fine_weights, pool_lists, packed, *halo)
-    packets = trade_packets(grid, packet)
+    )(nodes, aimed, far_sources, far_places, sums, fine_weights, pool_lists, *packed, *halo)
+    packets = trade_packets(grid, packets)
     (ahead,) = call(
         functools.partial(ahead_kernel, grid), [((features + 16, steps * halo_capacity), BF16)], flops=big, name="ahead"
     )(first, prolong_rows, halo_send)

time: 40.1 us -> 38.9 us (0.970)
  Pallas kernels: 16.7 us -> 16 us
  waiting for transfers between devices: 7.66 us -> 7.13 us
    pallas_call x3 -> x4, Pallas kernels: 8.02 us -> 7.37 us  [the longest x1 3.43 us: body(): call(functools.partial(near_kernel, grid), [far_lists, far_lists, aimed_t...]
  transfers between devices with their start and end apart: 12 -> 12, of which waited for: 7 -> 6; matrix products, arithmetic and copies ran while one was open for 0% -> 0% of each run, Pallas kernels for 21% -> 21%
where the time goes in v5:
time: 38.9 us; the launch traced here: 38.7 us
  Pallas kernels  16 us (41%)
  starting transfers between devices  15.4 us (40%)
  waiting for transfers between devices  7.13 us (18%)
    ppermute x9, starting transfers between devices, swap_dom(): lax.ppermute(arrays[index], 'dom', [(dom, grid.partner(dom, step)) for do...  13.5 us
    ppermute x9, waiting for transfers between devices, swap_dom(): lax.ppermute(arrays[index], 'dom', [(dom, grid.partner(dom, step)) for do...  5.79 us
    pallas_call x1, Pallas kernels, body(): call(functools.partial(lift_near_kernel, grid), [table, aimed_table, sums...  3.61 us
    pallas_call x1, Pallas kernels, body(): call(functools.partial(near_kernel, grid), [far_lists, far_lists, aimed_t...  3.43 us
    pallas_call x1, Pallas kernels, body(): call(far_kernel, [((node_count, features), BF16)], [two_tables, pltpu.VME...  2.38 us
    pallas_call x1, Pallas kernels, body(): call(functools.partial(far_pool_kernel, grid), [table, *[((grid.packet, f...  1.8 us
    ppermute x1, starting transfers between devices, trade_packets(): over = lax.ppermute(far, 'sub', pairs)  1.55 us
    pallas_call x1, Pallas kernels, body(): call(turn_kernel, [table], [pltpu.VMEM((node_count, features), BF16), plt...  1.34 us
  transfers between devices with their start and end apart: 12, of which 6 were waited for; matrix products, arithmetic and copies ran while one was open for 0% of the time, Pallas kernels for 21%

profile of v5, /device:TPU:0, one launch (start us, length us, event | category | flops | bytes accessed | tf_op | source)
XLA Modules:
  0.0 38.7 jit_solution(17079106169392079618)
XLA Ops:
  0.0 1.3 %turn.1.table_ref = bf16[128,2048]{1,0:T(8,128)(2,1)S(1)} custom-call(bf16[2048,128]{1,0:T(8,128)(2,1)} %latent_hbm.1), custom_call_target="tpu_custom_call" | custom-call | bytes 4194304 | tf_op jit(solution)/shard_map/turn/pallas_call | solution.py:539
  1.4 0.0 copy-start.2
  1.4 0.0 copy-start.3
  1.4 0.0 copy-start.6
  1.4 0.0 copy-start.7
  1.4 0.8 %send.1 = (bf16[128,256]{1,0:T(8,128)(2,1)S(1)}, bf16[128,256]{1,0:T(8,128)(2,1)S(1)}, bf16[128,256]{1,0:T(8,128)(2,1)S(1)}) custom-call(bf16[128,2048]{1,0:T(8,128)(2,1)S(1)} %turn.1.table_ref, s32[1,4,256]{2,1,0:T(4,128)S(1)} %copy-done.8, bf16[2,4,128,128]{3,2,1,0:T(8,128)(2,1)S(1)} %copy-done), custom_call_target="tpu_custom_call" | custom-call | flops 1073741824 | bytes 4194304 | tf_op jit(solution)/shard_map/send/pallas_call | solution.py:547
  2.2 0.0 copy-start.10
  2.3 4.1 %collective-permute-start = (bf16[128,256]{1,0:T(8,128)(2,1)S(1)}, bf16[128,256]{1,0:T(8,128)(2,1)S(1)}, u32[]{:S(2)}, u32[]{:S(2)}) collective-permute-start(bf16[128,256]{1,0:T(8,128)(2,1)S(1)} %get-tuple-element.39), channel_id=1, source_target_pairs={{0,8},{4,12},{8,0},{12,4},{1,9},{5,13},{9,1},{13,5},{2,10},{6,14},... | collective-permute-start | bytes 196616 | tf_op jit(solution)/shard_map/ppermute | solution.py:489
  6.4 1.4 %collective-permute-start.1 = (bf16[128,256]{1,0:T(8,128)(2,1)S(1)}, bf16[128,256]{1,0:T(8,128)(2,1)S(1)}, u32[]{:S(2)}, u32[]{:S(2)}) collective-permute-start(bf16[128,256]{1,0:T(8,128)(2,1)S(1)} %get-tuple-element.40), channel_id=1, source_target_pairs={{0,12},{4,8},{8,4},{12,0},{1,13},{5,9},{9,5},{13,1},{2,14},{6,10},... | collective-permute-start | bytes 196616 | tf_op jit(solution)/shard_map/ppermute | solution.py:489
  7.7 0.2 collective-permute-start.2
  8.0 3.4 %near.1 = (s32[4,768]{1,0:T(4,128)S(1)}, s32[4,768]{1,0:T(4,128)S(1)}, bf16[128,3072]{1,0:T(8,128)(2,1)S(1)}, f32[128,2048]{1,0:T(8,128)S(1)}, s32[1,64]{1,0:T(1...) custom-call(bf16[128,2048]{1,0:T(8,128)(2,1)S(1)} %turn.1.table_ref, s32[16,768]{1,0:T(8,128)S(1)} %copy-done.2, ...), custom_call_target="tpu_custom_call" | custom-call | flops 4294967296 | bytes 4194304 | tf_op jit(solution)/shard_map/near/pallas_call | solution.py:551
  11.4 1.2 %collective-permute-done.1.rest_3_ = bf16[128,256]{1,0:T(8,128)(2,1)S(1)} collective-permute-done((bf16[128,256]{1,0:T(8,128)(2,1)S(1)}, bf16[128,256]{1,0:T(8,128)(2,1)S(1)}, u32[]{:S(2)}, u32[]{:S(2)}) %collective-permute-start.1) | collective-permute-done | bytes 65568 | tf_op jit(solution)/shard_map/ppermute | solution.py:489
  12.6 0.1 collective-permute-done.2.rest_4_
  12.7 1.8 %far_pool.1 = (bf16[128,2048]{1,0:T(8,128)(2,1)S(1)}, bf16[80,128]{1,0:T(8,128)(2,1)S(1)}, bf16[80,128]{1,0:T(8,128)(2,1)S(1)}) custom-call(bf16[128,2048]{1,0:T(8,128)(2,1)S(1)} %turn.1.table_ref, bf16[128,3072]{1,0:T(8,128)(2,1)S(1)} %get-tuple-element.32.aimed_ref, s32[4,768]{1,0:T(4,128)S(1)} %get-tuple-element.33.sources_ref, ...), custom_call_target="tpu_custom_call" | custom-call | flops 2147483648 | bytes 4194304 | tf_op jit(solution)/shard_map/far_pool/pallas_call | solution.py:565
  14.5 0.0 collective-permute-start.5
  14.5 1.6 %collective-permute-start.4 = (bf16[80,128]{1,0:T(8,128)(2,1)S(1)}, bf16[80,128]{1,0:T(8,128)(2,1)S(1)}, u32[]{:S(2)}, u32[]{:S(2)}) collective-permute-start(bf16[80,128]{1,0:T(8,128)(2,1)S(1)} %get-tuple-element.44), channel_id=1, source_target_pairs={{0,2},{2,0},{1,3},{3,1},{4,6},{6,4},{5,7},{7,5},{8,10},{10,8},{9,1... | collective-permute-start | bytes 61448 | tf_op jit(solution)/shard_map/ppermute | solution.py:499
  16.1 0.3 collective-permute-start.3
  16.4 0.6 %ahead.1.ahead_ref = bf16[144,768]{1,0:T(8,128)(2,1)S(1)} custom-call(bf16[128,2048]{1,0:T(8,128)(2,1)S(1)} %get-tuple-element.42.first_ref, s32[16,128]{1,0:T(8,128)S(1)} %bitcast.1, s32[1,4,256]{2,1,0:T(4,128)S(1)} %copy-done.8), custom_call_target="tpu_custom_call" | custom-call | flops 1073741824 | bytes 4194304 | tf_op jit(solution)/shard_map/ahead/pallas_call | solution.py:573
  17.0 0.9 %collective-permute-done.5.refs_3_ = bf16[80,128]{1,0:T(8,128)(2,1)S(1)} collective-permute-done((bf16[80,128]{1,0:T(8,128)(2,1)S(1)}, bf16[80,128]{1,0:T(8,128)(2,1)S(1)}, u32[]{:S(2)}, u32[]{:S(2)}) %collective-permute-start.5) | collective-permute-done | bytes 20512 | tf_op jit(solution)/shard_map/ppermute | solution.py:501
  17.9 0.5 %collective-permute-done.4.refs_2_ = bf16[80,128]{1,0:T(8,128)(2,1)S(1)} collective-permute-done((bf16[80,128]{1,0:T(8,128)(2,1)S(1)}, bf16[80,128]{1,0:T(8,128)(2,1)S(1)}, u32[]{:S(2)}, u32[]{:S(2)}) %collective-permute-start.4) | collective-permute-done | bytes 20512 | tf_op jit(solution)/shard_map/ppermute | solution.py:499
  18.4 0.4 coarse_send.1
  18.8 3.5 %collective-permute-start.6 = (bf16[128,128]{1,0:T(8,128)(2,1)S(1)}, bf16[128,128]{1,0:T(8,128)(2,1)S(1)}, u32[]{:S(2)}, u32[]{:S(2)}) collective-permute-start(bf16[128,128]{1,0:T(8,128)(2,1)S(1)} %get-tuple-element.49), channel_id=1, source_target_pairs={{0,8},{4,12},{8,0},{12,4},{1,9},{5,13},{9,1},{13,5},{2,10},{6,14},... | collective-permute-start | bytes 98312 | tf_op jit(solution)/shard_map/ppermute | solution.py:489
  22.3 0.7 %collective-permute-start.7 = (bf16[128,128]{1,0:T(8,128)(2,1)S(1)}, bf16[128,128]{1,0:T(8,128)(2,1)S(1)}, u32[]{:S(2)}, u32[]{:S(2)}) collective-permute-start(bf16[128,128]{1,0:T(8,128)(2,1)S(1)} %get-tuple-element.50), channel_id=1, source_target_pairs={{0,12},{4,8},{8,4},{12,0},{1,13},{5,9},{9,5},{13,1},{2,14},{6,10},... | collective-permute-start | bytes 98312 | tf_op jit(solution)/shard_map/ppermute | solution.py:489
  23.0 0.5 %coarse_own.1 = (f32[1,128,768]{2,1,0:T(8,128)S(1)}, s32[1,768]{1,0:T(1,128)S(1)}, s32[1,768]{1,0:T(1,128)S(1)}, bf16[1,128,64]{2,1,0:T(8,128)(2,1)S(1)}) custom-call(bf16[4,128,128]{2,1,0:T(8,128)(2,1)S(1)} %copy-done.1, bf16[80,128]{1,0:T(8,128)(2,1)S(1)} %get-tuple-element.43.refs_0_, bf16[80,128]{1,0:T(8,128)(2,1)S(1)} %collective-permute-done.3.refs_1_, ...), custom_call_target="tpu_custom_call" | custom-call | flops 4294967296 | bytes 4194304 | tf_op jit(solution)/shard_map/coarse_own/pallas_call | solution.py:585
  23.5 0.7 %collective-permute-done.6.rest_0_ = bf16[128,128]{1,0:T(8,128)(2,1)S(1)} collective-permute-done((bf16[128,128]{1,0:T(8,128)(2,1)S(1)}, bf16[128,128]{1,0:T(8,128)(2,1)S(1)}, u32[]{:S(2)}, u32[]{:S(2)}) %collective-permute-start.6) | collective-permute-done | bytes 32800 | tf_op jit(solution)/shard_map/ppermute | solution.py:489
  24.2 3.8 %collective-permute-done.7.rest_1_ = bf16[128,128]{1,0:T(8,128)(2,1)S(1)} collective-permute-done((bf16[128,128]{1,0:T(8,128)(2,1)S(1)}, bf16[128,128]{1,0:T(8,128)(2,1)S(1)}, u32[]{:S(2)}, u32[]{:S(2)}) %collective-permute-start.7) | collective-permute-done | bytes 32800 | tf_op jit(solution)/shard_map/ppermute | solution.py:489
  28.0 1.1 %lift_halo.1 = (bf16[128,128]{1,0:T(8,128)(2,1)S(1)}, bf16[128,256]{1,0:T(8,128)(2,1)S(1)}, bf16[128,256]{1,0:T(8,128)(2,1)S(1)}, bf16[128,256]{1,0:T(8,128)(2,1)S(1)}) custom-call(f32[1,128,768]{2,1,0:T(8,128)S(1)} %get-tuple-element.45.picked_ref, s32[1,768]{1,0:T(1,128)S(1)} %get-tuple-element.46.source_ref, s32[1,768]{1,0:T(1,128)S(1)} %get-tuple-element.47.place_ref, ...), custom_call_target="tpu_custom_call" | custom-call | flops 1073741824 | bytes 4194304 | tf_op jit(solution)/shard_map/lift_halo/pallas_call | solution.py:597
  29.2 1.0 %collective-permute-start.9 = (bf16[128,256]{1,0:T(8,128)(2,1)S(1)}, bf16[128,256]{1,0:T(8,128)(2,1)S(1)}, u32[]{:S(2)}, u32[]{:S(2)}) collective-permute-start(bf16[128,256]{1,0:T(8,128)(2,1)S(1)} %get-tuple-element.56), channel_id=1, source_target_pairs={{0,8},{4,12},{8,0},{12,4},{1,9},{5,13},{9,1},{13,5},{2,10},{6,14},... | collective-permute-start | bytes 196616 | tf_op jit(solution)/shard_map/ppermute | solution.py:489
  30.1 1.2 %collective-permute-start.10 = (bf16[128,256]{1,0:T(8,128)(2,1)S(1)}, bf16[128,256]{1,0:T(8,128)(2,1)S(1)}, u32[]{:S(2)}, u32[]{:S(2)}) collective-permute-start(bf16[128,256]{1,0:T(8,128)(2,1)S(1)} %get-tuple-element.57), channel_id=1, source_target_pairs={{0,12},{4,8},{8,4},{12,0},{1,13},{5,9},{9,5},{13,1},{2,14},{6,10},... | collective-permute-start | bytes 196616 | tf_op jit(solution)/shard_map/ppermute | solution.py:489
  31.3 1.4 %collective-permute-start.11 = (bf16[128,256]{1,0:T(8,128)(2,1)S(1)}, bf16[128,256]{1,0:T(8,128)(2,1)S(1)}, u32[]{:S(2)}, u32[]{:S(2)}) collective-permute-start(bf16[128,256]{1,0:T(8,128)(2,1)S(1)} %get-tuple-element.58), channel_id=1, source_target_pairs={{0,4},{4,0},{8,12},{12,8},{1,5},{5,1},{9,13},{13,9},{2,6},{6,2},{1... | collective-permute-start | bytes 196616 | tf_op jit(solution)/shard_map/ppermute | solution.py:489
  32.7 3.6 %lift_near.1 = (bf16[128,2048]{1,0:T(8,128)(2,1)S(1)}, bf16[128,3072]{1,0:T(8,128)(2,1)S(1)}, f32[128,2048]{1,0:T(8,128)S(1)}) custom-call(bf16[128,2048]{1,0:T(8,128)(2,1)S(1)} %get-tuple-element.42.first_ref, bf16[128,128]{1,0:T(8,128)(2,1)S(1)} %get-tuple-element.52.prolonged_ref, s32[16,128]{1,0:T(8,128)S(1)} %bitcast.2, s32[16,768]{1,0:T(8,128)S(1)} %copy-done.2, ...), custom_call_target="tpu_custom_call" | custom-call | flops 4294967296 | bytes 4194304 | tf_op jit(solution)/shard_map/lift_near/pallas_call | solution.py:604
  36.4 2.4 %far.1 = bf16[2048,128]{1,0:T(8,128)(2,1)} custom-call(bf16[128,2048]{1,0:T(8,128)(2,1)S(1)} %get-tuple-element.53.table_ref, bf16[128,3072]{1,0:T(8,128)(2,1)S(1)} %get-tuple-element.54.aimed_ref, s32[4,768]{1,0:T(4,128)S(1)} %get-tuple-element.33.sources_ref, s32[4,768]{1,0:T(4,128)S(1)} %get-tuple-element.34.places_ref, ...), custom_call_target="tpu_custom_call" | custom-call | flops 2147483648 | bytes 4194304 | tf_op jit(solution)/shard_map/far/pallas_call | solution.py:611
  (24 shorter events, 0.1 us)
Async XLA Ops:
  0.0 1.4 %copy-start = (bf16[2,4,128,128]{3,2,1,0:T(8,128)(2,1)S(1)}, bf16[2,4,128,128]{3,2,1,0:T(8,128)(2,1)}, u32[]{:S(2)}) copy-start(bf16[2,4,128,128]{3,2,1,0:T(8,128)(2,1)} %weights_ref.15) | copy-start | bytes 786436
  0.0 1.4 %copy-start.8 = (s32[1,4,256]{2,1,0:T(4,128)S(1)}, s32[1,4,256]{2,1,0:T(4,128)}, u32[]{:S(2)}) copy-start(s32[1,4,256]{2,1,0:T(4,128)} %lists_ref.3) | copy-start | bytes 12292
  1.4 6.6 %copy-start.2 = (s32[16,768]{1,0:T(8,128)S(1)}, s32[16,768]{1,0:T(8,128)}, u32[]{:S(2)}) copy-start(s32[16,768]{1,0:T(8,128)} %source_ref.3) | copy-start | bytes 147460
  1.4 6.6 %copy-start.3 = (s32[16,768]{1,0:T(8,128)S(1)}, s32[16,768]{1,0:T(8,128)}, u32[]{:S(2)}) copy-start(s32[16,768]{1,0:T(8,128)} %place_ref.3) | copy-start | bytes 147460
  1.4 6.6 %copy-start.6 = (s32[2,768]{1,0:T(2,128)S(1)}, s32[2,768]{1,0:T(2,128)}, u32[]{:S(2)}) copy-start(s32[2,768]{1,0:T(2,128)} %coarse_source_ref.1) | copy-start | bytes 18436
  1.4 6.5 %copy-start.7 = (s32[2,768]{1,0:T(2,128)S(1)}, s32[2,768]{1,0:T(2,128)}, u32[]{:S(2)}) copy-start(s32[2,768]{1,0:T(2,128)} %coarse_place_ref.1) | copy-start | bytes 18436
  2.2 5.7 %copy-start.10 = (s32[1,4,64]{2,1,0:T(4,128)S(1)}, s32[1,4,64]{2,1,0:T(4,128)}, u32[]{:S(2)}) copy-start(s32[1,4,64]{2,1,0:T(4,128)} %pool_ref.1) | copy-start | bytes 3076
  2.2 5.7 %copy-start.9 = (s32[1,4,128]{2,1,0:T(4,128)S(1)}, s32[1,4,128]{2,1,0:T(4,128)}, u32[]{:S(2)}) copy-start(s32[1,4,128]{2,1,0:T(4,128)} %coarse_send_ref.1) | copy-start | bytes 6148
  2.3 9.2 %collective-permute-start = (bf16[128,256]{1,0:T(8,128)(2,1)S(1)}, bf16[128,256]{1,0:T(8,128)(2,1)S(1)}, u32[]{:S(2)}, u32[]{:S(2)}) collective-permute-start(bf16[128,256]{1,0:T(8,128)(2,1)S(1)} %get-tuple-element.39), channel_id=1, source_target_pairs={{0,8},{4,12},{8,0},{12,4},{1,9},{5,13},{9,1},{13,5},{2,10},{6,14},... | collective-permute-start | bytes 196616 | tf_op jit(solution)/shard_map/ppermute | solution.py:489
  6.4 6.2 %collective-permute-start.1 = (bf16[128,256]{1,0:T(8,128)(2,1)S(1)}, bf16[128,256]{1,0:T(8,128)(2,1)S(1)}, u32[]{:S(2)}, u32[]{:S(2)}) collective-permute-start(bf16[128,256]{1,0:T(8,128)(2,1)S(1)} %get-tuple-element.40), channel_id=1, source_target_pairs={{0,12},{4,8},{8,4},{12,0},{1,13},{5,9},{9,5},{13,1},{2,14},{6,10},... | collective-permute-start | bytes 196616 | tf_op jit(solution)/shard_map/ppermute | solution.py:489
  7.7 5.0 %collective-permute-start.2 = (bf16[128,256]{1,0:T(8,128)(2,1)S(1)}, bf16[128,256]{1,0:T(8,128)(2,1)S(1)}, u32[]{:S(2)}, u32[]{:S(2)}) collective-permute-start(bf16[128,256]{1,0:T(8,128)(2,1)S(1)} %get-tuple-element.41), channel_id=1, source_target_pairs={{0,4},{4,0},{8,12},{12,8},{1,5},{5,1},{9,13},{13,9},{2,6},{6,2},{1... | collective-permute-start | bytes 196616 | tf_op jit(solution)/shard_map/ppermute | solution.py:489
  12.7 3.7 %copy-start.5 = (s32[2048]{0:T(1024)S(1)}, s32[2048]{0:T(1024)}, u32[]{:S(2)}) copy-start(s32[2048]{0:T(1024)} %param.20) | copy-start | bytes 24580
  14.5 3.4 %collective-permute-start.5 = (bf16[80,128]{1,0:T(8,128)(2,1)S(1)}, bf16[80,128]{1,0:T(8,128)(2,1)S(1)}, u32[]{:S(2)}, u32[]{:S(2)}) collective-permute-start(bf16[80,128]{1,0:T(8,128)(2,1)S(1)} %get-tuple-element.44), channel_id=1, source_target_pairs={{0,3},{1,2},{2,1},{3,0},{4,7},{5,6},{6,5},{7,4},{8,11},{9,10},{10,... | collective-permute-start | bytes 61448 | tf_op jit(solution)/shard_map/ppermute | solution.py:501
  14.5 3.8 %collective-permute-start.4 = (bf16[80,128]{1,0:T(8,128)(2,1)S(1)}, bf16[80,128]{1,0:T(8,128)(2,1)S(1)}, u32[]{:S(2)}, u32[]{:S(2)}) collective-permute-start(bf16[80,128]{1,0:T(8,128)(2,1)S(1)} %get-tuple-element.44), channel_id=1, source_target_pairs={{0,2},{2,0},{1,3},{3,1},{4,6},{6,4},{5,7},{7,5},{8,10},{10,8},{9,1... | collective-permute-start | bytes 61448 | tf_op jit(solution)/shard_map/ppermute | solution.py:499
  16.1 2.3 %collective-permute-start.3 = (bf16[80,128]{1,0:T(8,128)(2,1)S(1)}, bf16[80,128]{1,0:T(8,128)(2,1)S(1)}, u32[]{:S(2)}, u32[]{:S(2)}) collective-permute-start(bf16[80,128]{1,0:T(8,128)(2,1)S(1)} %get-tuple-element.43.refs_0_), channel_id=1, source_target_pairs={{0,1},{1,0},{2,3},{3,2},{4,5},{5,4},{6,7},{7,6},{8,9},{9,8},{10,11... | collective-permute-start | bytes 61448 | tf_op jit(solution)/shard_map/ppermute | solution.py:500
  16.4 2.0 %copy-start.1 = (bf16[4,128,128]{2,1,0:T(8,128)(2,1)S(1)}, bf16[4,128,128]{2,1,0:T(8,128)(2,1)}, u32[]{:S(2)}) copy-start(bf16[4,128,128]{2,1,0:T(8,128)(2,1)} %coarse_weights_ref.1) | copy-start | bytes 393220
  18.8 5.4 %collective-permute-start.6 = (bf16[128,128]{1,0:T(8,128)(2,1)S(1)}, bf16[128,128]{1,0:T(8,128)(2,1)S(1)}, u32[]{:S(2)}, u32[]{:S(2)}) collective-permute-start(bf16[128,128]{1,0:T(8,128)(2,1)S(1)} %get-tuple-element.49), channel_id=1, source_target_pairs={{0,8},{4,12},{8,0},{12,4},{1,9},{5,13},{9,1},{13,5},{2,10},{6,14},... | collective-permute-start | bytes 98312 | tf_op jit(solution)/shard_map/ppermute | solution.py:489
  22.3 5.7 %collective-permute-start.7 = (bf16[128,128]{1,0:T(8,128)(2,1)S(1)}, bf16[128,128]{1,0:T(8,128)(2,1)S(1)}, u32[]{:S(2)}, u32[]{:S(2)}) collective-permute-start(bf16[128,128]{1,0:T(8,128)(2,1)S(1)} %get-tuple-element.50), channel_id=1, source_target_pairs={{0,12},{4,8},{8,4},{12,0},{1,13},{5,9},{9,5},{13,1},{2,14},{6,10},... | collective-permute-start | bytes 98312 | tf_op jit(solution)/shard_map/ppermute | solution.py:489
  23.0 5.0 %copy-start.4 = (bf16[128,128]{1,0:T(8,128)(2,1)S(1)}, bf16[128,128]{1,0:T(8,128)(2,1)}, u32[]{:S(2)}) copy-start(bf16[128,128]{1,0:T(8,128)(2,1)} %prolong_weight_ref.1) | copy-start | bytes 98308
  23.0 5.0 %collective-permute-start.8 = (bf16[128,128]{1,0:T(8,128)(2,1)S(1)}, bf16[128,128]{1,0:T(8,128)(2,1)S(1)}, u32[]{:S(2)}, u32[]{:S(2)}) collective-permute-start(bf16[128,128]{1,0:T(8,128)(2,1)S(1)} %get-tuple-element.51), channel_id=1, source_target_pairs={{0,4},{4,0},{8,12},{12,8},{1,5},{5,1},{9,13},{13,9},{2,6},{6,2},{1... | collective-permute-start | bytes 98312 | tf_op jit(solution)/shard_map/ppermute | solution.py:489
  29.2 7.2 %collective-permute-start.9 = (bf16[128,256]{1,0:T(8,128)(2,1)S(1)}, bf16[128,256]{1,0:T(8,128)(2,1)S(1)}, u32[]{:S(2)}, u32[]{:S(2)}) collective-permute-start(bf16[128,256]{1,0:T(8,128)(2,1)S(1)} %get-tuple-element.56), channel_id=1, source_target_pairs={{0,8},{4,12},{8,0},{12,4},{1,9},{5,13},{9,1},{13,5},{2,10},{6,14},... | collective-permute-start | bytes 196616 | tf_op jit(solution)/shard_map/ppermute | solution.py:489
  30.1 6.2 %collective-permute-start.10 = (bf16[128,256]{1,0:T(8,128)(2,1)S(1)}, bf16[128,256]{1,0:T(8,128)(2,1)S(1)}, u32[]{:S(2)}, u32[]{:S(2)}) collective-permute-start(bf16[128,256]{1,0:T(8,128)(2,1)S(1)} %get-tuple-element.57), channel_id=1, source_target_pairs={{0,12},{4,8},{8,4},{12,0},{1,13},{5,9},{9,5},{13,1},{2,14},{6,10},... | collective-permute-start | bytes 196616 | tf_op jit(solution)/shard_map/ppermute | solution.py:489
  31.3 5.0 %collective-permute-start.11 = (bf16[128,256]{1,0:T(8,128)(2,1)S(1)}, bf16[128,256]{1,0:T(8,128)(2,1)S(1)}, u32[]{:S(2)}, u32[]{:S(2)}) collective-permute-start(bf16[128,256]{1,0:T(8,128)(2,1)S(1)} %get-tuple-element.58), channel_id=1, source_target_pairs={{0,4},{4,0},{8,12},{12,8},{1,5},{5,1},{9,13},{13,9},{2,6},{6,2},{1... | collective-permute-start | bytes 196616 | tf_op jit(solution)/shard_map/ppermute | solution.py:489

commit v6 on v5

--- a/solution.py
+++ b/solution.py
@@ -13,8 +13,8 @@
 BLOCK = 128
 VMEM_BYTES = 32 << 20
 BATCH = 4
-PARTS = 4
-PAIR = 2
+PARTS = 2
+PAIR = 1
 
 
 def dot(left, right):
@@ -131,20 +131,13 @@
     return jnp.concatenate(sources, axis=1), jnp.concatenate(places, axis=1)
 
 
-def near_edges(table, source_ref, place_ref, places_ref, weights_ref, layer, aimed_ref, sums_ref, terms_ref):
+def near_edges(table, source_ref, place_ref, weights_ref, layer, aimed_ref, sums_ref, terms_ref):
     features, node_count = table.shape
     block_count, slot_count = source_ref.shape
     local_count = slot_count * 3 // 4
     window = min(3 * BLOCK, node_count)
     both = jnp.concatenate([turned(weights_ref[layer, 0]), turned(weights_ref[layer, 1])], axis=0)
     terms_ref[...] = dot(both, table).astype(BF16)
-
-    def far_targets(batch):
-        columns = slice(batch * BATCH * BLOCK, (batch + 1) * BATCH * BLOCK)
-        hot = rows_hot(places_ref[batch : batch + 1, :], BATCH * BLOCK)
-        aimed_ref[:, batch * hot.shape[1] : (batch + 1) * hot.shape[1]] = dot(
-            terms_ref[features:, columns], hot
-        ).astype(BF16)
 
     def messages(block):
         start = min(max(block * BLOCK - BLOCK, 0), node_count - window)
@@ -155,10 +148,12 @@
             ],
             axis=1,
         )
-        places = rows_hot(place_ref[block : block + 1, :local_count], BLOCK)
-        sources = rows_hot(source_ref[block : block + 1, :local_count] - start, window)
+        places = rows_hot(place_ref[block : block + 1, :], BLOCK)
+        sources = rows_hot(source_ref[block : block + 1, :] - start, window)
         picked = dot(terms, jnp.concatenate([sources, places], axis=0))
-        return silu_of_half(picked).astype(BF16)
+        far_count = slot_count - local_count
+        aimed_ref[:, block * far_count : (block + 1) * far_count] = picked[:, local_count:].astype(BF16)
+        return silu_of_half(picked[:, :local_count]).astype(BF16)
 
     def add_up(block, message):
         places = rows_hot(place_ref[block : block + 1, :local_count], BLOCK)
@@ -170,8 +165,6 @@
         if waiting is not None:
             add_up(*waiting)
         waiting = (block, message)
-        if block % BATCH == 0:
-            far_targets(block // BATCH)
     add_up(*waiting)
 
 
@@ -203,7 +196,7 @@
             slots & (halo_capacity - 1)
         )
         places_ref[batch : batch + 1, :] = places
-    near_edges(table, source_ref, place_ref, places_ref, weights_ref, 0, aimed_ref, sums_ref, terms_ref)
+    near_edges(table, source_ref, place_ref, weights_ref, 0, aimed_ref, sums_ref, terms_ref)
 
     place = grid.own_place()
     for index, packed_ref in enumerate(packed_refs):
@@ -402,7 +395,7 @@
     pooled_rows = prolonged.shape[1] // 2
     hot = rows_hot(index_row, pooled_rows)
     hot = jnp.concatenate([hot, hot], axis=0)
-    return (table.astype(F32) + silu_of_half(dot(prolonged, hot))).astype(BF16)
+    return (table.astype(F32) + dot(prolonged, hot)).astype(BF16)
 
 
 def lift_halo_kernel(
@@ -432,7 +425,7 @@
         rows = rows_ref[owner]
         update = dot(update_weights, jnp.concatenate([summed, rows], axis=0))
         coarse = (rows.astype(F32) + silu_of_half(update)).astype(BF16)
-        prolonged.append(dot(prolong_weight, coarse))
+        prolonged.append(silu_of_half(dot(prolong_weight, coarse)))
     prolonged = jnp.concatenate(prolonged, axis=1)
     high = prolonged.astype(BF16)
     low = (prolonged - high.astype(F32)).astype(BF16)
@@ -454,7 +447,6 @@
     prolong_ref,
     source_ref,
     place_ref,
-    places_ref,
     weights_ref,
     lifted_ref,
     aimed_ref,
@@ -467,7 +459,7 @@
     row = jnp.concatenate([indices[block : block + 1, :] for block in range(indices.shape[0])], axis=1)
     lifted = lift(first_ref[...], prolonged_ref[...], row)
     lifted_ref[...] = lifted
-    near_edges(lifted, source_ref, place_ref, places_ref, weights_ref, 1, aimed_ref, sums_ref, terms_ref)
+    near_edges(lifted, source_ref, place_ref, weights_ref, 1, aimed_ref, sums_ref, terms_ref)
 
 
 def call(kernel, outs, scratch=(), flops=0, name=None, limit=VMEM_BYTES, **specs):
@@ -607,7 +599,7 @@
         [two_tables],
         flops=4 * big,
         name="lift_near",
-    )(first, prolonged, prolong_rows, fine_src, fine_dst, far_places, fine_weights)
+    )(first, prolonged, prolong_rows, fine_src, fine_dst, fine_weights)
     (fine_out,) = call(
         far_kernel,
         [((node_count, features), BF16)],

time: 38.9 us -> 38.6 us (level)
  Pallas kernels: 16 us -> 15 us
  waiting for transfers between devices: 7.13 us -> 7.84 us
    ppermute x9, waiting for transfers between devices: 5.79 us -> 6.5 us  [swap_dom(): lax.ppermute(arrays[index], 'dom', [(dom, grid.partner(dom, step)) for do...]
    pallas_call x1, Pallas kernels: 3.61 us -> 3.2 us  [body(): call(functools.partial(lift_near_kernel, grid), [table, aimed_table, sums...]
  transfers between devices with their start and end apart: 12 -> 12, of which waited for: 6 -> 7; matrix products, arithmetic and copies ran while one was open for 0% -> 0% of each run, Pallas kernels for 21% -> 19%
where the time goes in v6:
time: 38.6 us; the launch traced here: 38.4 us
  starting transfers between devices  15.4 us (40%)
  Pallas kernels  15 us (39%)
  waiting for transfers between devices  7.84 us (20%)
    ppermute x9, starting transfers between devices, swap_dom(): lax.ppermute(arrays[index], 'dom', [(dom, grid.partner(dom, step)) for do...  13.5 us
    ppermute x9, waiting for transfers between devices, swap_dom(): lax.ppermute(arrays[index], 'dom', [(dom, grid.partner(dom, step)) for do...  6.5 us
    pallas_call x1, Pallas kernels, body(): call(functools.partial(lift_near_kernel, grid), [table, aimed_table, sums...  3.2 us
    pallas_call x1, Pallas kernels, body(): call(functools.partial(near_kernel, grid), [far_lists, far_lists, aimed_t...  3.08 us
    pallas_call x1, Pallas kernels, body(): call(far_kernel, [((node_count, features), BF16)], [two_tables, pltpu.VME...  2.32 us
    pallas_call x1, Pallas kernels, body(): call(functools.partial(far_pool_kernel, grid), [table, *[((grid.packet, f...  1.68 us
    ppermute x1, starting transfers between devices, trade_packets(): over = lax.ppermute(far, 'sub', pairs)  1.57 us
    pallas_call x1, Pallas kernels, body(): call(turn_kernel, [table], [pltpu.VMEM((node_count, features), BF16), plt...  1.25 us
  transfers between devices with their start and end apart: 12, of which 7 were waited for; matrix products, arithmetic and copies ran while one was open for 0% of the time, Pallas kernels for 19%

profile of v6, /device:TPU:0, one launch (start us, length us, event | category | flops | bytes accessed | tf_op | source)
XLA Modules:
  0.0 38.4 jit_solution(18083442892181150338)
XLA Ops:
  0.0 1.3 %turn.1.table_ref = bf16[128,2048]{1,0:T(8,128)(2,1)S(1)} custom-call(bf16[2048,128]{1,0:T(8,128)(2,1)} %latent_hbm.1), custom_call_target="tpu_custom_call" | custom-call | bytes 4194304 | tf_op jit(solution)/shard_map/turn/pallas_call | solution.py:531
  1.3 0.0 copy-start.6
  1.3 0.0 copy-start.7
  1.3 0.8 %send.1 = (bf16[128,256]{1,0:T(8,128)(2,1)S(1)}, bf16[128,256]{1,0:T(8,128)(2,1)S(1)}, bf16[128,256]{1,0:T(8,128)(2,1)S(1)}) custom-call(bf16[128,2048]{1,0:T(8,128)(2,1)S(1)} %turn.1.table_ref, s32[1,4,256]{2,1,0:T(4,128)S(1)} %copy-done.8, bf16[2,4,128,128]{3,2,1,0:T(8,128)(2,1)S(1)} %copy-done), custom_call_target="tpu_custom_call" | custom-call | flops 1073741824 | bytes 4194304 | tf_op jit(solution)/shard_map/send/pallas_call | solution.py:539
  2.1 0.0 copy-start.10
  2.2 0.0 copy-start.9
  2.2 4.1 %collective-permute-start = (bf16[128,256]{1,0:T(8,128)(2,1)S(1)}, bf16[128,256]{1,0:T(8,128)(2,1)S(1)}, u32[]{:S(2)}, u32[]{:S(2)}) collective-permute-start(bf16[128,256]{1,0:T(8,128)(2,1)S(1)} %get-tuple-element.39), channel_id=1, source_target_pairs={{0,8},{4,12},{8,0},{12,4},{1,9},{5,13},{9,1},{13,5},{2,10},{6,14},... | collective-permute-start | bytes 196616 | tf_op jit(solution)/shard_map/ppermute | solution.py:481
  6.3 1.3 %collective-permute-start.1 = (bf16[128,256]{1,0:T(8,128)(2,1)S(1)}, bf16[128,256]{1,0:T(8,128)(2,1)S(1)}, u32[]{:S(2)}, u32[]{:S(2)}) collective-permute-start(bf16[128,256]{1,0:T(8,128)(2,1)S(1)} %get-tuple-element.40), channel_id=1, source_target_pairs={{0,12},{4,8},{8,4},{12,0},{1,13},{5,9},{9,5},{13,1},{2,14},{6,10},... | collective-permute-start | bytes 196616 | tf_op jit(solution)/shard_map/ppermute | solution.py:481
  7.6 0.2 collective-permute-start.2
  7.9 3.1 %near.1 = (s32[4,768]{1,0:T(4,128)S(1)}, s32[4,768]{1,0:T(4,128)S(1)}, bf16[128,3072]{1,0:T(8,128)(2,1)S(1)}, f32[128,2048]{1,0:T(8,128)S(1)}, s32[1,64]{1,0:T(1...) custom-call(bf16[128,2048]{1,0:T(8,128)(2,1)S(1)} %turn.1.table_ref, s32[16,768]{1,0:T(8,128)S(1)} %copy-done.2, ...), custom_call_target="tpu_custom_call" | custom-call | flops 4294967296 | bytes 4194304 | tf_op jit(solution)/shard_map/near/pallas_call | solution.py:543
  11.0 1.5 %collective-permute-done.1.rest_3_ = bf16[128,256]{1,0:T(8,128)(2,1)S(1)} collective-permute-done((bf16[128,256]{1,0:T(8,128)(2,1)S(1)}, bf16[128,256]{1,0:T(8,128)(2,1)S(1)}, u32[]{:S(2)}, u32[]{:S(2)}) %collective-permute-start.1) | collective-permute-done | bytes 65568 | tf_op jit(solution)/shard_map/ppermute | solution.py:481
  12.5 0.1 collective-permute-done.2.rest_4_
  12.6 1.7 %far_pool.1 = (bf16[128,2048]{1,0:T(8,128)(2,1)S(1)}, bf16[80,128]{1,0:T(8,128)(2,1)S(1)}, bf16[80,128]{1,0:T(8,128)(2,1)S(1)}) custom-call(bf16[128,2048]{1,0:T(8,128)(2,1)S(1)} %turn.1.table_ref, bf16[128,3072]{1,0:T(8,128)(2,1)S(1)} %get-tuple-element.32.aimed_ref, s32[4,768]{1,0:T(4,128)S(1)} %get-tuple-element.33.sources_ref, ...), custom_call_target="tpu_custom_call" | custom-call | flops 2147483648 | bytes 4194304 | tf_op jit(solution)/shard_map/far_pool/pallas_call | solution.py:557
  14.3 0.0 collective-permute-start.5
  14.3 1.6 %collective-permute-start.4 = (bf16[80,128]{1,0:T(8,128)(2,1)S(1)}, bf16[80,128]{1,0:T(8,128)(2,1)S(1)}, u32[]{:S(2)}, u32[]{:S(2)}) collective-permute-start(bf16[80,128]{1,0:T(8,128)(2,1)S(1)} %get-tuple-element.44), channel_id=1, source_target_pairs={{0,2},{2,0},{1,3},{3,1},{4,6},{6,4},{5,7},{7,5},{8,10},{10,8},{9,1... | collective-permute-start | bytes 61448 | tf_op jit(solution)/shard_map/ppermute | solution.py:491
  15.9 0.3 collective-permute-start.3
  16.2 0.6 %ahead.1.ahead_ref = bf16[144,768]{1,0:T(8,128)(2,1)S(1)} custom-call(bf16[128,2048]{1,0:T(8,128)(2,1)S(1)} %get-tuple-element.42.first_ref, s32[16,128]{1,0:T(8,128)S(1)} %bitcast.1, s32[1,4,256]{2,1,0:T(4,128)S(1)} %copy-done.8), custom_call_target="tpu_custom_call" | custom-call | flops 1073741824 | bytes 4194304 | tf_op jit(solution)/shard_map/ahead/pallas_call | solution.py:565
  16.8 0.8 %collective-permute-done.5.refs_3_ = bf16[80,128]{1,0:T(8,128)(2,1)S(1)} collective-permute-done((bf16[80,128]{1,0:T(8,128)(2,1)S(1)}, bf16[80,128]{1,0:T(8,128)(2,1)S(1)}, u32[]{:S(2)}, u32[]{:S(2)}) %collective-permute-start.5) | collective-permute-done | bytes 20512 | tf_op jit(solution)/shard_map/ppermute | solution.py:493
  17.7 0.5 %collective-permute-done.4.refs_2_ = bf16[80,128]{1,0:T(8,128)(2,1)S(1)} collective-permute-done((bf16[80,128]{1,0:T(8,128)(2,1)S(1)}, bf16[80,128]{1,0:T(8,128)(2,1)S(1)}, u32[]{:S(2)}, u32[]{:S(2)}) %collective-permute-start.4) | collective-permute-done | bytes 20512 | tf_op jit(solution)/shard_map/ppermute | solution.py:491
  18.2 0.4 coarse_send.1
  18.6 3.5 %collective-permute-start.6 = (bf16[128,128]{1,0:T(8,128)(2,1)S(1)}, bf16[128,128]{1,0:T(8,128)(2,1)S(1)}, u32[]{:S(2)}, u32[]{:S(2)}) collective-permute-start(bf16[128,128]{1,0:T(8,128)(2,1)S(1)} %get-tuple-element.49), channel_id=1, source_target_pairs={{0,8},{4,12},{8,0},{12,4},{1,9},{5,13},{9,1},{13,5},{2,10},{6,14},... | collective-permute-start | bytes 98312 | tf_op jit(solution)/shard_map/ppermute | solution.py:481
  22.1 0.7 %collective-permute-start.7 = (bf16[128,128]{1,0:T(8,128)(2,1)S(1)}, bf16[128,128]{1,0:T(8,128)(2,1)S(1)}, u32[]{:S(2)}, u32[]{:S(2)}) collective-permute-start(bf16[128,128]{1,0:T(8,128)(2,1)S(1)} %get-tuple-element.50), channel_id=1, source_target_pairs={{0,12},{4,8},{8,4},{12,0},{1,13},{5,9},{9,5},{13,1},{2,14},{6,10},... | collective-permute-start | bytes 98312 | tf_op jit(solution)/shard_map/ppermute | solution.py:481
  22.8 0.5 %coarse_own.1 = (f32[1,128,768]{2,1,0:T(8,128)S(1)}, s32[1,768]{1,0:T(1,128)S(1)}, s32[1,768]{1,0:T(1,128)S(1)}, bf16[1,128,64]{2,1,0:T(8,128)(2,1)S(1)}) custom-call(bf16[4,128,128]{2,1,0:T(8,128)(2,1)S(1)} %copy-done.1, bf16[80,128]{1,0:T(8,128)(2,1)S(1)} %get-tuple-element.43.refs_0_, bf16[80,128]{1,0:T(8,128)(2,1)S(1)} %collective-permute-done.3.refs_1_, ...), custom_call_target="tpu_custom_call" | custom-call | flops 4294967296 | bytes 4194304 | tf_op jit(solution)/shard_map/coarse_own/pallas_call | solution.py:577
  23.3 0.7 %collective-permute-done.6.rest_0_ = bf16[128,128]{1,0:T(8,128)(2,1)S(1)} collective-permute-done((bf16[128,128]{1,0:T(8,128)(2,1)S(1)}, bf16[128,128]{1,0:T(8,128)(2,1)S(1)}, u32[]{:S(2)}, u32[]{:S(2)}) %collective-permute-start.6) | collective-permute-done | bytes 32800 | tf_op jit(solution)/shard_map/ppermute | solution.py:481
  24.0 3.8 %collective-permute-done.7.rest_1_ = bf16[128,128]{1,0:T(8,128)(2,1)S(1)} collective-permute-done((bf16[128,128]{1,0:T(8,128)(2,1)S(1)}, bf16[128,128]{1,0:T(8,128)(2,1)S(1)}, u32[]{:S(2)}, u32[]{:S(2)}) %collective-permute-start.7) | collective-permute-done | bytes 32800 | tf_op jit(solution)/shard_map/ppermute | solution.py:481
  27.8 1.1 %lift_halo.1 = (bf16[128,128]{1,0:T(8,128)(2,1)S(1)}, bf16[128,256]{1,0:T(8,128)(2,1)S(1)}, bf16[128,256]{1,0:T(8,128)(2,1)S(1)}, bf16[128,256]{1,0:T(8,128)(2,1)S(1)}) custom-call(f32[1,128,768]{2,1,0:T(8,128)S(1)} %get-tuple-element.45.picked_ref, s32[1,768]{1,0:T(1,128)S(1)} %get-tuple-element.46.source_ref, s32[1,768]{1,0:T(1,128)S(1)} %get-tuple-element.47.place_ref, ...), custom_call_target="tpu_custom_call" | custom-call | flops 1073741824 | bytes 4194304 | tf_op jit(solution)/shard_map/lift_halo/pallas_call | solution.py:589
  29.0 1.0 %collective-permute-start.9 = (bf16[128,256]{1,0:T(8,128)(2,1)S(1)}, bf16[128,256]{1,0:T(8,128)(2,1)S(1)}, u32[]{:S(2)}, u32[]{:S(2)}) collective-permute-start(bf16[128,256]{1,0:T(8,128)(2,1)S(1)} %get-tuple-element.56), channel_id=1, source_target_pairs={{0,8},{4,12},{8,0},{12,4},{1,9},{5,13},{9,1},{13,5},{2,10},{6,14},... | collective-permute-start | bytes 196616 | tf_op jit(solution)/shard_map/ppermute | solution.py:481
  29.9 1.2 %collective-permute-start.10 = (bf16[128,256]{1,0:T(8,128)(2,1)S(1)}, bf16[128,256]{1,0:T(8,128)(2,1)S(1)}, u32[]{:S(2)}, u32[]{:S(2)}) collective-permute-start(bf16[128,256]{1,0:T(8,128)(2,1)S(1)} %get-tuple-element.57), channel_id=1, source_target_pairs={{0,12},{4,8},{8,4},{12,0},{1,13},{5,9},{9,5},{13,1},{2,14},{6,10},... | collective-permute-start | bytes 196616 | tf_op jit(solution)/shard_map/ppermute | solution.py:481
  31.1 1.4 %collective-permute-start.11 = (bf16[128,256]{1,0:T(8,128)(2,1)S(1)}, bf16[128,256]{1,0:T(8,128)(2,1)S(1)}, u32[]{:S(2)}, u32[]{:S(2)}) collective-permute-start(bf16[128,256]{1,0:T(8,128)(2,1)S(1)} %get-tuple-element.58), channel_id=1, source_target_pairs={{0,4},{4,0},{8,12},{12,8},{1,5},{5,1},{9,13},{13,9},{2,6},{6,2},{1... | collective-permute-start | bytes 196616 | tf_op jit(solution)/shard_map/ppermute | solution.py:481
  32.5 3.2 %lift_near.1 = (bf16[128,2048]{1,0:T(8,128)(2,1)S(1)}, bf16[128,3072]{1,0:T(8,128)(2,1)S(1)}, f32[128,2048]{1,0:T(8,128)S(1)}) custom-call(bf16[128,2048]{1,0:T(8,128)(2,1)S(1)} %get-tuple-element.42.first_ref, bf16[128,128]{1,0:T(8,128)(2,1)S(1)} %get-tuple-element.52.prolonged_ref, s32[16,128]{1,0:T(8,128)S(1)} %bitcast.2, s32[16,768]{1,0:T(8,128)S(1)} %copy-done.2, ...), custom_call_target="tpu_custom_call" | custom-call | flops 4294967296 | bytes 4194304 | tf_op jit(solution)/shard_map/lift_near/pallas_call | solution.py:596
  35.7 0.4 collective-permute-done.10.rest_1_
  36.1 2.3 %far.1 = bf16[2048,128]{1,0:T(8,128)(2,1)} custom-call(bf16[128,2048]{1,0:T(8,128)(2,1)S(1)} %get-tuple-element.53.table_ref, bf16[128,3072]{1,0:T(8,128)(2,1)S(1)} %get-tuple-element.54.aimed_ref, s32[4,768]{1,0:T(4,128)S(1)} %get-tuple-element.33.sources_ref, s32[4,768]{1,0:T(4,128)S(1)} %get-tuple-element.34.places_ref, ...), custom_call_target="tpu_custom_call" | custom-call | flops 2147483648 | bytes 4194304 | tf_op jit(solution)/shard_map/far/pallas_call | solution.py:603
  (24 shorter events, 0.1 us)
Async XLA Ops:
  0.0 1.3 %copy-start = (bf16[2,4,128,128]{3,2,1,0:T(8,128)(2,1)S(1)}, bf16[2,4,128,128]{3,2,1,0:T(8,128)(2,1)}, u32[]{:S(2)}) copy-start(bf16[2,4,128,128]{3,2,1,0:T(8,128)(2,1)} %weights_ref.15) | copy-start | bytes 786436
  0.0 1.3 %copy-start.8 = (s32[1,4,256]{2,1,0:T(4,128)S(1)}, s32[1,4,256]{2,1,0:T(4,128)}, u32[]{:S(2)}) copy-start(s32[1,4,256]{2,1,0:T(4,128)} %lists_ref.3) | copy-start | bytes 12292
  1.3 6.6 %copy-start.2 = (s32[16,768]{1,0:T(8,128)S(1)}, s32[16,768]{1,0:T(8,128)}, u32[]{:S(2)}) copy-start(s32[16,768]{1,0:T(8,128)} %source_ref.3) | copy-start | bytes 147460
  1.3 6.6 %copy-start.3 = (s32[16,768]{1,0:T(8,128)S(1)}, s32[16,768]{1,0:T(8,128)}, u32[]{:S(2)}) copy-start(s32[16,768]{1,0:T(8,128)} %place_ref.3) | copy-start | bytes 147460
  1.3 6.6 %copy-start.6 = (s32[2,768]{1,0:T(2,128)S(1)}, s32[2,768]{1,0:T(2,128)}, u32[]{:S(2)}) copy-start(s32[2,768]{1,0:T(2,128)} %coarse_source_ref.1) | copy-start | bytes 18436
  1.3 6.5 %copy-start.7 = (s32[2,768]{1,0:T(2,128)S(1)}, s32[2,768]{1,0:T(2,128)}, u32[]{:S(2)}) copy-start(s32[2,768]{1,0:T(2,128)} %coarse_place_ref.1) | copy-start | bytes 18436
  2.1 5.7 %copy-start.10 = (s32[1,4,64]{2,1,0:T(4,128)S(1)}, s32[1,4,64]{2,1,0:T(4,128)}, u32[]{:S(2)}) copy-start(s32[1,4,64]{2,1,0:T(4,128)} %pool_ref.1) | copy-start | bytes 3076
  2.2 5.7 %copy-start.9 = (s32[1,4,128]{2,1,0:T(4,128)S(1)}, s32[1,4,128]{2,1,0:T(4,128)}, u32[]{:S(2)}) copy-start(s32[1,4,128]{2,1,0:T(4,128)} %coarse_send_ref.1) | copy-start | bytes 6148
  2.2 8.8 %collective-permute-start = (bf16[128,256]{1,0:T(8,128)(2,1)S(1)}, bf16[128,256]{1,0:T(8,128)(2,1)S(1)}, u32[]{:S(2)}, u32[]{:S(2)}) collective-permute-start(bf16[128,256]{1,0:T(8,128)(2,1)S(1)} %get-tuple-element.39), channel_id=1, source_target_pairs={{0,8},{4,12},{8,0},{12,4},{1,9},{5,13},{9,1},{13,5},{2,10},{6,14},... | collective-permute-start | bytes 196616 | tf_op jit(solution)/shard_map/ppermute | solution.py:481
  6.3 6.2 %collective-permute-start.1 = (bf16[128,256]{1,0:T(8,128)(2,1)S(1)}, bf16[128,256]{1,0:T(8,128)(2,1)S(1)}, u32[]{:S(2)}, u32[]{:S(2)}) collective-permute-start(bf16[128,256]{1,0:T(8,128)(2,1)S(1)} %get-tuple-element.40), channel_id=1, source_target_pairs={{0,12},{4,8},{8,4},{12,0},{1,13},{5,9},{9,5},{13,1},{2,14},{6,10},... | collective-permute-start | bytes 196616 | tf_op jit(solution)/shard_map/ppermute | solution.py:481
  7.6 5.0 %collective-permute-start.2 = (bf16[128,256]{1,0:T(8,128)(2,1)S(1)}, bf16[128,256]{1,0:T(8,128)(2,1)S(1)}, u32[]{:S(2)}, u32[]{:S(2)}) collective-permute-start(bf16[128,256]{1,0:T(8,128)(2,1)S(1)} %get-tuple-element.41), channel_id=1, source_target_pairs={{0,4},{4,0},{8,12},{12,8},{1,5},{5,1},{9,13},{13,9},{2,6},{6,2},{1... | collective-permute-start | bytes 196616 | tf_op jit(solution)/shard_map/ppermute | solution.py:481
  12.6 3.6 %copy-start.5 = (s32[2048]{0:T(1024)S(1)}, s32[2048]{0:T(1024)}, u32[]{:S(2)}) copy-start(s32[2048]{0:T(1024)} %param.20) | copy-start | bytes 24580
  14.3 3.4 %collective-permute-start.5 = (bf16[80,128]{1,0:T(8,128)(2,1)S(1)}, bf16[80,128]{1,0:T(8,128)(2,1)S(1)}, u32[]{:S(2)}, u32[]{:S(2)}) collective-permute-start(bf16[80,128]{1,0:T(8,128)(2,1)S(1)} %get-tuple-element.44), channel_id=1, source_target_pairs={{0,3},{1,2},{2,1},{3,0},{4,7},{5,6},{6,5},{7,4},{8,11},{9,10},{10,... | collective-permute-start | bytes 61448 | tf_op jit(solution)/shard_map/ppermute | solution.py:493
  14.3 3.8 %collective-permute-start.4 = (bf16[80,128]{1,0:T(8,128)(2,1)S(1)}, bf16[80,128]{1,0:T(8,128)(2,1)S(1)}, u32[]{:S(2)}, u32[]{:S(2)}) collective-permute-start(bf16[80,128]{1,0:T(8,128)(2,1)S(1)} %get-tuple-element.44), channel_id=1, source_target_pairs={{0,2},{2,0},{1,3},{3,1},{4,6},{6,4},{5,7},{7,5},{8,10},{10,8},{9,1... | collective-permute-start | bytes 61448 | tf_op jit(solution)/shard_map/ppermute | solution.py:491
  15.9 2.3 %collective-permute-start.3 = (bf16[80,128]{1,0:T(8,128)(2,1)S(1)}, bf16[80,128]{1,0:T(8,128)(2,1)S(1)}, u32[]{:S(2)}, u32[]{:S(2)}) collective-permute-start(bf16[80,128]{1,0:T(8,128)(2,1)S(1)} %get-tuple-element.43.refs_0_), channel_id=1, source_target_pairs={{0,1},{1,0},{2,3},{3,2},{4,5},{5,4},{6,7},{7,6},{8,9},{9,8},{10,11... | collective-permute-start | bytes 61448 | tf_op jit(solution)/shard_map/ppermute | solution.py:492
  16.2 2.0 %copy-start.1 = (bf16[4,128,128]{2,1,0:T(8,128)(2,1)S(1)}, bf16[4,128,128]{2,1,0:T(8,128)(2,1)}, u32[]{:S(2)}) copy-start(bf16[4,128,128]{2,1,0:T(8,128)(2,1)} %coarse_weights_ref.1) | copy-start | bytes 393220
  18.6 5.4 %collective-permute-start.6 = (bf16[128,128]{1,0:T(8,128)(2,1)S(1)}, bf16[128,128]{1,0:T(8,128)(2,1)S(1)}, u32[]{:S(2)}, u32[]{:S(2)}) collective-permute-start(bf16[128,128]{1,0:T(8,128)(2,1)S(1)} %get-tuple-element.49), channel_id=1, source_target_pairs={{0,8},{4,12},{8,0},{12,4},{1,9},{5,13},{9,1},{13,5},{2,10},{6,14},... | collective-permute-start | bytes 98312 | tf_op jit(solution)/shard_map/ppermute | solution.py:481
  22.1 5.7 %collective-permute-start.7 = (bf16[128,128]{1,0:T(8,128)(2,1)S(1)}, bf16[128,128]{1,0:T(8,128)(2,1)S(1)}, u32[]{:S(2)}, u32[]{:S(2)}) collective-permute-start(bf16[128,128]{1,0:T(8,128)(2,1)S(1)} %get-tuple-element.50), channel_id=1, source_target_pairs={{0,12},{4,8},{8,4},{12,0},{1,13},{5,9},{9,5},{13,1},{2,14},{6,10},... | collective-permute-start | bytes 98312 | tf_op jit(solution)/shard_map/ppermute | solution.py:481
  22.8 5.0 %copy-start.4 = (bf16[128,128]{1,0:T(8,128)(2,1)S(1)}, bf16[128,128]{1,0:T(8,128)(2,1)}, u32[]{:S(2)}) copy-start(bf16[128,128]{1,0:T(8,128)(2,1)} %prolong_weight_ref.1) | copy-start | bytes 98308
  22.8 5.0 %collective-permute-start.8 = (bf16[128,128]{1,0:T(8,128)(2,1)S(1)}, bf16[128,128]{1,0:T(8,128)(2,1)S(1)}, u32[]{:S(2)}, u32[]{:S(2)}) collective-permute-start(bf16[128,128]{1,0:T(8,128)(2,1)S(1)} %get-tuple-element.51), channel_id=1, source_target_pairs={{0,4},{4,0},{8,12},{12,8},{1,5},{5,1},{9,13},{13,9},{2,6},{6,2},{1... | collective-permute-start | bytes 98312 | tf_op jit(solution)/shard_map/ppermute | solution.py:481
  29.0 6.8 %collective-permute-start.9 = (bf16[128,256]{1,0:T(8,128)(2,1)S(1)}, bf16[128,256]{1,0:T(8,128)(2,1)S(1)}, u32[]{:S(2)}, u32[]{:S(2)}) collective-permute-start(bf16[128,256]{1,0:T(8,128)(2,1)S(1)} %get-tuple-element.56), channel_id=1, source_target_pairs={{0,8},{4,12},{8,0},{12,4},{1,9},{5,13},{9,1},{13,5},{2,10},{6,14},... | collective-permute-start | bytes 196616 | tf_op jit(solution)/shard_map/ppermute | solution.py:481
  29.9 6.2 %collective-permute-start.10 = (bf16[128,256]{1,0:T(8,128)(2,1)S(1)}, bf16[128,256]{1,0:T(8,128)(2,1)S(1)}, u32[]{:S(2)}, u32[]{:S(2)}) collective-permute-start(bf16[128,256]{1,0:T(8,128)(2,1)S(1)} %get-tuple-element.57), channel_id=1, source_target_pairs={{0,12},{4,8},{8,4},{12,0},{1,13},{5,9},{9,5},{13,1},{2,14},{6,10},... | collective-permute-start | bytes 196616 | tf_op jit(solution)/shard_map/ppermute | solution.py:481
  31.1 5.0 %collective-permute-start.11 = (bf16[128,256]{1,0:T(8,128)(2,1)S(1)}, bf16[128,256]{1,0:T(8,128)(2,1)S(1)}, u32[]{:S(2)}, u32[]{:S(2)}) collective-permute-start(bf16[128,256]{1,0:T(8,128)(2,1)S(1)} %get-tuple-element.58), channel_id=1, source_target_pairs={{0,4},{4,0},{8,12},{12,8},{1,5},{5,1},{9,13},{13,9},{2,6},{6,2},{1... | collective-permute-start | bytes 196616 | tf_op jit(solution)/shard_map/ppermute | solution.py:481

commit v7 on v6

--- a/solution.py
+++ b/solution.py
@@ -13,6 +13,7 @@
 BLOCK = 128
 VMEM_BYTES = 32 << 20
 BATCH = 4
+FIRST_ORDER, SECOND_ORDER = (1, 0, 2), (1, 2, 0)
 PARTS = 2
 PAIR = 1
 
@@ -92,6 +93,14 @@
 
     def slot_order(self, slots, place):
         return slots ^ (place * self.pool_capacity) if self.swapped else slots
+
+
+def handed(halos, order):
+    return [halos[turn] for turn in order]
+
+
+def taken(refs, order):
+    return [refs[order.index(turn)] for turn in range(len(refs))]
 
 
 def turned(weight):
@@ -267,7 +276,7 @@
     grid, table_ref, aimed_ref, sources_ref, places_ref, sums_ref, weights_ref, pool_ref, *rest
 ):
     count = grid.packets
-    packed_refs, halo_refs = rest[:count], rest[count : count + len(grid.steps)]
+    packed_refs, halo_refs = rest[:count], taken(rest[count : count + len(grid.steps)], FIRST_ORDER)
     first_ref, packet_refs, both_ref = rest[-2 - count], rest[-1 - count : -1], rest[-1]
 
     def write(columns, value):
@@ -284,7 +293,7 @@
 
 
 def far_kernel(table_ref, aimed_ref, sources_ref, places_ref, sums_ref, weights_ref, *rest):
-    halo_refs, (out_hbm, both_ref, rows_ref, written) = rest[:-4], rest[-4:]
+    halo_refs, (out_hbm, both_ref, rows_ref, written) = taken(rest[:-4], SECOND_ORDER), rest[-4:]
     copies = []
 
     def write(columns, value):
@@ -474,14 +483,11 @@
     )
 
 
-def swap_dom(grid, arrays, order=(0, 1, 2)):
-    arrived = {}
-    for index in order:
-        step = grid.steps[index]
-        arrived[index] = lax.ppermute(
-            arrays[index], "dom", [(dom, grid.partner(dom, step)) for dom in range(grid.dom_count)]
-        )
-    return [arrived[index] for index in range(len(arrays))]
+def swap_dom(grid, arrays):
+    return [
+        lax.ppermute(array, "dom", [(dom, grid.partner(dom, step)) for dom in range(grid.dom_count)])
+        for array, step in zip(arrays, grid.steps)
+    ]
 
 
 def trade_packets(grid, packets):
@@ -560,7 +566,7 @@
         [two_tables],
         flops=2 * big,
         name="far_pool",
-    )(nodes, aimed, far_sources, far_places, sums, fine_weights, pool_lists, *packed, *halo)
+    )(nodes, aimed, far_sources, far_places, sums, fine_weights, pool_lists, *packed, *handed(halo, FIRST_ORDER))
     packets = trade_packets(grid, packets)
     (ahead,) = call(
         functools.partial(ahead_kernel, grid), [((features + 16, steps * halo_capacity), BF16)], flops=big, name="ahead"
@@ -611,7 +617,7 @@
         flops=2 * big,
         name="far",
         out_specs=(pl.BlockSpec(memory_space=pltpu.HBM),),
-    )(lifted, aimed, far_sources, far_places, sums, fine_weights, *halo)
+    )(lifted, aimed, far_sources, far_places, sums, fine_weights, *handed(halo, SECOND_ORDER))
     return fine_out
 
 

time: 38.6 us -> 38 us (0.984)
  waiting for transfers between devices: 7.84 us -> 6.93 us
    ppermute x9, waiting for transfers between devices: 6.5 us -> 4.72 us  [swap_dom(): lax.ppermute(array, 'dom', [(dom, grid.partner(dom, step)) for dom in ran...]
    ppermute x1, starting transfers between devices: 1.57 us -> 0.62 us  [trade_packets(): over = lax.ppermute(far, 'sub', pairs)]
    ppermute x1, starting transfers between devices: 0.04 us -> 0.98 us  [trade_packets(): both = lax.ppermute(far, ('sub', 'chip'), [(0, 3), (1, 2), (2, 1), (3, 0)])]
    ppermute x1, waiting for transfers between devices: 0.49 us -> 1.35 us  [trade_packets(): over = lax.ppermute(far, 'sub', pairs)]
  transfers between devices with their start and end apart: 12 -> 12, of which waited for: 7 -> 6; matrix products, arithmetic and copies ran while one was open for 0% -> 0% of each run, Pallas kernels for 19% -> 20%
where the time goes in v7:
time: 38 us; the launch traced here: 37.8 us
  starting transfers between devices  15.7 us (41%)
  Pallas kernels  15 us (39%)
  waiting for transfers between devices  6.93 us (18%)
    ppermute x9, starting transfers between devices, swap_dom(): lax.ppermute(array, 'dom', [(dom, grid.partner(dom, step)) for dom in ran...  13.8 us
    ppermute x9, waiting for transfers between devices, swap_dom(): lax.ppermute(array, 'dom', [(dom, grid.partner(dom, step)) for dom in ran...  4.72 us
    pallas_call x1, Pallas kernels, body(): call(functools.partial(lift_near_kernel, grid), [table, aimed_table, sums...  3.21 us
    pallas_call x1, Pallas kernels, body(): call(functools.partial(near_kernel, grid), [far_lists, far_lists, aimed_t...  3.08 us
    pallas_call x1, Pallas kernels, body(): call(far_kernel, [((node_count, features), BF16)], [two_tables, pltpu.VME...  2.33 us
    pallas_call x1, Pallas kernels, body(): call(functools.partial(far_pool_kernel, grid), [table, *[((grid.packet, f...  1.69 us
    ppermute x1, waiting for transfers between devices, trade_packets(): over = lax.ppermute(far, 'sub', pairs)  1.35 us
    pallas_call x1, Pallas kernels, body(): call(turn_kernel, [table], [pltpu.VMEM((node_count, features), BF16), plt...  1.25 us
  transfers between devices with their start and end apart: 12, of which 6 were waited for; matrix products, arithmetic and copies ran while one was open for 0% of the time, Pallas kernels for 20%

profile of v7, /device:TPU:0, one launch (start us, length us, event | category | flops | bytes accessed | tf_op | source)
XLA Modules:
  0.0 37.8 jit_solution(9372402994808913337)
XLA Ops:
  0.0 1.3 %turn.1.table_ref = bf16[128,2048]{1,0:T(8,128)(2,1)S(1)} custom-call(bf16[2048,128]{1,0:T(8,128)(2,1)} %latent_hbm.1), custom_call_target="tpu_custom_call" | custom-call | bytes 4194304 | tf_op jit(solution)/shard_map/turn/pallas_call | solution.py:537
  1.3 0.0 copy-start.2
  1.3 0.0 copy-start.3
  1.3 0.0 copy-start.6
  1.3 0.0 copy-start.7
  1.3 0.8 %send.1 = (bf16[128,256]{1,0:T(8,128)(2,1)S(1)}, bf16[128,256]{1,0:T(8,128)(2,1)S(1)}, bf16[128,256]{1,0:T(8,128)(2,1)S(1)}) custom-call(bf16[128,2048]{1,0:T(8,128)(2,1)S(1)} %turn.1.table_ref, s32[1,4,256]{2,1,0:T(4,128)S(1)} %copy-done.8, bf16[2,4,128,128]{3,2,1,0:T(8,128)(2,1)S(1)} %copy-done), custom_call_target="tpu_custom_call" | custom-call | flops 1073741824 | bytes 4194304 | tf_op jit(solution)/shard_map/send/pallas_call | solution.py:545
  2.1 0.0 copy-start.10
  2.2 5.1 %collective-permute-start = (bf16[128,256]{1,0:T(8,128)(2,1)S(1)}, bf16[128,256]{1,0:T(8,128)(2,1)S(1)}, u32[]{:S(2)}, u32[]{:S(2)}) collective-permute-start(bf16[128,256]{1,0:T(8,128)(2,1)S(1)} %get-tuple-element.39), channel_id=1, source_target_pairs={{0,12},{4,8},{8,4},{12,0},{1,13},{5,9},{9,5},{13,1},{2,14},{6,10},... | collective-permute-start | bytes 196616 | tf_op jit(solution)/shard_map/ppermute | solution.py:488
  7.3 0.6 %collective-permute-start.2 = (bf16[128,256]{1,0:T(8,128)(2,1)S(1)}, bf16[128,256]{1,0:T(8,128)(2,1)S(1)}, u32[]{:S(2)}, u32[]{:S(2)}) collective-permute-start(bf16[128,256]{1,0:T(8,128)(2,1)S(1)} %get-tuple-element.41), channel_id=1, source_target_pairs={{0,4},{4,0},{8,12},{12,8},{1,5},{5,1},{9,13},{13,9},{2,6},{6,2},{1... | collective-permute-start | bytes 196616 | tf_op jit(solution)/shard_map/ppermute | solution.py:488
  8.0 3.1 %near.1 = (s32[4,768]{1,0:T(4,128)S(1)}, s32[4,768]{1,0:T(4,128)S(1)}, bf16[128,3072]{1,0:T(8,128)(2,1)S(1)}, f32[128,2048]{1,0:T(8,128)S(1)}, s32[1,64]{1,0:T(1...) custom-call(bf16[128,2048]{1,0:T(8,128)(2,1)S(1)} %turn.1.table_ref, s32[16,768]{1,0:T(8,128)S(1)} %copy-done.2, ...), custom_call_target="tpu_custom_call" | custom-call | flops 4294967296 | bytes 4194304 | tf_op jit(solution)/shard_map/near/pallas_call | solution.py:549
  11.1 1.8 %collective-permute-done.1.rest_3_ = bf16[128,256]{1,0:T(8,128)(2,1)S(1)} collective-permute-done((bf16[128,256]{1,0:T(8,128)(2,1)S(1)}, bf16[128,256]{1,0:T(8,128)(2,1)S(1)}, u32[]{:S(2)}, u32[]{:S(2)}) %collective-permute-start.1) | collective-permute-done | bytes 65568 | tf_op jit(solution)/shard_map/ppermute | solution.py:488
  12.9 1.7 %far_pool.1 = (bf16[128,2048]{1,0:T(8,128)(2,1)S(1)}, bf16[80,128]{1,0:T(8,128)(2,1)S(1)}, bf16[80,128]{1,0:T(8,128)(2,1)S(1)}) custom-call(bf16[128,2048]{1,0:T(8,128)(2,1)S(1)} %turn.1.table_ref, bf16[128,3072]{1,0:T(8,128)(2,1)S(1)} %get-tuple-element.32.aimed_ref, s32[4,768]{1,0:T(4,128)S(1)} %get-tuple-element.33.sources_ref, ...), custom_call_target="tpu_custom_call" | custom-call | flops 2147483648 | bytes 4194304 | tf_op jit(solution)/shard_map/far_pool/pallas_call | solution.py:563
  14.6 1.0 %collective-permute-start.5 = (bf16[80,128]{1,0:T(8,128)(2,1)S(1)}, bf16[80,128]{1,0:T(8,128)(2,1)S(1)}, u32[]{:S(2)}, u32[]{:S(2)}) collective-permute-start(bf16[80,128]{1,0:T(8,128)(2,1)S(1)} %get-tuple-element.44), channel_id=1, source_target_pairs={{0,3},{1,2},{2,1},{3,0},{4,7},{5,6},{6,5},{7,4},{8,11},{9,10},{10,... | collective-permute-start | bytes 61448 | tf_op jit(solution)/shard_map/ppermute | solution.py:499
  15.6 0.6 %collective-permute-start.4 = (bf16[80,128]{1,0:T(8,128)(2,1)S(1)}, bf16[80,128]{1,0:T(8,128)(2,1)S(1)}, u32[]{:S(2)}, u32[]{:S(2)}) collective-permute-start(bf16[80,128]{1,0:T(8,128)(2,1)S(1)} %get-tuple-element.44), channel_id=1, source_target_pairs={{0,2},{2,0},{1,3},{3,1},{4,6},{6,4},{5,7},{7,5},{8,10},{10,8},{9,1... | collective-permute-start | bytes 61448 | tf_op jit(solution)/shard_map/ppermute | solution.py:497
  16.2 0.3 collective-permute-start.3
  16.5 0.6 %ahead.1.ahead_ref = bf16[144,768]{1,0:T(8,128)(2,1)S(1)} custom-call(bf16[128,2048]{1,0:T(8,128)(2,1)S(1)} %get-tuple-element.42.first_ref, s32[16,128]{1,0:T(8,128)S(1)} %bitcast.1, s32[1,4,256]{2,1,0:T(4,128)S(1)} %copy-done.8), custom_call_target="tpu_custom_call" | custom-call | flops 1073741824 | bytes 4194304 | tf_op jit(solution)/shard_map/ahead/pallas_call | solution.py:571
  17.1 0.9 %collective-permute-done.5.refs_3_ = bf16[80,128]{1,0:T(8,128)(2,1)S(1)} collective-permute-done((bf16[80,128]{1,0:T(8,128)(2,1)S(1)}, bf16[80,128]{1,0:T(8,128)(2,1)S(1)}, u32[]{:S(2)}, u32[]{:S(2)}) %collective-permute-start.5) | collective-permute-done | bytes 20512 | tf_op jit(solution)/shard_map/ppermute | solution.py:499
  18.0 1.4 %collective-permute-done.4.refs_2_ = bf16[80,128]{1,0:T(8,128)(2,1)S(1)} collective-permute-done((bf16[80,128]{1,0:T(8,128)(2,1)S(1)}, bf16[80,128]{1,0:T(8,128)(2,1)S(1)}, u32[]{:S(2)}, u32[]{:S(2)}) %collective-permute-start.4) | collective-permute-done | bytes 20512 | tf_op jit(solution)/shard_map/ppermute | solution.py:497
  19.4 0.4 coarse_send.1
  19.7 0.8 %collective-permute-start.6 = (bf16[128,128]{1,0:T(8,128)(2,1)S(1)}, bf16[128,128]{1,0:T(8,128)(2,1)S(1)}, u32[]{:S(2)}, u32[]{:S(2)}) collective-permute-start(bf16[128,128]{1,0:T(8,128)(2,1)S(1)} %get-tuple-element.49), channel_id=1, source_target_pairs={{0,8},{4,12},{8,0},{12,4},{1,9},{5,13},{9,1},{13,5},{2,10},{6,14},... | collective-permute-start | bytes 98312 | tf_op jit(solution)/shard_map/ppermute | solution.py:488
  20.5 1.9 %collective-permute-start.7 = (bf16[128,128]{1,0:T(8,128)(2,1)S(1)}, bf16[128,128]{1,0:T(8,128)(2,1)S(1)}, u32[]{:S(2)}, u32[]{:S(2)}) collective-permute-start(bf16[128,128]{1,0:T(8,128)(2,1)S(1)} %get-tuple-element.50), channel_id=1, source_target_pairs={{0,12},{4,8},{8,4},{12,0},{1,13},{5,9},{9,5},{13,1},{2,14},{6,10},... | collective-permute-start | bytes 98312 | tf_op jit(solution)/shard_map/ppermute | solution.py:488
  22.4 0.9 %collective-permute-start.8 = (bf16[128,128]{1,0:T(8,128)(2,1)S(1)}, bf16[128,128]{1,0:T(8,128)(2,1)S(1)}, u32[]{:S(2)}, u32[]{:S(2)}) collective-permute-start(bf16[128,128]{1,0:T(8,128)(2,1)S(1)} %get-tuple-element.51), channel_id=1, source_target_pairs={{0,4},{4,0},{8,12},{12,8},{1,5},{5,1},{9,13},{13,9},{2,6},{6,2},{1... | collective-permute-start | bytes 98312 | tf_op jit(solution)/shard_map/ppermute | solution.py:488
  23.3 0.5 %coarse_own.1 = (f32[1,128,768]{2,1,0:T(8,128)S(1)}, s32[1,768]{1,0:T(1,128)S(1)}, s32[1,768]{1,0:T(1,128)S(1)}, bf16[1,128,64]{2,1,0:T(8,128)(2,1)S(1)}) custom-call(bf16[4,128,128]{2,1,0:T(8,128)(2,1)S(1)} %copy-done.1, bf16[80,128]{1,0:T(8,128)(2,1)S(1)} %get-tuple-element.43.refs_0_, bf16[80,128]{1,0:T(8,128)(2,1)S(1)} %collective-permute-done.3.refs_1_, ...), custom_call_target="tpu_custom_call" | custom-call | flops 4294967296 | bytes 4194304 | tf_op jit(solution)/shard_map/coarse_own/pallas_call | solution.py:583
  23.8 1.1 %collective-permute-done.6.rest_0_ = bf16[128,128]{1,0:T(8,128)(2,1)S(1)} collective-permute-done((bf16[128,128]{1,0:T(8,128)(2,1)S(1)}, bf16[128,128]{1,0:T(8,128)(2,1)S(1)}, u32[]{:S(2)}, u32[]{:S(2)}) %collective-permute-start.6) | collective-permute-done | bytes 32800 | tf_op jit(solution)/shard_map/ppermute | solution.py:488
  24.9 1.4 %collective-permute-done.7.rest_1_ = bf16[128,128]{1,0:T(8,128)(2,1)S(1)} collective-permute-done((bf16[128,128]{1,0:T(8,128)(2,1)S(1)}, bf16[128,128]{1,0:T(8,128)(2,1)S(1)}, u32[]{:S(2)}, u32[]{:S(2)}) %collective-permute-start.7) | collective-permute-done | bytes 32800 | tf_op jit(solution)/shard_map/ppermute | solution.py:488
  26.3 0.3 collective-permute-done.8.rest_2_
  26.6 1.1 %lift_halo.1 = (bf16[128,128]{1,0:T(8,128)(2,1)S(1)}, bf16[128,256]{1,0:T(8,128)(2,1)S(1)}, bf16[128,256]{1,0:T(8,128)(2,1)S(1)}, bf16[128,256]{1,0:T(8,128)(2,1)S(1)}) custom-call(f32[1,128,768]{2,1,0:T(8,128)S(1)} %get-tuple-element.45.picked_ref, s32[1,768]{1,0:T(1,128)S(1)} %get-tuple-element.46.source_ref, s32[1,768]{1,0:T(1,128)S(1)} %get-tuple-element.47.place_ref, ...), custom_call_target="tpu_custom_call" | custom-call | flops 1073741824 | bytes 4194304 | tf_op jit(solution)/shard_map/lift_halo/pallas_call | solution.py:595
  27.7 1.9 %collective-permute-start.9 = (bf16[128,256]{1,0:T(8,128)(2,1)S(1)}, bf16[128,256]{1,0:T(8,128)(2,1)S(1)}, u32[]{:S(2)}, u32[]{:S(2)}) collective-permute-start(bf16[128,256]{1,0:T(8,128)(2,1)S(1)} %get-tuple-element.56), channel_id=1, source_target_pairs={{0,12},{4,8},{8,4},{12,0},{1,13},{5,9},{9,5},{13,1},{2,14},{6,10},... | collective-permute-start | bytes 196616 | tf_op jit(solution)/shard_map/ppermute | solution.py:488
  29.7 2.5 %collective-permute-start.11 = (bf16[128,256]{1,0:T(8,128)(2,1)S(1)}, bf16[128,256]{1,0:T(8,128)(2,1)S(1)}, u32[]{:S(2)}, u32[]{:S(2)}) collective-permute-start(bf16[128,256]{1,0:T(8,128)(2,1)S(1)} %get-tuple-element.58), channel_id=1, source_target_pairs={{0,8},{4,12},{8,0},{12,4},{1,9},{5,13},{9,1},{13,5},{2,10},{6,14},... | collective-permute-start | bytes 196616 | tf_op jit(solution)/shard_map/ppermute | solution.py:488
  32.2 3.2 %lift_near.1 = (bf16[128,2048]{1,0:T(8,128)(2,1)S(1)}, bf16[128,3072]{1,0:T(8,128)(2,1)S(1)}, f32[128,2048]{1,0:T(8,128)S(1)}) custom-call(bf16[128,2048]{1,0:T(8,128)(2,1)S(1)} %get-tuple-element.42.first_ref, bf16[128,128]{1,0:T(8,128)(2,1)S(1)} %get-tuple-element.52.prolonged_ref, s32[16,128]{1,0:T(8,128)S(1)} %bitcast.2, s32[16,768]{1,0:T(8,128)S(1)} %copy-done.2, ...), custom_call_target="tpu_custom_call" | custom-call | flops 4294967296 | bytes 4194304 | tf_op jit(solution)/shard_map/lift_near/pallas_call | solution.py:602
  35.4 0.0 collective-permute-done.11.rest_2_
  35.5 2.3 %far.1 = bf16[2048,128]{1,0:T(8,128)(2,1)} custom-call(bf16[128,2048]{1,0:T(8,128)(2,1)S(1)} %get-tuple-element.53.table_ref, bf16[128,3072]{1,0:T(8,128)(2,1)S(1)} %get-tuple-element.54.aimed_ref, s32[4,768]{1,0:T(4,128)S(1)} %get-tuple-element.33.sources_ref, s32[4,768]{1,0:T(4,128)S(1)} %get-tuple-element.34.places_ref, ...), custom_call_target="tpu_custom_call" | custom-call | flops 2147483648 | bytes 4194304 | tf_op jit(solution)/shard_map/far/pallas_call | solution.py:609
  (24 shorter events, 0.1 us)
Async XLA Ops:
  0.0 1.3 %copy-start = (bf16[2,4,128,128]{3,2,1,0:T(8,128)(2,1)S(1)}, bf16[2,4,128,128]{3,2,1,0:T(8,128)(2,1)}, u32[]{:S(2)}) copy-start(bf16[2,4,128,128]{3,2,1,0:T(8,128)(2,1)} %weights_ref.15) | copy-start | bytes 786436
  0.0 1.3 %copy-start.8 = (s32[1,4,256]{2,1,0:T(4,128)S(1)}, s32[1,4,256]{2,1,0:T(4,128)}, u32[]{:S(2)}) copy-start(s32[1,4,256]{2,1,0:T(4,128)} %lists_ref.3) | copy-start | bytes 12292
  1.3 6.6 %copy-start.2 = (s32[16,768]{1,0:T(8,128)S(1)}, s32[16,768]{1,0:T(8,128)}, u32[]{:S(2)}) copy-start(s32[16,768]{1,0:T(8,128)} %source_ref.3) | copy-start | bytes 147460
  1.3 6.6 %copy-start.3 = (s32[16,768]{1,0:T(8,128)S(1)}, s32[16,768]{1,0:T(8,128)}, u32[]{:S(2)}) copy-start(s32[16,768]{1,0:T(8,128)} %place_ref.3) | copy-start | bytes 147460
  1.3 6.6 %copy-start.6 = (s32[2,768]{1,0:T(2,128)S(1)}, s32[2,768]{1,0:T(2,128)}, u32[]{:S(2)}) copy-start(s32[2,768]{1,0:T(2,128)} %coarse_source_ref.1) | copy-start | bytes 18436
  1.3 6.6 %copy-start.7 = (s32[2,768]{1,0:T(2,128)S(1)}, s32[2,768]{1,0:T(2,128)}, u32[]{:S(2)}) copy-start(s32[2,768]{1,0:T(2,128)} %coarse_place_ref.1) | copy-start | bytes 18436
  2.1 5.8 %copy-start.10 = (s32[1,4,64]{2,1,0:T(4,128)S(1)}, s32[1,4,64]{2,1,0:T(4,128)}, u32[]{:S(2)}) copy-start(s32[1,4,64]{2,1,0:T(4,128)} %pool_ref.1) | copy-start | bytes 3076
  2.2 5.8 %copy-start.9 = (s32[1,4,128]{2,1,0:T(4,128)S(1)}, s32[1,4,128]{2,1,0:T(4,128)}, u32[]{:S(2)}) copy-start(s32[1,4,128]{2,1,0:T(4,128)} %coarse_send_ref.1) | copy-start | bytes 6148
  2.2 8.9 %collective-permute-start = (bf16[128,256]{1,0:T(8,128)(2,1)S(1)}, bf16[128,256]{1,0:T(8,128)(2,1)S(1)}, u32[]{:S(2)}, u32[]{:S(2)}) collective-permute-start(bf16[128,256]{1,0:T(8,128)(2,1)S(1)} %get-tuple-element.39), channel_id=1, source_target_pairs={{0,12},{4,8},{8,4},{12,0},{1,13},{5,9},{9,5},{13,1},{2,14},{6,10},... | collective-permute-start | bytes 196616 | tf_op jit(solution)/shard_map/ppermute | solution.py:488
  7.3 5.6 %collective-permute-start.1 = (bf16[128,256]{1,0:T(8,128)(2,1)S(1)}, bf16[128,256]{1,0:T(8,128)(2,1)S(1)}, u32[]{:S(2)}, u32[]{:S(2)}) collective-permute-start(bf16[128,256]{1,0:T(8,128)(2,1)S(1)} %get-tuple-element.40), channel_id=1, source_target_pairs={{0,8},{4,12},{8,0},{12,4},{1,9},{5,13},{9,1},{13,5},{2,10},{6,14},... | collective-permute-start | bytes 196616 | tf_op jit(solution)/shard_map/ppermute | solution.py:488
  7.3 5.6 %collective-permute-start.2 = (bf16[128,256]{1,0:T(8,128)(2,1)S(1)}, bf16[128,256]{1,0:T(8,128)(2,1)S(1)}, u32[]{:S(2)}, u32[]{:S(2)}) collective-permute-start(bf16[128,256]{1,0:T(8,128)(2,1)S(1)} %get-tuple-element.41), channel_id=1, source_target_pairs={{0,4},{4,0},{8,12},{12,8},{1,5},{5,1},{9,13},{13,9},{2,6},{6,2},{1... | collective-permute-start | bytes 196616 | tf_op jit(solution)/shard_map/ppermute | solution.py:488
  12.9 3.6 %copy-start.5 = (s32[2048]{0:T(1024)S(1)}, s32[2048]{0:T(1024)}, u32[]{:S(2)}) copy-start(s32[2048]{0:T(1024)} %param.20) | copy-start | bytes 24580
  14.6 3.4 %collective-permute-start.5 = (bf16[80,128]{1,0:T(8,128)(2,1)S(1)}, bf16[80,128]{1,0:T(8,128)(2,1)S(1)}, u32[]{:S(2)}, u32[]{:S(2)}) collective-permute-start(bf16[80,128]{1,0:T(8,128)(2,1)S(1)} %get-tuple-element.44), channel_id=1, source_target_pairs={{0,3},{1,2},{2,1},{3,0},{4,7},{5,6},{6,5},{7,4},{8,11},{9,10},{10,... | collective-permute-start | bytes 61448 | tf_op jit(solution)/shard_map/ppermute | solution.py:499
  15.6 3.8 %collective-permute-start.4 = (bf16[80,128]{1,0:T(8,128)(2,1)S(1)}, bf16[80,128]{1,0:T(8,128)(2,1)S(1)}, u32[]{:S(2)}, u32[]{:S(2)}) collective-permute-start(bf16[80,128]{1,0:T(8,128)(2,1)S(1)} %get-tuple-element.44), channel_id=1, source_target_pairs={{0,2},{2,0},{1,3},{3,1},{4,6},{6,4},{5,7},{7,5},{8,10},{10,8},{9,1... | collective-permute-start | bytes 61448 | tf_op jit(solution)/shard_map/ppermute | solution.py:497
  16.2 3.2 %collective-permute-start.3 = (bf16[80,128]{1,0:T(8,128)(2,1)S(1)}, bf16[80,128]{1,0:T(8,128)(2,1)S(1)}, u32[]{:S(2)}, u32[]{:S(2)}) collective-permute-start(bf16[80,128]{1,0:T(8,128)(2,1)S(1)} %get-tuple-element.43.refs_0_), channel_id=1, source_target_pairs={{0,1},{1,0},{2,3},{3,2},{4,5},{5,4},{6,7},{7,6},{8,9},{9,8},{10,11... | collective-permute-start | bytes 61448 | tf_op jit(solution)/shard_map/ppermute | solution.py:498
  16.5 2.9 %copy-start.1 = (bf16[4,128,128]{2,1,0:T(8,128)(2,1)S(1)}, bf16[4,128,128]{2,1,0:T(8,128)(2,1)}, u32[]{:S(2)}) copy-start(bf16[4,128,128]{2,1,0:T(8,128)(2,1)} %coarse_weights_ref.1) | copy-start | bytes 393220
  19.7 5.2 %collective-permute-start.6 = (bf16[128,128]{1,0:T(8,128)(2,1)S(1)}, bf16[128,128]{1,0:T(8,128)(2,1)S(1)}, u32[]{:S(2)}, u32[]{:S(2)}) collective-permute-start(bf16[128,128]{1,0:T(8,128)(2,1)S(1)} %get-tuple-element.49), channel_id=1, source_target_pairs={{0,8},{4,12},{8,0},{12,4},{1,9},{5,13},{9,1},{13,5},{2,10},{6,14},... | collective-permute-start | bytes 98312 | tf_op jit(solution)/shard_map/ppermute | solution.py:488
  20.5 5.7 %collective-permute-start.7 = (bf16[128,128]{1,0:T(8,128)(2,1)S(1)}, bf16[128,128]{1,0:T(8,128)(2,1)S(1)}, u32[]{:S(2)}, u32[]{:S(2)}) collective-permute-start(bf16[128,128]{1,0:T(8,128)(2,1)S(1)} %get-tuple-element.50), channel_id=1, source_target_pairs={{0,12},{4,8},{8,4},{12,0},{1,13},{5,9},{9,5},{13,1},{2,14},{6,10},... | collective-permute-start | bytes 98312 | tf_op jit(solution)/shard_map/ppermute | solution.py:488
  22.4 4.2 %copy-start.4 = (bf16[128,128]{1,0:T(8,128)(2,1)S(1)}, bf16[128,128]{1,0:T(8,128)(2,1)}, u32[]{:S(2)}) copy-start(bf16[128,128]{1,0:T(8,128)(2,1)} %prolong_weight_ref.1) | copy-start | bytes 98308
  22.4 4.2 %collective-permute-start.8 = (bf16[128,128]{1,0:T(8,128)(2,1)S(1)}, bf16[128,128]{1,0:T(8,128)(2,1)S(1)}, u32[]{:S(2)}, u32[]{:S(2)}) collective-permute-start(bf16[128,128]{1,0:T(8,128)(2,1)S(1)} %get-tuple-element.51), channel_id=1, source_target_pairs={{0,4},{4,0},{8,12},{12,8},{1,5},{5,1},{9,13},{13,9},{2,6},{6,2},{1... | collective-permute-start | bytes 98312 | tf_op jit(solution)/shard_map/ppermute | solution.py:488
  27.7 7.7 %collective-permute-start.9 = (bf16[128,256]{1,0:T(8,128)(2,1)S(1)}, bf16[128,256]{1,0:T(8,128)(2,1)S(1)}, u32[]{:S(2)}, u32[]{:S(2)}) collective-permute-start(bf16[128,256]{1,0:T(8,128)(2,1)S(1)} %get-tuple-element.56), channel_id=1, source_target_pairs={{0,12},{4,8},{8,4},{12,0},{1,13},{5,9},{9,5},{13,1},{2,14},{6,10},... | collective-permute-start | bytes 196616 | tf_op jit(solution)/shard_map/ppermute | solution.py:488
  29.7 5.8 %collective-permute-start.10 = (bf16[128,256]{1,0:T(8,128)(2,1)S(1)}, bf16[128,256]{1,0:T(8,128)(2,1)S(1)}, u32[]{:S(2)}, u32[]{:S(2)}) collective-permute-start(bf16[128,256]{1,0:T(8,128)(2,1)S(1)} %get-tuple-element.57), channel_id=1, source_target_pairs={{0,4},{4,0},{8,12},{12,8},{1,5},{5,1},{9,13},{13,9},{2,6},{6,2},{1... | collective-permute-start | bytes 196616 | tf_op jit(solution)/shard_map/ppermute | solution.py:488
  29.7 5.8 %collective-permute-start.11 = (bf16[128,256]{1,0:T(8,128)(2,1)S(1)}, bf16[128,256]{1,0:T(8,128)(2,1)S(1)}, u32[]{:S(2)}, u32[]{:S(2)}) collective-permute-start(bf16[128,256]{1,0:T(8,128)(2,1)S(1)} %get-tuple-element.58), channel_id=1, source_target_pairs={{0,8},{4,12},{8,0},{12,4},{1,9},{5,13},{9,1},{13,5},{2,10},{6,14},... | collective-permute-start | bytes 196616 | tf_op jit(solution)/shard_map/ppermute | solution.py:488

commit v8 on v7

--- a/solution.py
+++ b/solution.py
@@ -107,6 +107,10 @@
     return halved(weight).T
 
 
+def turned_update(weights_ref, *layer):
+    return jnp.concatenate([turned(weights_ref[*layer, 2]), turned(weights_ref[*layer, 3])], axis=1)
+
+
 def turn_kernel(latent_hbm, table_ref, latent_ref, arrived):
     part = latent_ref.shape[0] // PARTS
     copies = []
@@ -191,9 +195,11 @@
     places_ref,
     aimed_ref,
     sums_ref,
+    update_ref,
     pooled_ref,
     *rest,
 ):
+    update_ref[...] = turned_update(weights_ref, 0)
     packed_refs, terms_ref = rest[:-1], rest[-1]
     table = table_ref[...]
     halo_capacity = grid.halo_capacity
@@ -226,11 +232,10 @@
         pooled_ref[owner : owner + 1, :] = pool_ref[0, 4 * owner : 4 * owner + 1, :]
 
 
-def far_edges(layer, table_ref, aimed_ref, sources_ref, places_ref, sums_ref, weights_ref, halo_refs, both_ref, write):
+def far_edges(table_ref, aimed_ref, sources_ref, places_ref, sums_ref, update_ref, halo_refs, both_ref, write):
     features, node_count = table_ref.shape
     batch_count, slot_count = sources_ref.shape
     halo = jnp.concatenate([ref[...] for ref in halo_refs], axis=1)
-    update_weights = jnp.concatenate([turned(weights_ref[layer, 2]), turned(weights_ref[layer, 3])], axis=1)
     pair_slots = slot_count * PAIR // BATCH
     pair_rows = PAIR * BLOCK
     batch_rows = BATCH * BLOCK
@@ -251,7 +256,7 @@
 
     def update(batch):
         columns = slice(batch * batch_rows, (batch + 1) * batch_rows)
-        change = silu_of_half(dot(update_weights, both_ref[:, columns]))
+        change = silu_of_half(dot(update_ref[...], both_ref[:, columns]))
         write(columns, (both_ref[features:, columns].astype(F32) + change).astype(BF16))
 
     message = messages(0)
@@ -273,7 +278,7 @@
 
 
 def far_pool_kernel(
-    grid, table_ref, aimed_ref, sources_ref, places_ref, sums_ref, weights_ref, pool_ref, *rest
+    grid, table_ref, aimed_ref, sources_ref, places_ref, sums_ref, update_ref, pool_ref, *rest
 ):
     count = grid.packets
     packed_refs, halo_refs = rest[:count], taken(rest[count : count + len(grid.steps)], FIRST_ORDER)
@@ -284,7 +289,7 @@
 
     for packet_ref, packed_ref in zip(packet_refs, packed_refs):
         packet_ref[grid.pooled_rows :, :] = packed_ref[...]
-    far_edges(0, table_ref, aimed_ref, sources_ref, places_ref, sums_ref, weights_ref, halo_refs, both_ref, write)
+    far_edges(table_ref, aimed_ref, sources_ref, places_ref, sums_ref, update_ref, halo_refs, both_ref, write)
     for owner in range(grid.owners):
         hot = rows_hot(pool_ref[owner : owner + 1, :], first_ref.shape[1])
         pooled = dot(first_ref[...], hot).astype(BF16).T
@@ -292,7 +297,7 @@
             packet_ref[owner * grid.pool_capacity : (owner + 1) * grid.pool_capacity, :] = pooled
 
 
-def far_kernel(table_ref, aimed_ref, sources_ref, places_ref, sums_ref, weights_ref, *rest):
+def far_kernel(table_ref, aimed_ref, sources_ref, places_ref, sums_ref, update_ref, *rest):
     halo_refs, (out_hbm, both_ref, rows_ref, written) = taken(rest[:-4], SECOND_ORDER), rest[-4:]
     copies = []
 
@@ -302,7 +307,7 @@
         copies.append(pltpu.make_async_copy(rows_ref.at[rows], out_hbm.at[rows], written.at[len(copies)]))
         copies[-1].start()
 
-    far_edges(1, table_ref, aimed_ref, sources_ref, places_ref, sums_ref, weights_ref, halo_refs, both_ref, write)
+    far_edges(table_ref, aimed_ref, sources_ref, places_ref, sums_ref, update_ref, halo_refs, both_ref, write)
     for copy in copies:
         copy.wait()
 
@@ -360,9 +365,12 @@
             out_ref[owner * BLOCK : (owner + 1) * BLOCK, :] = picked[:, index * capacity : (index + 1) * capacity]
 
 
-def coarse_own_kernel(grid, weights_ref, *refs):
+def coarse_own_kernel(grid, weights_ref, prolong_weight_ref, fine_weights_ref, *refs):
     packets = refs[: grid.places]
-    picked_ref, source_out, place_out, rows_out, lists_ref = refs[grid.places :]
+    picked_ref, source_out, place_out, rows_out, turned_out, lists_ref = refs[grid.places :]
+    turned_out[...] = jnp.concatenate(
+        [turned_update(weights_ref), turned(prolong_weight_ref[...]), turned(fine_weights_ref[1, 0])], axis=1
+    )
     place = grid.own_place()
     first_slot = place * grid.pool_capacity
     block = 0 if grid.swapped else grid.block_of(place)
@@ -414,16 +422,14 @@
     place_ref,
     rows_ref,
     ahead_ref,
-    coarse_weights_ref,
-    prolong_weight_ref,
-    weights_ref,
+    turned_ref,
     *rest,
 ):
     count = len(grid.steps)
     halo_refs, prolonged_ref, sent_refs = rest[:count], rest[count], rest[count + 1 :]
     features = rows_ref.shape[1]
-    update_weights = jnp.concatenate([turned(coarse_weights_ref[2]), turned(coarse_weights_ref[3])], axis=1)
-    prolong_weight = turned(prolong_weight_ref[...])
+    update_weights = turned_ref[:, : 2 * features]
+    prolong_weight = turned_ref[:, 2 * features : 3 * features]
     prolonged = []
     for owner in range(grid.owners):
         halo = jnp.concatenate([ref[owner * BLOCK : (owner + 1) * BLOCK, :] for ref in halo_refs], axis=1)
@@ -440,8 +446,8 @@
     low = (prolonged - high.astype(F32)).astype(BF16)
     parts = jnp.concatenate([high, low], axis=1)
     prolonged_ref[...] = parts
-    weight = turned(weights_ref[1, 0])
-    index_row = ahead_ref[features : features + 1, :].astype(F32).astype(I32)
+    weight = turned_ref[:, 3 * features :]
+    index_row = ahead_ref[features : features + 16, :].astype(F32).astype(I32)[:1]
     lifted = lift(ahead_ref[:features, :], parts, index_row)
     terms = dot(weight, lifted).astype(BF16)
     capacity = sent_refs[0].shape[1]
@@ -460,8 +466,10 @@
     lifted_ref,
     aimed_ref,
     sums_ref,
+    update_ref,
     terms_ref,
 ):
+    update_ref[...] = turned_update(weights_ref, 1)
     indices = prolong_ref[...]
     shift = (4 * grid.pool_capacity).bit_length() - 1
     indices = lax.shift_right_logical(indices, shift) * grid.pool_capacity + (indices & (grid.pool_capacity - 1))
@@ -526,6 +534,7 @@
     far_count = slot_count - slot_count * 3 // 4
     table = ((features, node_count), BF16)
     sums_table = ((features, node_count), F32)
+    update_table = ((features, 2 * features), BF16)
     aimed_table = ((features, block_count * far_count), BF16)
     far_lists = ((block_count // BATCH, BATCH * far_count), I32)
     halo_outs = [((features, halo_capacity), BF16)] * steps
@@ -546,13 +555,14 @@
         nodes, halo_send, fine_weights
     )
     halo = swap_dom(grid, sent)
-    far_sources, far_places, aimed, sums, pool_lists, *packed = call(
+    far_sources, far_places, aimed, sums, update, pool_lists, *packed = call(
         functools.partial(near_kernel, grid),
         [
             far_lists,
             far_lists,
             aimed_table,
             sums_table,
+            update_table,
             ((grid.owners, grid.pool_capacity), I32),
             *[((grid.packed_rows, features), BF16)] * grid.packets,
         ],
@@ -566,7 +576,7 @@
         [two_tables],
         flops=2 * big,
         name="far_pool",
-    )(nodes, aimed, far_sources, far_places, sums, fine_weights, pool_lists, *packed, *handed(halo, FIRST_ORDER))
+    )(nodes, aimed, far_sources, far_places, sums, update, pool_lists, *packed, *handed(halo, FIRST_ORDER))
     packets = trade_packets(grid, packets)
     (ahead,) = call(
         functools.partial(ahead_kernel, grid), [((features + 16, steps * halo_capacity), BF16)], flops=big, name="ahead"
@@ -580,28 +590,29 @@
         name="coarse_send",
     )(coarse_weights, *packets)
     coarse_halo = swap_dom(grid, sent)
-    picked, sources, places, rows = call(
+    picked, sources, places, rows, weights = call(
         functools.partial(coarse_own_kernel, grid),
         [
             ((grid.owners, features, coarse_slots), F32),
             ((grid.owners, coarse_slots), I32),
             ((grid.owners, coarse_slots), I32),
             ((grid.owners, features, grid.pool_capacity), BF16),
+            ((features, 4 * features), BF16),
         ],
         [lists_scratch],
         flops=4 * big,
         name="coarse_own",
-    )(coarse_weights, *packets)
+    )(coarse_weights, prolong_weight, fine_weights, *packets)
     prolonged, *sent = call(
         functools.partial(lift_halo_kernel, grid),
         [((features, 2 * grid.pooled_rows), BF16), *halo_outs],
         flops=big,
         name="lift_halo",
-    )(picked, sources, places, rows, ahead, coarse_weights, prolong_weight, fine_weights, *coarse_halo)
+    )(picked, sources, places, rows, ahead, weights, *coarse_halo)
     halo = swap_dom(grid, sent)
-    lifted, aimed, sums = call(
+    lifted, aimed, sums, update = call(
         functools.partial(lift_near_kernel, grid),
-        [table, aimed_table, sums_table],
+        [table, aimed_table, sums_table, update_table],
         [two_tables],
         flops=4 * big,
         name="lift_near",
@@ -617,7 +628,7 @@
         flops=2 * big,
         name="far",
         out_specs=(pl.BlockSpec(memory_space=pltpu.HBM),),
-    )(lifted, aimed, far_sources, far_places, sums, fine_weights, *handed(halo, SECOND_ORDER))
+    )(lifted, aimed, far_sources, far_places, sums, update, *handed(halo, SECOND_ORDER))
     return fine_out
 
 

time: 38 us -> 38 us (level)
  transfers between devices with their start and end apart: 12 -> 12, of which waited for: 6 -> 7; matrix products, arithmetic and copies ran while one was open for 0% -> 0% of each run, Pallas kernels for 20% -> 20%
where the time goes in v8:
time: 38 us; the launch traced here: 37.8 us
  starting transfers between devices  15.7 us (41%)
  Pallas kernels  15 us (39%)
  waiting for transfers between devices  6.94 us (18%)
    ppermute x9, starting transfers between devices, swap_dom(): lax.ppermute(array, 'dom', [(dom, grid.partner(dom, step)) for dom in ran...  13.8 us
    ppermute x9, waiting for transfers between devices, swap_dom(): lax.ppermute(array, 'dom', [(dom, grid.partner(dom, step)) for dom in ran...  4.73 us
    pallas_call x1, Pallas kernels, body(): call(functools.partial(lift_near_kernel, grid), [table, aimed_table, sums...  3.2 us
    pallas_call x1, Pallas kernels, body(): call(functools.partial(near_kernel, grid), [far_lists, far_lists, aimed_t...  3.08 us
    pallas_call x1, Pallas kernels, body(): call(far_kernel, [((node_count, features), BF16)], [two_tables, pltpu.VME...  2.32 us
    pallas_call x1, Pallas kernels, body(): call(functools.partial(far_pool_kernel, grid), [table, *[((grid.packet, f...  1.71 us
    ppermute x1, waiting for transfers between devices, trade_packets(): over = lax.ppermute(far, 'sub', pairs)  1.36 us
    pallas_call x1, Pallas kernels, body(): call(turn_kernel, [table], [pltpu.VMEM((node_count, features), BF16), plt...  1.25 us
  transfers between devices with their start and end apart: 12, of which 7 were waited for; matrix products, arithmetic and copies ran while one was open for 0% of the time, Pallas kernels for 20%

profile of v8, /device:TPU:0, one launch (start us, length us, event | category | flops | bytes accessed | tf_op | source)
XLA Modules:
  0.0 37.8 jit_solution(7317830617729961564)
XLA Ops:
  0.0 1.3 %turn.1.table_ref = bf16[128,2048]{1,0:T(8,128)(2,1)S(1)} custom-call(bf16[2048,128]{1,0:T(8,128)(2,1)} %latent_hbm.1), custom_call_target="tpu_custom_call" | custom-call | bytes 4194304 | tf_op jit(solution)/shard_map/turn/pallas_call | solution.py:546
  1.3 0.0 copy-start.2
  1.3 0.0 copy-start.3
  1.3 0.0 copy-start.7
  1.3 0.8 %send.1 = (bf16[128,256]{1,0:T(8,128)(2,1)S(1)}, bf16[128,256]{1,0:T(8,128)(2,1)S(1)}, bf16[128,256]{1,0:T(8,128)(2,1)S(1)}) custom-call(bf16[128,2048]{1,0:T(8,128)(2,1)S(1)} %turn.1.table_ref, s32[1,4,256]{2,1,0:T(4,128)S(1)} %copy-done.8, bf16[2,4,128,128]{3,2,1,0:T(8,128)(2,1)S(1)} %copy-done), custom_call_target="tpu_custom_call" | custom-call | flops 1073741824 | bytes 4194304 | tf_op jit(solution)/shard_map/send/pallas_call | solution.py:554
  2.2 0.0 copy-start.9
  2.2 5.1 %collective-permute-start = (bf16[128,256]{1,0:T(8,128)(2,1)S(1)}, bf16[128,256]{1,0:T(8,128)(2,1)S(1)}, u32[]{:S(2)}, u32[]{:S(2)}) collective-permute-start(bf16[128,256]{1,0:T(8,128)(2,1)S(1)} %get-tuple-element.43), channel_id=1, source_target_pairs={{0,12},{4,8},{8,4},{12,0},{1,13},{5,9},{9,5},{13,1},{2,14},{6,10},... | collective-permute-start | bytes 196616 | tf_op jit(solution)/shard_map/ppermute | solution.py:496
  7.3 0.6 %collective-permute-start.2 = (bf16[128,256]{1,0:T(8,128)(2,1)S(1)}, bf16[128,256]{1,0:T(8,128)(2,1)S(1)}, u32[]{:S(2)}, u32[]{:S(2)}) collective-permute-start(bf16[128,256]{1,0:T(8,128)(2,1)S(1)} %get-tuple-element.45), channel_id=1, source_target_pairs={{0,4},{4,0},{8,12},{12,8},{1,5},{5,1},{9,13},{13,9},{2,6},{6,2},{1... | collective-permute-start | bytes 196616 | tf_op jit(solution)/shard_map/ppermute | solution.py:496
  8.0 3.1 %near.1 = (s32[4,768]{1,0:T(4,128)S(1)}, s32[4,768]{1,0:T(4,128)S(1)}, bf16[128,3072]{1,0:T(8,128)(2,1)S(1)}, f32[128,2048]{1,0:T(8,128)S(1)}, bf16[128,256]{1,0...) custom-call(bf16[128,2048]{1,0:T(8,128)(2,1)S(1)} %turn.1.table_ref, ...), custom_call_target="tpu_custom_call" | custom-call | flops 4294967296 | bytes 4194304 | tf_op jit(solution)/shard_map/near/pallas_call | solution.py:558
  11.1 1.8 %collective-permute-done.1.rest_3_ = bf16[128,256]{1,0:T(8,128)(2,1)S(1)} collective-permute-done((bf16[128,256]{1,0:T(8,128)(2,1)S(1)}, bf16[128,256]{1,0:T(8,128)(2,1)S(1)}, u32[]{:S(2)}, u32[]{:S(2)}) %collective-permute-start.1) | collective-permute-done | bytes 65568 | tf_op jit(solution)/shard_map/ppermute | solution.py:496
  12.9 1.7 %far_pool.1 = (bf16[128,2048]{1,0:T(8,128)(2,1)S(1)}, bf16[80,128]{1,0:T(8,128)(2,1)S(1)}, bf16[80,128]{1,0:T(8,128)(2,1)S(1)}) custom-call(bf16[128,2048]{1,0:T(8,128)(2,1)S(1)} %turn.1.table_ref, bf16[128,3072]{1,0:T(8,128)(2,1)S(1)} %get-tuple-element.35.aimed_ref, s32[4,768]{1,0:T(4,128)S(1)} %get-tuple-element.36.sources_ref, ...), custom_call_target="tpu_custom_call" | custom-call | flops 2147483648 | bytes 4194304 | tf_op jit(solution)/shard_map/far_pool/pallas_call | solution.py:573
  14.6 1.0 %collective-permute-start.5 = (bf16[80,128]{1,0:T(8,128)(2,1)S(1)}, bf16[80,128]{1,0:T(8,128)(2,1)S(1)}, u32[]{:S(2)}, u32[]{:S(2)}) collective-permute-start(bf16[80,128]{1,0:T(8,128)(2,1)S(1)} %get-tuple-element.48), channel_id=1, source_target_pairs={{0,3},{1,2},{2,1},{3,0},{4,7},{5,6},{6,5},{7,4},{8,11},{9,10},{10,... | collective-permute-start | bytes 61448 | tf_op jit(solution)/shard_map/ppermute | solution.py:507
  15.6 0.6 %collective-permute-start.4 = (bf16[80,128]{1,0:T(8,128)(2,1)S(1)}, bf16[80,128]{1,0:T(8,128)(2,1)S(1)}, u32[]{:S(2)}, u32[]{:S(2)}) collective-permute-start(bf16[80,128]{1,0:T(8,128)(2,1)S(1)} %get-tuple-element.48), channel_id=1, source_target_pairs={{0,2},{2,0},{1,3},{3,1},{4,6},{6,4},{5,7},{7,5},{8,10},{10,8},{9,1... | collective-permute-start | bytes 61448 | tf_op jit(solution)/shard_map/ppermute | solution.py:505
  16.2 0.3 collective-permute-start.3
  16.5 0.6 %ahead.1.ahead_ref = bf16[144,768]{1,0:T(8,128)(2,1)S(1)} custom-call(bf16[128,2048]{1,0:T(8,128)(2,1)S(1)} %get-tuple-element.46.first_ref, s32[16,128]{1,0:T(8,128)S(1)} %bitcast.1, s32[1,4,256]{2,1,0:T(4,128)S(1)} %copy-done.8), custom_call_target="tpu_custom_call" | custom-call | flops 1073741824 | bytes 4194304 | tf_op jit(solution)/shard_map/ahead/pallas_call | solution.py:581
  17.2 0.0 copy-start.4
  17.2 0.8 %collective-permute-done.5.refs_3_ = bf16[80,128]{1,0:T(8,128)(2,1)S(1)} collective-permute-done((bf16[80,128]{1,0:T(8,128)(2,1)S(1)}, bf16[80,128]{1,0:T(8,128)(2,1)S(1)}, u32[]{:S(2)}, u32[]{:S(2)}) %collective-permute-start.5) | collective-permute-done | bytes 20512 | tf_op jit(solution)/shard_map/ppermute | solution.py:507
  18.0 1.4 %collective-permute-done.4.refs_2_ = bf16[80,128]{1,0:T(8,128)(2,1)S(1)} collective-permute-done((bf16[80,128]{1,0:T(8,128)(2,1)S(1)}, bf16[80,128]{1,0:T(8,128)(2,1)S(1)}, u32[]{:S(2)}, u32[]{:S(2)}) %collective-permute-start.4) | collective-permute-done | bytes 20512 | tf_op jit(solution)/shard_map/ppermute | solution.py:505
  19.4 0.4 coarse_send.1
  19.8 0.8 %collective-permute-start.6 = (bf16[128,128]{1,0:T(8,128)(2,1)S(1)}, bf16[128,128]{1,0:T(8,128)(2,1)S(1)}, u32[]{:S(2)}, u32[]{:S(2)}) collective-permute-start(bf16[128,128]{1,0:T(8,128)(2,1)S(1)} %get-tuple-element.54), channel_id=1, source_target_pairs={{0,8},{4,12},{8,0},{12,4},{1,9},{5,13},{9,1},{13,5},{2,10},{6,14},... | collective-permute-start | bytes 98312 | tf_op jit(solution)/shard_map/ppermute | solution.py:496
  20.6 1.9 %collective-permute-start.7 = (bf16[128,128]{1,0:T(8,128)(2,1)S(1)}, bf16[128,128]{1,0:T(8,128)(2,1)S(1)}, u32[]{:S(2)}, u32[]{:S(2)}) collective-permute-start(bf16[128,128]{1,0:T(8,128)(2,1)S(1)} %get-tuple-element.55), channel_id=1, source_target_pairs={{0,12},{4,8},{8,4},{12,0},{1,13},{5,9},{9,5},{13,1},{2,14},{6,10},... | collective-permute-start | bytes 98312 | tf_op jit(solution)/shard_map/ppermute | solution.py:496
  22.4 0.9 %collective-permute-start.8 = (bf16[128,128]{1,0:T(8,128)(2,1)S(1)}, bf16[128,128]{1,0:T(8,128)(2,1)S(1)}, u32[]{:S(2)}, u32[]{:S(2)}) collective-permute-start(bf16[128,128]{1,0:T(8,128)(2,1)S(1)} %get-tuple-element.56), channel_id=1, source_target_pairs={{0,4},{4,0},{8,12},{12,8},{1,5},{5,1},{9,13},{13,9},{2,6},{6,2},{1... | collective-permute-start | bytes 98312 | tf_op jit(solution)/shard_map/ppermute | solution.py:496
  23.3 0.5 %coarse_own.1 = (f32[1,128,768]{2,1,0:T(8,128)S(1)}, s32[1,768]{1,0:T(1,128)S(1)}, s32[1,768]{1,0:T(1,128)S(1)}, bf16[1,128,64]{2,1,0:T(8,128)(2,1)S(1)}, bf16[128,512]{1,0:T(8,128)(2,1)S(1)}) custom-call(bf16[4,128,128]{2,1,0:T(8,128)(2,1)S(1)} %copy-done.1, bf16[128,128]{1,0:T(8,128)(2,1)S(1)} %copy-done.4, bf16[2,4,128,128]{3,2,1,0:T(8,128)(2,1)S(1)} %copy-done, ...), custom_call_target="tpu_custom_call" | custom-call | flops 4294967296 | bytes 4194304 | tf_op jit(solution)/shard_map/coarse_own/pallas_call | solution.py:593
  23.8 1.1 %collective-permute-done.6.rest_0_ = bf16[128,128]{1,0:T(8,128)(2,1)S(1)} collective-permute-done((bf16[128,128]{1,0:T(8,128)(2,1)S(1)}, bf16[128,128]{1,0:T(8,128)(2,1)S(1)}, u32[]{:S(2)}, u32[]{:S(2)}) %collective-permute-start.6) | collective-permute-done | bytes 32800 | tf_op jit(solution)/shard_map/ppermute | solution.py:496
  24.9 1.4 %collective-permute-done.7.rest_1_ = bf16[128,128]{1,0:T(8,128)(2,1)S(1)} collective-permute-done((bf16[128,128]{1,0:T(8,128)(2,1)S(1)}, bf16[128,128]{1,0:T(8,128)(2,1)S(1)}, u32[]{:S(2)}, u32[]{:S(2)}) %collective-permute-start.7) | collective-permute-done | bytes 32800 | tf_op jit(solution)/shard_map/ppermute | solution.py:496
  26.3 0.3 collective-permute-done.8.rest_2_
  26.6 1.1 %lift_halo.1 = (bf16[128,128]{1,0:T(8,128)(2,1)S(1)}, bf16[128,256]{1,0:T(8,128)(2,1)S(1)}, bf16[128,256]{1,0:T(8,128)(2,1)S(1)}, bf16[128,256]{1,0:T(8,128)(2,1)S(1)}) custom-call(f32[1,128,768]{2,1,0:T(8,128)S(1)} %get-tuple-element.49.picked_ref, s32[1,768]{1,0:T(1,128)S(1)} %get-tuple-element.50.source_ref, s32[1,768]{1,0:T(1,128)S(1)} %get-tuple-element.51.place_ref, ...), custom_call_target="tpu_custom_call" | custom-call | flops 1073741824 | bytes 4194304 | tf_op jit(solution)/shard_map/lift_halo/pallas_call | solution.py:606
  27.8 1.9 %collective-permute-start.9 = (bf16[128,256]{1,0:T(8,128)(2,1)S(1)}, bf16[128,256]{1,0:T(8,128)(2,1)S(1)}, u32[]{:S(2)}, u32[]{:S(2)}) collective-permute-start(bf16[128,256]{1,0:T(8,128)(2,1)S(1)} %get-tuple-element.62), channel_id=1, source_target_pairs={{0,12},{4,8},{8,4},{12,0},{1,13},{5,9},{9,5},{13,1},{2,14},{6,10},... | collective-permute-start | bytes 196616 | tf_op jit(solution)/shard_map/ppermute | solution.py:496
  29.7 2.5 %collective-permute-start.11 = (bf16[128,256]{1,0:T(8,128)(2,1)S(1)}, bf16[128,256]{1,0:T(8,128)(2,1)S(1)}, u32[]{:S(2)}, u32[]{:S(2)}) collective-permute-start(bf16[128,256]{1,0:T(8,128)(2,1)S(1)} %get-tuple-element.64), channel_id=1, source_target_pairs={{0,8},{4,12},{8,0},{12,4},{1,9},{5,13},{9,1},{13,5},{2,10},{6,14},... | collective-permute-start | bytes 196616 | tf_op jit(solution)/shard_map/ppermute | solution.py:496
  32.2 3.2 %lift_near.1 = (bf16[128,2048]{1,0:T(8,128)(2,1)S(1)}, bf16[128,3072]{1,0:T(8,128)(2,1)S(1)}, f32[128,2048]{1,0:T(8,128)S(1)}, bf16[128,256]{1,0:T(8,128)(2,1)S(1)}) custom-call(bf16[128,2048]{1,0:T(8,128)(2,1)S(1)} %get-tuple-element.46.first_ref, bf16[128,128]{1,0:T(8,128)(2,1)S(1)} %get-tuple-element.57.prolonged_ref, s32[16,128]{1,0:T(8,128)S(1)} %bitcast.2, ...), custom_call_target="tpu_custom_call" | custom-call | flops 4294967296 | bytes 4194304 | tf_op jit(solution)/shard_map/lift_near/pallas_call | solution.py:613
  35.4 0.1 collective-permute-done.11.rest_2_
  35.5 2.3 %far.1 = bf16[2048,128]{1,0:T(8,128)(2,1)} custom-call(bf16[128,2048]{1,0:T(8,128)(2,1)S(1)} %get-tuple-element.58.table_ref, bf16[128,3072]{1,0:T(8,128)(2,1)S(1)} %get-tuple-element.59.aimed_ref, s32[4,768]{1,0:T(4,128)S(1)} %get-tuple-element.36.sources_ref, s32[4,768]{1,0:T(4,128)S(1)} %get-tuple-element.37.places_ref, ...), custom_call_target="tpu_custom_call" | custom-call | flops 2147483648 | bytes 4194304 | tf_op jit(solution)/shard_map/far/pallas_call | solution.py:620
  (24 shorter events, 0.1 us)
Async XLA Ops:
  0.0 1.3 %copy-start = (bf16[2,4,128,128]{3,2,1,0:T(8,128)(2,1)S(1)}, bf16[2,4,128,128]{3,2,1,0:T(8,128)(2,1)}, u32[]{:S(2)}) copy-start(bf16[2,4,128,128]{3,2,1,0:T(8,128)(2,1)} %weights_ref.9) | copy-start | bytes 786436
  0.0 1.3 %copy-start.8 = (s32[1,4,256]{2,1,0:T(4,128)S(1)}, s32[1,4,256]{2,1,0:T(4,128)}, u32[]{:S(2)}) copy-start(s32[1,4,256]{2,1,0:T(4,128)} %lists_ref.3) | copy-start | bytes 12292
  1.3 6.6 %copy-start.2 = (s32[16,768]{1,0:T(8,128)S(1)}, s32[16,768]{1,0:T(8,128)}, u32[]{:S(2)}) copy-start(s32[16,768]{1,0:T(8,128)} %source_ref.3) | copy-start | bytes 147460
  1.3 6.6 %copy-start.3 = (s32[16,768]{1,0:T(8,128)S(1)}, s32[16,768]{1,0:T(8,128)}, u32[]{:S(2)}) copy-start(s32[16,768]{1,0:T(8,128)} %place_ref.3) | copy-start | bytes 147460
  1.3 6.6 %copy-start.6 = (s32[2,768]{1,0:T(2,128)S(1)}, s32[2,768]{1,0:T(2,128)}, u32[]{:S(2)}) copy-start(s32[2,768]{1,0:T(2,128)} %coarse_source_ref.1) | copy-start | bytes 18436
  1.3 6.6 %copy-start.7 = (s32[2,768]{1,0:T(2,128)S(1)}, s32[2,768]{1,0:T(2,128)}, u32[]{:S(2)}) copy-start(s32[2,768]{1,0:T(2,128)} %coarse_place_ref.1) | copy-start | bytes 18436
  2.1 5.8 %copy-start.10 = (s32[1,4,64]{2,1,0:T(4,128)S(1)}, s32[1,4,64]{2,1,0:T(4,128)}, u32[]{:S(2)}) copy-start(s32[1,4,64]{2,1,0:T(4,128)} %pool_ref.1) | copy-start | bytes 3076
  2.2 5.8 %copy-start.9 = (s32[1,4,128]{2,1,0:T(4,128)S(1)}, s32[1,4,128]{2,1,0:T(4,128)}, u32[]{:S(2)}) copy-start(s32[1,4,128]{2,1,0:T(4,128)} %coarse_send_ref.1) | copy-start | bytes 6148
  2.2 8.9 %collective-permute-start = (bf16[128,256]{1,0:T(8,128)(2,1)S(1)}, bf16[128,256]{1,0:T(8,128)(2,1)S(1)}, u32[]{:S(2)}, u32[]{:S(2)}) collective-permute-start(bf16[128,256]{1,0:T(8,128)(2,1)S(1)} %get-tuple-element.43), channel_id=1, source_target_pairs={{0,12},{4,8},{8,4},{12,0},{1,13},{5,9},{9,5},{13,1},{2,14},{6,10},... | collective-permute-start | bytes 196616 | tf_op jit(solution)/shard_map/ppermute | solution.py:496
  7.3 5.6 %collective-permute-start.1 = (bf16[128,256]{1,0:T(8,128)(2,1)S(1)}, bf16[128,256]{1,0:T(8,128)(2,1)S(1)}, u32[]{:S(2)}, u32[]{:S(2)}) collective-permute-start(bf16[128,256]{1,0:T(8,128)(2,1)S(1)} %get-tuple-element.44), channel_id=1, source_target_pairs={{0,8},{4,12},{8,0},{12,4},{1,9},{5,13},{9,1},{13,5},{2,10},{6,14},... | collective-permute-start | bytes 196616 | tf_op jit(solution)/shard_map/ppermute | solution.py:496
  7.3 5.6 %collective-permute-start.2 = (bf16[128,256]{1,0:T(8,128)(2,1)S(1)}, bf16[128,256]{1,0:T(8,128)(2,1)S(1)}, u32[]{:S(2)}, u32[]{:S(2)}) collective-permute-start(bf16[128,256]{1,0:T(8,128)(2,1)S(1)} %get-tuple-element.45), channel_id=1, source_target_pairs={{0,4},{4,0},{8,12},{12,8},{1,5},{5,1},{9,13},{13,9},{2,6},{6,2},{1... | collective-permute-start | bytes 196616 | tf_op jit(solution)/shard_map/ppermute | solution.py:496
  12.9 3.6 %copy-start.5 = (s32[2048]{0:T(1024)S(1)}, s32[2048]{0:T(1024)}, u32[]{:S(2)}) copy-start(s32[2048]{0:T(1024)} %param.20) | copy-start | bytes 24580
  14.6 3.4 %collective-permute-start.5 = (bf16[80,128]{1,0:T(8,128)(2,1)S(1)}, bf16[80,128]{1,0:T(8,128)(2,1)S(1)}, u32[]{:S(2)}, u32[]{:S(2)}) collective-permute-start(bf16[80,128]{1,0:T(8,128)(2,1)S(1)} %get-tuple-element.48), channel_id=1, source_target_pairs={{0,3},{1,2},{2,1},{3,0},{4,7},{5,6},{6,5},{7,4},{8,11},{9,10},{10,... | collective-permute-start | bytes 61448 | tf_op jit(solution)/shard_map/ppermute | solution.py:507
  15.6 3.8 %collective-permute-start.4 = (bf16[80,128]{1,0:T(8,128)(2,1)S(1)}, bf16[80,128]{1,0:T(8,128)(2,1)S(1)}, u32[]{:S(2)}, u32[]{:S(2)}) collective-permute-start(bf16[80,128]{1,0:T(8,128)(2,1)S(1)} %get-tuple-element.48), channel_id=1, source_target_pairs={{0,2},{2,0},{1,3},{3,1},{4,6},{6,4},{5,7},{7,5},{8,10},{10,8},{9,1... | collective-permute-start | bytes 61448 | tf_op jit(solution)/shard_map/ppermute | solution.py:505
  16.2 3.2 %collective-permute-start.3 = (bf16[80,128]{1,0:T(8,128)(2,1)S(1)}, bf16[80,128]{1,0:T(8,128)(2,1)S(1)}, u32[]{:S(2)}, u32[]{:S(2)}) collective-permute-start(bf16[80,128]{1,0:T(8,128)(2,1)S(1)} %get-tuple-element.47.refs_0_), channel_id=1, source_target_pairs={{0,1},{1,0},{2,3},{3,2},{4,5},{5,4},{6,7},{7,6},{8,9},{9,8},{10,11... | collective-permute-start | bytes 61448 | tf_op jit(solution)/shard_map/ppermute | solution.py:506
  16.5 2.9 %copy-start.1 = (bf16[4,128,128]{2,1,0:T(8,128)(2,1)S(1)}, bf16[4,128,128]{2,1,0:T(8,128)(2,1)}, u32[]{:S(2)}) copy-start(bf16[4,128,128]{2,1,0:T(8,128)(2,1)} %weights_ref.8) | copy-start | bytes 393220
  17.2 6.2 %copy-start.4 = (bf16[128,128]{1,0:T(8,128)(2,1)S(1)}, bf16[128,128]{1,0:T(8,128)(2,1)}, u32[]{:S(2)}) copy-start(bf16[128,128]{1,0:T(8,128)(2,1)} %prolong_weight_ref.1) | copy-start | bytes 98308
  19.8 5.2 %collective-permute-start.6 = (bf16[128,128]{1,0:T(8,128)(2,1)S(1)}, bf16[128,128]{1,0:T(8,128)(2,1)S(1)}, u32[]{:S(2)}, u32[]{:S(2)}) collective-permute-start(bf16[128,128]{1,0:T(8,128)(2,1)S(1)} %get-tuple-element.54), channel_id=1, source_target_pairs={{0,8},{4,12},{8,0},{12,4},{1,9},{5,13},{9,1},{13,5},{2,10},{6,14},... | collective-permute-start | bytes 98312 | tf_op jit(solution)/shard_map/ppermute | solution.py:496
  20.6 5.7 %collective-permute-start.7 = (bf16[128,128]{1,0:T(8,128)(2,1)S(1)}, bf16[128,128]{1,0:T(8,128)(2,1)S(1)}, u32[]{:S(2)}, u32[]{:S(2)}) collective-permute-start(bf16[128,128]{1,0:T(8,128)(2,1)S(1)} %get-tuple-element.55), channel_id=1, source_target_pairs={{0,12},{4,8},{8,4},{12,0},{1,13},{5,9},{9,5},{13,1},{2,14},{6,10},... | collective-permute-start | bytes 98312 | tf_op jit(solution)/shard_map/ppermute | solution.py:496
  22.4 4.2 %collective-permute-start.8 = (bf16[128,128]{1,0:T(8,128)(2,1)S(1)}, bf16[128,128]{1,0:T(8,128)(2,1)S(1)}, u32[]{:S(2)}, u32[]{:S(2)}) collective-permute-start(bf16[128,128]{1,0:T(8,128)(2,1)S(1)} %get-tuple-element.56), channel_id=1, source_target_pairs={{0,4},{4,0},{8,12},{12,8},{1,5},{5,1},{9,13},{13,9},{2,6},{6,2},{1... | collective-permute-start | bytes 98312 | tf_op jit(solution)/shard_map/ppermute | solution.py:496
  27.8 7.7 %collective-permute-start.9 = (bf16[128,256]{1,0:T(8,128)(2,1)S(1)}, bf16[128,256]{1,0:T(8,128)(2,1)S(1)}, u32[]{:S(2)}, u32[]{:S(2)}) collective-permute-start(bf16[128,256]{1,0:T(8,128)(2,1)S(1)} %get-tuple-element.62), channel_id=1, source_target_pairs={{0,12},{4,8},{8,4},{12,0},{1,13},{5,9},{9,5},{13,1},{2,14},{6,10},... | collective-permute-start | bytes 196616 | tf_op jit(solution)/shard_map/ppermute | solution.py:496
  29.7 5.7 %collective-permute-start.10 = (bf16[128,256]{1,0:T(8,128)(2,1)S(1)}, bf16[128,256]{1,0:T(8,128)(2,1)S(1)}, u32[]{:S(2)}, u32[]{:S(2)}) collective-permute-start(bf16[128,256]{1,0:T(8,128)(2,1)S(1)} %get-tuple-element.63), channel_id=1, source_target_pairs={{0,4},{4,0},{8,12},{12,8},{1,5},{5,1},{9,13},{13,9},{2,6},{6,2},{1... | collective-permute-start | bytes 196616 | tf_op jit(solution)/shard_map/ppermute | solution.py:496
  29.7 5.8 %collective-permute-start.11 = (bf16[128,256]{1,0:T(8,128)(2,1)S(1)}, bf16[128,256]{1,0:T(8,128)(2,1)S(1)}, u32[]{:S(2)}, u32[]{:S(2)}) collective-permute-start(bf16[128,256]{1,0:T(8,128)(2,1)S(1)} %get-tuple-element.64), channel_id=1, source_target_pairs={{0,8},{4,12},{8,0},{12,4},{1,9},{5,13},{9,1},{13,5},{2,10},{6,14},... | collective-permute-start | bytes 196616 | tf_op jit(solution)/shard_map/ppermute | solution.py:496

commit v9 on v7

--- a/solution.py
+++ b/solution.py
@@ -12,7 +12,7 @@
 I32 = jnp.int32
 BLOCK = 128
 VMEM_BYTES = 32 << 20
-BATCH = 4
+BATCH = 8
 FIRST_ORDER, SECOND_ORDER = (1, 0, 2), (1, 2, 0)
 PARTS = 2
 PAIR = 1
@@ -254,14 +254,11 @@
         change = silu_of_half(dot(update_weights, both_ref[:, columns]))
         write(columns, (both_ref[features:, columns].astype(F32) + change).astype(BF16))
 
-    message = messages(0)
+    held = [messages(batch) for batch in range(batch_count)]
     for batch in range(batch_count):
-        following = messages(batch + 1) if batch + 1 < batch_count else None
-        add_up(batch, message)
-        if batch:
-            update(batch - 1)
-        message = following
-    update(batch_count - 1)
+        add_up(batch, held[batch])
+    for batch in range(batch_count):
+        update(batch)
 
 
 def lane_rows(values):
@@ -441,7 +438,7 @@
     parts = jnp.concatenate([high, low], axis=1)
     prolonged_ref[...] = parts
     weight = turned(weights_ref[1, 0])
-    index_row = ahead_ref[features : features + 1, :].astype(F32).astype(I32)
+    index_row = ahead_ref[features : features + 16, :].astype(F32).astype(I32)[:1]
     lifted = lift(ahead_ref[:features, :], parts, index_row)
     terms = dot(weight, lifted).astype(BF16)
     capacity = sent_refs[0].shape[1]

time: 38 us -> 37.8 us (level)
  transfers between devices with their start and end apart: 12 -> 12, of which waited for: 6 -> 7; matrix products, arithmetic and copies ran while one was open for 0% -> 0% of each run, Pallas kernels for 20% -> 20%
where the time goes in v9:
time: 37.8 us; the launch traced here: 37.7 us
  starting transfers between devices  15.7 us (42%)
  Pallas kernels  14.9 us (39%)
  waiting for transfers between devices  6.95 us (18%)
    ppermute x9, starting transfers between devices, swap_dom(): lax.ppermute(array, 'dom', [(dom, grid.partner(dom, step)) for dom in ran...  13.8 us
    ppermute x9, waiting for transfers between devices, swap_dom(): lax.ppermute(array, 'dom', [(dom, grid.partner(dom, step)) for dom in ran...  4.73 us
    pallas_call x1, Pallas kernels, body(): call(functools.partial(lift_near_kernel, grid), [table, aimed_table, sums...  3.21 us
    pallas_call x1, Pallas kernels, body(): call(functools.partial(near_kernel, grid), [far_lists, far_lists, aimed_t...  3.08 us
    pallas_call x1, Pallas kernels, body(): call(far_kernel, [((node_count, features), BF16)], [two_tables, pltpu.VME...  2.24 us
    pallas_call x1, Pallas kernels, body(): call(functools.partial(far_pool_kernel, grid), [table, *[((grid.packet, f...  1.63 us
    ppermute x1, waiting for transfers between devices, trade_packets(): over = lax.ppermute(far, 'sub', pairs)  1.36 us
    pallas_call x1, Pallas kernels, body(): call(turn_kernel, [table], [pltpu.VMEM((node_count, features), BF16), plt...  1.25 us
  transfers between devices with their start and end apart: 12, of which 7 were waited for; matrix products, arithmetic and copies ran while one was open for 0% of the time, Pallas kernels for 20%

profile of v9, /device:TPU:0, one launch (start us, length us, event | category | flops | bytes accessed | tf_op | source)
XLA Modules:
  0.0 37.7 jit_solution(10010499273406834143)
XLA Ops:
  0.0 1.3 %turn.1.table_ref = bf16[128,2048]{1,0:T(8,128)(2,1)S(1)} custom-call(bf16[2048,128]{1,0:T(8,128)(2,1)} %latent_hbm.1), custom_call_target="tpu_custom_call" | custom-call | bytes 4194304 | tf_op jit(solution)/shard_map/turn/pallas_call | solution.py:534
  1.3 0.0 copy-start.2
  1.3 0.0 copy-start.3
  1.3 0.0 copy-start.7
  1.3 0.8 %send.1 = (bf16[128,256]{1,0:T(8,128)(2,1)S(1)}, bf16[128,256]{1,0:T(8,128)(2,1)S(1)}, bf16[128,256]{1,0:T(8,128)(2,1)S(1)}) custom-call(bf16[128,2048]{1,0:T(8,128)(2,1)S(1)} %turn.1.table_ref, s32[1,4,256]{2,1,0:T(4,128)S(1)} %copy-done.8, bf16[2,4,128,128]{3,2,1,0:T(8,128)(2,1)S(1)} %copy-done), custom_call_target="tpu_custom_call" | custom-call | flops 1073741824 | bytes 4194304 | tf_op jit(solution)/shard_map/send/pallas_call | solution.py:542
  2.1 0.0 copy-start.10
  2.2 0.0 copy-start.9
  2.2 5.1 %collective-permute-start = (bf16[128,256]{1,0:T(8,128)(2,1)S(1)}, bf16[128,256]{1,0:T(8,128)(2,1)S(1)}, u32[]{:S(2)}, u32[]{:S(2)}) collective-permute-start(bf16[128,256]{1,0:T(8,128)(2,1)S(1)} %get-tuple-element.39), channel_id=1, source_target_pairs={{0,12},{4,8},{8,4},{12,0},{1,13},{5,9},{9,5},{13,1},{2,14},{6,10},... | collective-permute-start | bytes 196616 | tf_op jit(solution)/shard_map/ppermute | solution.py:485
  7.3 0.6 %collective-permute-start.2 = (bf16[128,256]{1,0:T(8,128)(2,1)S(1)}, bf16[128,256]{1,0:T(8,128)(2,1)S(1)}, u32[]{:S(2)}, u32[]{:S(2)}) collective-permute-start(bf16[128,256]{1,0:T(8,128)(2,1)S(1)} %get-tuple-element.41), channel_id=1, source_target_pairs={{0,4},{4,0},{8,12},{12,8},{1,5},{5,1},{9,13},{13,9},{2,6},{6,2},{1... | collective-permute-start | bytes 196616 | tf_op jit(solution)/shard_map/ppermute | solution.py:485
  8.0 3.1 %near.1 = (s32[2,1536]{1,0:T(2,128)S(1)}, s32[2,1536]{1,0:T(2,128)S(1)}, bf16[128,3072]{1,0:T(8,128)(2,1)S(1)}, f32[128,2048]{1,0:T(8,128)S(1)}, s32[1,64]{1,0:T...) custom-call(bf16[128,2048]{1,0:T(8,128)(2,1)S(1)} %turn.1.table_ref, s32[16,768]{1,0:T(8,128)S(1)} %copy-done.2, ...), custom_call_target="tpu_custom_call" | custom-call | flops 4294967296 | bytes 4194304 | tf_op jit(solution)/shard_map/near/pallas_call | solution.py:546
  11.1 1.8 %collective-permute-done.1.rest_3_ = bf16[128,256]{1,0:T(8,128)(2,1)S(1)} collective-permute-done((bf16[128,256]{1,0:T(8,128)(2,1)S(1)}, bf16[128,256]{1,0:T(8,128)(2,1)S(1)}, u32[]{:S(2)}, u32[]{:S(2)}) %collective-permute-start.1) | collective-permute-done | bytes 65568 | tf_op jit(solution)/shard_map/ppermute | solution.py:485
  12.9 1.6 %far_pool.1 = (bf16[128,2048]{1,0:T(8,128)(2,1)S(1)}, bf16[80,128]{1,0:T(8,128)(2,1)S(1)}, bf16[80,128]{1,0:T(8,128)(2,1)S(1)}) custom-call(bf16[128,2048]{1,0:T(8,128)(2,1)S(1)} %turn.1.table_ref, bf16[128,3072]{1,0:T(8,128)(2,1)S(1)} %get-tuple-element.32.aimed_ref, s32[2,1536]{1,0:T(2,128)S(1)} %get-tuple-element.33.sources_ref, ...), custom_call_target="tpu_custom_call" | custom-call | flops 2147483648 | bytes 4194304 | tf_op jit(solution)/shard_map/far_pool/pallas_call | solution.py:560
  14.5 1.0 %collective-permute-start.5 = (bf16[80,128]{1,0:T(8,128)(2,1)S(1)}, bf16[80,128]{1,0:T(8,128)(2,1)S(1)}, u32[]{:S(2)}, u32[]{:S(2)}) collective-permute-start(bf16[80,128]{1,0:T(8,128)(2,1)S(1)} %get-tuple-element.44), channel_id=1, source_target_pairs={{0,3},{1,2},{2,1},{3,0},{4,7},{5,6},{6,5},{7,4},{8,11},{9,10},{10,... | collective-permute-start | bytes 61448 | tf_op jit(solution)/shard_map/ppermute | solution.py:496
  15.5 0.6 %collective-permute-start.4 = (bf16[80,128]{1,0:T(8,128)(2,1)S(1)}, bf16[80,128]{1,0:T(8,128)(2,1)S(1)}, u32[]{:S(2)}, u32[]{:S(2)}) collective-permute-start(bf16[80,128]{1,0:T(8,128)(2,1)S(1)} %get-tuple-element.44), channel_id=1, source_target_pairs={{0,2},{2,0},{1,3},{3,1},{4,6},{6,4},{5,7},{7,5},{8,10},{10,8},{9,1... | collective-permute-start | bytes 61448 | tf_op jit(solution)/shard_map/ppermute | solution.py:494
  16.1 0.3 collective-permute-start.3
  16.4 0.6 %ahead.1.ahead_ref = bf16[144,768]{1,0:T(8,128)(2,1)S(1)} custom-call(bf16[128,2048]{1,0:T(8,128)(2,1)S(1)} %get-tuple-element.42.first_ref, s32[16,128]{1,0:T(8,128)S(1)} %bitcast.1, s32[1,4,256]{2,1,0:T(4,128)S(1)} %copy-done.8), custom_call_target="tpu_custom_call" | custom-call | flops 1073741824 | bytes 4194304 | tf_op jit(solution)/shard_map/ahead/pallas_call | solution.py:568
  17.1 0.9 %collective-permute-done.5.refs_3_ = bf16[80,128]{1,0:T(8,128)(2,1)S(1)} collective-permute-done((bf16[80,128]{1,0:T(8,128)(2,1)S(1)}, bf16[80,128]{1,0:T(8,128)(2,1)S(1)}, u32[]{:S(2)}, u32[]{:S(2)}) %collective-permute-start.5) | collective-permute-done | bytes 20512 | tf_op jit(solution)/shard_map/ppermute | solution.py:496
  17.9 1.4 %collective-permute-done.4.refs_2_ = bf16[80,128]{1,0:T(8,128)(2,1)S(1)} collective-permute-done((bf16[80,128]{1,0:T(8,128)(2,1)S(1)}, bf16[80,128]{1,0:T(8,128)(2,1)S(1)}, u32[]{:S(2)}, u32[]{:S(2)}) %collective-permute-start.4) | collective-permute-done | bytes 20512 | tf_op jit(solution)/shard_map/ppermute | solution.py:494
  19.3 0.4 coarse_send.1
  19.7 0.8 %collective-permute-start.6 = (bf16[128,128]{1,0:T(8,128)(2,1)S(1)}, bf16[128,128]{1,0:T(8,128)(2,1)S(1)}, u32[]{:S(2)}, u32[]{:S(2)}) collective-permute-start(bf16[128,128]{1,0:T(8,128)(2,1)S(1)} %get-tuple-element.49), channel_id=1, source_target_pairs={{0,8},{4,12},{8,0},{12,4},{1,9},{5,13},{9,1},{13,5},{2,10},{6,14},... | collective-permute-start | bytes 98312 | tf_op jit(solution)/shard_map/ppermute | solution.py:485
  20.5 1.9 %collective-permute-start.7 = (bf16[128,128]{1,0:T(8,128)(2,1)S(1)}, bf16[128,128]{1,0:T(8,128)(2,1)S(1)}, u32[]{:S(2)}, u32[]{:S(2)}) collective-permute-start(bf16[128,128]{1,0:T(8,128)(2,1)S(1)} %get-tuple-element.50), channel_id=1, source_target_pairs={{0,12},{4,8},{8,4},{12,0},{1,13},{5,9},{9,5},{13,1},{2,14},{6,10},... | collective-permute-start | bytes 98312 | tf_op jit(solution)/shard_map/ppermute | solution.py:485
  22.3 0.9 %collective-permute-start.8 = (bf16[128,128]{1,0:T(8,128)(2,1)S(1)}, bf16[128,128]{1,0:T(8,128)(2,1)S(1)}, u32[]{:S(2)}, u32[]{:S(2)}) collective-permute-start(bf16[128,128]{1,0:T(8,128)(2,1)S(1)} %get-tuple-element.51), channel_id=1, source_target_pairs={{0,4},{4,0},{8,12},{12,8},{1,5},{5,1},{9,13},{13,9},{2,6},{6,2},{1... | collective-permute-start | bytes 98312 | tf_op jit(solution)/shard_map/ppermute | solution.py:485
  23.2 0.5 %coarse_own.1 = (f32[1,128,768]{2,1,0:T(8,128)S(1)}, s32[1,768]{1,0:T(1,128)S(1)}, s32[1,768]{1,0:T(1,128)S(1)}, bf16[1,128,64]{2,1,0:T(8,128)(2,1)S(1)}) custom-call(bf16[4,128,128]{2,1,0:T(8,128)(2,1)S(1)} %copy-done.1, bf16[80,128]{1,0:T(8,128)(2,1)S(1)} %get-tuple-element.43.refs_0_, bf16[80,128]{1,0:T(8,128)(2,1)S(1)} %collective-permute-done.3.refs_1_, ...), custom_call_target="tpu_custom_call" | custom-call | flops 4294967296 | bytes 4194304 | tf_op jit(solution)/shard_map/coarse_own/pallas_call | solution.py:580
  23.7 1.1 %collective-permute-done.6.rest_0_ = bf16[128,128]{1,0:T(8,128)(2,1)S(1)} collective-permute-done((bf16[128,128]{1,0:T(8,128)(2,1)S(1)}, bf16[128,128]{1,0:T(8,128)(2,1)S(1)}, u32[]{:S(2)}, u32[]{:S(2)}) %collective-permute-start.6) | collective-permute-done | bytes 32800 | tf_op jit(solution)/shard_map/ppermute | solution.py:485
  24.9 1.4 %collective-permute-done.7.rest_1_ = bf16[128,128]{1,0:T(8,128)(2,1)S(1)} collective-permute-done((bf16[128,128]{1,0:T(8,128)(2,1)S(1)}, bf16[128,128]{1,0:T(8,128)(2,1)S(1)}, u32[]{:S(2)}, u32[]{:S(2)}) %collective-permute-start.7) | collective-permute-done | bytes 32800 | tf_op jit(solution)/shard_map/ppermute | solution.py:485
  26.2 0.3 collective-permute-done.8.rest_2_
  26.5 1.1 %lift_halo.1 = (bf16[128,128]{1,0:T(8,128)(2,1)S(1)}, bf16[128,256]{1,0:T(8,128)(2,1)S(1)}, bf16[128,256]{1,0:T(8,128)(2,1)S(1)}, bf16[128,256]{1,0:T(8,128)(2,1)S(1)}) custom-call(f32[1,128,768]{2,1,0:T(8,128)S(1)} %get-tuple-element.45.picked_ref, s32[1,768]{1,0:T(1,128)S(1)} %get-tuple-element.46.source_ref, s32[1,768]{1,0:T(1,128)S(1)} %get-tuple-element.47.place_ref, ...), custom_call_target="tpu_custom_call" | custom-call | flops 1073741824 | bytes 4194304 | tf_op jit(solution)/shard_map/lift_halo/pallas_call | solution.py:592
  27.7 1.9 %collective-permute-start.9 = (bf16[128,256]{1,0:T(8,128)(2,1)S(1)}, bf16[128,256]{1,0:T(8,128)(2,1)S(1)}, u32[]{:S(2)}, u32[]{:S(2)}) collective-permute-start(bf16[128,256]{1,0:T(8,128)(2,1)S(1)} %get-tuple-element.56), channel_id=1, source_target_pairs={{0,12},{4,8},{8,4},{12,0},{1,13},{5,9},{9,5},{13,1},{2,14},{6,10},... | collective-permute-start | bytes 196616 | tf_op jit(solution)/shard_map/ppermute | solution.py:485
  29.6 2.5 %collective-permute-start.11 = (bf16[128,256]{1,0:T(8,128)(2,1)S(1)}, bf16[128,256]{1,0:T(8,128)(2,1)S(1)}, u32[]{:S(2)}, u32[]{:S(2)}) collective-permute-start(bf16[128,256]{1,0:T(8,128)(2,1)S(1)} %get-tuple-element.58), channel_id=1, source_target_pairs={{0,8},{4,12},{8,0},{12,4},{1,9},{5,13},{9,1},{13,5},{2,10},{6,14},... | collective-permute-start | bytes 196616 | tf_op jit(solution)/shard_map/ppermute | solution.py:485
  32.1 3.2 %lift_near.1 = (bf16[128,2048]{1,0:T(8,128)(2,1)S(1)}, bf16[128,3072]{1,0:T(8,128)(2,1)S(1)}, f32[128,2048]{1,0:T(8,128)S(1)}) custom-call(bf16[128,2048]{1,0:T(8,128)(2,1)S(1)} %get-tuple-element.42.first_ref, bf16[128,128]{1,0:T(8,128)(2,1)S(1)} %get-tuple-element.52.prolonged_ref, s32[16,128]{1,0:T(8,128)S(1)} %bitcast.2, s32[16,768]{1,0:T(8,128)S(1)} %copy-done.2, ...), custom_call_target="tpu_custom_call" | custom-call | flops 4294967296 | bytes 4194304 | tf_op jit(solution)/shard_map/lift_near/pallas_call | solution.py:599
  35.4 0.1 collective-permute-done.11.rest_2_
  35.4 2.2 %far.1 = bf16[2048,128]{1,0:T(8,128)(2,1)} custom-call(bf16[128,2048]{1,0:T(8,128)(2,1)S(1)} %get-tuple-element.53.table_ref, bf16[128,3072]{1,0:T(8,128)(2,1)S(1)} %get-tuple-element.54.aimed_ref, s32[2,1536]{1,0:T(2,128)S(1)} %get-tuple-element.33.sources_ref, s32[2,1536]{1,0:T(2,128)S(1)} %get-tuple-element.34.places_ref, ...), custom_call_target="tpu_custom_call" | custom-call | flops 2147483648 | bytes 4194304 | tf_op jit(solution)/shard_map/far/pallas_call | solution.py:606
  (24 shorter events, 0.1 us)
Async XLA Ops:
  0.0 1.3 %copy-start = (bf16[2,4,128,128]{3,2,1,0:T(8,128)(2,1)S(1)}, bf16[2,4,128,128]{3,2,1,0:T(8,128)(2,1)}, u32[]{:S(2)}) copy-start(bf16[2,4,128,128]{3,2,1,0:T(8,128)(2,1)} %weights_ref.15) | copy-start | bytes 786436
  0.0 1.3 %copy-start.8 = (s32[1,4,256]{2,1,0:T(4,128)S(1)}, s32[1,4,256]{2,1,0:T(4,128)}, u32[]{:S(2)}) copy-start(s32[1,4,256]{2,1,0:T(4,128)} %lists_ref.3) | copy-start | bytes 12292
  1.3 6.6 %copy-start.2 = (s32[16,768]{1,0:T(8,128)S(1)}, s32[16,768]{1,0:T(8,128)}, u32[]{:S(2)}) copy-start(s32[16,768]{1,0:T(8,128)} %source_ref.3) | copy-start | bytes 147460
  1.3 6.6 %copy-start.3 = (s32[16,768]{1,0:T(8,128)S(1)}, s32[16,768]{1,0:T(8,128)}, u32[]{:S(2)}) copy-start(s32[16,768]{1,0:T(8,128)} %place_ref.3) | copy-start | bytes 147460
  1.3 6.6 %copy-start.6 = (s32[2,768]{1,0:T(2,128)S(1)}, s32[2,768]{1,0:T(2,128)}, u32[]{:S(2)}) copy-start(s32[2,768]{1,0:T(2,128)} %coarse_source_ref.1) | copy-start | bytes 18436
  1.3 6.6 %copy-start.7 = (s32[2,768]{1,0:T(2,128)S(1)}, s32[2,768]{1,0:T(2,128)}, u32[]{:S(2)}) copy-start(s32[2,768]{1,0:T(2,128)} %coarse_place_ref.1) | copy-start | bytes 18436
  2.1 5.8 %copy-start.10 = (s32[1,4,64]{2,1,0:T(4,128)S(1)}, s32[1,4,64]{2,1,0:T(4,128)}, u32[]{:S(2)}) copy-start(s32[1,4,64]{2,1,0:T(4,128)} %pool_ref.1) | copy-start | bytes 3076
  2.2 5.8 %copy-start.9 = (s32[1,4,128]{2,1,0:T(4,128)S(1)}, s32[1,4,128]{2,1,0:T(4,128)}, u32[]{:S(2)}) copy-start(s32[1,4,128]{2,1,0:T(4,128)} %coarse_send_ref.1) | copy-start | bytes 6148
  2.2 8.9 %collective-permute-start = (bf16[128,256]{1,0:T(8,128)(2,1)S(1)}, bf16[128,256]{1,0:T(8,128)(2,1)S(1)}, u32[]{:S(2)}, u32[]{:S(2)}) collective-permute-start(bf16[128,256]{1,0:T(8,128)(2,1)S(1)} %get-tuple-element.39), channel_id=1, source_target_pairs={{0,12},{4,8},{8,4},{12,0},{1,13},{5,9},{9,5},{13,1},{2,14},{6,10},... | collective-permute-start | bytes 196616 | tf_op jit(solution)/shard_map/ppermute | solution.py:485
  7.3 5.6 %collective-permute-start.1 = (bf16[128,256]{1,0:T(8,128)(2,1)S(1)}, bf16[128,256]{1,0:T(8,128)(2,1)S(1)}, u32[]{:S(2)}, u32[]{:S(2)}) collective-permute-start(bf16[128,256]{1,0:T(8,128)(2,1)S(1)} %get-tuple-element.40), channel_id=1, source_target_pairs={{0,8},{4,12},{8,0},{12,4},{1,9},{5,13},{9,1},{13,5},{2,10},{6,14},... | collective-permute-start | bytes 196616 | tf_op jit(solution)/shard_map/ppermute | solution.py:485
  7.3 5.6 %collective-permute-start.2 = (bf16[128,256]{1,0:T(8,128)(2,1)S(1)}, bf16[128,256]{1,0:T(8,128)(2,1)S(1)}, u32[]{:S(2)}, u32[]{:S(2)}) collective-permute-start(bf16[128,256]{1,0:T(8,128)(2,1)S(1)} %get-tuple-element.41), channel_id=1, source_target_pairs={{0,4},{4,0},{8,12},{12,8},{1,5},{5,1},{9,13},{13,9},{2,6},{6,2},{1... | collective-permute-start | bytes 196616 | tf_op jit(solution)/shard_map/ppermute | solution.py:485
  12.9 3.5 %copy-start.5 = (s32[2048]{0:T(1024)S(1)}, s32[2048]{0:T(1024)}, u32[]{:S(2)}) copy-start(s32[2048]{0:T(1024)} %param.20) | copy-start | bytes 24580
  14.5 3.4 %collective-permute-start.5 = (bf16[80,128]{1,0:T(8,128)(2,1)S(1)}, bf16[80,128]{1,0:T(8,128)(2,1)S(1)}, u32[]{:S(2)}, u32[]{:S(2)}) collective-permute-start(bf16[80,128]{1,0:T(8,128)(2,1)S(1)} %get-tuple-element.44), channel_id=1, source_target_pairs={{0,3},{1,2},{2,1},{3,0},{4,7},{5,6},{6,5},{7,4},{8,11},{9,10},{10,... | collective-permute-start | bytes 61448 | tf_op jit(solution)/shard_map/ppermute | solution.py:496
  15.5 3.8 %collective-permute-start.4 = (bf16[80,128]{1,0:T(8,128)(2,1)S(1)}, bf16[80,128]{1,0:T(8,128)(2,1)S(1)}, u32[]{:S(2)}, u32[]{:S(2)}) collective-permute-start(bf16[80,128]{1,0:T(8,128)(2,1)S(1)} %get-tuple-element.44), channel_id=1, source_target_pairs={{0,2},{2,0},{1,3},{3,1},{4,6},{6,4},{5,7},{7,5},{8,10},{10,8},{9,1... | collective-permute-start | bytes 61448 | tf_op jit(solution)/shard_map/ppermute | solution.py:494
  16.1 3.2 %collective-permute-start.3 = (bf16[80,128]{1,0:T(8,128)(2,1)S(1)}, bf16[80,128]{1,0:T(8,128)(2,1)S(1)}, u32[]{:S(2)}, u32[]{:S(2)}) collective-permute-start(bf16[80,128]{1,0:T(8,128)(2,1)S(1)} %get-tuple-element.43.refs_0_), channel_id=1, source_target_pairs={{0,1},{1,0},{2,3},{3,2},{4,5},{5,4},{6,7},{7,6},{8,9},{9,8},{10,11... | collective-permute-start | bytes 61448 | tf_op jit(solution)/shard_map/ppermute | solution.py:495
  16.4 2.9 %copy-start.1 = (bf16[4,128,128]{2,1,0:T(8,128)(2,1)S(1)}, bf16[4,128,128]{2,1,0:T(8,128)(2,1)}, u32[]{:S(2)}) copy-start(bf16[4,128,128]{2,1,0:T(8,128)(2,1)} %coarse_weights_ref.1) | copy-start | bytes 393220
  19.7 5.2 %collective-permute-start.6 = (bf16[128,128]{1,0:T(8,128)(2,1)S(1)}, bf16[128,128]{1,0:T(8,128)(2,1)S(1)}, u32[]{:S(2)}, u32[]{:S(2)}) collective-permute-start(bf16[128,128]{1,0:T(8,128)(2,1)S(1)} %get-tuple-element.49), channel_id=1, source_target_pairs={{0,8},{4,12},{8,0},{12,4},{1,9},{5,13},{9,1},{13,5},{2,10},{6,14},... | collective-permute-start | bytes 98312 | tf_op jit(solution)/shard_map/ppermute | solution.py:485
  20.5 5.7 %collective-permute-start.7 = (bf16[128,128]{1,0:T(8,128)(2,1)S(1)}, bf16[128,128]{1,0:T(8,128)(2,1)S(1)}, u32[]{:S(2)}, u32[]{:S(2)}) collective-permute-start(bf16[128,128]{1,0:T(8,128)(2,1)S(1)} %get-tuple-element.50), channel_id=1, source_target_pairs={{0,12},{4,8},{8,4},{12,0},{1,13},{5,9},{9,5},{13,1},{2,14},{6,10},... | collective-permute-start | bytes 98312 | tf_op jit(solution)/shard_map/ppermute | solution.py:485
  22.3 4.2 %copy-start.4 = (bf16[128,128]{1,0:T(8,128)(2,1)S(1)}, bf16[128,128]{1,0:T(8,128)(2,1)}, u32[]{:S(2)}) copy-start(bf16[128,128]{1,0:T(8,128)(2,1)} %prolong_weight_ref.1) | copy-start | bytes 98308
  22.3 4.2 %collective-permute-start.8 = (bf16[128,128]{1,0:T(8,128)(2,1)S(1)}, bf16[128,128]{1,0:T(8,128)(2,1)S(1)}, u32[]{:S(2)}, u32[]{:S(2)}) collective-permute-start(bf16[128,128]{1,0:T(8,128)(2,1)S(1)} %get-tuple-element.51), channel_id=1, source_target_pairs={{0,4},{4,0},{8,12},{12,8},{1,5},{5,1},{9,13},{13,9},{2,6},{6,2},{1... | collective-permute-start | bytes 98312 | tf_op jit(solution)/shard_map/ppermute | solution.py:485
  27.7 7.7 %collective-permute-start.9 = (bf16[128,256]{1,0:T(8,128)(2,1)S(1)}, bf16[128,256]{1,0:T(8,128)(2,1)S(1)}, u32[]{:S(2)}, u32[]{:S(2)}) collective-permute-start(bf16[128,256]{1,0:T(8,128)(2,1)S(1)} %get-tuple-element.56), channel_id=1, source_target_pairs={{0,12},{4,8},{8,4},{12,0},{1,13},{5,9},{9,5},{13,1},{2,14},{6,10},... | collective-permute-start | bytes 196616 | tf_op jit(solution)/shard_map/ppermute | solution.py:485
  29.6 5.8 %collective-permute-start.10 = (bf16[128,256]{1,0:T(8,128)(2,1)S(1)}, bf16[128,256]{1,0:T(8,128)(2,1)S(1)}, u32[]{:S(2)}, u32[]{:S(2)}) collective-permute-start(bf16[128,256]{1,0:T(8,128)(2,1)S(1)} %get-tuple-element.57), channel_id=1, source_target_pairs={{0,4},{4,0},{8,12},{12,8},{1,5},{5,1},{9,13},{13,9},{2,6},{6,2},{1... | collective-permute-start | bytes 196616 | tf_op jit(solution)/shard_map/ppermute | solution.py:485
  29.6 5.8 %collective-permute-start.11 = (bf16[128,256]{1,0:T(8,128)(2,1)S(1)}, bf16[128,256]{1,0:T(8,128)(2,1)S(1)}, u32[]{:S(2)}, u32[]{:S(2)}) collective-permute-start(bf16[128,256]{1,0:T(8,128)(2,1)S(1)} %get-tuple-element.58), channel_id=1, source_target_pairs={{0,8},{4,12},{8,0},{12,4},{1,9},{5,13},{9,1},{13,5},{2,10},{6,14},... | collective-permute-start | bytes 196616 | tf_op jit(solution)/shard_map/ppermute | solution.py:485

commit v10 on v9

--- a/solution.py
+++ b/solution.py
@@ -168,13 +168,13 @@
         places = rows_hot(place_ref[block : block + 1, :local_count], BLOCK)
         sums_ref[:, block * BLOCK : (block + 1) * BLOCK] = dot_last(message, places)
 
-    waiting = None
+    waiting = []
     for block in range(block_count):
-        message = messages(block)
-        if waiting is not None:
-            add_up(*waiting)
-        waiting = (block, message)
-    add_up(*waiting)
+        waiting.append((block, messages(block)))
+        if len(waiting) > 16:
+            add_up(*waiting.pop(0))
+    for held in waiting:
+        add_up(*held)
 
 
 def near_kernel(
@@ -380,8 +380,8 @@
         source_dom = lax.shift_right_arithmetic(halo_slots, shift)
         halo_sources = grid.halo_place(source_dom) * grid.coarse_capacity + (halo_slots & (grid.coarse_capacity - 1))
         is_halo = halo_slots >= 0
-        source_out[owner : owner + 1, :] = jnp.where(is_halo, halo_sources, -1)
-        place_out[owner : owner + 1, :] = places
+        source_out[owner] = rows_hot(jnp.where(is_halo, halo_sources, -1), source_out.shape[1])
+        place_out[owner] = rows_hot(places, grid.pool_capacity)
         own_sources = jnp.where(is_halo, -1, grid.slot_order(sources, place))
 
         table = owner_table(grid, packets, owner)
@@ -424,9 +424,9 @@
     prolonged = []
     for owner in range(grid.owners):
         halo = jnp.concatenate([ref[owner * BLOCK : (owner + 1) * BLOCK, :] for ref in halo_refs], axis=1)
-        picked = picked_ref[owner] + dot(halo, rows_hot(source_ref[owner : owner + 1, :], halo.shape[1]))
+        picked = picked_ref[owner] + dot(halo, source_ref[owner])
         message = silu_of_half(picked).astype(BF16)
-        places = rows_hot(place_ref[owner : owner + 1, :], grid.pool_capacity)
+        places = place_ref[owner]
         summed = dot_last(message, places).astype(BF16)
         rows = rows_ref[owner]
         update = dot(update_weights, jnp.concatenate([summed, rows], axis=0))
@@ -581,8 +581,8 @@
         functools.partial(coarse_own_kernel, grid),
         [
             ((grid.owners, features, coarse_slots), F32),
-            ((grid.owners, coarse_slots), I32),
-            ((grid.owners, coarse_slots), I32),
+            ((grid.owners, steps * grid.coarse_capacity, coarse_slots), BF16),
+            ((grid.owners, grid.pool_capacity, coarse_slots), BF16),
             ((grid.owners, features, grid.pool_capacity), BF16),
         ],
         [lists_scratch],

time: 37.8 us -> 37.8 us (level)
  transfers between devices with their start and end apart: 12 -> 12, of which waited for: 7 -> 7; matrix products, arithmetic and copies ran while one was open for 0% -> 0% of each run, Pallas kernels for 20% -> 19%
where the time goes in v10:
time: 37.8 us; the launch traced here: 37.7 us
  starting transfers between devices  15.7 us (42%)
  Pallas kernels  14.8 us (39%)
  waiting for transfers between devices  7.06 us (19%)
    ppermute x9, starting transfers between devices, swap_dom(): lax.ppermute(array, 'dom', [(dom, grid.partner(dom, step)) for dom in ran...  13.8 us
    ppermute x9, waiting for transfers between devices, swap_dom(): lax.ppermute(array, 'dom', [(dom, grid.partner(dom, step)) for dom in ran...  4.84 us
    pallas_call x1, Pallas kernels, body(): call(functools.partial(lift_near_kernel, grid), [table, aimed_table, sums...  3.16 us
    pallas_call x1, Pallas kernels, body(): call(functools.partial(near_kernel, grid), [far_lists, far_lists, aimed_t...  3.03 us
    pallas_call x1, Pallas kernels, body(): call(far_kernel, [((node_count, features), BF16)], [two_tables, pltpu.VME...  2.25 us
    pallas_call x1, Pallas kernels, body(): call(functools.partial(far_pool_kernel, grid), [table, *[((grid.packet, f...  1.64 us
    ppermute x1, waiting for transfers between devices, trade_packets(): over = lax.ppermute(far, 'sub', pairs)  1.36 us
    pallas_call x1, Pallas kernels, body(): call(turn_kernel, [table], [pltpu.VMEM((node_count, features), BF16), plt...  1.25 us
  transfers between devices with their start and end apart: 12, of which 7 were waited for; matrix products, arithmetic and copies ran while one was open for 0% of the time, Pallas kernels for 19%

profile of v10, /device:TPU:0, one launch (start us, length us, event | category | flops | bytes accessed | tf_op | source)
XLA Modules:
  0.0 37.7 jit_solution(813132317757096794)
XLA Ops:
  0.0 1.3 %turn.1.table_ref = bf16[128,2048]{1,0:T(8,128)(2,1)S(1)} custom-call(bf16[2048,128]{1,0:T(8,128)(2,1)} %latent_hbm.1), custom_call_target="tpu_custom_call" | custom-call | bytes 4194304 | tf_op jit(solution)/shard_map/turn/pallas_call | solution.py:534
  1.3 0.0 copy-start.2
  1.3 0.0 copy-start.3
  1.3 0.0 copy-start.6
  1.3 0.0 copy-start.7
  1.3 0.8 %send.1 = (bf16[128,256]{1,0:T(8,128)(2,1)S(1)}, bf16[128,256]{1,0:T(8,128)(2,1)S(1)}, bf16[128,256]{1,0:T(8,128)(2,1)S(1)}) custom-call(bf16[128,2048]{1,0:T(8,128)(2,1)S(1)} %turn.1.table_ref, s32[1,4,256]{2,1,0:T(4,128)S(1)} %copy-done.8, bf16[2,4,128,128]{3,2,1,0:T(8,128)(2,1)S(1)} %copy-done), custom_call_target="tpu_custom_call" | custom-call | flops 1073741824 | bytes 4194304 | tf_op jit(solution)/shard_map/send/pallas_call | solution.py:542
  2.1 0.0 copy-start.10
  2.2 5.1 %collective-permute-start = (bf16[128,256]{1,0:T(8,128)(2,1)S(1)}, bf16[128,256]{1,0:T(8,128)(2,1)S(1)}, u32[]{:S(2)}, u32[]{:S(2)}) collective-permute-start(bf16[128,256]{1,0:T(8,128)(2,1)S(1)} %get-tuple-element.39), channel_id=1, source_target_pairs={{0,12},{4,8},{8,4},{12,0},{1,13},{5,9},{9,5},{13,1},{2,14},{6,10},... | collective-permute-start | bytes 196616 | tf_op jit(solution)/shard_map/ppermute | solution.py:485
  7.3 0.6 %collective-permute-start.2 = (bf16[128,256]{1,0:T(8,128)(2,1)S(1)}, bf16[128,256]{1,0:T(8,128)(2,1)S(1)}, u32[]{:S(2)}, u32[]{:S(2)}) collective-permute-start(bf16[128,256]{1,0:T(8,128)(2,1)S(1)} %get-tuple-element.41), channel_id=1, source_target_pairs={{0,4},{4,0},{8,12},{12,8},{1,5},{5,1},{9,13},{13,9},{2,6},{6,2},{1... | collective-permute-start | bytes 196616 | tf_op jit(solution)/shard_map/ppermute | solution.py:485
  8.0 3.0 %near.1 = (s32[2,1536]{1,0:T(2,128)S(1)}, s32[2,1536]{1,0:T(2,128)S(1)}, bf16[128,3072]{1,0:T(8,128)(2,1)S(1)}, f32[128,2048]{1,0:T(8,128)S(1)}, s32[1,64]{1,0:T...) custom-call(bf16[128,2048]{1,0:T(8,128)(2,1)S(1)} %turn.1.table_ref, s32[16,768]{1,0:T(8,128)S(1)} %copy-done.2, ...), custom_call_target="tpu_custom_call" | custom-call | flops 4294967296 | bytes 4194304 | tf_op jit(solution)/shard_map/near/pallas_call | solution.py:546
  11.0 1.9 %collective-permute-done.1.rest_3_ = bf16[128,256]{1,0:T(8,128)(2,1)S(1)} collective-permute-done((bf16[128,256]{1,0:T(8,128)(2,1)S(1)}, bf16[128,256]{1,0:T(8,128)(2,1)S(1)}, u32[]{:S(2)}, u32[]{:S(2)}) %collective-permute-start.1) | collective-permute-done | bytes 65568 | tf_op jit(solution)/shard_map/ppermute | solution.py:485
  12.9 1.6 %far_pool.1 = (bf16[128,2048]{1,0:T(8,128)(2,1)S(1)}, bf16[80,128]{1,0:T(8,128)(2,1)S(1)}, bf16[80,128]{1,0:T(8,128)(2,1)S(1)}) custom-call(bf16[128,2048]{1,0:T(8,128)(2,1)S(1)} %turn.1.table_ref, bf16[128,3072]{1,0:T(8,128)(2,1)S(1)} %get-tuple-element.32.aimed_ref, s32[2,1536]{1,0:T(2,128)S(1)} %get-tuple-element.33.sources_ref, ...), custom_call_target="tpu_custom_call" | custom-call | flops 2147483648 | bytes 4194304 | tf_op jit(solution)/shard_map/far_pool/pallas_call | solution.py:560
  14.5 1.0 %collective-permute-start.5 = (bf16[80,128]{1,0:T(8,128)(2,1)S(1)}, bf16[80,128]{1,0:T(8,128)(2,1)S(1)}, u32[]{:S(2)}, u32[]{:S(2)}) collective-permute-start(bf16[80,128]{1,0:T(8,128)(2,1)S(1)} %get-tuple-element.44), channel_id=1, source_target_pairs={{0,3},{1,2},{2,1},{3,0},{4,7},{5,6},{6,5},{7,4},{8,11},{9,10},{10,... | collective-permute-start | bytes 61448 | tf_op jit(solution)/shard_map/ppermute | solution.py:496
  15.5 0.6 %collective-permute-start.4 = (bf16[80,128]{1,0:T(8,128)(2,1)S(1)}, bf16[80,128]{1,0:T(8,128)(2,1)S(1)}, u32[]{:S(2)}, u32[]{:S(2)}) collective-permute-start(bf16[80,128]{1,0:T(8,128)(2,1)S(1)} %get-tuple-element.44), channel_id=1, source_target_pairs={{0,2},{2,0},{1,3},{3,1},{4,6},{6,4},{5,7},{7,5},{8,10},{10,8},{9,1... | collective-permute-start | bytes 61448 | tf_op jit(solution)/shard_map/ppermute | solution.py:494
  16.1 0.3 collective-permute-start.3
  16.4 0.6 %ahead.1.ahead_ref = bf16[144,768]{1,0:T(8,128)(2,1)S(1)} custom-call(bf16[128,2048]{1,0:T(8,128)(2,1)S(1)} %get-tuple-element.42.first_ref, s32[16,128]{1,0:T(8,128)S(1)} %bitcast.1, s32[1,4,256]{2,1,0:T(4,128)S(1)} %copy-done.8), custom_call_target="tpu_custom_call" | custom-call | flops 1073741824 | bytes 4194304 | tf_op jit(solution)/shard_map/ahead/pallas_call | solution.py:568
  17.1 0.9 %collective-permute-done.5.refs_3_ = bf16[80,128]{1,0:T(8,128)(2,1)S(1)} collective-permute-done((bf16[80,128]{1,0:T(8,128)(2,1)S(1)}, bf16[80,128]{1,0:T(8,128)(2,1)S(1)}, u32[]{:S(2)}, u32[]{:S(2)}) %collective-permute-start.5) | collective-permute-done | bytes 20512 | tf_op jit(solution)/shard_map/ppermute | solution.py:496
  17.9 1.4 %collective-permute-done.4.refs_2_ = bf16[80,128]{1,0:T(8,128)(2,1)S(1)} collective-permute-done((bf16[80,128]{1,0:T(8,128)(2,1)S(1)}, bf16[80,128]{1,0:T(8,128)(2,1)S(1)}, u32[]{:S(2)}, u32[]{:S(2)}) %collective-permute-start.4) | collective-permute-done | bytes 20512 | tf_op jit(solution)/shard_map/ppermute | solution.py:494
  19.3 0.4 coarse_send.1
  19.7 0.8 %collective-permute-start.6 = (bf16[128,128]{1,0:T(8,128)(2,1)S(1)}, bf16[128,128]{1,0:T(8,128)(2,1)S(1)}, u32[]{:S(2)}, u32[]{:S(2)}) collective-permute-start(bf16[128,128]{1,0:T(8,128)(2,1)S(1)} %get-tuple-element.49), channel_id=1, source_target_pairs={{0,8},{4,12},{8,0},{12,4},{1,9},{5,13},{9,1},{13,5},{2,10},{6,14},... | collective-permute-start | bytes 98312 | tf_op jit(solution)/shard_map/ppermute | solution.py:485
  20.5 1.9 %collective-permute-start.7 = (bf16[128,128]{1,0:T(8,128)(2,1)S(1)}, bf16[128,128]{1,0:T(8,128)(2,1)S(1)}, u32[]{:S(2)}, u32[]{:S(2)}) collective-permute-start(bf16[128,128]{1,0:T(8,128)(2,1)S(1)} %get-tuple-element.50), channel_id=1, source_target_pairs={{0,12},{4,8},{8,4},{12,0},{1,13},{5,9},{9,5},{13,1},{2,14},{6,10},... | collective-permute-start | bytes 98312 | tf_op jit(solution)/shard_map/ppermute | solution.py:485
  22.3 0.9 %collective-permute-start.8 = (bf16[128,128]{1,0:T(8,128)(2,1)S(1)}, bf16[128,128]{1,0:T(8,128)(2,1)S(1)}, u32[]{:S(2)}, u32[]{:S(2)}) collective-permute-start(bf16[128,128]{1,0:T(8,128)(2,1)S(1)} %get-tuple-element.51), channel_id=1, source_target_pairs={{0,4},{4,0},{8,12},{12,8},{1,5},{5,1},{9,13},{13,9},{2,6},{6,2},{1... | collective-permute-start | bytes 98312 | tf_op jit(solution)/shard_map/ppermute | solution.py:485
  23.2 0.5 %coarse_own.1 = (f32[1,128,768]{2,1,0:T(8,128)S(1)}, bf16[1,384,768]{2,1,0:T(8,128)(2,1)S(1)}, bf16[1,64,768]{2,1,0:T(8,128)(2,1)S(1)}, bf16[1,128,64]{2,1,0:T(8,128)(2,1)S(1)}) custom-call(bf16[4,128,128]{2,1,0:T(8,128)(2,1)S(1)} %copy-done.1, bf16[80,128]{1,0:T(8,128)(2,1)S(1)} %get-tuple-element.43.refs_0_, ...), custom_call_target="tpu_custom_call" | custom-call | flops 4294967296 | bytes 4194304 | tf_op jit(solution)/shard_map/coarse_own/pallas_call | solution.py:580
  23.7 1.2 %collective-permute-done.6.rest_0_ = bf16[128,128]{1,0:T(8,128)(2,1)S(1)} collective-permute-done((bf16[128,128]{1,0:T(8,128)(2,1)S(1)}, bf16[128,128]{1,0:T(8,128)(2,1)S(1)}, u32[]{:S(2)}, u32[]{:S(2)}) %collective-permute-start.6) | collective-permute-done | bytes 32800 | tf_op jit(solution)/shard_map/ppermute | solution.py:485
  24.9 1.4 %collective-permute-done.7.rest_1_ = bf16[128,128]{1,0:T(8,128)(2,1)S(1)} collective-permute-done((bf16[128,128]{1,0:T(8,128)(2,1)S(1)}, bf16[128,128]{1,0:T(8,128)(2,1)S(1)}, u32[]{:S(2)}, u32[]{:S(2)}) %collective-permute-start.7) | collective-permute-done | bytes 32800 | tf_op jit(solution)/shard_map/ppermute | solution.py:485
  26.2 0.3 collective-permute-done.8.rest_2_
  26.5 1.1 %lift_halo.1 = (bf16[128,128]{1,0:T(8,128)(2,1)S(1)}, bf16[128,256]{1,0:T(8,128)(2,1)S(1)}, bf16[128,256]{1,0:T(8,128)(2,1)S(1)}, bf16[128,256]{1,0:T(8,128)(2,1)S(1)}) custom-call(f32[1,128,768]{2,1,0:T(8,128)S(1)} %get-tuple-element.45.picked_ref, bf16[1,384,768]{2,1,0:T(8,128)(2,1)S(1)} %get-tuple-element.46.source_ref, ...), custom_call_target="tpu_custom_call" | custom-call | flops 1073741824 | bytes 4194304 | tf_op jit(solution)/shard_map/lift_halo/pallas_call | solution.py:592
  27.7 1.9 %collective-permute-start.9 = (bf16[128,256]{1,0:T(8,128)(2,1)S(1)}, bf16[128,256]{1,0:T(8,128)(2,1)S(1)}, u32[]{:S(2)}, u32[]{:S(2)}) collective-permute-start(bf16[128,256]{1,0:T(8,128)(2,1)S(1)} %get-tuple-element.56), channel_id=1, source_target_pairs={{0,12},{4,8},{8,4},{12,0},{1,13},{5,9},{9,5},{13,1},{2,14},{6,10},... | collective-permute-start | bytes 196616 | tf_op jit(solution)/shard_map/ppermute | solution.py:485
  29.6 2.5 %collective-permute-start.11 = (bf16[128,256]{1,0:T(8,128)(2,1)S(1)}, bf16[128,256]{1,0:T(8,128)(2,1)S(1)}, u32[]{:S(2)}, u32[]{:S(2)}) collective-permute-start(bf16[128,256]{1,0:T(8,128)(2,1)S(1)} %get-tuple-element.58), channel_id=1, source_target_pairs={{0,8},{4,12},{8,0},{12,4},{1,9},{5,13},{9,1},{13,5},{2,10},{6,14},... | collective-permute-start | bytes 196616 | tf_op jit(solution)/shard_map/ppermute | solution.py:485
  32.1 3.2 %lift_near.1 = (bf16[128,2048]{1,0:T(8,128)(2,1)S(1)}, bf16[128,3072]{1,0:T(8,128)(2,1)S(1)}, f32[128,2048]{1,0:T(8,128)S(1)}) custom-call(bf16[128,2048]{1,0:T(8,128)(2,1)S(1)} %get-tuple-element.42.first_ref, bf16[128,128]{1,0:T(8,128)(2,1)S(1)} %get-tuple-element.52.prolonged_ref, s32[16,128]{1,0:T(8,128)S(1)} %bitcast.2, s32[16,768]{1,0:T(8,128)S(1)} %copy-done.2, ...), custom_call_target="tpu_custom_call" | custom-call | flops 4294967296 | bytes 4194304 | tf_op jit(solution)/shard_map/lift_near/pallas_call | solution.py:599
  35.3 0.1 collective-permute-done.11.rest_2_
  35.4 2.3 %far.1 = bf16[2048,128]{1,0:T(8,128)(2,1)} custom-call(bf16[128,2048]{1,0:T(8,128)(2,1)S(1)} %get-tuple-element.53.table_ref, bf16[128,3072]{1,0:T(8,128)(2,1)S(1)} %get-tuple-element.54.aimed_ref, s32[2,1536]{1,0:T(2,128)S(1)} %get-tuple-element.33.sources_ref, s32[2,1536]{1,0:T(2,128)S(1)} %get-tuple-element.34.places_ref, ...), custom_call_target="tpu_custom_call" | custom-call | flops 2147483648 | bytes 4194304 | tf_op jit(solution)/shard_map/far/pallas_call | solution.py:606
  (24 shorter events, 0.1 us)
Async XLA Ops:
  0.0 1.3 %copy-start = (bf16[2,4,128,128]{3,2,1,0:T(8,128)(2,1)S(1)}, bf16[2,4,128,128]{3,2,1,0:T(8,128)(2,1)}, u32[]{:S(2)}) copy-start(bf16[2,4,128,128]{3,2,1,0:T(8,128)(2,1)} %weights_ref.15) | copy-start | bytes 786436
  0.0 1.3 %copy-start.8 = (s32[1,4,256]{2,1,0:T(4,128)S(1)}, s32[1,4,256]{2,1,0:T(4,128)}, u32[]{:S(2)}) copy-start(s32[1,4,256]{2,1,0:T(4,128)} %lists_ref.3) | copy-start | bytes 12292
  1.3 6.6 %copy-start.2 = (s32[16,768]{1,0:T(8,128)S(1)}, s32[16,768]{1,0:T(8,128)}, u32[]{:S(2)}) copy-start(s32[16,768]{1,0:T(8,128)} %source_ref.3) | copy-start | bytes 147460
  1.3 6.6 %copy-start.3 = (s32[16,768]{1,0:T(8,128)S(1)}, s32[16,768]{1,0:T(8,128)}, u32[]{:S(2)}) copy-start(s32[16,768]{1,0:T(8,128)} %place_ref.3) | copy-start | bytes 147460
  1.3 6.6 %copy-start.6 = (s32[2,768]{1,0:T(2,128)S(1)}, s32[2,768]{1,0:T(2,128)}, u32[]{:S(2)}) copy-start(s32[2,768]{1,0:T(2,128)} %coarse_source_ref.1) | copy-start | bytes 18436
  1.3 6.6 %copy-start.7 = (s32[2,768]{1,0:T(2,128)S(1)}, s32[2,768]{1,0:T(2,128)}, u32[]{:S(2)}) copy-start(s32[2,768]{1,0:T(2,128)} %coarse_place_ref.1) | copy-start | bytes 18436
  2.1 5.8 %copy-start.10 = (s32[1,4,64]{2,1,0:T(4,128)S(1)}, s32[1,4,64]{2,1,0:T(4,128)}, u32[]{:S(2)}) copy-start(s32[1,4,64]{2,1,0:T(4,128)} %pool_ref.1) | copy-start | bytes 3076
  2.2 5.8 %copy-start.9 = (s32[1,4,128]{2,1,0:T(4,128)S(1)}, s32[1,4,128]{2,1,0:T(4,128)}, u32[]{:S(2)}) copy-start(s32[1,4,128]{2,1,0:T(4,128)} %coarse_send_ref.1) | copy-start | bytes 6148
  2.2 8.8 %collective-permute-start = (bf16[128,256]{1,0:T(8,128)(2,1)S(1)}, bf16[128,256]{1,0:T(8,128)(2,1)S(1)}, u32[]{:S(2)}, u32[]{:S(2)}) collective-permute-start(bf16[128,256]{1,0:T(8,128)(2,1)S(1)} %get-tuple-element.39), channel_id=1, source_target_pairs={{0,12},{4,8},{8,4},{12,0},{1,13},{5,9},{9,5},{13,1},{2,14},{6,10},... | collective-permute-start | bytes 196616 | tf_op jit(solution)/shard_map/ppermute | solution.py:485
  7.3 5.6 %collective-permute-start.1 = (bf16[128,256]{1,0:T(8,128)(2,1)S(1)}, bf16[128,256]{1,0:T(8,128)(2,1)S(1)}, u32[]{:S(2)}, u32[]{:S(2)}) collective-permute-start(bf16[128,256]{1,0:T(8,128)(2,1)S(1)} %get-tuple-element.40), channel_id=1, source_target_pairs={{0,8},{4,12},{8,0},{12,4},{1,9},{5,13},{9,1},{13,5},{2,10},{6,14},... | collective-permute-start | bytes 196616 | tf_op jit(solution)/shard_map/ppermute | solution.py:485
  7.3 5.6 %collective-permute-start.2 = (bf16[128,256]{1,0:T(8,128)(2,1)S(1)}, bf16[128,256]{1,0:T(8,128)(2,1)S(1)}, u32[]{:S(2)}, u32[]{:S(2)}) collective-permute-start(bf16[128,256]{1,0:T(8,128)(2,1)S(1)} %get-tuple-element.41), channel_id=1, source_target_pairs={{0,4},{4,0},{8,12},{12,8},{1,5},{5,1},{9,13},{13,9},{2,6},{6,2},{1... | collective-permute-start | bytes 196616 | tf_op jit(solution)/shard_map/ppermute | solution.py:485
  12.9 3.5 %copy-start.5 = (s32[2048]{0:T(1024)S(1)}, s32[2048]{0:T(1024)}, u32[]{:S(2)}) copy-start(s32[2048]{0:T(1024)} %param.20) | copy-start | bytes 24580
  14.5 3.4 %collective-permute-start.5 = (bf16[80,128]{1,0:T(8,128)(2,1)S(1)}, bf16[80,128]{1,0:T(8,128)(2,1)S(1)}, u32[]{:S(2)}, u32[]{:S(2)}) collective-permute-start(bf16[80,128]{1,0:T(8,128)(2,1)S(1)} %get-tuple-element.44), channel_id=1, source_target_pairs={{0,3},{1,2},{2,1},{3,0},{4,7},{5,6},{6,5},{7,4},{8,11},{9,10},{10,... | collective-permute-start | bytes 61448 | tf_op jit(solution)/shard_map/ppermute | solution.py:496
  15.5 3.8 %collective-permute-start.4 = (bf16[80,128]{1,0:T(8,128)(2,1)S(1)}, bf16[80,128]{1,0:T(8,128)(2,1)S(1)}, u32[]{:S(2)}, u32[]{:S(2)}) collective-permute-start(bf16[80,128]{1,0:T(8,128)(2,1)S(1)} %get-tuple-element.44), channel_id=1, source_target_pairs={{0,2},{2,0},{1,3},{3,1},{4,6},{6,4},{5,7},{7,5},{8,10},{10,8},{9,1... | collective-permute-start | bytes 61448 | tf_op jit(solution)/shard_map/ppermute | solution.py:494
  16.1 3.2 %collective-permute-start.3 = (bf16[80,128]{1,0:T(8,128)(2,1)S(1)}, bf16[80,128]{1,0:T(8,128)(2,1)S(1)}, u32[]{:S(2)}, u32[]{:S(2)}) collective-permute-start(bf16[80,128]{1,0:T(8,128)(2,1)S(1)} %get-tuple-element.43.refs_0_), channel_id=1, source_target_pairs={{0,1},{1,0},{2,3},{3,2},{4,5},{5,4},{6,7},{7,6},{8,9},{9,8},{10,11... | collective-permute-start | bytes 61448 | tf_op jit(solution)/shard_map/ppermute | solution.py:495
  16.4 2.9 %copy-start.1 = (bf16[4,128,128]{2,1,0:T(8,128)(2,1)S(1)}, bf16[4,128,128]{2,1,0:T(8,128)(2,1)}, u32[]{:S(2)}) copy-start(bf16[4,128,128]{2,1,0:T(8,128)(2,1)} %coarse_weights_ref.1) | copy-start | bytes 393220
  19.7 5.2 %collective-permute-start.6 = (bf16[128,128]{1,0:T(8,128)(2,1)S(1)}, bf16[128,128]{1,0:T(8,128)(2,1)S(1)}, u32[]{:S(2)}, u32[]{:S(2)}) collective-permute-start(bf16[128,128]{1,0:T(8,128)(2,1)S(1)} %get-tuple-element.49), channel_id=1, source_target_pairs={{0,8},{4,12},{8,0},{12,4},{1,9},{5,13},{9,1},{13,5},{2,10},{6,14},... | collective-permute-start | bytes 98312 | tf_op jit(solution)/shard_map/ppermute | solution.py:485
  20.5 5.7 %collective-permute-start.7 = (bf16[128,128]{1,0:T(8,128)(2,1)S(1)}, bf16[128,128]{1,0:T(8,128)(2,1)S(1)}, u32[]{:S(2)}, u32[]{:S(2)}) collective-permute-start(bf16[128,128]{1,0:T(8,128)(2,1)S(1)} %get-tuple-element.50), channel_id=1, source_target_pairs={{0,12},{4,8},{8,4},{12,0},{1,13},{5,9},{9,5},{13,1},{2,14},{6,10},... | collective-permute-start | bytes 98312 | tf_op jit(solution)/shard_map/ppermute | solution.py:485
  22.3 4.2 %copy-start.4 = (bf16[128,128]{1,0:T(8,128)(2,1)S(1)}, bf16[128,128]{1,0:T(8,128)(2,1)}, u32[]{:S(2)}) copy-start(bf16[128,128]{1,0:T(8,128)(2,1)} %prolong_weight_ref.1) | copy-start | bytes 98308
  22.3 4.2 %collective-permute-start.8 = (bf16[128,128]{1,0:T(8,128)(2,1)S(1)}, bf16[128,128]{1,0:T(8,128)(2,1)S(1)}, u32[]{:S(2)}, u32[]{:S(2)}) collective-permute-start(bf16[128,128]{1,0:T(8,128)(2,1)S(1)} %get-tuple-element.51), channel_id=1, source_target_pairs={{0,4},{4,0},{8,12},{12,8},{1,5},{5,1},{9,13},{13,9},{2,6},{6,2},{1... | collective-permute-start | bytes 98312 | tf_op jit(solution)/shard_map/ppermute | solution.py:485
  27.7 7.6 %collective-permute-start.9 = (bf16[128,256]{1,0:T(8,128)(2,1)S(1)}, bf16[128,256]{1,0:T(8,128)(2,1)S(1)}, u32[]{:S(2)}, u32[]{:S(2)}) collective-permute-start(bf16[128,256]{1,0:T(8,128)(2,1)S(1)} %get-tuple-element.56), channel_id=1, source_target_pairs={{0,12},{4,8},{8,4},{12,0},{1,13},{5,9},{9,5},{13,1},{2,14},{6,10},... | collective-permute-start | bytes 196616 | tf_op jit(solution)/shard_map/ppermute | solution.py:485
  29.6 5.7 %collective-permute-start.10 = (bf16[128,256]{1,0:T(8,128)(2,1)S(1)}, bf16[128,256]{1,0:T(8,128)(2,1)S(1)}, u32[]{:S(2)}, u32[]{:S(2)}) collective-permute-start(bf16[128,256]{1,0:T(8,128)(2,1)S(1)} %get-tuple-element.57), channel_id=1, source_target_pairs={{0,4},{4,0},{8,12},{12,8},{1,5},{5,1},{9,13},{13,9},{2,6},{6,2},{1... | collective-permute-start | bytes 196616 | tf_op jit(solution)/shard_map/ppermute | solution.py:485
  29.6 5.8 %collective-permute-start.11 = (bf16[128,256]{1,0:T(8,128)(2,1)S(1)}, bf16[128,256]{1,0:T(8,128)(2,1)S(1)}, u32[]{:S(2)}, u32[]{:S(2)}) collective-permute-start(bf16[128,256]{1,0:T(8,128)(2,1)S(1)} %get-tuple-element.58), channel_id=1, source_target_pairs={{0,8},{4,12},{8,0},{12,4},{1,9},{5,13},{9,1},{13,5},{2,10},{6,14},... | collective-permute-start | bytes 196616 | tf_op jit(solution)/shard_map/ppermute | solution.py:485

commit v11 on v9

--- a/solution.py
+++ b/solution.py
@@ -250,9 +250,11 @@
             both_ref[:features, columns] = (sums_ref[:, columns] + dot_last(message[:, slots], hot)).astype(BF16)
 
     def update(batch):
-        columns = slice(batch * batch_rows, (batch + 1) * batch_rows)
-        change = silu_of_half(dot(update_weights, both_ref[:, columns]))
-        write(columns, (both_ref[features:, columns].astype(F32) + change).astype(BF16))
+        part = batch_rows // 2
+        for first in range(batch * batch_rows, (batch + 1) * batch_rows, part):
+            columns = slice(first, first + part)
+            change = silu_of_half(dot(update_weights, both_ref[:, columns]))
+            write(columns, (both_ref[features:, columns].astype(F32) + change).astype(BF16))
 
     held = [messages(batch) for batch in range(batch_count)]
     for batch in range(batch_count):
@@ -609,7 +611,7 @@
         [
             two_tables,
             pltpu.VMEM((node_count, features), BF16),
-            pltpu.SemaphoreType.DMA((block_count // BATCH,)),
+            pltpu.SemaphoreType.DMA((2 * block_count // BATCH,)),
         ],
         flops=2 * big,
         name="far",

time: 37.8 us -> 37.8 us (level)
  no operation moved by 1% of the time
where the time goes in v11:
time: 37.8 us; the launch traced here: 37.7 us
  starting transfers between devices  15.7 us (42%)
  Pallas kernels  14.8 us (39%)
  waiting for transfers between devices  6.95 us (18%)
    ppermute x9, starting transfers between devices, swap_dom(): lax.ppermute(array, 'dom', [(dom, grid.partner(dom, step)) for dom in ran...  13.8 us
    ppermute x9, waiting for transfers between devices, swap_dom(): lax.ppermute(array, 'dom', [(dom, grid.partner(dom, step)) for dom in ran...  4.73 us
    pallas_call x1, Pallas kernels, body(): call(functools.partial(lift_near_kernel, grid), [table, aimed_table, sums...  3.21 us
    pallas_call x1, Pallas kernels, body(): call(functools.partial(near_kernel, grid), [far_lists, far_lists, aimed_t...  3.08 us
    pallas_call x1, Pallas kernels, body(): call(far_kernel, [((node_count, features), BF16)], [two_tables, pltpu.VME...  2.22 us
    pallas_call x1, Pallas kernels, body(): call(functools.partial(far_pool_kernel, grid), [table, *[((grid.packet, f...  1.63 us
    ppermute x1, waiting for transfers between devices, trade_packets(): over = lax.ppermute(far, 'sub', pairs)  1.36 us
    pallas_call x1, Pallas kernels, body(): call(turn_kernel, [table], [pltpu.VMEM((node_count, features), BF16), plt...  1.25 us
  transfers between devices with their start and end apart: 12, of which 7 were waited for; matrix products, arithmetic and copies ran while one was open for 0% of the time, Pallas kernels for 20%

profile of v11, /device:TPU:0, one launch (start us, length us, event | category | flops | bytes accessed | tf_op | source)
XLA Modules:
  0.0 37.7 jit_solution(4622025051984318646)
XLA Ops:
  0.0 1.3 %turn.1.table_ref = bf16[128,2048]{1,0:T(8,128)(2,1)S(1)} custom-call(bf16[2048,128]{1,0:T(8,128)(2,1)} %latent_hbm.1), custom_call_target="tpu_custom_call" | custom-call | bytes 4194304 | tf_op jit(solution)/shard_map/turn/pallas_call | solution.py:536
  1.3 0.0 copy-start.2
  1.3 0.0 copy-start.3
  1.3 0.0 copy-start.7
  1.3 0.8 %send.1 = (bf16[128,256]{1,0:T(8,128)(2,1)S(1)}, bf16[128,256]{1,0:T(8,128)(2,1)S(1)}, bf16[128,256]{1,0:T(8,128)(2,1)S(1)}) custom-call(bf16[128,2048]{1,0:T(8,128)(2,1)S(1)} %turn.1.table_ref, s32[1,4,256]{2,1,0:T(4,128)S(1)} %copy-done.8, bf16[2,4,128,128]{3,2,1,0:T(8,128)(2,1)S(1)} %copy-done), custom_call_target="tpu_custom_call" | custom-call | flops 1073741824 | bytes 4194304 | tf_op jit(solution)/shard_map/send/pallas_call | solution.py:544
  2.1 0.0 copy-start.10
  2.2 0.0 copy-start.9
  2.2 5.1 %collective-permute-start = (bf16[128,256]{1,0:T(8,128)(2,1)S(1)}, bf16[128,256]{1,0:T(8,128)(2,1)S(1)}, u32[]{:S(2)}, u32[]{:S(2)}) collective-permute-start(bf16[128,256]{1,0:T(8,128)(2,1)S(1)} %get-tuple-element.39), channel_id=1, source_target_pairs={{0,12},{4,8},{8,4},{12,0},{1,13},{5,9},{9,5},{13,1},{2,14},{6,10},... | collective-permute-start | bytes 196616 | tf_op jit(solution)/shard_map/ppermute | solution.py:487
  7.3 0.6 %collective-permute-start.2 = (bf16[128,256]{1,0:T(8,128)(2,1)S(1)}, bf16[128,256]{1,0:T(8,128)(2,1)S(1)}, u32[]{:S(2)}, u32[]{:S(2)}) collective-permute-start(bf16[128,256]{1,0:T(8,128)(2,1)S(1)} %get-tuple-element.41), channel_id=1, source_target_pairs={{0,4},{4,0},{8,12},{12,8},{1,5},{5,1},{9,13},{13,9},{2,6},{6,2},{1... | collective-permute-start | bytes 196616 | tf_op jit(solution)/shard_map/ppermute | solution.py:487
  8.0 3.1 %near.1 = (s32[2,1536]{1,0:T(2,128)S(1)}, s32[2,1536]{1,0:T(2,128)S(1)}, bf16[128,3072]{1,0:T(8,128)(2,1)S(1)}, f32[128,2048]{1,0:T(8,128)S(1)}, s32[1,64]{1,0:T...) custom-call(bf16[128,2048]{1,0:T(8,128)(2,1)S(1)} %turn.1.table_ref, s32[16,768]{1,0:T(8,128)S(1)} %copy-done.2, ...), custom_call_target="tpu_custom_call" | custom-call | flops 4294967296 | bytes 4194304 | tf_op jit(solution)/shard_map/near/pallas_call | solution.py:548
  11.1 1.8 %collective-permute-done.1.rest_3_ = bf16[128,256]{1,0:T(8,128)(2,1)S(1)} collective-permute-done((bf16[128,256]{1,0:T(8,128)(2,1)S(1)}, bf16[128,256]{1,0:T(8,128)(2,1)S(1)}, u32[]{:S(2)}, u32[]{:S(2)}) %collective-permute-start.1) | collective-permute-done | bytes 65568 | tf_op jit(solution)/shard_map/ppermute | solution.py:487
  12.9 1.6 %far_pool.1 = (bf16[128,2048]{1,0:T(8,128)(2,1)S(1)}, bf16[80,128]{1,0:T(8,128)(2,1)S(1)}, bf16[80,128]{1,0:T(8,128)(2,1)S(1)}) custom-call(bf16[128,2048]{1,0:T(8,128)(2,1)S(1)} %turn.1.table_ref, bf16[128,3072]{1,0:T(8,128)(2,1)S(1)} %get-tuple-element.32.aimed_ref, s32[2,1536]{1,0:T(2,128)S(1)} %get-tuple-element.33.sources_ref, ...), custom_call_target="tpu_custom_call" | custom-call | flops 2147483648 | bytes 4194304 | tf_op jit(solution)/shard_map/far_pool/pallas_call | solution.py:562
  14.5 1.0 %collective-permute-start.5 = (bf16[80,128]{1,0:T(8,128)(2,1)S(1)}, bf16[80,128]{1,0:T(8,128)(2,1)S(1)}, u32[]{:S(2)}, u32[]{:S(2)}) collective-permute-start(bf16[80,128]{1,0:T(8,128)(2,1)S(1)} %get-tuple-element.44), channel_id=1, source_target_pairs={{0,3},{1,2},{2,1},{3,0},{4,7},{5,6},{6,5},{7,4},{8,11},{9,10},{10,... | collective-permute-start | bytes 61448 | tf_op jit(solution)/shard_map/ppermute | solution.py:498
  15.5 0.6 %collective-permute-start.4 = (bf16[80,128]{1,0:T(8,128)(2,1)S(1)}, bf16[80,128]{1,0:T(8,128)(2,1)S(1)}, u32[]{:S(2)}, u32[]{:S(2)}) collective-permute-start(bf16[80,128]{1,0:T(8,128)(2,1)S(1)} %get-tuple-element.44), channel_id=1, source_target_pairs={{0,2},{2,0},{1,3},{3,1},{4,6},{6,4},{5,7},{7,5},{8,10},{10,8},{9,1... | collective-permute-start | bytes 61448 | tf_op jit(solution)/shard_map/ppermute | solution.py:496
  16.1 0.3 collective-permute-start.3
  16.4 0.6 %ahead.1.ahead_ref = bf16[144,768]{1,0:T(8,128)(2,1)S(1)} custom-call(bf16[128,2048]{1,0:T(8,128)(2,1)S(1)} %get-tuple-element.42.first_ref, s32[16,128]{1,0:T(8,128)S(1)} %bitcast.1, s32[1,4,256]{2,1,0:T(4,128)S(1)} %copy-done.8), custom_call_target="tpu_custom_call" | custom-call | flops 1073741824 | bytes 4194304 | tf_op jit(solution)/shard_map/ahead/pallas_call | solution.py:570
  17.1 0.9 %collective-permute-done.5.refs_3_ = bf16[80,128]{1,0:T(8,128)(2,1)S(1)} collective-permute-done((bf16[80,128]{1,0:T(8,128)(2,1)S(1)}, bf16[80,128]{1,0:T(8,128)(2,1)S(1)}, u32[]{:S(2)}, u32[]{:S(2)}) %collective-permute-start.5) | collective-permute-done | bytes 20512 | tf_op jit(solution)/shard_map/ppermute | solution.py:498
  17.9 1.4 %collective-permute-done.4.refs_2_ = bf16[80,128]{1,0:T(8,128)(2,1)S(1)} collective-permute-done((bf16[80,128]{1,0:T(8,128)(2,1)S(1)}, bf16[80,128]{1,0:T(8,128)(2,1)S(1)}, u32[]{:S(2)}, u32[]{:S(2)}) %collective-permute-start.4) | collective-permute-done | bytes 20512 | tf_op jit(solution)/shard_map/ppermute | solution.py:496
  19.3 0.4 %coarse_send.1 = (bf16[128,128]{1,0:T(8,128)(2,1)S(1)}, bf16[128,128]{1,0:T(8,128)(2,1)S(1)}, bf16[128,128]{1,0:T(8,128)(2,1)S(1)}) custom-call(bf16[4,128,128]{2,1,0:T(8,128)(2,1)S(1)} %copy-done.1, bf16[80,128]{1,0:T(8,128)(2,1)S(1)} %get-tuple-element.43.refs_0_, bf16[80,128]{1,0:T(8,128)(2,1)S(1)} %collective-permute-done.3.refs_1_, ...), custom_call_target="tpu_custom_call" | custom-call | flops 536870912 | bytes 4194304 | tf_op jit(solution)/shard_map/coarse_send/pallas_call | solution.py:574
  19.7 0.8 %collective-permute-start.6 = (bf16[128,128]{1,0:T(8,128)(2,1)S(1)}, bf16[128,128]{1,0:T(8,128)(2,1)S(1)}, u32[]{:S(2)}, u32[]{:S(2)}) collective-permute-start(bf16[128,128]{1,0:T(8,128)(2,1)S(1)} %get-tuple-element.49), channel_id=1, source_target_pairs={{0,8},{4,12},{8,0},{12,4},{1,9},{5,13},{9,1},{13,5},{2,10},{6,14},... | collective-permute-start | bytes 98312 | tf_op jit(solution)/shard_map/ppermute | solution.py:487
  20.5 1.9 %collective-permute-start.7 = (bf16[128,128]{1,0:T(8,128)(2,1)S(1)}, bf16[128,128]{1,0:T(8,128)(2,1)S(1)}, u32[]{:S(2)}, u32[]{:S(2)}) collective-permute-start(bf16[128,128]{1,0:T(8,128)(2,1)S(1)} %get-tuple-element.50), channel_id=1, source_target_pairs={{0,12},{4,8},{8,4},{12,0},{1,13},{5,9},{9,5},{13,1},{2,14},{6,10},... | collective-permute-start | bytes 98312 | tf_op jit(solution)/shard_map/ppermute | solution.py:487
  22.3 0.9 %collective-permute-start.8 = (bf16[128,128]{1,0:T(8,128)(2,1)S(1)}, bf16[128,128]{1,0:T(8,128)(2,1)S(1)}, u32[]{:S(2)}, u32[]{:S(2)}) collective-permute-start(bf16[128,128]{1,0:T(8,128)(2,1)S(1)} %get-tuple-element.51), channel_id=1, source_target_pairs={{0,4},{4,0},{8,12},{12,8},{1,5},{5,1},{9,13},{13,9},{2,6},{6,2},{1... | collective-permute-start | bytes 98312 | tf_op jit(solution)/shard_map/ppermute | solution.py:487
  23.2 0.5 %coarse_own.1 = (f32[1,128,768]{2,1,0:T(8,128)S(1)}, s32[1,768]{1,0:T(1,128)S(1)}, s32[1,768]{1,0:T(1,128)S(1)}, bf16[1,128,64]{2,1,0:T(8,128)(2,1)S(1)}) custom-call(bf16[4,128,128]{2,1,0:T(8,128)(2,1)S(1)} %copy-done.1, bf16[80,128]{1,0:T(8,128)(2,1)S(1)} %get-tuple-element.43.refs_0_, bf16[80,128]{1,0:T(8,128)(2,1)S(1)} %collective-permute-done.3.refs_1_, ...), custom_call_target="tpu_custom_call" | custom-call | flops 4294967296 | bytes 4194304 | tf_op jit(solution)/shard_map/coarse_own/pallas_call | solution.py:582
  23.7 1.1 %collective-permute-done.6.rest_0_ = bf16[128,128]{1,0:T(8,128)(2,1)S(1)} collective-permute-done((bf16[128,128]{1,0:T(8,128)(2,1)S(1)}, bf16[128,128]{1,0:T(8,128)(2,1)S(1)}, u32[]{:S(2)}, u32[]{:S(2)}) %collective-permute-start.6) | collective-permute-done | bytes 32800 | tf_op jit(solution)/shard_map/ppermute | solution.py:487
  24.9 1.4 %collective-permute-done.7.rest_1_ = bf16[128,128]{1,0:T(8,128)(2,1)S(1)} collective-permute-done((bf16[128,128]{1,0:T(8,128)(2,1)S(1)}, bf16[128,128]{1,0:T(8,128)(2,1)S(1)}, u32[]{:S(2)}, u32[]{:S(2)}) %collective-permute-start.7) | collective-permute-done | bytes 32800 | tf_op jit(solution)/shard_map/ppermute | solution.py:487
  26.2 0.3 collective-permute-done.8.rest_2_
  26.5 1.1 %lift_halo.1 = (bf16[128,128]{1,0:T(8,128)(2,1)S(1)}, bf16[128,256]{1,0:T(8,128)(2,1)S(1)}, bf16[128,256]{1,0:T(8,128)(2,1)S(1)}, bf16[128,256]{1,0:T(8,128)(2,1)S(1)}) custom-call(f32[1,128,768]{2,1,0:T(8,128)S(1)} %get-tuple-element.45.picked_ref, s32[1,768]{1,0:T(1,128)S(1)} %get-tuple-element.46.source_ref, s32[1,768]{1,0:T(1,128)S(1)} %get-tuple-element.47.place_ref, ...), custom_call_target="tpu_custom_call" | custom-call | flops 1073741824 | bytes 4194304 | tf_op jit(solution)/shard_map/lift_halo/pallas_call | solution.py:594
  27.7 1.9 %collective-permute-start.9 = (bf16[128,256]{1,0:T(8,128)(2,1)S(1)}, bf16[128,256]{1,0:T(8,128)(2,1)S(1)}, u32[]{:S(2)}, u32[]{:S(2)}) collective-permute-start(bf16[128,256]{1,0:T(8,128)(2,1)S(1)} %get-tuple-element.56), channel_id=1, source_target_pairs={{0,12},{4,8},{8,4},{12,0},{1,13},{5,9},{9,5},{13,1},{2,14},{6,10},... | collective-permute-start | bytes 196616 | tf_op jit(solution)/shard_map/ppermute | solution.py:487
  29.6 2.5 %collective-permute-start.11 = (bf16[128,256]{1,0:T(8,128)(2,1)S(1)}, bf16[128,256]{1,0:T(8,128)(2,1)S(1)}, u32[]{:S(2)}, u32[]{:S(2)}) collective-permute-start(bf16[128,256]{1,0:T(8,128)(2,1)S(1)} %get-tuple-element.58), channel_id=1, source_target_pairs={{0,8},{4,12},{8,0},{12,4},{1,9},{5,13},{9,1},{13,5},{2,10},{6,14},... | collective-permute-start | bytes 196616 | tf_op jit(solution)/shard_map/ppermute | solution.py:487
  32.1 3.2 %lift_near.1 = (bf16[128,2048]{1,0:T(8,128)(2,1)S(1)}, bf16[128,3072]{1,0:T(8,128)(2,1)S(1)}, f32[128,2048]{1,0:T(8,128)S(1)}) custom-call(bf16[128,2048]{1,0:T(8,128)(2,1)S(1)} %get-tuple-element.42.first_ref, bf16[128,128]{1,0:T(8,128)(2,1)S(1)} %get-tuple-element.52.prolonged_ref, s32[16,128]{1,0:T(8,128)S(1)} %bitcast.2, s32[16,768]{1,0:T(8,128)S(1)} %copy-done.2, ...), custom_call_target="tpu_custom_call" | custom-call | flops 4294967296 | bytes 4194304 | tf_op jit(solution)/shard_map/lift_near/pallas_call | solution.py:601
  35.4 0.1 collective-permute-done.11.rest_2_
  35.4 2.2 %far.1 = bf16[2048,128]{1,0:T(8,128)(2,1)} custom-call(bf16[128,2048]{1,0:T(8,128)(2,1)S(1)} %get-tuple-element.53.table_ref, bf16[128,3072]{1,0:T(8,128)(2,1)S(1)} %get-tuple-element.54.aimed_ref, s32[2,1536]{1,0:T(2,128)S(1)} %get-tuple-element.33.sources_ref, s32[2,1536]{1,0:T(2,128)S(1)} %get-tuple-element.34.places_ref, ...), custom_call_target="tpu_custom_call" | custom-call | flops 2147483648 | bytes 4194304 | tf_op jit(solution)/shard_map/far/pallas_call | solution.py:608
  (24 shorter events, 0.1 us)
Async XLA Ops:
  0.0 1.3 %copy-start = (bf16[2,4,128,128]{3,2,1,0:T(8,128)(2,1)S(1)}, bf16[2,4,128,128]{3,2,1,0:T(8,128)(2,1)}, u32[]{:S(2)}) copy-start(bf16[2,4,128,128]{3,2,1,0:T(8,128)(2,1)} %weights_ref.15) | copy-start | bytes 786436
  0.0 1.3 %copy-start.8 = (s32[1,4,256]{2,1,0:T(4,128)S(1)}, s32[1,4,256]{2,1,0:T(4,128)}, u32[]{:S(2)}) copy-start(s32[1,4,256]{2,1,0:T(4,128)} %lists_ref.3) | copy-start | bytes 12292
  1.3 6.6 %copy-start.2 = (s32[16,768]{1,0:T(8,128)S(1)}, s32[16,768]{1,0:T(8,128)}, u32[]{:S(2)}) copy-start(s32[16,768]{1,0:T(8,128)} %source_ref.3) | copy-start | bytes 147460
  1.3 6.6 %copy-start.3 = (s32[16,768]{1,0:T(8,128)S(1)}, s32[16,768]{1,0:T(8,128)}, u32[]{:S(2)}) copy-start(s32[16,768]{1,0:T(8,128)} %place_ref.3) | copy-start | bytes 147460
  1.3 6.6 %copy-start.6 = (s32[2,768]{1,0:T(2,128)S(1)}, s32[2,768]{1,0:T(2,128)}, u32[]{:S(2)}) copy-start(s32[2,768]{1,0:T(2,128)} %coarse_source_ref.1) | copy-start | bytes 18436
  1.3 6.6 %copy-start.7 = (s32[2,768]{1,0:T(2,128)S(1)}, s32[2,768]{1,0:T(2,128)}, u32[]{:S(2)}) copy-start(s32[2,768]{1,0:T(2,128)} %coarse_place_ref.1) | copy-start | bytes 18436
  2.1 5.8 %copy-start.10 = (s32[1,4,64]{2,1,0:T(4,128)S(1)}, s32[1,4,64]{2,1,0:T(4,128)}, u32[]{:S(2)}) copy-start(s32[1,4,64]{2,1,0:T(4,128)} %pool_ref.1) | copy-start | bytes 3076
  2.2 5.8 %copy-start.9 = (s32[1,4,128]{2,1,0:T(4,128)S(1)}, s32[1,4,128]{2,1,0:T(4,128)}, u32[]{:S(2)}) copy-start(s32[1,4,128]{2,1,0:T(4,128)} %coarse_send_ref.1) | copy-start | bytes 6148
  2.2 8.9 %collective-permute-start = (bf16[128,256]{1,0:T(8,128)(2,1)S(1)}, bf16[128,256]{1,0:T(8,128)(2,1)S(1)}, u32[]{:S(2)}, u32[]{:S(2)}) collective-permute-start(bf16[128,256]{1,0:T(8,128)(2,1)S(1)} %get-tuple-element.39), channel_id=1, source_target_pairs={{0,12},{4,8},{8,4},{12,0},{1,13},{5,9},{9,5},{13,1},{2,14},{6,10},... | collective-permute-start | bytes 196616 | tf_op jit(solution)/shard_map/ppermute | solution.py:487
  7.3 5.6 %collective-permute-start.1 = (bf16[128,256]{1,0:T(8,128)(2,1)S(1)}, bf16[128,256]{1,0:T(8,128)(2,1)S(1)}, u32[]{:S(2)}, u32[]{:S(2)}) collective-permute-start(bf16[128,256]{1,0:T(8,128)(2,1)S(1)} %get-tuple-element.40), channel_id=1, source_target_pairs={{0,8},{4,12},{8,0},{12,4},{1,9},{5,13},{9,1},{13,5},{2,10},{6,14},... | collective-permute-start | bytes 196616 | tf_op jit(solution)/shard_map/ppermute | solution.py:487
  7.3 5.6 %collective-permute-start.2 = (bf16[128,256]{1,0:T(8,128)(2,1)S(1)}, bf16[128,256]{1,0:T(8,128)(2,1)S(1)}, u32[]{:S(2)}, u32[]{:S(2)}) collective-permute-start(bf16[128,256]{1,0:T(8,128)(2,1)S(1)} %get-tuple-element.41), channel_id=1, source_target_pairs={{0,4},{4,0},{8,12},{12,8},{1,5},{5,1},{9,13},{13,9},{2,6},{6,2},{1... | collective-permute-start | bytes 196616 | tf_op jit(solution)/shard_map/ppermute | solution.py:487
  12.9 3.5 %copy-start.5 = (s32[2048]{0:T(1024)S(1)}, s32[2048]{0:T(1024)}, u32[]{:S(2)}) copy-start(s32[2048]{0:T(1024)} %param.20) | copy-start | bytes 24580
  14.5 3.4 %collective-permute-start.5 = (bf16[80,128]{1,0:T(8,128)(2,1)S(1)}, bf16[80,128]{1,0:T(8,128)(2,1)S(1)}, u32[]{:S(2)}, u32[]{:S(2)}) collective-permute-start(bf16[80,128]{1,0:T(8,128)(2,1)S(1)} %get-tuple-element.44), channel_id=1, source_target_pairs={{0,3},{1,2},{2,1},{3,0},{4,7},{5,6},{6,5},{7,4},{8,11},{9,10},{10,... | collective-permute-start | bytes 61448 | tf_op jit(solution)/shard_map/ppermute | solution.py:498
  15.5 3.8 %collective-permute-start.4 = (bf16[80,128]{1,0:T(8,128)(2,1)S(1)}, bf16[80,128]{1,0:T(8,128)(2,1)S(1)}, u32[]{:S(2)}, u32[]{:S(2)}) collective-permute-start(bf16[80,128]{1,0:T(8,128)(2,1)S(1)} %get-tuple-element.44), channel_id=1, source_target_pairs={{0,2},{2,0},{1,3},{3,1},{4,6},{6,4},{5,7},{7,5},{8,10},{10,8},{9,1... | collective-permute-start | bytes 61448 | tf_op jit(solution)/shard_map/ppermute | solution.py:496
  16.1 3.2 %collective-permute-start.3 = (bf16[80,128]{1,0:T(8,128)(2,1)S(1)}, bf16[80,128]{1,0:T(8,128)(2,1)S(1)}, u32[]{:S(2)}, u32[]{:S(2)}) collective-permute-start(bf16[80,128]{1,0:T(8,128)(2,1)S(1)} %get-tuple-element.43.refs_0_), channel_id=1, source_target_pairs={{0,1},{1,0},{2,3},{3,2},{4,5},{5,4},{6,7},{7,6},{8,9},{9,8},{10,11... | collective-permute-start | bytes 61448 | tf_op jit(solution)/shard_map/ppermute | solution.py:497
  16.4 2.9 %copy-start.1 = (bf16[4,128,128]{2,1,0:T(8,128)(2,1)S(1)}, bf16[4,128,128]{2,1,0:T(8,128)(2,1)}, u32[]{:S(2)}) copy-start(bf16[4,128,128]{2,1,0:T(8,128)(2,1)} %coarse_weights_ref.1) | copy-start | bytes 393220
  19.7 5.2 %collective-permute-start.6 = (bf16[128,128]{1,0:T(8,128)(2,1)S(1)}, bf16[128,128]{1,0:T(8,128)(2,1)S(1)}, u32[]{:S(2)}, u32[]{:S(2)}) collective-permute-start(bf16[128,128]{1,0:T(8,128)(2,1)S(1)} %get-tuple-element.49), channel_id=1, source_target_pairs={{0,8},{4,12},{8,0},{12,4},{1,9},{5,13},{9,1},{13,5},{2,10},{6,14},... | collective-permute-start | bytes 98312 | tf_op jit(solution)/shard_map/ppermute | solution.py:487
  20.5 5.7 %collective-permute-start.7 = (bf16[128,128]{1,0:T(8,128)(2,1)S(1)}, bf16[128,128]{1,0:T(8,128)(2,1)S(1)}, u32[]{:S(2)}, u32[]{:S(2)}) collective-permute-start(bf16[128,128]{1,0:T(8,128)(2,1)S(1)} %get-tuple-element.50), channel_id=1, source_target_pairs={{0,12},{4,8},{8,4},{12,0},{1,13},{5,9},{9,5},{13,1},{2,14},{6,10},... | collective-permute-start | bytes 98312 | tf_op jit(solution)/shard_map/ppermute | solution.py:487
  22.3 4.2 %copy-start.4 = (bf16[128,128]{1,0:T(8,128)(2,1)S(1)}, bf16[128,128]{1,0:T(8,128)(2,1)}, u32[]{:S(2)}) copy-start(bf16[128,128]{1,0:T(8,128)(2,1)} %prolong_weight_ref.1) | copy-start | bytes 98308
  22.3 4.2 %collective-permute-start.8 = (bf16[128,128]{1,0:T(8,128)(2,1)S(1)}, bf16[128,128]{1,0:T(8,128)(2,1)S(1)}, u32[]{:S(2)}, u32[]{:S(2)}) collective-permute-start(bf16[128,128]{1,0:T(8,128)(2,1)S(1)} %get-tuple-element.51), channel_id=1, source_target_pairs={{0,4},{4,0},{8,12},{12,8},{1,5},{5,1},{9,13},{13,9},{2,6},{6,2},{1... | collective-permute-start | bytes 98312 | tf_op jit(solution)/shard_map/ppermute | solution.py:487
  27.7 7.7 %collective-permute-start.9 = (bf16[128,256]{1,0:T(8,128)(2,1)S(1)}, bf16[128,256]{1,0:T(8,128)(2,1)S(1)}, u32[]{:S(2)}, u32[]{:S(2)}) collective-permute-start(bf16[128,256]{1,0:T(8,128)(2,1)S(1)} %get-tuple-element.56), channel_id=1, source_target_pairs={{0,12},{4,8},{8,4},{12,0},{1,13},{5,9},{9,5},{13,1},{2,14},{6,10},... | collective-permute-start | bytes 196616 | tf_op jit(solution)/shard_map/ppermute | solution.py:487
  29.6 5.8 %collective-permute-start.10 = (bf16[128,256]{1,0:T(8,128)(2,1)S(1)}, bf16[128,256]{1,0:T(8,128)(2,1)S(1)}, u32[]{:S(2)}, u32[]{:S(2)}) collective-permute-start(bf16[128,256]{1,0:T(8,128)(2,1)S(1)} %get-tuple-element.57), channel_id=1, source_target_pairs={{0,4},{4,0},{8,12},{12,8},{1,5},{5,1},{9,13},{13,9},{2,6},{6,2},{1... | collective-permute-start | bytes 196616 | tf_op jit(solution)/shard_map/ppermute | solution.py:487
  29.6 5.8 %collective-permute-start.11 = (bf16[128,256]{1,0:T(8,128)(2,1)S(1)}, bf16[128,256]{1,0:T(8,128)(2,1)S(1)}, u32[]{:S(2)}, u32[]{:S(2)}) collective-permute-start(bf16[128,256]{1,0:T(8,128)(2,1)S(1)} %get-tuple-element.58), channel_id=1, source_target_pairs={{0,8},{4,12},{8,0},{12,4},{1,9},{5,13},{9,1},{13,5},{2,10},{6,14},... | collective-permute-start | bytes 196616 | tf_op jit(solution)/shard_map/ppermute | solution.py:487

commit v12 on v9

--- a/solution.py
+++ b/solution.py
@@ -14,7 +14,7 @@
 VMEM_BYTES = 32 << 20
 BATCH = 8
 FIRST_ORDER, SECOND_ORDER = (1, 0, 2), (1, 2, 0)
-PARTS = 2
+PARTS = 1
 PAIR = 1
 
 

time: 37.8 us -> 37.9 us (level)
  transfers between devices with their start and end apart: 12 -> 12, of which waited for: 7 -> 6; matrix products, arithmetic and copies ran while one was open for 0% -> 0% of each run, Pallas kernels for 20% -> 20%
where the time goes in v12:
time: 37.9 us; the launch traced here: 37.7 us
  starting transfers between devices  15.7 us (41%)
  Pallas kernels  14.9 us (39%)
  waiting for transfers between devices  6.94 us (18%)
    ppermute x9, starting transfers between devices, swap_dom(): lax.ppermute(array, 'dom', [(dom, grid.partner(dom, step)) for dom in ran...  13.8 us
    ppermute x9, waiting for transfers between devices, swap_dom(): lax.ppermute(array, 'dom', [(dom, grid.partner(dom, step)) for dom in ran...  4.73 us
    pallas_call x1, Pallas kernels, body(): call(functools.partial(lift_near_kernel, grid), [table, aimed_table, sums...  3.21 us
    pallas_call x1, Pallas kernels, body(): call(functools.partial(near_kernel, grid), [far_lists, far_lists, aimed_t...  3.08 us
    pallas_call x1, Pallas kernels, body(): call(far_kernel, [((node_count, features), BF16)], [two_tables, pltpu.VME...  2.25 us
    pallas_call x1, Pallas kernels, body(): call(functools.partial(far_pool_kernel, grid), [table, *[((grid.packet, f...  1.63 us
    ppermute x1, waiting for transfers between devices, trade_packets(): over = lax.ppermute(far, 'sub', pairs)  1.34 us
    pallas_call x1, Pallas kernels, body(): call(turn_kernel, [table], [pltpu.VMEM((node_count, features), BF16), plt...  1.28 us
  transfers between devices with their start and end apart: 12, of which 6 were waited for; matrix products, arithmetic and copies ran while one was open for 0% of the time, Pallas kernels for 20%

profile of v12, /device:TPU:0, one launch (start us, length us, event | category | flops | bytes accessed | tf_op | source)
XLA Modules:
  0.0 37.7 jit_solution(3790138451017172227)
XLA Ops:
  0.0 1.3 %turn.1.table_ref = bf16[128,2048]{1,0:T(8,128)(2,1)S(1)} custom-call(bf16[2048,128]{1,0:T(8,128)(2,1)} %latent_hbm.1), custom_call_target="tpu_custom_call" | custom-call | bytes 4194304 | tf_op jit(solution)/shard_map/turn/pallas_call | solution.py:534
  1.3 0.0 copy-start.2
  1.3 0.0 copy-start.6
  1.4 0.0 copy-start.7
  1.4 0.8 %send.1 = (bf16[128,256]{1,0:T(8,128)(2,1)S(1)}, bf16[128,256]{1,0:T(8,128)(2,1)S(1)}, bf16[128,256]{1,0:T(8,128)(2,1)S(1)}) custom-call(bf16[128,2048]{1,0:T(8,128)(2,1)S(1)} %turn.1.table_ref, s32[1,4,256]{2,1,0:T(4,128)S(1)} %copy-done.8, bf16[2,4,128,128]{3,2,1,0:T(8,128)(2,1)S(1)} %copy-done), custom_call_target="tpu_custom_call" | custom-call | flops 1073741824 | bytes 4194304 | tf_op jit(solution)/shard_map/send/pallas_call | solution.py:542
  2.2 0.0 copy-start.10
  2.2 0.0 copy-start.9
  2.2 5.1 %collective-permute-start = (bf16[128,256]{1,0:T(8,128)(2,1)S(1)}, bf16[128,256]{1,0:T(8,128)(2,1)S(1)}, u32[]{:S(2)}, u32[]{:S(2)}) collective-permute-start(bf16[128,256]{1,0:T(8,128)(2,1)S(1)} %get-tuple-element.39), channel_id=1, source_target_pairs={{0,12},{4,8},{8,4},{12,0},{1,13},{5,9},{9,5},{13,1},{2,14},{6,10},... | collective-permute-start | bytes 196616 | tf_op jit(solution)/shard_map/ppermute | solution.py:485
  7.3 0.6 %collective-permute-start.2 = (bf16[128,256]{1,0:T(8,128)(2,1)S(1)}, bf16[128,256]{1,0:T(8,128)(2,1)S(1)}, u32[]{:S(2)}, u32[]{:S(2)}) collective-permute-start(bf16[128,256]{1,0:T(8,128)(2,1)S(1)} %get-tuple-element.41), channel_id=1, source_target_pairs={{0,4},{4,0},{8,12},{12,8},{1,5},{5,1},{9,13},{13,9},{2,6},{6,2},{1... | collective-permute-start | bytes 196616 | tf_op jit(solution)/shard_map/ppermute | solution.py:485
  8.0 3.1 %near.1 = (s32[2,1536]{1,0:T(2,128)S(1)}, s32[2,1536]{1,0:T(2,128)S(1)}, bf16[128,3072]{1,0:T(8,128)(2,1)S(1)}, f32[128,2048]{1,0:T(8,128)S(1)}, s32[1,64]{1,0:T...) custom-call(bf16[128,2048]{1,0:T(8,128)(2,1)S(1)} %turn.1.table_ref, s32[16,768]{1,0:T(8,128)S(1)} %copy-done.2, ...), custom_call_target="tpu_custom_call" | custom-call | flops 4294967296 | bytes 4194304 | tf_op jit(solution)/shard_map/near/pallas_call | solution.py:546
  11.1 1.8 %collective-permute-done.1.rest_3_ = bf16[128,256]{1,0:T(8,128)(2,1)S(1)} collective-permute-done((bf16[128,256]{1,0:T(8,128)(2,1)S(1)}, bf16[128,256]{1,0:T(8,128)(2,1)S(1)}, u32[]{:S(2)}, u32[]{:S(2)}) %collective-permute-start.1) | collective-permute-done | bytes 65568 | tf_op jit(solution)/shard_map/ppermute | solution.py:485
  12.9 1.6 %far_pool.1 = (bf16[128,2048]{1,0:T(8,128)(2,1)S(1)}, bf16[80,128]{1,0:T(8,128)(2,1)S(1)}, bf16[80,128]{1,0:T(8,128)(2,1)S(1)}) custom-call(bf16[128,2048]{1,0:T(8,128)(2,1)S(1)} %turn.1.table_ref, bf16[128,3072]{1,0:T(8,128)(2,1)S(1)} %get-tuple-element.32.aimed_ref, s32[2,1536]{1,0:T(2,128)S(1)} %get-tuple-element.33.sources_ref, ...), custom_call_target="tpu_custom_call" | custom-call | flops 2147483648 | bytes 4194304 | tf_op jit(solution)/shard_map/far_pool/pallas_call | solution.py:560
  14.6 1.0 %collective-permute-start.5 = (bf16[80,128]{1,0:T(8,128)(2,1)S(1)}, bf16[80,128]{1,0:T(8,128)(2,1)S(1)}, u32[]{:S(2)}, u32[]{:S(2)}) collective-permute-start(bf16[80,128]{1,0:T(8,128)(2,1)S(1)} %get-tuple-element.44), channel_id=1, source_target_pairs={{0,3},{1,2},{2,1},{3,0},{4,7},{5,6},{6,5},{7,4},{8,11},{9,10},{10,... | collective-permute-start | bytes 61448 | tf_op jit(solution)/shard_map/ppermute | solution.py:496
  15.5 0.6 %collective-permute-start.4 = (bf16[80,128]{1,0:T(8,128)(2,1)S(1)}, bf16[80,128]{1,0:T(8,128)(2,1)S(1)}, u32[]{:S(2)}, u32[]{:S(2)}) collective-permute-start(bf16[80,128]{1,0:T(8,128)(2,1)S(1)} %get-tuple-element.44), channel_id=1, source_target_pairs={{0,2},{2,0},{1,3},{3,1},{4,6},{6,4},{5,7},{7,5},{8,10},{10,8},{9,1... | collective-permute-start | bytes 61448 | tf_op jit(solution)/shard_map/ppermute | solution.py:494
  16.2 0.3 collective-permute-start.3
  16.5 0.6 %ahead.1.ahead_ref = bf16[144,768]{1,0:T(8,128)(2,1)S(1)} custom-call(bf16[128,2048]{1,0:T(8,128)(2,1)S(1)} %get-tuple-element.42.first_ref, s32[16,128]{1,0:T(8,128)S(1)} %bitcast.1, s32[1,4,256]{2,1,0:T(4,128)S(1)} %copy-done.8), custom_call_target="tpu_custom_call" | custom-call | flops 1073741824 | bytes 4194304 | tf_op jit(solution)/shard_map/ahead/pallas_call | solution.py:568
  17.1 0.9 %collective-permute-done.5.refs_3_ = bf16[80,128]{1,0:T(8,128)(2,1)S(1)} collective-permute-done((bf16[80,128]{1,0:T(8,128)(2,1)S(1)}, bf16[80,128]{1,0:T(8,128)(2,1)S(1)}, u32[]{:S(2)}, u32[]{:S(2)}) %collective-permute-start.5) | collective-permute-done | bytes 20512 | tf_op jit(solution)/shard_map/ppermute | solution.py:496
  18.0 1.3 %collective-permute-done.4.refs_2_ = bf16[80,128]{1,0:T(8,128)(2,1)S(1)} collective-permute-done((bf16[80,128]{1,0:T(8,128)(2,1)S(1)}, bf16[80,128]{1,0:T(8,128)(2,1)S(1)}, u32[]{:S(2)}, u32[]{:S(2)}) %collective-permute-start.4) | collective-permute-done | bytes 20512 | tf_op jit(solution)/shard_map/ppermute | solution.py:494
  19.3 0.4 coarse_send.1
  19.7 0.8 %collective-permute-start.6 = (bf16[128,128]{1,0:T(8,128)(2,1)S(1)}, bf16[128,128]{1,0:T(8,128)(2,1)S(1)}, u32[]{:S(2)}, u32[]{:S(2)}) collective-permute-start(bf16[128,128]{1,0:T(8,128)(2,1)S(1)} %get-tuple-element.49), channel_id=1, source_target_pairs={{0,8},{4,12},{8,0},{12,4},{1,9},{5,13},{9,1},{13,5},{2,10},{6,14},... | collective-permute-start | bytes 98312 | tf_op jit(solution)/shard_map/ppermute | solution.py:485
  20.5 1.9 %collective-permute-start.7 = (bf16[128,128]{1,0:T(8,128)(2,1)S(1)}, bf16[128,128]{1,0:T(8,128)(2,1)S(1)}, u32[]{:S(2)}, u32[]{:S(2)}) collective-permute-start(bf16[128,128]{1,0:T(8,128)(2,1)S(1)} %get-tuple-element.50), channel_id=1, source_target_pairs={{0,12},{4,8},{8,4},{12,0},{1,13},{5,9},{9,5},{13,1},{2,14},{6,10},... | collective-permute-start | bytes 98312 | tf_op jit(solution)/shard_map/ppermute | solution.py:485
  22.4 0.9 %collective-permute-start.8 = (bf16[128,128]{1,0:T(8,128)(2,1)S(1)}, bf16[128,128]{1,0:T(8,128)(2,1)S(1)}, u32[]{:S(2)}, u32[]{:S(2)}) collective-permute-start(bf16[128,128]{1,0:T(8,128)(2,1)S(1)} %get-tuple-element.51), channel_id=1, source_target_pairs={{0,4},{4,0},{8,12},{12,8},{1,5},{5,1},{9,13},{13,9},{2,6},{6,2},{1... | collective-permute-start | bytes 98312 | tf_op jit(solution)/shard_map/ppermute | solution.py:485
  23.3 0.5 %coarse_own.1 = (f32[1,128,768]{2,1,0:T(8,128)S(1)}, s32[1,768]{1,0:T(1,128)S(1)}, s32[1,768]{1,0:T(1,128)S(1)}, bf16[1,128,64]{2,1,0:T(8,128)(2,1)S(1)}) custom-call(bf16[4,128,128]{2,1,0:T(8,128)(2,1)S(1)} %copy-done.1, bf16[80,128]{1,0:T(8,128)(2,1)S(1)} %get-tuple-element.43.refs_0_, bf16[80,128]{1,0:T(8,128)(2,1)S(1)} %collective-permute-done.3.refs_1_, ...), custom_call_target="tpu_custom_call" | custom-call | flops 4294967296 | bytes 4194304 | tf_op jit(solution)/shard_map/coarse_own/pallas_call | solution.py:580
  23.7 1.2 %collective-permute-done.6.rest_0_ = bf16[128,128]{1,0:T(8,128)(2,1)S(1)} collective-permute-done((bf16[128,128]{1,0:T(8,128)(2,1)S(1)}, bf16[128,128]{1,0:T(8,128)(2,1)S(1)}, u32[]{:S(2)}, u32[]{:S(2)}) %collective-permute-start.6) | collective-permute-done | bytes 32800 | tf_op jit(solution)/shard_map/ppermute | solution.py:485
  24.9 1.4 %collective-permute-done.7.rest_1_ = bf16[128,128]{1,0:T(8,128)(2,1)S(1)} collective-permute-done((bf16[128,128]{1,0:T(8,128)(2,1)S(1)}, bf16[128,128]{1,0:T(8,128)(2,1)S(1)}, u32[]{:S(2)}, u32[]{:S(2)}) %collective-permute-start.7) | collective-permute-done | bytes 32800 | tf_op jit(solution)/shard_map/ppermute | solution.py:485
  26.2 0.3 collective-permute-done.8.rest_2_
  26.6 1.1 %lift_halo.1 = (bf16[128,128]{1,0:T(8,128)(2,1)S(1)}, bf16[128,256]{1,0:T(8,128)(2,1)S(1)}, bf16[128,256]{1,0:T(8,128)(2,1)S(1)}, bf16[128,256]{1,0:T(8,128)(2,1)S(1)}) custom-call(f32[1,128,768]{2,1,0:T(8,128)S(1)} %get-tuple-element.45.picked_ref, s32[1,768]{1,0:T(1,128)S(1)} %get-tuple-element.46.source_ref, s32[1,768]{1,0:T(1,128)S(1)} %get-tuple-element.47.place_ref, ...), custom_call_target="tpu_custom_call" | custom-call | flops 1073741824 | bytes 4194304 | tf_op jit(solution)/shard_map/lift_halo/pallas_call | solution.py:592
  27.7 1.9 %collective-permute-start.9 = (bf16[128,256]{1,0:T(8,128)(2,1)S(1)}, bf16[128,256]{1,0:T(8,128)(2,1)S(1)}, u32[]{:S(2)}, u32[]{:S(2)}) collective-permute-start(bf16[128,256]{1,0:T(8,128)(2,1)S(1)} %get-tuple-element.56), channel_id=1, source_target_pairs={{0,12},{4,8},{8,4},{12,0},{1,13},{5,9},{9,5},{13,1},{2,14},{6,10},... | collective-permute-start | bytes 196616 | tf_op jit(solution)/shard_map/ppermute | solution.py:485
  29.6 2.5 %collective-permute-start.11 = (bf16[128,256]{1,0:T(8,128)(2,1)S(1)}, bf16[128,256]{1,0:T(8,128)(2,1)S(1)}, u32[]{:S(2)}, u32[]{:S(2)}) collective-permute-start(bf16[128,256]{1,0:T(8,128)(2,1)S(1)} %get-tuple-element.58), channel_id=1, source_target_pairs={{0,8},{4,12},{8,0},{12,4},{1,9},{5,13},{9,1},{13,5},{2,10},{6,14},... | collective-permute-start | bytes 196616 | tf_op jit(solution)/shard_map/ppermute | solution.py:485
  32.2 3.2 %lift_near.1 = (bf16[128,2048]{1,0:T(8,128)(2,1)S(1)}, bf16[128,3072]{1,0:T(8,128)(2,1)S(1)}, f32[128,2048]{1,0:T(8,128)S(1)}) custom-call(bf16[128,2048]{1,0:T(8,128)(2,1)S(1)} %get-tuple-element.42.first_ref, bf16[128,128]{1,0:T(8,128)(2,1)S(1)} %get-tuple-element.52.prolonged_ref, s32[16,128]{1,0:T(8,128)S(1)} %bitcast.2, s32[16,768]{1,0:T(8,128)S(1)} %copy-done.2, ...), custom_call_target="tpu_custom_call" | custom-call | flops 4294967296 | bytes 4194304 | tf_op jit(solution)/shard_map/lift_near/pallas_call | solution.py:599
  35.4 0.0 collective-permute-done.11.rest_2_
  35.5 2.3 %far.1 = bf16[2048,128]{1,0:T(8,128)(2,1)} custom-call(bf16[128,2048]{1,0:T(8,128)(2,1)S(1)} %get-tuple-element.53.table_ref, bf16[128,3072]{1,0:T(8,128)(2,1)S(1)} %get-tuple-element.54.aimed_ref, s32[2,1536]{1,0:T(2,128)S(1)} %get-tuple-element.33.sources_ref, s32[2,1536]{1,0:T(2,128)S(1)} %get-tuple-element.34.places_ref, ...), custom_call_target="tpu_custom_call" | custom-call | flops 2147483648 | bytes 4194304 | tf_op jit(solution)/shard_map/far/pallas_call | solution.py:606
  (24 shorter events, 0.1 us)
Async XLA Ops:
  0.0 1.3 %copy-start = (bf16[2,4,128,128]{3,2,1,0:T(8,128)(2,1)S(1)}, bf16[2,4,128,128]{3,2,1,0:T(8,128)(2,1)}, u32[]{:S(2)}) copy-start(bf16[2,4,128,128]{3,2,1,0:T(8,128)(2,1)} %weights_ref.15) | copy-start | bytes 786436
  0.0 1.3 %copy-start.8 = (s32[1,4,256]{2,1,0:T(4,128)S(1)}, s32[1,4,256]{2,1,0:T(4,128)}, u32[]{:S(2)}) copy-start(s32[1,4,256]{2,1,0:T(4,128)} %lists_ref.3) | copy-start | bytes 12292
  1.3 6.6 %copy-start.2 = (s32[16,768]{1,0:T(8,128)S(1)}, s32[16,768]{1,0:T(8,128)}, u32[]{:S(2)}) copy-start(s32[16,768]{1,0:T(8,128)} %source_ref.3) | copy-start | bytes 147460
  1.3 6.6 %copy-start.3 = (s32[16,768]{1,0:T(8,128)S(1)}, s32[16,768]{1,0:T(8,128)}, u32[]{:S(2)}) copy-start(s32[16,768]{1,0:T(8,128)} %place_ref.3) | copy-start | bytes 147460
  1.3 6.6 %copy-start.6 = (s32[2,768]{1,0:T(2,128)S(1)}, s32[2,768]{1,0:T(2,128)}, u32[]{:S(2)}) copy-start(s32[2,768]{1,0:T(2,128)} %coarse_source_ref.1) | copy-start | bytes 18436
  1.4 6.6 %copy-start.7 = (s32[2,768]{1,0:T(2,128)S(1)}, s32[2,768]{1,0:T(2,128)}, u32[]{:S(2)}) copy-start(s32[2,768]{1,0:T(2,128)} %coarse_place_ref.1) | copy-start | bytes 18436
  2.2 5.8 %copy-start.10 = (s32[1,4,64]{2,1,0:T(4,128)S(1)}, s32[1,4,64]{2,1,0:T(4,128)}, u32[]{:S(2)}) copy-start(s32[1,4,64]{2,1,0:T(4,128)} %pool_ref.1) | copy-start | bytes 3076
  2.2 5.8 %copy-start.9 = (s32[1,4,128]{2,1,0:T(4,128)S(1)}, s32[1,4,128]{2,1,0:T(4,128)}, u32[]{:S(2)}) copy-start(s32[1,4,128]{2,1,0:T(4,128)} %coarse_send_ref.1) | copy-start | bytes 6148
  2.2 8.9 %collective-permute-start = (bf16[128,256]{1,0:T(8,128)(2,1)S(1)}, bf16[128,256]{1,0:T(8,128)(2,1)S(1)}, u32[]{:S(2)}, u32[]{:S(2)}) collective-permute-start(bf16[128,256]{1,0:T(8,128)(2,1)S(1)} %get-tuple-element.39), channel_id=1, source_target_pairs={{0,12},{4,8},{8,4},{12,0},{1,13},{5,9},{9,5},{13,1},{2,14},{6,10},... | collective-permute-start | bytes 196616 | tf_op jit(solution)/shard_map/ppermute | solution.py:485
  7.3 5.6 %collective-permute-start.1 = (bf16[128,256]{1,0:T(8,128)(2,1)S(1)}, bf16[128,256]{1,0:T(8,128)(2,1)S(1)}, u32[]{:S(2)}, u32[]{:S(2)}) collective-permute-start(bf16[128,256]{1,0:T(8,128)(2,1)S(1)} %get-tuple-element.40), channel_id=1, source_target_pairs={{0,8},{4,12},{8,0},{12,4},{1,9},{5,13},{9,1},{13,5},{2,10},{6,14},... | collective-permute-start | bytes 196616 | tf_op jit(solution)/shard_map/ppermute | solution.py:485
  7.3 5.6 %collective-permute-start.2 = (bf16[128,256]{1,0:T(8,128)(2,1)S(1)}, bf16[128,256]{1,0:T(8,128)(2,1)S(1)}, u32[]{:S(2)}, u32[]{:S(2)}) collective-permute-start(bf16[128,256]{1,0:T(8,128)(2,1)S(1)} %get-tuple-element.41), channel_id=1, source_target_pairs={{0,4},{4,0},{8,12},{12,8},{1,5},{5,1},{9,13},{13,9},{2,6},{6,2},{1... | collective-permute-start | bytes 196616 | tf_op jit(solution)/shard_map/ppermute | solution.py:485
  12.9 3.5 %copy-start.5 = (s32[2048]{0:T(1024)S(1)}, s32[2048]{0:T(1024)}, u32[]{:S(2)}) copy-start(s32[2048]{0:T(1024)} %param.20) | copy-start | bytes 24580
  14.6 3.4 %collective-permute-start.5 = (bf16[80,128]{1,0:T(8,128)(2,1)S(1)}, bf16[80,128]{1,0:T(8,128)(2,1)S(1)}, u32[]{:S(2)}, u32[]{:S(2)}) collective-permute-start(bf16[80,128]{1,0:T(8,128)(2,1)S(1)} %get-tuple-element.44), channel_id=1, source_target_pairs={{0,3},{1,2},{2,1},{3,0},{4,7},{5,6},{6,5},{7,4},{8,11},{9,10},{10,... | collective-permute-start | bytes 61448 | tf_op jit(solution)/shard_map/ppermute | solution.py:496
  15.5 3.8 %collective-permute-start.4 = (bf16[80,128]{1,0:T(8,128)(2,1)S(1)}, bf16[80,128]{1,0:T(8,128)(2,1)S(1)}, u32[]{:S(2)}, u32[]{:S(2)}) collective-permute-start(bf16[80,128]{1,0:T(8,128)(2,1)S(1)} %get-tuple-element.44), channel_id=1, source_target_pairs={{0,2},{2,0},{1,3},{3,1},{4,6},{6,4},{5,7},{7,5},{8,10},{10,8},{9,1... | collective-permute-start | bytes 61448 | tf_op jit(solution)/shard_map/ppermute | solution.py:494
  16.2 3.2 %collective-permute-start.3 = (bf16[80,128]{1,0:T(8,128)(2,1)S(1)}, bf16[80,128]{1,0:T(8,128)(2,1)S(1)}, u32[]{:S(2)}, u32[]{:S(2)}) collective-permute-start(bf16[80,128]{1,0:T(8,128)(2,1)S(1)} %get-tuple-element.43.refs_0_), channel_id=1, source_target_pairs={{0,1},{1,0},{2,3},{3,2},{4,5},{5,4},{6,7},{7,6},{8,9},{9,8},{10,11... | collective-permute-start | bytes 61448 | tf_op jit(solution)/shard_map/ppermute | solution.py:495
  16.5 2.9 %copy-start.1 = (bf16[4,128,128]{2,1,0:T(8,128)(2,1)S(1)}, bf16[4,128,128]{2,1,0:T(8,128)(2,1)}, u32[]{:S(2)}) copy-start(bf16[4,128,128]{2,1,0:T(8,128)(2,1)} %coarse_weights_ref.1) | copy-start | bytes 393220
  19.7 5.2 %collective-permute-start.6 = (bf16[128,128]{1,0:T(8,128)(2,1)S(1)}, bf16[128,128]{1,0:T(8,128)(2,1)S(1)}, u32[]{:S(2)}, u32[]{:S(2)}) collective-permute-start(bf16[128,128]{1,0:T(8,128)(2,1)S(1)} %get-tuple-element.49), channel_id=1, source_target_pairs={{0,8},{4,12},{8,0},{12,4},{1,9},{5,13},{9,1},{13,5},{2,10},{6,14},... | collective-permute-start | bytes 98312 | tf_op jit(solution)/shard_map/ppermute | solution.py:485
  20.5 5.7 %collective-permute-start.7 = (bf16[128,128]{1,0:T(8,128)(2,1)S(1)}, bf16[128,128]{1,0:T(8,128)(2,1)S(1)}, u32[]{:S(2)}, u32[]{:S(2)}) collective-permute-start(bf16[128,128]{1,0:T(8,128)(2,1)S(1)} %get-tuple-element.50), channel_id=1, source_target_pairs={{0,12},{4,8},{8,4},{12,0},{1,13},{5,9},{9,5},{13,1},{2,14},{6,10},... | collective-permute-start | bytes 98312 | tf_op jit(solution)/shard_map/ppermute | solution.py:485
  22.4 4.2 %copy-start.4 = (bf16[128,128]{1,0:T(8,128)(2,1)S(1)}, bf16[128,128]{1,0:T(8,128)(2,1)}, u32[]{:S(2)}) copy-start(bf16[128,128]{1,0:T(8,128)(2,1)} %prolong_weight_ref.1) | copy-start | bytes 98308
  22.4 4.2 %collective-permute-start.8 = (bf16[128,128]{1,0:T(8,128)(2,1)S(1)}, bf16[128,128]{1,0:T(8,128)(2,1)S(1)}, u32[]{:S(2)}, u32[]{:S(2)}) collective-permute-start(bf16[128,128]{1,0:T(8,128)(2,1)S(1)} %get-tuple-element.51), channel_id=1, source_target_pairs={{0,4},{4,0},{8,12},{12,8},{1,5},{5,1},{9,13},{13,9},{2,6},{6,2},{1... | collective-permute-start | bytes 98312 | tf_op jit(solution)/shard_map/ppermute | solution.py:485
  27.7 7.7 %collective-permute-start.9 = (bf16[128,256]{1,0:T(8,128)(2,1)S(1)}, bf16[128,256]{1,0:T(8,128)(2,1)S(1)}, u32[]{:S(2)}, u32[]{:S(2)}) collective-permute-start(bf16[128,256]{1,0:T(8,128)(2,1)S(1)} %get-tuple-element.56), channel_id=1, source_target_pairs={{0,12},{4,8},{8,4},{12,0},{1,13},{5,9},{9,5},{13,1},{2,14},{6,10},... | collective-permute-start | bytes 196616 | tf_op jit(solution)/shard_map/ppermute | solution.py:485
  29.6 5.8 %collective-permute-start.10 = (bf16[128,256]{1,0:T(8,128)(2,1)S(1)}, bf16[128,256]{1,0:T(8,128)(2,1)S(1)}, u32[]{:S(2)}, u32[]{:S(2)}) collective-permute-start(bf16[128,256]{1,0:T(8,128)(2,1)S(1)} %get-tuple-element.57), channel_id=1, source_target_pairs={{0,4},{4,0},{8,12},{12,8},{1,5},{5,1},{9,13},{13,9},{2,6},{6,2},{1... | collective-permute-start | bytes 196616 | tf_op jit(solution)/shard_map/ppermute | solution.py:485
  29.6 5.8 %collective-permute-start.11 = (bf16[128,256]{1,0:T(8,128)(2,1)S(1)}, bf16[128,256]{1,0:T(8,128)(2,1)S(1)}, u32[]{:S(2)}, u32[]{:S(2)}) collective-permute-start(bf16[128,256]{1,0:T(8,128)(2,1)S(1)} %get-tuple-element.58), channel_id=1, source_target_pairs={{0,8},{4,12},{8,0},{12,4},{1,9},{5,13},{9,1},{13,5},{2,10},{6,14},... | collective-permute-start | bytes 196616 | tf_op jit(solution)/shard_map/ppermute | solution.py:485
